TPU v7x, 128 devices: a whole 4x4x4 slice. The times are simulated.
128 devices in a mesh: req: 8 (over y_lo, x), patch: 16 (over y_hi, z, core).
Axes of the slice: x: 4, y: 4 (y_hi: 2, y_lo: 2; y = y_hi * 2 + y_lo), z: 4, core: 2. Of those that a mesh axis runs over, the one named last changes fastest.
Arguments:
- latent: bfloat16 [16384, 1536], P(('req', 'patch')), parts along dimension 0, may hold values from -6 to 6
- stale_kv: bfloat16 [16384, 3072], P(('req', 'patch')), parts along dimension 0, may hold values from -6 to 6
- timesteps: int32 [16], P('req'), parts along dimension 0, may hold values from 0 to 999
- counts: int32 [128], P('req'), parts along dimension 0, may hold values from 1 to 128, as said below
- conv_weight: float32 [3, 1536], replicated, may hold values from -3 to 3
- w_mod: float32 [256, 4608], replicated, may hold values from -0.375 to 0.375
- w_qkv: bfloat16 [1536, 4608], replicated
- q_gain: float32 [1536], replicated, may hold values from 0.5 to 4.5
- k_gain: float32 [1536], replicated, may hold values from 0.5 to 4.5
- w_out: bfloat16 [1536, 1536], replicated, may hold values from -0.15625 to 0.15625
Outputs:
- latent_out: bfloat16 [16384, 1536], P(('req', 'patch')), parts along dimension 0
- next_cache: bfloat16 [16384, 3072], P(('req', 'patch')), parts along dimension 0
There are 8 independent parts, one for each index of `req`. A program takes and returns all parts, laid end to end along the dimension named above; an argument that names none is the same for every part. Nothing has to cross between parts.
Inputs may be any that keep to these rules, and one draw needn't show every extreme that they name: `counts`: some slab holds 128 live tokens.
All inputs are finite; a program needn't handle non-finite values.
Results may differ from a plain program's by a relative error of at most 0.0085.
Values may be sent and summed in bfloat16 or wider, within the bound.
No kernel may reach another device: no remote copies, remote signals or barrier semaphores. Data moves between devices by JAX's collectives and lax.ppermute only.
A program may use at most 192 MiB of HBM per device.

v0:
```python
import math

import jax
import jax.numpy as jnp
from jax import lax
from jax.sharding import PartitionSpec as P

HEAD = 128
FREQ = 256
FRAME = 80
STEPS = 2


epsilon = 1e-06
masked_score = -1e30


def padded_2(block, sides, width):
    for axis, dim in sides:
        count = lax.axis_size(axis)
        forward = [(i, i + 1) for i in range(count - 1)]
        backward = [(target, source) for source, target in forward]
        low = lax.ppermute(
            lax.slice_in_dim(block, block.shape[dim] - width, None, axis=dim), axis, forward
        )
        high = lax.ppermute(lax.slice_in_dim(block, 0, width, axis=dim), axis, backward)
        block = jnp.concatenate([low, block, high], axis=dim)
    return block


def embedding(moment):
    halfway = FREQ // 2
    frequency = jnp.exp(-math.log(10000.0) * jnp.arange(halfway, dtype=jnp.float32) / halfway)
    angles = moment.astype(jnp.float32) * frequency
    return jnp.concatenate([jnp.cos(angles), jnp.sin(angles)])


def modulation(moment, w_mod):
    activated = jax.nn.silu(embedding(moment))[None, :]
    mod_terms = jnp.dot(
        activated, w_mod, precision=lax.Precision.HIGHEST, preferred_element_type=jnp.float32
    )[0]
    features = w_mod.shape[1] // 3
    return (mod_terms[:features], mod_terms[features : 2 * features], mod_terms[2 * features :])


def layer_normed(mixed_rows, shift_vec, scale_vec):
    centred = mixed_rows - jnp.mean(mixed_rows, -1, keepdims=True)
    variance = jnp.mean(centred * centred, -1, keepdims=True)
    return (centred * lax.rsqrt(variance + epsilon) * (1.0 + scale_vec) + shift_vec).astype(
        jnp.bfloat16
    )


def head_normed(projected, gain, heads_count):
    count_rows = projected.shape[0]
    split_rows = projected.reshape(count_rows, heads_count, -1)
    mean_square = jnp.mean(split_rows * split_rows, -1, keepdims=True)
    return (split_rows * lax.rsqrt(mean_square + epsilon) * gain.reshape(heads_count, -1)).astype(
        jnp.bfloat16
    )


def convolved(hidden_state, conv_weight, padded):
    count_rows = hidden_state.shape[0]
    as_float = hidden_state.astype(jnp.float32)
    before = padded[:count_rows].astype(jnp.float32)
    after_rows = padded[2 * FRAME :].astype(jnp.float32)
    return (
        as_float + conv_weight[0] * before + conv_weight[1] * as_float + conv_weight[2] * after_rows
    )


def attend(running, queries, keys_block, values_block, usable):
    highest, denominator, summed = running
    scores = jnp.einsum("qhd,khd->qhk", queries, keys_block, preferred_element_type=jnp.float32) * (
        1.0 / math.sqrt(queries.shape[2])
    )
    scores = jnp.where(usable[None, None, :], scores, masked_score)
    new_highest = jnp.maximum(highest, jnp.max(scores, -1))
    weights = jnp.where(usable[None, None, :], jnp.exp(scores - new_highest[:, :, None]), 0.0)
    factor = jnp.exp(highest - new_highest)
    denominator = denominator * factor + jnp.sum(weights, -1)
    summed = summed * factor[:, :, None] + jnp.einsum(
        "qhk,khd->qhd",
        weights.astype(jnp.bfloat16),
        values_block,
        preferred_element_type=jnp.float32,
    )
    return (new_highest, denominator, summed)


def remote_usable(count_rows, slab_rows, counts, own_slab):
    key_index = jnp.arange(count_rows, dtype=jnp.int32)
    slab_of = key_index // slab_rows
    places = jnp.arange(counts.shape[0], dtype=jnp.int32)
    live_limit = jnp.sum(jnp.where(slab_of[:, None] == places[None, :], counts[None, :], 0), 1)
    return (key_index - slab_of * slab_rows < live_limit) & (slab_of != own_slab)


def shards(latent, stale_kv, timesteps, counts, conv_weight, w_mod, w_qkv, q_gain, k_gain, w_out):
    slab_rows = latent.shape[0]
    head_total = w_out.shape[0]
    heads_count = head_total // HEAD
    own_slab = lax.axis_index("patch")
    places = jnp.arange(counts.shape[0], dtype=jnp.int32)
    own_count = jnp.sum(jnp.where(places == own_slab, counts, 0))
    own_usable = jnp.arange(slab_rows, dtype=jnp.int32) < own_count
    hidden_state = latent
    cache_rows = stale_kv
    for step_index in range(STEPS):
        padded = padded_2(hidden_state, (("patch", 0),), FRAME)
        mixed_rows = convolved(hidden_state, conv_weight, padded)
        shift_vec, scale_vec, gate_vec = modulation(timesteps[step_index], w_mod)
        normed = layer_normed(mixed_rows, shift_vec, scale_vec)
        projected = jnp.dot(normed, w_qkv, preferred_element_type=jnp.float32)
        queries = head_normed(projected[:, :head_total], q_gain, heads_count)
        fresh_keys = head_normed(projected[:, head_total : 2 * head_total], k_gain, heads_count)
        fresh_values = (
            projected[:, 2 * head_total :]
            .reshape(slab_rows, heads_count, HEAD)
            .astype(jnp.bfloat16)
        )
        start_state = (
            jnp.full((slab_rows, heads_count), masked_score, jnp.float32),
            jnp.zeros((slab_rows, heads_count), jnp.float32),
            jnp.zeros((slab_rows, heads_count, HEAD), jnp.float32),
        )
        running = attend(start_state, queries, fresh_keys, fresh_values, own_usable)

        def cached_step(carried, block_rows):
            count_rows = block_rows.shape[0]
            keys_block = block_rows[:, :head_total].reshape(count_rows, heads_count, HEAD)
            values_block = block_rows[:, head_total:].reshape(count_rows, heads_count, HEAD)
            return attend(
                carried,
                queries,
                keys_block,
                values_block,
                remote_usable(count_rows, slab_rows, counts, own_slab),
            )

        if step_index == 0:
            running = cached_step(running, lax.all_gather(cache_rows, "patch", axis=0, tiled=True))
        else:
            running = cached_step(running, lax.all_gather(cache_rows, "patch", axis=0, tiled=True))
        highest, denominator, summed = running
        attended = (
            (summed / denominator[:, :, None]).astype(jnp.bfloat16).reshape(slab_rows, head_total)
        )
        output_rows = jnp.dot(attended, w_out, preferred_element_type=jnp.float32)
        hidden_state = (mixed_rows + gate_vec * output_rows).astype(jnp.bfloat16)
        cache_rows = jnp.concatenate(
            [
                fresh_keys.reshape(slab_rows, head_total),
                fresh_values.reshape(slab_rows, head_total),
            ],
            1,
        )
    return (hidden_state, cache_rows)


def solution(mesh):
    return jax.shard_map(
        shards,
        mesh=mesh,
        in_specs=(
            P(("req", "patch"), None),
            P(("req", "patch"), None),
            P("req"),
            P("req"),
            P(),
            P(),
            P(),
            P(),
            P(),
            P(),
        ),
        out_specs=(P(("req", "patch"), None), P(("req", "patch"), None)),
        check_vma=False,
    )
```

profile of v0, /device:TPU:0, one launch (start us, length us, event | category | flops | bytes accessed | tf_op | source)
XLA Modules:
  0.0 262.5 jit_solution(7277388630337968330)
XLA Ops:
  7.2 2.3 copy.54
  15.4 4.7 %convolution_reduce_fusion.1 = f32[4608]{0:T(1024)S(1)} fusion(f32[256,1]{0,1:T(1,128)S(1)} %bitcast.129, f32[256,4608]{1,0:T(8,128)} %param.15), kind=kOutput, calls=%fused_computation.47 | convolution fusion | flops 14155776 | bytes 4738048 | tf_op jit(solution)/shard_map/dot_general | solution.py:40
  21.0 1.6 fusion.97
  22.6 1.6 multiply_reduce_fusion.5
  24.2 7.6 %fusion.50 = f32[128,4608]{1,0:T(8,128)S(1)} fusion(bf16[1536,4608]{1,0:T(8,128)(2,1)} %param.16, f32[1536]{0:T(1024)S(1)} %get-tuple-element.25, f32[1536]{0:T(1024)S(1)} %get-tuple-element.26, f32[128]{0:T(128)S(1)} %add_rsqrt_fusion.5, f32[128]{0:T(128)S(1)} %broadcast_multiply_fusion.1, bf16[128,1536]{1,0:T(8,128)(2,1)} %param.10, ...), kind=kOutput, calls=%fused_computation.80 | convolution fusion | flops 1815871488 | bytes 17431552 | tf_op jit(solution)/shard_map/dot_general | solution.py:116
  36.0 2.3 copy.63
  38.3 2.2 fusion.100
  40.5 1.9 pad_maximum_fusion
  44.6 1.9 copy.52
  48.8 62.1 %all-gather.3.cloned.1.call-done = bf16[2048,3072]{0,1:T(8,128)(2,1)} async-done(((bf16[128,3072]{0,1:T(8,128)(2,1)}), bf16[2048,3072]{0,1:T(8,128)(2,1)}) %all-gather.3.cloned.1.call-update) | async-done | bytes 12582928 | tf_op jit(solution)/shard_map/all_gather | solution.py:144
  110.9 8.4 %fusion.98 = (bf16[2048,1536]{0,1:T(8,128)(2,1)S(1)}, bf16[2048,1536]{0,1:T(8,128)(2,1)}) fusion(bf16[2048,3072]{0,1:T(8,128)(2,1)} %all-gather.3.cloned.1.call-done), kind=kLoop, calls=%fused_computation.165 | loop fusion | bytes 25165824 | tf_op jit(solution)/shard_map/slice | solution.py:133
  119.3 2.6 bitcast_reduce_fusion.1
  122.1 4.3 %copy-done = f32[12,128,2048]{2,1,0:T(8,128)} copy-done((f32[12,128,2048]{2,1,0:T(8,128)}, f32[12,128,2048]{2,1,0:T(8,128)S(1)}, u32[]{:S(2)}) %copy-start) | copy-done | bytes 12582936
  126.4 3.3 %fusion.4 = f32[128,12]{0,1:T(8,128)S(1)} fusion(f32[12,128,2048]{2,1,0:T(8,128)S(1)} %get-tuple-element.38, f32[128,12]{0,1:T(8,128)S(1)} %get-tuple-element.31, pred[2048]{0:T(1024)(128)(4,1)S(1)} %fusion.75), kind=kLoop, calls=%fused_computation.10 | loop fusion | flops 15727104 | bytes 12597248 | tf_op jit(solution)/shard_map/reduce_sum | solution.py:83
  129.8 10.1 %fusion.20 = f32[128,12,128]{0,2,1:T(8,128)S(1)} fusion(bf16[2048,12,128]{0,2,1:T(8,128)(2,1)} %bitcast.115, f32[12,128,2048]{2,1,0:T(8,128)} %copy-done, f32[128,12]{0,1:T(8,128)S(1)} %get-tuple-element.31, pred[2048]{0:T(1024)(128)(4,1)S(1)} %fusion.75), kind=kOutput, calls=%fused_computation.26 | convolution fusion | flops 821035008 | bytes 19668992 | tf_op jit(solution)/shard_map/qhk,khd->qhd/dot_general | solution.py:84
  141.3 2.2 collective-permute-start.2
  143.5 1.5 collective-permute-start.3
  145.0 2.3 convolution_reduce_fusion
  148.8 8.8 %fusion.51 = f32[128,4608]{1,0:T(8,128)S(1)} fusion(bf16[1536,4608]{1,0:T(8,128)(2,1)} %param.16, f32[1536]{0:T(1024)S(1)} %get-tuple-element.22, f32[1536]{0:T(1024)S(1)} %get-tuple-element.23, f32[128]{0:T(128)S(1)} %add_rsqrt_fusion.4, f32[128]{0:T(128)S(1)} %broadcast_multiply_fusion, bf16[128,1536]{1,0:T(8,128)(2,1)S(1)} %fusion.18, ...), kind=kOutput, calls=%fused_computation.81 | convolution fusion | flops 1815871488 | bytes 17431552 | tf_op jit(solution)/shard_map/dot_general | solution.py:116
  162.3 2.3 copy.69
  164.6 2.3 multiply_convert_fusion
  167.0 1.4 copy.58
  169.7 1.6 fusion.107
  171.2 2.1 pad_maximum_fusion.1
  173.3 28.3 %all-gather.5.cloned.1.call-done = bf16[2048,3072]{1,0:T(8,128)(2,1)} async-done(((bf16[128,3072]{1,0:T(8,128)(2,1)}), bf16[2048,3072]{1,0:T(8,128)(2,1)}) %all-gather.5.cloned.1.call-update) | async-done | bytes 12582928 | tf_op jit(solution)/shard_map/all_gather | solution.py:146
  201.6 10.3 %fusion.99 = (bf16[2048,1536]{1,0:T(8,128)(2,1)}, bf16[2048,1536]{1,0:T(8,128)(2,1)}) fusion(bf16[2048,3072]{1,0:T(8,128)(2,1)} %all-gather.5.cloned.1.call-done), kind=kLoop, calls=%fused_computation.166 | loop fusion | bytes 25165824 | tf_op jit(solution)/shard_map/slice | solution.py:133
  211.8 8.7 %copy.64 = bf16[2048,1536]{0,1:T(8,128)(2,1)} copy(bf16[2048,1536]{1,0:T(8,128)(2,1)} %get-tuple-element.11) | data formatting | bytes 12582912 | tf_op jit(solution)/shard_map/slice | solution.py:133
  220.6 9.8 %bitcast_reduce_fusion = (f32[128,12]{0,1:T(8,128)S(1)}, f32[12,2048,128]{1,2,0:T(8,128)}) fusion(pred[2048]{0:T(1024)(128)(4,1)S(1)} %copy-done.16, bf16[2048,12,128]{0,2,1:T(8,128)(2,1)} %bitcast.101, f32[128,12,128]{0,2,1:T(8,128)S(1)} %bitcast.109, f32[128,12]{0,1:T(8,128)S(1)} %add_rsqrt_fusion, f32[12,128]{1,0:T(8,128)S(1)} %bitcast.125), kind=kOutput, calls=%fused_computation.1 | convolution fusion | flops 815331840 | bytes 19681280 | tf_op jit(solution)/shard_map/qhd,khd->qhk/dot_general | solution.py:76
  230.4 8.7 %copy.68 = bf16[2048,1536]{0,1:T(8,128)(2,1)} copy(bf16[2048,1536]{1,0:T(8,128)(2,1)} %get-tuple-element.12) | data formatting | bytes 12582912 | tf_op jit(solution)/shard_map/slice | solution.py:134
  239.1 7.6 %fusion.6 = f32[128,12]{0,1:T(8,128)S(1)} fusion(f32[12,2048,128]{1,2,0:T(8,128)} %get-tuple-element.42, f32[128,12]{0,1:T(8,128)S(1)} %get-tuple-element.28, pred[2048]{0:T(1024)(128)(4,1)S(1)} %copy-done.16), kind=kLoop, calls=%fused_computation.12 | loop fusion | flops 15727104 | bytes 12597248 | tf_op jit(solution)/shard_map/reduce_sum | solution.py:83
  246.8 6.5 %fusion.23 = f32[128,12,128]{0,2,1:T(8,128)S(1)} fusion(bf16[2048,12,128]{0,2,1:T(8,128)(2,1)S(1)} %bitcast.114, f32[12,2048,128]{1,2,0:T(8,128)} %get-tuple-element.42, f32[128,12]{0,1:T(8,128)S(1)} %get-tuple-element.28, pred[2048]{0:T(1024)(128)(4,1)S(1)} %copy-done.16), kind=kOutput, calls=%fused_computation.27 | convolution fusion | flops 821035008 | bytes 19668992 | tf_op jit(solution)/shard_map/qhk,khd->qhd/dot_general | solution.py:84
  253.9 1.7 fusion.19
  (117 shorter events, 23.6 us)
Async XLA Ops:
  7.2 103.8 %all-gather.3.cloned.1.call-start = ((), (), s32[]{:S(2)}) async-start(), calls=%async_computation | async-start | bytes 13369344 | tf_op jit(solution)/shard_map/all_gather | solution.py:144
  9.6 192.0 %all-gather.5.cloned.1.call-start = ((), (), s32[]{:S(2)}) async-start(), calls=%async_computation.1 | async-start | bytes 13369344 | tf_op jit(solution)/shard_map/all_gather | solution.py:146
  10.7 10.3 %collective-permute-start = (bf16[80,1536]{1,0:T(8,128)(2,1)S(1)}, bf16[80,1536]{1,0:T(8,128)(2,1)S(1)}, u32[]{:S(2)}, u32[]{:S(2)}) collective-permute-start(bf16[80,1536]{1,0:T(8,128)(2,1)S(1)} %get-tuple-element.19), channel_id=1, source_target_pairs={{0,1},{1,2},{2,3},{3,4},{4,5},{5,6},{6,7},{7,8},{8,9},{9,10},{10,1... | collective-permute-start | bytes 737288 | tf_op jit(solution)/shard_map/ppermute | solution.py:23
  12.0 9.0 %collective-permute-start.1 = (bf16[80,1536]{1,0:T(8,128)(2,1)S(1)}, bf16[80,1536]{1,0:T(8,128)(2,1)S(1)}, u32[]{:S(2)}, u32[]{:S(2)}) collective-permute-start(bf16[80,1536]{1,0:T(8,128)(2,1)S(1)} %get-tuple-element.20), channel_id=1, source_target_pairs={{1,0},{2,1},{3,2},{4,3},{5,4},{6,5},{7,6},{8,7},{9,8},{10,9},{11,1... | collective-permute-start | bytes 737288 | tf_op jit(solution)/shard_map/ppermute | solution.py:26
  21.0 127.8 %copy-start.9 = (f32[1536]{0:T(1024)}, f32[1536]{0:T(1024)S(1)}, u32[]{:S(2)}) copy-start(f32[1536]{0:T(1024)S(1)} %get-tuple-element.4) | copy-start | bytes 18436
  21.0 11.8 %copy-start.3 = (bf16[80,1536]{1,0:T(8,128)(2,1)}, bf16[80,1536]{1,0:T(8,128)(2,1)S(1)}, u32[]{:S(2)}) copy-start(bf16[80,1536]{1,0:T(8,128)(2,1)S(1)} %collective-permute-done.1) | copy-start | bytes 737284
  24.2 14.1 %copy-start.14 = (f32[1536]{0:T(1024)S(1)}, f32[1536]{0:T(1024)}, u32[]{:S(2)}) copy-start(f32[1536]{0:T(1024)} %param.18) | copy-start | bytes 18436
  24.2 18.8 %copy-start.21 = (s32[16]{0:T(128)S(1)}, s32[16]{0:T(128)}, u32[]{:S(2)}) copy-start(s32[16]{0:T(128)} %param.13) | copy-start | bytes 196
  31.9 16.1 %copy-start.12 = (f32[1536]{0:T(1024)S(1)}, f32[1536]{0:T(1024)}, u32[]{:S(2)}) copy-start(f32[1536]{0:T(1024)} %param.17) | copy-start | bytes 18436
  44.3 95.5 %copy-start.19 = (pred[128]{0:T(512)(128)(4,1)}, pred[128]{0:T(512)(128)(4,1)S(1)}, u32[]{:S(2)}) copy-start(pred[128]{0:T(512)(128)(4,1)S(1)} %iota_compare_fusion.1) | copy-start | bytes 388
  44.5 85.2 %copy-start.15 = (pred[2048]{0:T(1024)(128)(4,1)}, pred[2048]{0:T(1024)(128)(4,1)S(1)}, u32[]{:S(2)}) copy-start(pred[2048]{0:T(1024)(128)(4,1)S(1)} %fusion.75) | copy-start | bytes 6148
  126.4 13.9 %slice-start = ((s8[4718592]{0:T(1024)(128)(4,1)}), s8[4194304]{0:T(1024)(128)(4,1)S(1)}, s32[]{:S(2)}) async-start(s8[4718592]{0:T(1024)(128)(4,1)} %bitcast.96), calls=%async_computation.2 | async-start | bytes 8388608
  129.7 10.1 %copy-start.11 = (bf16[128,1536]{0,1:T(8,128)(2,1)S(1)}, bf16[128,1536]{0,1:T(8,128)(2,1)}, u32[]{:S(2)}) copy-start(bf16[128,1536]{0,1:T(8,128)(2,1)} %copy.52) | copy-start | bytes 1179652
  129.7 10.5 %slice-start.1 = ((s8[4718592]{0:T(1024)(128)(4,1)}), s8[524288]{0:T(1024)(128)(4,1)S(1)}, s32[]{:S(2)}) async-start(s8[4718592]{0:T(1024)(128)(4,1)} %bitcast.96), calls=%async_computation.3 | async-start | bytes 1048576
  129.7 10.5 %copy-start.1 = (bf16[128,1536]{1,0:T(8,128)(2,1)S(1)}, bf16[128,1536]{1,0:T(8,128)(2,1)}, u32[]{:S(2)}) copy-start(bf16[128,1536]{1,0:T(8,128)(2,1)} %param.10) | copy-start | bytes 1179652
  129.7 10.5 %copy-start.4 = (bf16[80,1536]{1,0:T(8,128)(2,1)S(1)}, bf16[80,1536]{1,0:T(8,128)(2,1)}, u32[]{:S(2)}) copy-start(bf16[80,1536]{1,0:T(8,128)(2,1)} %copy-done.3) | copy-start | bytes 737284
  139.8 5.2 %slice-start.4 = ((s8[4718592]{0:T(1024)(128)(4,1)}), s8[4194304]{0:T(1024)(128)(4,1)S(1)}, s32[]{:S(2)}) async-start(s8[4718592]{0:T(1024)(128)(4,1)} %bitcast.102), calls=%async_computation.6 | async-start | bytes 8388608
  140.3 4.7 %slice-start.5 = ((s8[4718592]{0:T(1024)(128)(4,1)}), s8[524288]{0:T(1024)(128)(4,1)S(1)}, s32[]{:S(2)}) async-start(s8[4718592]{0:T(1024)(128)(4,1)} %bitcast.102), calls=%async_computation.7 | async-start | bytes 1048576
  141.3 6.7 %collective-permute-start.2 = (bf16[80,1536]{1,0:T(8,128)(2,1)S(1)}, bf16[80,1536]{1,0:T(8,128)(2,1)S(1)}, u32[]{:S(2)}, u32[]{:S(2)}) collective-permute-start(bf16[80,1536]{1,0:T(8,128)(2,1)S(1)} %get-tuple-element.17), channel_id=1, source_target_pairs={{0,1},{1,2},{2,3},{3,4},{4,5},{5,6},{6,7},{7,8},{8,9},{9,10},{10,1... | collective-permute-start | bytes 737288 | tf_op jit(solution)/shard_map/ppermute | solution.py:23
  143.5 4.5 %collective-permute-start.3 = (bf16[80,1536]{1,0:T(8,128)(2,1)S(1)}, bf16[80,1536]{1,0:T(8,128)(2,1)S(1)}, u32[]{:S(2)}, u32[]{:S(2)}) collective-permute-start(bf16[80,1536]{1,0:T(8,128)(2,1)S(1)} %get-tuple-element.18), channel_id=1, source_target_pairs={{1,0},{2,1},{3,2},{4,3},{5,4},{6,5},{7,6},{8,7},{9,8},{10,9},{11,1... | collective-permute-start | bytes 737288 | tf_op jit(solution)/shard_map/ppermute | solution.py:26
  148.0 10.5 %copy-start.5 = (bf16[80,1536]{1,0:T(8,128)(2,1)}, bf16[80,1536]{1,0:T(8,128)(2,1)S(1)}, u32[]{:S(2)}) copy-start(bf16[80,1536]{1,0:T(8,128)(2,1)S(1)} %collective-permute-done.2) | copy-start | bytes 737284
  148.0 10.5 %copy-start.7 = (bf16[80,1536]{1,0:T(8,128)(2,1)}, bf16[80,1536]{1,0:T(8,128)(2,1)S(1)}, u32[]{:S(2)}) copy-start(bf16[80,1536]{1,0:T(8,128)(2,1)S(1)} %collective-permute-done.3) | copy-start | bytes 737284
  211.8 8.7 %copy-start.13 = (f32[1536]{0:T(1024)S(1)}, f32[1536]{0:T(1024)}, u32[]{:S(2)}) copy-start(f32[1536]{0:T(1024)} %param.17) | copy-start | bytes 18436
  211.8 8.7 %copy-start.16 = (pred[2048]{0:T(1024)(128)(4,1)S(1)}, pred[2048]{0:T(1024)(128)(4,1)}, u32[]{:S(2)}) copy-start(pred[2048]{0:T(1024)(128)(4,1)} %copy-done.15) | copy-start | bytes 6148
  239.1 7.6 %copy-start.2 = (bf16[2048,1536]{0,1:T(8,128)(2,1)S(1)}, bf16[2048,1536]{0,1:T(8,128)(2,1)}, u32[]{:S(2)}) copy-start(bf16[2048,1536]{0,1:T(8,128)(2,1)} %copy.68) | copy-start | bytes 18874372
  239.1 14.7 %slice-start.2 = ((s8[4718592]{0:T(1024)(128)(4,1)}), s8[4194304]{0:T(1024)(128)(4,1)S(1)}, s32[]{:S(2)}) async-start(s8[4718592]{0:T(1024)(128)(4,1)} %bitcast.98), calls=%async_computation.4 | async-start | bytes 8388608
  246.7 6.6 %copy-start.20 = (pred[128]{0:T(512)(128)(4,1)S(1)}, pred[128]{0:T(512)(128)(4,1)}, u32[]{:S(2)}) copy-start(pred[128]{0:T(512)(128)(4,1)} %copy-done.19) | copy-start | bytes 388
  246.7 7.2 %slice-start.3 = ((s8[4718592]{0:T(1024)(128)(4,1)}), s8[524288]{0:T(1024)(128)(4,1)S(1)}, s32[]{:S(2)}) async-start(s8[4718592]{0:T(1024)(128)(4,1)} %bitcast.98), calls=%async_computation.5 | async-start | bytes 1048576
  246.7 7.2 %copy-start.6 = (bf16[80,1536]{1,0:T(8,128)(2,1)S(1)}, bf16[80,1536]{1,0:T(8,128)(2,1)}, u32[]{:S(2)}) copy-start(bf16[80,1536]{1,0:T(8,128)(2,1)} %copy-done.5) | copy-start | bytes 737284
  246.7 7.2 %copy-start.8 = (bf16[80,1536]{1,0:T(8,128)(2,1)S(1)}, bf16[80,1536]{1,0:T(8,128)(2,1)}, u32[]{:S(2)}) copy-start(bf16[80,1536]{1,0:T(8,128)(2,1)} %copy-done.7) | copy-start | bytes 737284
  246.7 7.2 %copy-start.10 = (f32[1536]{0:T(1024)S(1)}, f32[1536]{0:T(1024)}, u32[]{:S(2)}) copy-start(f32[1536]{0:T(1024)} %copy-done.9) | copy-start | bytes 18436
  246.7 7.2 %copy-start.18 = (f32[1536]{0:T(1024)S(1)}, f32[1536]{0:T(1024)}, u32[]{:S(2)}) copy-start(f32[1536]{0:T(1024)} %get-tuple-element.21) | copy-start | bytes 18436
  (2 other events, 5.1 us)
Sparse Core Ops, SparseCore 0:
  10.3 100.6 all-gather.2
  113.4 88.1 all-gather.4
where the time goes:
time: 265 us; the launch traced here: 262 us
  waiting for transfers between devices  90.4 us (34%)
  local copies, waits for them, and re-layouts  65.4 us (25%)
  matrix products  58.3 us (22%)
  other arithmetic  26 us (10%)
  between operations  16 us (6%)
  starting transfers between devices  6.37 us (2%)
    all_gather x2, waiting for transfers between devices, shards(): lax.all_gather(cache_rows, 'patch', axis=0, tiled=True)  90.4 us
    slice x3, local copies, waits for them, and re-layouts, cached_step(): block_rows[:, :head_total].reshape(count_rows, heads_count, HEAD)  27.3 us
    dot_general x4, matrix products, attend(): jnp.einsum('qhk,khd->qhd', weights.astype(jnp.bfloat16), values_block, pr...  17.3 us
    dot_general x2, matrix products, shards(): projected = jnp.dot(normed, w_qkv, preferred_element_type=jnp.float32)  16.4 us
    dot_general x4, matrix products, attend(): jnp.einsum('qhd,khd->qhk', queries, keys_block, preferred_element_type=jn...  14.9 us
    reduce_sum x4, other arithmetic, attend(): denominator = denominator * factor + jnp.sum(weights, -1)  11.2 us
    slice x1, local copies, waits for them, and re-layouts, cached_step(): block_rows[:, head_total:].reshape(count_rows, heads_count, HEAD)  8.7 us
    unnamed x57, local copies, waits for them, and re-layouts  7.34 us
  transfers between devices with their start and end apart: 6, of which 2 were waited for; matrix products, arithmetic and copies ran while one was open for 34% of the time, Pallas kernels for 0%

commit v1 on v0

v1 whole, which is shorter than its diff:
```python
import math

import jax
import jax.numpy as jnp
from jax import lax
from jax.experimental import pallas as pl
from jax.experimental.pallas import tpu as pltpu
from jax.sharding import PartitionSpec as P

HEAD = 128
FREQ = 256
FRAME = 80
STEPS = 2
SLAB = 128
D = 1536
GROUP = 3
WIDE = GROUP * HEAD
RING = 4
LOG2E = math.log2(math.e)

epsilon = 1e-06
masked_score = -1e30
f32 = jnp.float32
bf16 = jnp.bfloat16


def place(y, z, c):
    return 8 * y + 2 * z + c


DEVICES = [(y, z, c) for y in range(2) for z in range(RING) for c in range(2)]
CORE = [(place(y, z, c), place(y, z, 1 - c)) for y, z, c in DEVICES]
ACROSS = [(place(y, z, c), place(1 - y, z, c)) for y, z, c in DEVICES]


def ring(k):
    return [(place(y, z, c), place(y, (z + k) % RING, c)) for y, z, c in DEVICES]


NEXT_CHIP = [(p, p + 1) for p in range(1, 15, 2)] + [(p + 1, p) for p in range(1, 15, 2)]


def params(megabytes=48):
    return pltpu.CompilerParams(vmem_limit_bytes=megabytes * 2**20)


def embedding(moment):
    halfway = FREQ // 2
    frequency = jnp.exp(-math.log(10000.0) * jnp.arange(halfway, dtype=f32) / halfway)
    angles = moment.astype(f32) * frequency
    return jnp.concatenate([jnp.cos(angles), jnp.sin(angles)])


def modulation_kernel(active_ref, w_ref, out_ref):
    out_ref[...] = jnp.dot(
        active_ref[...], w_ref[...], precision=lax.Precision.HIGHEST, preferred_element_type=f32
    )


def modulation(timesteps, w_mod):
    rows = jnp.stack([jax.nn.silu(embedding(timesteps[s])) for s in range(STEPS)])
    active = jnp.concatenate([rows, jnp.zeros((8 - STEPS, FREQ), f32)], 0)
    columns = w_mod.shape[1]
    tile = columns // 6
    return pl.pallas_call(
        modulation_kernel,
        grid=(6,),
        in_specs=[
            pl.BlockSpec((8, FREQ), lambda i: (0, 0)),
            pl.BlockSpec((FREQ, tile), lambda i: (0, i)),
        ],
        out_specs=pl.BlockSpec((8, tile), lambda i: (0, i)),
        out_shape=jax.ShapeDtypeStruct((8, columns), f32),
        compiler_params=params(),
        name="modulation",
    )(active, w_mod)


def split_kernel(place_ref, keys_ref, values_ref, *out_refs):
    step = pl.program_id(0)
    for k in range(RING):

        @pl.when(step == k)
        def _():
            out_refs[k][:, :WIDE] = keys_ref[...]
            out_refs[k][:, WIDE:] = values_ref[...]


def split_cache(where, stale_kv):
    return pl.pallas_call(
        split_kernel,
        grid_spec=pltpu.PrefetchScalarGridSpec(
            num_scalar_prefetch=1,
            grid=(RING,),
            in_specs=[
                pl.BlockSpec((SLAB, WIDE), lambda i, p: (0, (p[0] + i) % RING)),
                pl.BlockSpec((SLAB, WIDE), lambda i, p: (0, RING + (p[0] + i) % RING)),
            ],
            out_specs=[pl.BlockSpec((SLAB, 2 * WIDE), lambda i, p: (0, 0))] * RING,
        ),
        out_shape=[jax.ShapeDtypeStruct((SLAB, 2 * WIDE), bf16)] * RING,
        compiler_params=params(),
        name="split_cache",
    )(where, stale_kv, stale_kv)


def head_normed(block, gain):
    mean_square = jnp.mean(block * block, -1, keepdims=True)
    return (block * lax.rsqrt(mean_square + epsilon) * gain).astype(bf16)


def project_kernel(
    place_ref, state_ref, core_ref, chip_ref, conv_ref, mod_ref, q_gain_ref, k_gain_ref,
    wq_ref, wk_ref, wv_ref, out0, out1, out2, out3, cache_ref, mixed_ref, normed_ref, *, row
):
    outs = (out0, out1, out2, out3)
    step = pl.program_id(0)
    core = place_ref[1]

    @pl.when(step == 0)
    def _():
        state = state_ref[...].astype(f32)
        core_rows = core_ref[...].astype(f32)
        chip_rows = chip_ref[...].astype(f32)
        first = core == 0
        above = jnp.where(first, chip_rows, core_rows)
        below = jnp.where(first, core_rows, chip_rows)
        before = jnp.concatenate([above, state[: SLAB - FRAME]], 0)
        after_rows = jnp.concatenate([state[FRAME:], below], 0)
        mixed = (
            state
            + conv_ref[0:1, :] * before
            + conv_ref[1:2, :] * state
            + conv_ref[2:3, :] * after_rows
        )
        mixed_ref[...] = mixed
        shift = mod_ref[row : row + 1, :D]
        scale = mod_ref[row : row + 1, D : 2 * D]
        centred = mixed - jnp.mean(mixed, -1, keepdims=True)
        variance = jnp.mean(centred * centred, -1, keepdims=True)
        normed_ref[...] = (
            centred * lax.rsqrt(variance + epsilon) * (1.0 + scale) + shift
        ).astype(bf16)

    normed = normed_ref[...]
    queries = jnp.dot(normed, wq_ref[...], preferred_element_type=f32)
    keys = jnp.dot(normed, wk_ref[...], preferred_element_type=f32)
    values = jnp.dot(normed, wv_ref[...], preferred_element_type=f32).astype(bf16)
    pieces = []
    for block, gain_ref in ((queries, q_gain_ref), (keys, k_gain_ref)):
        for h in range(GROUP):
            columns = slice(h * HEAD, (h + 1) * HEAD)
            pieces.append(head_normed(block[:, columns], gain_ref[:, columns]))
    queries, keys = jnp.concatenate(pieces[:GROUP], 1), jnp.concatenate(pieces[GROUP:], 1)
    group = (place_ref[0] + step) % RING
    start = pl.multiple_of(group * WIDE, WIDE)
    cache_ref[:, pl.ds(start, WIDE)] = keys
    cache_ref[:, pl.ds(pl.multiple_of(start + D, WIDE), WIDE)] = values
    for k in range(RING):

        @pl.when(step == k)
        def _():
            outs[k][:, :WIDE] = queries
            outs[k][:, WIDE : 2 * WIDE] = keys
            outs[k][:, 2 * WIDE :] = values


def project(where, state, core_rows, chip_rows, conv_weight, mod, q_gain, k_gain, w_qkv, row):
    def whole(shape):
        return pl.BlockSpec(shape, lambda i, p: (0, 0))

    def weight(part):
        return pl.BlockSpec((D, WIDE), lambda i, p: (0, part * RING + (p[0] + i) % RING))

    gain = pl.BlockSpec((1, WIDE), lambda i, p: (0, (p[0] + i) % RING))

    def body(*refs):
        project_kernel(*refs, row=row)

    return pl.pallas_call(
        body,
        grid_spec=pltpu.PrefetchScalarGridSpec(
            num_scalar_prefetch=1,
            grid=(RING,),
            in_specs=[
                whole((SLAB, D)),
                whole((FRAME, D)),
                whole((FRAME, D)),
                whole((3, D)),
                whole((8, 3 * D)),
                gain,
                gain,
                weight(0),
                weight(1),
                weight(2),
            ],
            out_specs=[whole((SLAB, 3 * WIDE))] * RING + [whole((SLAB, 2 * D)), whole((SLAB, D))],
            scratch_shapes=[pltpu.VMEM((SLAB, D), bf16)],
        ),
        out_shape=[jax.ShapeDtypeStruct((SLAB, 3 * WIDE), bf16)] * RING
        + [jax.ShapeDtypeStruct((SLAB, 2 * D), bf16), jax.ShapeDtypeStruct((SLAB, D), f32)],
        compiler_params=params(),
        name="project",
    )(
        where, state, core_rows, chip_rows, conv_weight, mod,
        q_gain.reshape(1, -1), k_gain.reshape(1, -1), w_qkv, w_qkv, w_qkv,
    )


def scores_of(queries, keys, bias):
    dots = lax.dot_general(
        queries, keys, (((1,), (1,)), ((), ())), preferred_element_type=f32
    )
    return dots * (LOG2E / math.sqrt(HEAD)) + bias


def attend_kernel(*refs):
    q_refs, k_refs, v_refs = refs[0:4], refs[4:8], refs[8:12]
    old_k, old_v = refs[12:16], refs[16:20]
    bias_ref = refs[20]
    outs = refs[21:25]
    scores, weights, own = refs[25:28]
    rows = RING * SLAB
    queries = jnp.concatenate([q[...] for q in q_refs], 0)
    for a in range(4):
        scores[:, a * rows : (a + 1) * rows] = scores_of(
            queries, old_k[a][...], bias_ref[a : a + 1, :]
        )
    for j in range(RING):
        here = slice(j * SLAB, (j + 1) * SLAB)
        scores[here, here] = scores_of(q_refs[j][...], k_refs[j][...], bias_ref[0:1, here])
    for j in range(RING):
        here = slice(j * SLAB, (j + 1) * SLAB)
        block = scores[here, :]
        highest = jnp.max(block, -1, keepdims=True)
        probs = jnp.exp2(block - highest)
        total = jnp.sum(probs, -1, keepdims=True)
        weights[here, :] = probs.astype(bf16)
        own[here, :] = weights[here, here]
        weights[here, here] = jnp.zeros((SLAB, SLAB), bf16)
        summed = jnp.dot(own[here, :], v_refs[j][...], preferred_element_type=f32)
        for a in range(4):
            summed += jnp.dot(
                weights[here, a * rows : (a + 1) * rows], old_v[a][...], preferred_element_type=f32
            )
        outs[j][...] = (summed / total).astype(bf16)


def attend(fresh, olds, bias):
    rows = RING * SLAB

    def column(n, part):
        return pl.BlockSpec((n, HEAD), lambda h: (0, part * GROUP + h))

    return pl.pallas_call(
        attend_kernel,
        grid=(GROUP,),
        in_specs=[column(SLAB, 0)] * 4
        + [column(SLAB, 1)] * 4
        + [column(SLAB, 2)] * 4
        + [column(rows, 0)] * 4
        + [column(rows, 1)] * 4
        + [pl.BlockSpec((4, rows), lambda h: (0, 0))],
        out_specs=[column(SLAB, 0)] * 4,
        out_shape=[jax.ShapeDtypeStruct((SLAB, WIDE), bf16)] * 4,
        scratch_shapes=[
            pltpu.VMEM((rows, 4 * rows), f32),
            pltpu.VMEM((rows, 4 * rows), bf16),
            pltpu.VMEM((rows, SLAB), bf16),
        ],
        compiler_params=params(),
        name="attend",
    )(*fresh, *fresh, *fresh, *olds, *olds, bias)


def output_kernel(place_ref, a0, a1, a2, a3, w0, w1, w2, w3, mixed_ref, gate_ref, out_ref, *, row):
    total = jnp.dot(a0[...], w0[...], preferred_element_type=f32)
    for a, w in ((a1, w1), (a2, w2), (a3, w3)):
        total += jnp.dot(a[...], w[...], preferred_element_type=f32)
    out_ref[...] = (mixed_ref[...] + gate_ref[row : row + 1, :] * total).astype(bf16)


def output(where, attended, w_out, mixed, mod, row):
    tiles = 4
    width = D // tiles

    def weight(k):
        return pl.BlockSpec((WIDE, width), lambda i, p: ((p[0] + k) % RING, i))

    def body(*refs):
        output_kernel(*refs, row=row)

    return pl.pallas_call(
        body,
        grid_spec=pltpu.PrefetchScalarGridSpec(
            num_scalar_prefetch=1,
            grid=(tiles,),
            in_specs=[pl.BlockSpec((SLAB, WIDE), lambda i, p: (0, 0))] * 4
            + [weight(k) for k in range(RING)]
            + [
                pl.BlockSpec((SLAB, width), lambda i, p: (0, i)),
                pl.BlockSpec((8, width), lambda i, p: (0, 2 * tiles + i)),
            ],
            out_specs=pl.BlockSpec((SLAB, width), lambda i, p: (0, i)),
        ),
        out_shape=jax.ShapeDtypeStruct((SLAB, D), bf16),
        compiler_params=params(),
        name="output",
    )(where, *attended, w_out, w_out, w_out, w_out, mixed, mod)


def sent_round(blocks):
    return [blocks[0]] + [lax.ppermute(blocks[k], "patch", ring(k)) for k in range(1, RING)]


def sent_back(blocks):
    return [blocks[0]] + [
        lax.ppermute(blocks[k], "patch", ring(RING - k)) for k in range(1, RING)
    ]


def spread(own):
    other_y = lax.ppermute(own, "patch", ACROSS)
    other_core = lax.ppermute(own, "patch", CORE)
    return [own, other_core, other_y, lax.ppermute(other_y, "patch", CORE)]


def live_bias(counts, y, z, c):
    back = jnp.arange(RING, dtype=jnp.int32)
    chips = 2 * ((z - back) % RING)
    slabs = jnp.stack(
        [8 * yy + chips + cc for yy, cc in ((y, c), (y, 1 - c), (1 - y, c), (1 - y, 1 - c))]
    )
    live = jnp.arange(SLAB, dtype=jnp.int32) < counts[slabs][:, :, None]
    return jnp.where(live, 0.0, masked_score).astype(f32).reshape(4, RING * SLAB)


def shards(latent, stale_kv, timesteps, counts, conv_weight, w_mod, w_qkv, q_gain, k_gain, w_out):
    own_slab = lax.axis_index("patch")
    y, z, c = own_slab // 8, (own_slab // 2) % RING, own_slab % 2
    where = jnp.stack([z, c]).astype(jnp.int32)
    state = latent
    olds = None
    mod = modulation(timesteps, w_mod)
    bias = live_bias(counts, y, z, c)
    cache = None
    for step in range(STEPS):
        to_core = lax.dynamic_slice_in_dim(state, jnp.where(c == 0, SLAB - FRAME, 0), FRAME, 0)
        to_chip = lax.dynamic_slice_in_dim(state, jnp.where(c == 0, 0, SLAB - FRAME), FRAME, 0)
        core_rows = lax.ppermute(to_core, "patch", CORE)
        chip_rows = lax.ppermute(to_chip, "patch", NEXT_CHIP)
        if step == 0:
            old_blocks = sent_round(split_cache(where, stale_kv))
            olds = spread(jnp.concatenate(old_blocks, 0))
        *blocks, cache, mixed = project(
            where, state, core_rows, chip_rows, conv_weight, mod, q_gain, k_gain, w_qkv, step
        )
        fresh = sent_round(blocks)
        attended = attend(fresh, olds, bias)
        if step + 1 < STEPS:
            olds = spread(jnp.concatenate([block[:, WIDE:] for block in fresh], 0))
        state = output(where, sent_back(attended), w_out, mixed, mod, step)
    return (state, cache)


def solution(mesh):
    rows = P(("req", "patch"), None)
    return jax.shard_map(
        shards,
        mesh=mesh,
        in_specs=(rows, rows, P("req"), P("req"), P(), P(), P(), P(), P(), P()),
        out_specs=(rows, rows),
        check_vma=False,
    )
```

time: 265 us -> 141 us (0.53)
  local copies, waits for them, and re-layouts: 65.4 us -> 6.15 us
  matrix products: 58.3 us -> 0 us
  Pallas kernels: 0 us -> 46.5 us
  waiting for transfers between devices: 90.4 us -> 49.9 us
  starting transfers between devices: 6.37 us -> 35.4 us
  other arithmetic: 26 us -> 0.4 us
  between operations: 16 us -> 2.26 us
    all_gather x2 -> x0, waiting for transfers between devices: 90.4 us -> none  [shards(): lax.all_gather(cache_rows, 'patch', axis=0, tiled=True)]
    dot_general x14 -> x0, matrix products: 58.3 us -> none  [the longest x4 17.3 us: attend(): jnp.einsum('qhk,khd->qhd', weights.astype(jnp.bfloat16), values_block, pr...]
    ppermute x4 -> x25, waiting for transfers between devices: 0.01 us -> 49.9 us  [the longest x9 34.2 us: sent_round(): lax.ppermute(blocks[k], 'patch', ring(k))]
    slice x16 -> x5, local copies, waits for them, and re-layouts: 48.4 us -> 0.64 us  [the longest x1 0.58 us: modulation(): timesteps[s]]
    pallas_call x0 -> x8, Pallas kernels: none -> 46.5 us  [the longest x2 18.1 us: project(): pl.pallas_call(body, grid_spec=pltpu.PrefetchScalarGridSpec(num_scalar_pr...]
    ppermute x4 -> x25, starting transfers between devices: 6.29 us -> 35.4 us  [the longest x9 20.6 us: sent_round(): lax.ppermute(blocks[k], 'patch', ring(k))]
    reduce_sum x14 -> x0, other arithmetic: 16.1 us -> none  [the longest x4 11.2 us: attend(): denominator = denominator * factor + jnp.sum(weights, -1)]
    mul x4 -> x0, local copies, waits for them, and re-layouts: 6.47 us -> none  [head_normed(): split_rows * lax.rsqrt(mean_square + epsilon)]
  transfers between devices with their start and end apart: 6 -> 25, of which waited for: 2 -> 17; matrix products, arithmetic and copies ran while one was open for 34% -> 2% of each run, Pallas kernels for 0% -> 25%
where the time goes in v1:
time: 141 us
  waiting for transfers between devices  49.9 us (35%)
  Pallas kernels  46.5 us (33%)
  starting transfers between devices  35.4 us (25%)
  local copies, waits for them, and re-layouts  6.15 us (4%)
  between operations  2.26 us (2%)
    ppermute x9, waiting for transfers between devices, sent_round(): lax.ppermute(blocks[k], 'patch', ring(k))  34.2 us
    ppermute x9, starting transfers between devices, sent_round(): lax.ppermute(blocks[k], 'patch', ring(k))  20.6 us
    pallas_call x2, Pallas kernels, project(): pl.pallas_call(body, grid_spec=pltpu.PrefetchScalarGridSpec(num_scalar_pr...  18.1 us
    pallas_call x2, Pallas kernels, attend(): pl.pallas_call(attend_kernel, grid=(GROUP,), in_specs=[column(SLAB, 0)] *...  16.4 us
    ppermute x6, waiting for transfers between devices, sent_back(): lax.ppermute(blocks[k], 'patch', ring(RING - k))  8.22 us
    pallas_call x2, Pallas kernels, output(): pl.pallas_call(body, grid_spec=pltpu.PrefetchScalarGridSpec(num_scalar_pr...  8.16 us
    ppermute x6, starting transfers between devices, sent_back(): lax.ppermute(blocks[k], 'patch', ring(RING - k))  8.11 us
    ppermute x2, waiting for transfers between devices, spread(): other_y = lax.ppermute(own, 'patch', ACROSS)  5.18 us
  transfers between devices with their start and end apart: 25, of which 17 were waited for; matrix products, arithmetic and copies ran while one was open for 2% of the time, Pallas kernels for 25%

profile of v1, /device:TPU:0, one launch (start us, length us, event | category | flops | bytes accessed | tf_op | source)
XLA Modules:
  0.0 140.7 jit_solution(4634605726703546157)
XLA Ops:
  0.7 1.2 constant_dynamic-slice_fusion.2
  3.7 3.4 %collective-permute-start.5 = (bf16[128,768]{1,0:T(8,128)(2,1)S(1)}, bf16[128,768]{1,0:T(8,128)(2,1)S(1)}, u32[]{:S(2)}, u32[]{:S(2)}) collective-permute-start(bf16[128,768]{1,0:T(8,128)(2,1)S(1)} %get-tuple-element.30), channel_id=1, source_target_pairs={{0,2},{1,3},{2,4},{3,5},{4,6},{5,7},{6,0},{7,1},{8,10},{9,11},{10,... | collective-permute-start | bytes 589832 | tf_op jit(solution)/shard_map/ppermute | solution.py:313
  7.1 4.0 %collective-permute-start.6 = (bf16[128,768]{1,0:T(8,128)(2,1)S(1)}, bf16[128,768]{1,0:T(8,128)(2,1)S(1)}, u32[]{:S(2)}, u32[]{:S(2)}) collective-permute-start(bf16[128,768]{1,0:T(8,128)(2,1)S(1)} %get-tuple-element.31), channel_id=1, source_target_pairs={{0,4},{1,5},{2,6},{3,7},{4,0},{5,1},{6,2},{7,3},{8,12},{9,13},{10,... | collective-permute-start | bytes 589832 | tf_op jit(solution)/shard_map/ppermute | solution.py:313
  14.7 6.4 %collective-permute-done.6 = bf16[128,768]{1,0:T(8,128)(2,1)S(1)} collective-permute-done((bf16[128,768]{1,0:T(8,128)(2,1)S(1)}, bf16[128,768]{1,0:T(8,128)(2,1)S(1)}, u32[]{:S(2)}, u32[]{:S(2)}) %collective-permute-start.6) | collective-permute-done | bytes 196640 | tf_op jit(solution)/shard_map/ppermute | solution.py:313
  21.1 1.7 %collective-permute-done.7 = bf16[128,768]{1,0:T(8,128)(2,1)S(1)} collective-permute-done((bf16[128,768]{1,0:T(8,128)(2,1)S(1)}, bf16[128,768]{1,0:T(8,128)(2,1)S(1)}, u32[]{:S(2)}, u32[]{:S(2)}) %collective-permute-start.7) | collective-permute-done | bytes 196640 | tf_op jit(solution)/shard_map/ppermute | solution.py:313
  22.8 2.1 %collective-permute-start.9 = (bf16[512,768]{1,0:T(8,128)(2,1)S(1)}, bf16[512,768]{1,0:T(8,128)(2,1)}, u32[]{:S(2)}, u32[]{:S(2)}) collective-permute-start(bf16[512,768]{1,0:T(8,128)(2,1)S(1)} %constant_dynamic-update-slice_fusion.refs_12_.refs_16_), channel_id=1, source_target_pairs={{0,8},{1,9},{2,10},{3,11},{4,12},{5,13},{6,14},{7,15},{8,0},{9,1},... | collective-permute-start | bytes 2359304 | tf_op jit(solution)/shard_map/ppermute | solution.py:323
  25.2 2.3 %copy-done.1 = f32[256,4608]{1,0:T(8,128)S(1)} copy-done((f32[256,4608]{1,0:T(8,128)S(1)}, f32[256,4608]{1,0:T(8,128)}, u32[]{:S(2)}) %copy-start.1) | copy-done | bytes 4718616
  27.5 2.9 %modulation.1.refs_5_.refs_10_ = f32[8,4608]{1,0:T(8,128)S(1)} custom-call(f32[8,256]{1,0:T(8,128)S(1)} %maximum_maximum_fusion.active_ref, f32[256,4608]{1,0:T(8,128)S(1)} %copy-done.1), custom_call_target="tpu_custom_call" | custom-call | tf_op jit(solution)/shard_map/modulation/pallas_call | solution.py:65
  30.5 9.2 %project.2 = (bf16[128,1152]{1,0:T(8,128)(2,1)S(1)}, bf16[128,1152]{1,0:T(8,128)(2,1)S(1)}, bf16[128,1152]{1,0:T(8,128)(2,1)}, bf16[128,1152]{1,0:T(8,128)(2,1)}...) custom-call(s32[2]{0:T(128)S(1)} %pad_add_fusion.refs_0_.place_ref, bf16[128,1536]{1,0:T(8,128)(2,1)S(1)} %copy-done.3, ...), custom_call_target="tpu_custom_call" | custom-call | tf_op jit(solution)/shard_map/project/pallas_call | solution.py:180
  40.5 1.2 collective-permute-start.4
  42.6 1.2 collective-permute-start.2
  44.0 6.7 %collective-permute-done.4.refs_3_.refs_7_.refs_11_ = bf16[128,1152]{1,0:T(8,128)(2,1)S(1)} collective-permute-done((bf16[128,1152]{1,0:T(8,128)(2,1)}, bf16[128,1152]{1,0:T(8,128)(2,1)S(1)}, u32[]{:S(2)}, u32[]{:S(2)}) %collective-permute-start.4) | collective-permute-done | bytes 294944 | tf_op jit(solution)/shard_map/ppermute | solution.py:313
  50.7 2.7 %collective-permute-done.3.refs_2_.refs_6_.refs_10_ = bf16[128,1152]{1,0:T(8,128)(2,1)S(1)} collective-permute-done((bf16[128,1152]{1,0:T(8,128)(2,1)}, bf16[128,1152]{1,0:T(8,128)(2,1)S(1)}, u32[]{:S(2)}, u32[]{:S(2)}) %collective-permute-start.3) | collective-permute-done | bytes 294944 | tf_op jit(solution)/shard_map/ppermute | solution.py:313
  53.4 4.9 %collective-permute-done.2.refs_1_.refs_5_.refs_9_ = bf16[128,1152]{1,0:T(8,128)(2,1)S(1)} collective-permute-done((bf16[128,1152]{1,0:T(8,128)(2,1)S(1)}, bf16[128,1152]{1,0:T(8,128)(2,1)S(1)}, u32[]{:S(2)}, u32[]{:S(2)}) %collective-permute-start.2) | collective-permute-done | bytes 294944 | tf_op jit(solution)/shard_map/ppermute | solution.py:313
  58.4 2.8 %collective-permute-start.20 = (bf16[512,768]{1,0:T(8,128)(2,1)S(1)}, bf16[512,768]{1,0:T(8,128)(2,1)}, u32[]{:S(2)}, u32[]{:S(2)}) collective-permute-start(bf16[512,768]{1,0:T(8,128)(2,1)S(1)} %pad_maximum_fusion.refs_12_.refs_16_), channel_id=1, source_target_pairs={{0,8},{1,9},{2,10},{3,11},{4,12},{5,13},{6,14},{7,15},{8,0},{9,1},... | collective-permute-start | bytes 2359304 | tf_op jit(solution)/shard_map/ppermute | solution.py:323
  62.2 1.6 %collective-permute-done.10.refs_15_.refs_19_ = bf16[512,768]{1,0:T(8,128)(2,1)} collective-permute-done((bf16[512,768]{1,0:T(8,128)(2,1)}, bf16[512,768]{1,0:T(8,128)(2,1)}, u32[]{:S(2)}, u32[]{:S(2)}) %collective-permute-start.10) | collective-permute-done | bytes 786464 | tf_op jit(solution)/shard_map/ppermute | solution.py:325
  63.8 8.2 %attend.2 = (bf16[128,384]{1,0:T(8,128)(2,1)S(1)}, bf16[128,384]{1,0:T(8,128)(2,1)S(1)}, bf16[128,384]{1,0:T(8,128)(2,1)S(1)}, bf16[128,384]{1,0:T(8,128)(2,1)S(1)}) custom-call(bf16[128,1152]{1,0:T(8,128)(2,1)S(1)} %get-tuple-element.25.refs_0_.refs_4_.refs_8_, bf16[128,1152]{1,0:T(8,128)(2,1)S(1)} %collective-permute-done.2.refs_1_.refs_5_.refs_9_, ...), custom_call_target="tpu_custom_call" | custom-call | tf_op jit(solution)/shard_map/attend/pallas_call | solution.py:255
  72.1 1.2 collective-permute-start.11
  74.3 5.2 %collective-permute-done.20.refs_14_.refs_18_ = bf16[512,768]{1,0:T(8,128)(2,1)} collective-permute-done((bf16[512,768]{1,0:T(8,128)(2,1)S(1)}, bf16[512,768]{1,0:T(8,128)(2,1)}, u32[]{:S(2)}, u32[]{:S(2)}) %collective-permute-start.20) | collective-permute-done | bytes 786464 | tf_op jit(solution)/shard_map/ppermute | solution.py:323
  81.4 4.5 %output.2.refs_1_ = bf16[128,1536]{1,0:T(8,128)(2,1)S(1)} custom-call(s32[2]{0:T(128)S(1)} %pad_add_fusion.refs_0_.place_ref, bf16[128,384]{1,0:T(8,128)(2,1)S(1)} %get-tuple-element.33.refs_1_, bf16[128,384]{1,0:T(8,128)(2,1)S(1)} %collective-permute-done.11.refs_2_, bf16[128,384]{1,0:T(8,128)(2,1)S(1)} %collective-permute-done.12.refs_3_, ...), custom_call_target="tpu_custom_call" | custom-call | tf_op jit(solution)/shard_map/output/pallas_call | solution.py:293
  87.6 9.0 %project.3 = (bf16[128,1152]{1,0:T(8,128)(2,1)S(1)}, bf16[128,1152]{1,0:T(8,128)(2,1)S(1)}, bf16[128,1152]{1,0:T(8,128)(2,1)S(1)}, bf16[128,1152]{1,0:T(8,128)(2...) custom-call(s32[2]{0:T(128)S(1)} %pad_add_fusion.refs_0_.place_ref, bf16[128,1536]{1,0:T(8,128)(2,1)S(1)} %output.2.refs_1_, ...), custom_call_target="tpu_custom_call" | custom-call | tf_op jit(solution)/shard_map/project/pallas_call | solution.py:180
  96.5 6.4 %collective-permute-start.16 = (bf16[128,1152]{1,0:T(8,128)(2,1)S(1)}, bf16[128,1152]{1,0:T(8,128)(2,1)S(1)}, u32[]{:S(2)}, u32[]{:S(2)}) collective-permute-start(bf16[128,1152]{1,0:T(8,128)(2,1)S(1)} %get-tuple-element.39), channel_id=1, source_target_pairs={{0,2},{1,3},{2,4},{3,5},{4,6},{5,7},{6,0},{7,1},{8,10},{9,11},{10,... | collective-permute-start | bytes 884744 | tf_op jit(solution)/shard_map/ppermute | solution.py:313
  102.9 1.7 %collective-permute-start.17 = (bf16[128,1152]{1,0:T(8,128)(2,1)S(1)}, bf16[128,1152]{1,0:T(8,128)(2,1)S(1)}, u32[]{:S(2)}, u32[]{:S(2)}) collective-permute-start(bf16[128,1152]{1,0:T(8,128)(2,1)S(1)} %get-tuple-element.40), channel_id=1, source_target_pairs={{0,4},{1,5},{2,6},{3,7},{4,0},{5,1},{6,2},{7,3},{8,12},{9,13},{10,... | collective-permute-start | bytes 884744 | tf_op jit(solution)/shard_map/ppermute | solution.py:313
  105.7 4.6 %collective-permute-done.16.refs_1_.refs_5_.refs_9_ = bf16[128,1152]{1,0:T(8,128)(2,1)S(1)} collective-permute-done((bf16[128,1152]{1,0:T(8,128)(2,1)S(1)}, bf16[128,1152]{1,0:T(8,128)(2,1)S(1)}, u32[]{:S(2)}, u32[]{:S(2)}) %collective-permute-start.16) | collective-permute-done | bytes 294944 | tf_op jit(solution)/shard_map/ppermute | solution.py:313
  110.3 5.8 %collective-permute-done.17.refs_2_.refs_6_.refs_10_ = bf16[128,1152]{1,0:T(8,128)(2,1)S(1)} collective-permute-done((bf16[128,1152]{1,0:T(8,128)(2,1)S(1)}, bf16[128,1152]{1,0:T(8,128)(2,1)S(1)}, u32[]{:S(2)}, u32[]{:S(2)}) %collective-permute-start.17) | collective-permute-done | bytes 294944 | tf_op jit(solution)/shard_map/ppermute | solution.py:313
  116.7 8.2 %attend.3 = (bf16[128,384]{1,0:T(8,128)(2,1)S(1)}, bf16[128,384]{1,0:T(8,128)(2,1)S(1)}, bf16[128,384]{1,0:T(8,128)(2,1)S(1)}, bf16[128,384]{1,0:T(8,128)(2,1)S(1)}) custom-call(bf16[128,1152]{1,0:T(8,128)(2,1)S(1)} %get-tuple-element.38.refs_0_.refs_4_.refs_8_, bf16[128,1152]{1,0:T(8,128)(2,1)S(1)} %collective-permute-done.16.refs_1_.refs_5_.refs_9_, ...), custom_call_target="tpu_custom_call" | custom-call | tf_op jit(solution)/shard_map/attend/pallas_call | solution.py:255
  124.8 3.8 %collective-permute-start.22 = (bf16[128,384]{1,0:T(8,128)(2,1)S(1)}, bf16[128,384]{1,0:T(8,128)(2,1)S(1)}, u32[]{:S(2)}, u32[]{:S(2)}) collective-permute-start(bf16[128,384]{1,0:T(8,128)(2,1)S(1)} %get-tuple-element.43), channel_id=1, source_target_pairs={{0,6},{1,7},{2,0},{3,1},{4,2},{5,3},{6,4},{7,5},{8,14},{9,15},{10,... | collective-permute-start | bytes 294920 | tf_op jit(solution)/shard_map/ppermute | solution.py:318
  128.6 2.1 %collective-permute-start.23 = (bf16[128,384]{1,0:T(8,128)(2,1)S(1)}, bf16[128,384]{1,0:T(8,128)(2,1)S(1)}, u32[]{:S(2)}, u32[]{:S(2)}) collective-permute-start(bf16[128,384]{1,0:T(8,128)(2,1)S(1)} %get-tuple-element.44), channel_id=1, source_target_pairs={{0,4},{1,5},{2,6},{3,7},{4,0},{5,1},{6,2},{7,3},{8,12},{9,13},{10,... | collective-permute-start | bytes 294920 | tf_op jit(solution)/shard_map/ppermute | solution.py:318
  130.7 2.6 %collective-permute-done.22.refs_2_ = bf16[128,384]{1,0:T(8,128)(2,1)S(1)} collective-permute-done((bf16[128,384]{1,0:T(8,128)(2,1)S(1)}, bf16[128,384]{1,0:T(8,128)(2,1)S(1)}, u32[]{:S(2)}, u32[]{:S(2)}) %collective-permute-start.22) | collective-permute-done | bytes 98336 | tf_op jit(solution)/shard_map/ppermute | solution.py:318
  133.3 2.5 %collective-permute-done.23.refs_3_ = bf16[128,384]{1,0:T(8,128)(2,1)S(1)} collective-permute-done((bf16[128,384]{1,0:T(8,128)(2,1)S(1)}, bf16[128,384]{1,0:T(8,128)(2,1)S(1)}, u32[]{:S(2)}, u32[]{:S(2)}) %collective-permute-start.23) | collective-permute-done | bytes 98336 | tf_op jit(solution)/shard_map/ppermute | solution.py:318
  135.8 1.2 collective-permute-done.24.refs_4_
  137.0 3.6 %output.3 = bf16[128,1536]{1,0:T(8,128)(2,1)} custom-call(s32[2]{0:T(128)S(1)} %pad_add_fusion.refs_0_.place_ref, bf16[128,384]{1,0:T(8,128)(2,1)S(1)} %get-tuple-element.42.refs_1_, bf16[128,384]{1,0:T(8,128)(2,1)S(1)} %collective-permute-done.22.refs_2_, bf16[128,384]{1,0:T(8,128)(2,1)S(1)} %collective-permute-done.23.refs_3_, ...), custom_call_target="tpu_custom_call" | custom-call | tf_op jit(solution)/shard_map/output/pallas_call | solution.py:293
  (83 shorter events, 13.5 us)
Async XLA Ops:
  0.6 60.7 %copy-start = (s32[16]{0:T(128)S(1)}, s32[16]{0:T(128)}, u32[]{:S(2)}) copy-start(s32[16]{0:T(128)} %param.13) | copy-start | bytes 196
  0.7 11.1 %copy-start.9 = (s32[2]{0:T(128)S(1)}, s32[2]{0:T(128)}, u32[]{:S(2)}) copy-start(s32[2]{0:T(128)} %param.12) | copy-start | bytes 28
  1.9 28.6 %collective-permute-start = (bf16[80,1536]{1,0:T(8,128)(2,1)S(1)}, bf16[80,1536]{1,0:T(8,128)(2,1)S(1)}, u32[]{:S(2)}, u32[]{:S(2)}) collective-permute-start(bf16[80,1536]{1,0:T(8,128)(2,1)S(1)} %get-tuple-element.51), channel_id=1, source_target_pairs={{0,1},{1,0},{2,3},{3,2},{4,5},{5,4},{6,7},{7,6},{8,9},{9,8},{10,11... | collective-permute-start | bytes 737288 | tf_op jit(solution)/shard_map/ppermute | solution.py:350
  1.9 28.5 %collective-permute-start.1 = (bf16[80,1536]{1,0:T(8,128)(2,1)S(1)}, bf16[80,1536]{1,0:T(8,128)(2,1)S(1)}, u32[]{:S(2)}, u32[]{:S(2)}) collective-permute-start(bf16[80,1536]{1,0:T(8,128)(2,1)S(1)} %get-tuple-element.50), channel_id=1, source_target_pairs={{1,2},{3,4},{5,6},{7,8},{9,10},{11,12},{13,14},{2,1},{4,3},{6,5},{... | collective-permute-start | bytes 737288 | tf_op jit(solution)/shard_map/ppermute | solution.py:351
  2.7 22.2 %copy-start.7 = (f32[1536]{0:T(1024)S(1)}, f32[1536]{0:T(1024)}, u32[]{:S(2)}) copy-start(f32[1536]{0:T(1024)} %param.17) | copy-start | bytes 18436
  2.7 22.3 %copy-start.8 = (f32[1536]{0:T(1024)S(1)}, f32[1536]{0:T(1024)}, u32[]{:S(2)}) copy-start(f32[1536]{0:T(1024)} %param.18) | copy-start | bytes 18436
  3.7 10.9 %collective-permute-start.5 = (bf16[128,768]{1,0:T(8,128)(2,1)S(1)}, bf16[128,768]{1,0:T(8,128)(2,1)S(1)}, u32[]{:S(2)}, u32[]{:S(2)}) collective-permute-start(bf16[128,768]{1,0:T(8,128)(2,1)S(1)} %get-tuple-element.30), channel_id=1, source_target_pairs={{0,2},{1,3},{2,4},{3,5},{4,6},{5,7},{6,0},{7,1},{8,10},{9,11},{10,... | collective-permute-start | bytes 589832 | tf_op jit(solution)/shard_map/ppermute | solution.py:313
  7.1 14.0 %collective-permute-start.6 = (bf16[128,768]{1,0:T(8,128)(2,1)S(1)}, bf16[128,768]{1,0:T(8,128)(2,1)S(1)}, u32[]{:S(2)}, u32[]{:S(2)}) collective-permute-start(bf16[128,768]{1,0:T(8,128)(2,1)S(1)} %get-tuple-element.31), channel_id=1, source_target_pairs={{0,4},{1,5},{2,6},{3,7},{4,0},{5,1},{6,2},{7,3},{8,12},{9,13},{10,... | collective-permute-start | bytes 589832 | tf_op jit(solution)/shard_map/ppermute | solution.py:313
  11.1 11.7 %collective-permute-start.7 = (bf16[128,768]{1,0:T(8,128)(2,1)S(1)}, bf16[128,768]{1,0:T(8,128)(2,1)S(1)}, u32[]{:S(2)}, u32[]{:S(2)}) collective-permute-start(bf16[128,768]{1,0:T(8,128)(2,1)S(1)} %get-tuple-element.32), channel_id=1, source_target_pairs={{0,6},{1,7},{2,0},{3,1},{4,2},{5,3},{6,4},{7,5},{8,14},{9,15},{10,... | collective-permute-start | bytes 589832 | tf_op jit(solution)/shard_map/ppermute | solution.py:313
  22.8 38.4 %collective-permute-start.9 = (bf16[512,768]{1,0:T(8,128)(2,1)S(1)}, bf16[512,768]{1,0:T(8,128)(2,1)}, u32[]{:S(2)}, u32[]{:S(2)}) collective-permute-start(bf16[512,768]{1,0:T(8,128)(2,1)S(1)} %constant_dynamic-update-slice_fusion.refs_12_.refs_16_), channel_id=1, source_target_pairs={{0,8},{1,9},{2,10},{3,11},{4,12},{5,13},{6,14},{7,15},{8,0},{9,1},... | collective-permute-start | bytes 2359304 | tf_op jit(solution)/shard_map/ppermute | solution.py:323
  40.5 10.2 %collective-permute-start.4 = (bf16[128,1152]{1,0:T(8,128)(2,1)}, bf16[128,1152]{1,0:T(8,128)(2,1)S(1)}, u32[]{:S(2)}, u32[]{:S(2)}) collective-permute-start(bf16[128,1152]{1,0:T(8,128)(2,1)} %get-tuple-element.28), channel_id=1, source_target_pairs={{0,6},{1,7},{2,0},{3,1},{4,2},{5,3},{6,4},{7,5},{8,14},{9,15},{10,... | collective-permute-start | bytes 884744 | tf_op jit(solution)/shard_map/ppermute | solution.py:313
  41.8 11.6 %collective-permute-start.3 = (bf16[128,1152]{1,0:T(8,128)(2,1)}, bf16[128,1152]{1,0:T(8,128)(2,1)S(1)}, u32[]{:S(2)}, u32[]{:S(2)}) collective-permute-start(bf16[128,1152]{1,0:T(8,128)(2,1)} %get-tuple-element.27), channel_id=1, source_target_pairs={{0,4},{1,5},{2,6},{3,7},{4,0},{5,1},{6,2},{7,3},{8,12},{9,13},{10,... | collective-permute-start | bytes 884744 | tf_op jit(solution)/shard_map/ppermute | solution.py:313
  42.6 15.7 %collective-permute-start.2 = (bf16[128,1152]{1,0:T(8,128)(2,1)S(1)}, bf16[128,1152]{1,0:T(8,128)(2,1)S(1)}, u32[]{:S(2)}, u32[]{:S(2)}) collective-permute-start(bf16[128,1152]{1,0:T(8,128)(2,1)S(1)} %get-tuple-element.26), channel_id=1, source_target_pairs={{0,2},{1,3},{2,4},{3,5},{4,6},{5,7},{6,0},{7,1},{8,10},{9,11},{10,... | collective-permute-start | bytes 884744 | tf_op jit(solution)/shard_map/ppermute | solution.py:313
  43.9 18.3 %collective-permute-start.8 = (bf16[512,768]{1,0:T(8,128)(2,1)S(1)}, bf16[512,768]{1,0:T(8,128)(2,1)}, u32[]{:S(2)}, u32[]{:S(2)}) collective-permute-start(bf16[512,768]{1,0:T(8,128)(2,1)S(1)} %constant_dynamic-update-slice_fusion.refs_12_.refs_16_), channel_id=1, source_target_pairs={{0,1},{1,0},{2,3},{3,2},{4,5},{5,4},{6,7},{7,6},{8,9},{9,8},{10,11... | collective-permute-start | bytes 2359304 | tf_op jit(solution)/shard_map/ppermute | solution.py:324
  58.4 21.1 %collective-permute-start.20 = (bf16[512,768]{1,0:T(8,128)(2,1)S(1)}, bf16[512,768]{1,0:T(8,128)(2,1)}, u32[]{:S(2)}, u32[]{:S(2)}) collective-permute-start(bf16[512,768]{1,0:T(8,128)(2,1)S(1)} %pad_maximum_fusion.refs_12_.refs_16_), channel_id=1, source_target_pairs={{0,8},{1,9},{2,10},{3,11},{4,12},{5,13},{6,14},{7,15},{8,0},{9,1},... | collective-permute-start | bytes 2359304 | tf_op jit(solution)/shard_map/ppermute | solution.py:323
  61.2 2.6 %collective-permute-start.10 = (bf16[512,768]{1,0:T(8,128)(2,1)}, bf16[512,768]{1,0:T(8,128)(2,1)}, u32[]{:S(2)}, u32[]{:S(2)}) collective-permute-start(bf16[512,768]{1,0:T(8,128)(2,1)} %collective-permute-done.9.refs_14_.refs_18_), channel_id=1, source_target_pairs={{0,1},{1,0},{2,3},{3,2},{4,5},{5,4},{6,7},{7,6},{8,9},{9,8},{10,11... | collective-permute-start | bytes 2359304 | tf_op jit(solution)/shard_map/ppermute | solution.py:325
  62.2 19.2 %copy-start.5 = (f32[128,1536]{1,0:T(8,128)S(1)}, f32[128,1536]{1,0:T(8,128)}, u32[]{:S(2)}) copy-start(f32[128,1536]{1,0:T(8,128)} %copy-done.4) | copy-start | bytes 2359300
  72.1 7.5 %collective-permute-start.11 = (bf16[128,384]{1,0:T(8,128)(2,1)S(1)}, bf16[128,384]{1,0:T(8,128)(2,1)S(1)}, u32[]{:S(2)}, u32[]{:S(2)}) collective-permute-start(bf16[128,384]{1,0:T(8,128)(2,1)S(1)} %get-tuple-element.34), channel_id=1, source_target_pairs={{0,6},{1,7},{2,0},{3,1},{4,2},{5,3},{6,4},{7,5},{8,14},{9,15},{10,... | collective-permute-start | bytes 294920 | tf_op jit(solution)/shard_map/ppermute | solution.py:318
  73.2 7.0 %collective-permute-start.12 = (bf16[128,384]{1,0:T(8,128)(2,1)S(1)}, bf16[128,384]{1,0:T(8,128)(2,1)S(1)}, u32[]{:S(2)}, u32[]{:S(2)}) collective-permute-start(bf16[128,384]{1,0:T(8,128)(2,1)S(1)} %get-tuple-element.35), channel_id=1, source_target_pairs={{0,4},{1,5},{2,6},{3,7},{4,0},{5,1},{6,2},{7,3},{8,12},{9,13},{10,... | collective-permute-start | bytes 294920 | tf_op jit(solution)/shard_map/ppermute | solution.py:318
  73.5 7.9 %collective-permute-start.13 = (bf16[128,384]{1,0:T(8,128)(2,1)S(1)}, bf16[128,384]{1,0:T(8,128)(2,1)S(1)}, u32[]{:S(2)}, u32[]{:S(2)}) collective-permute-start(bf16[128,384]{1,0:T(8,128)(2,1)S(1)} %get-tuple-element.36), channel_id=1, source_target_pairs={{0,2},{1,3},{2,4},{3,5},{4,6},{5,7},{6,0},{7,1},{8,10},{9,11},{10,... | collective-permute-start | bytes 294920 | tf_op jit(solution)/shard_map/ppermute | solution.py:318
  74.3 31.4 %collective-permute-start.19 = (bf16[512,768]{1,0:T(8,128)(2,1)S(1)}, bf16[512,768]{1,0:T(8,128)(2,1)S(1)}, u32[]{:S(2)}, u32[]{:S(2)}) collective-permute-start(bf16[512,768]{1,0:T(8,128)(2,1)S(1)} %pad_maximum_fusion.refs_12_.refs_16_), channel_id=1, source_target_pairs={{0,1},{1,0},{2,3},{3,2},{4,5},{5,4},{6,7},{7,6},{8,9},{9,8},{10,11... | collective-permute-start | bytes 2359304 | tf_op jit(solution)/shard_map/ppermute | solution.py:324
  79.5 26.2 %collective-permute-start.21 = (bf16[512,768]{1,0:T(8,128)(2,1)}, bf16[512,768]{1,0:T(8,128)(2,1)S(1)}, u32[]{:S(2)}, u32[]{:S(2)}) collective-permute-start(bf16[512,768]{1,0:T(8,128)(2,1)} %collective-permute-done.20.refs_14_.refs_18_), channel_id=1, source_target_pairs={{0,1},{1,0},{2,3},{3,2},{4,5},{5,4},{6,7},{7,6},{8,9},{9,8},{10,11... | collective-permute-start | bytes 2359304 | tf_op jit(solution)/shard_map/ppermute | solution.py:325
  86.0 1.6 %collective-permute-start.14 = (bf16[80,1536]{1,0:T(8,128)(2,1)S(1)}, bf16[80,1536]{1,0:T(8,128)(2,1)S(1)}, u32[]{:S(2)}, u32[]{:S(2)}) collective-permute-start(bf16[80,1536]{1,0:T(8,128)(2,1)S(1)} %get-tuple-element.49), channel_id=1, source_target_pairs={{0,1},{1,0},{2,3},{3,2},{4,5},{5,4},{6,7},{7,6},{8,9},{9,8},{10,11... | collective-permute-start | bytes 737288 | tf_op jit(solution)/shard_map/ppermute | solution.py:350
  86.1 1.5 %collective-permute-start.15 = (bf16[80,1536]{1,0:T(8,128)(2,1)S(1)}, bf16[80,1536]{1,0:T(8,128)(2,1)S(1)}, u32[]{:S(2)}, u32[]{:S(2)}) collective-permute-start(bf16[80,1536]{1,0:T(8,128)(2,1)S(1)} %get-tuple-element.48), channel_id=1, source_target_pairs={{1,2},{3,4},{5,6},{7,8},{9,10},{11,12},{13,14},{2,1},{4,3},{6,5},{... | collective-permute-start | bytes 737288 | tf_op jit(solution)/shard_map/ppermute | solution.py:351
  96.5 13.7 %collective-permute-start.16 = (bf16[128,1152]{1,0:T(8,128)(2,1)S(1)}, bf16[128,1152]{1,0:T(8,128)(2,1)S(1)}, u32[]{:S(2)}, u32[]{:S(2)}) collective-permute-start(bf16[128,1152]{1,0:T(8,128)(2,1)S(1)} %get-tuple-element.39), channel_id=1, source_target_pairs={{0,2},{1,3},{2,4},{3,5},{4,6},{5,7},{6,0},{7,1},{8,10},{9,11},{10,... | collective-permute-start | bytes 884744 | tf_op jit(solution)/shard_map/ppermute | solution.py:313
  102.9 13.1 %collective-permute-start.17 = (bf16[128,1152]{1,0:T(8,128)(2,1)S(1)}, bf16[128,1152]{1,0:T(8,128)(2,1)S(1)}, u32[]{:S(2)}, u32[]{:S(2)}) collective-permute-start(bf16[128,1152]{1,0:T(8,128)(2,1)S(1)} %get-tuple-element.40), channel_id=1, source_target_pairs={{0,4},{1,5},{2,6},{3,7},{4,0},{5,1},{6,2},{7,3},{8,12},{9,13},{10,... | collective-permute-start | bytes 884744 | tf_op jit(solution)/shard_map/ppermute | solution.py:313
  104.6 12.0 %collective-permute-start.18 = (bf16[128,1152]{1,0:T(8,128)(2,1)S(1)}, bf16[128,1152]{1,0:T(8,128)(2,1)S(1)}, u32[]{:S(2)}, u32[]{:S(2)}) collective-permute-start(bf16[128,1152]{1,0:T(8,128)(2,1)S(1)} %get-tuple-element.41), channel_id=1, source_target_pairs={{0,6},{1,7},{2,0},{3,1},{4,2},{5,3},{6,4},{7,5},{8,14},{9,15},{10,... | collective-permute-start | bytes 884744 | tf_op jit(solution)/shard_map/ppermute | solution.py:313
  116.7 20.3 %slice-start = ((s8[4718592]{0:T(1024)(128)(4,1)}), s8[4194304]{0:T(1024)(128)(4,1)S(1)}, s32[]{:S(2)}) async-start(s8[4718592]{0:T(1024)(128)(4,1)} %bitcast.28), calls=%async_computation | async-start | bytes 8388608
  116.7 20.3 %slice-start.1 = ((s8[4718592]{0:T(1024)(128)(4,1)}), s8[524288]{0:T(1024)(128)(4,1)S(1)}, s32[]{:S(2)}) async-start(s8[4718592]{0:T(1024)(128)(4,1)} %bitcast.28), calls=%async_computation.1 | async-start | bytes 1048576
  124.8 8.5 %collective-permute-start.22 = (bf16[128,384]{1,0:T(8,128)(2,1)S(1)}, bf16[128,384]{1,0:T(8,128)(2,1)S(1)}, u32[]{:S(2)}, u32[]{:S(2)}) collective-permute-start(bf16[128,384]{1,0:T(8,128)(2,1)S(1)} %get-tuple-element.43), channel_id=1, source_target_pairs={{0,6},{1,7},{2,0},{3,1},{4,2},{5,3},{6,4},{7,5},{8,14},{9,15},{10,... | collective-permute-start | bytes 294920 | tf_op jit(solution)/shard_map/ppermute | solution.py:318
  128.6 7.2 %collective-permute-start.23 = (bf16[128,384]{1,0:T(8,128)(2,1)S(1)}, bf16[128,384]{1,0:T(8,128)(2,1)S(1)}, u32[]{:S(2)}, u32[]{:S(2)}) collective-permute-start(bf16[128,384]{1,0:T(8,128)(2,1)S(1)} %get-tuple-element.44), channel_id=1, source_target_pairs={{0,4},{1,5},{2,6},{3,7},{4,0},{5,1},{6,2},{7,3},{8,12},{9,13},{10,... | collective-permute-start | bytes 294920 | tf_op jit(solution)/shard_map/ppermute | solution.py:318
  130.7 6.3 %collective-permute-start.24 = (bf16[128,384]{1,0:T(8,128)(2,1)S(1)}, bf16[128,384]{1,0:T(8,128)(2,1)S(1)}, u32[]{:S(2)}, u32[]{:S(2)}) collective-permute-start(bf16[128,384]{1,0:T(8,128)(2,1)S(1)} %get-tuple-element.45), channel_id=1, source_target_pairs={{0,2},{1,3},{2,4},{3,5},{4,6},{5,7},{6,0},{7,1},{8,10},{9,11},{10,... | collective-permute-start | bytes 294920 | tf_op jit(solution)/shard_map/ppermute | solution.py:318
  (5 other events, 11.2 us)

commit v2 on v0

v2 whole, which is shorter than its diff:
```python
import functools
import math

import jax
import jax.numpy as jnp
from jax import lax
from jax.experimental import pallas as pl
from jax.experimental.pallas import tpu as pltpu
from jax.sharding import PartitionSpec as P

HEAD = 128
FREQ = 256
FRAME = 80
STEPS = 2
SLAB = 128
D = 1536
GROUP = 3
WIDE = GROUP * HEAD
RING = 4
LOG2E = math.log2(math.e)

epsilon = 1e-06
masked_score = -1e30
f32 = jnp.float32
bf16 = jnp.bfloat16


def place(y, z, c):
    return 8 * y + 2 * z + c


DEVICES = [(y, z, c) for y in range(2) for z in range(RING) for c in range(2)]
CORE = [(place(y, z, c), place(y, z, 1 - c)) for y, z, c in DEVICES]
ACROSS = [(place(y, z, c), place(1 - y, z, c)) for y, z, c in DEVICES]


def ring(k):
    return [(place(y, z, c), place(y, (z + k) % RING, c)) for y, z, c in DEVICES]


NEXT_CHIP = [(p, p + 1) for p in range(1, 15, 2)] + [(p + 1, p) for p in range(1, 15, 2)]


VMEM = pl.BlockSpec(memory_space=pltpu.VMEM)
SMEM = pl.BlockSpec(memory_space=pltpu.SMEM)
ANY = pl.BlockSpec(memory_space=pl.ANY)
HBM = pl.BlockSpec(memory_space=pltpu.HBM)


def cost(microseconds):
    return pl.CostEstimate(
        flops=int(microseconds * 1e9), bytes_accessed=int(microseconds * 3e6), transcendentals=0
    )


KEPT = "kept"


def in_vmem(array):
    return pltpu.with_memory_space_constraint(array, pltpu.VMEM)


def in_hbm(array):
    return pltpu.with_memory_space_constraint(array, pltpu.HBM)


def call(body, name, microseconds, in_specs, outs, scratch=(), aliases=None, megabytes=12):
    return pl.pallas_call(
        body,
        in_specs=in_specs,
        out_specs=[VMEM if spec is KEPT else spec for _, _, spec in outs],
        out_shape=[
            (pltpu.VMEM if spec is KEPT else jax.ShapeDtypeStruct)(shape, dtype)
            for shape, dtype, spec in outs
        ],
        scratch_shapes=list(scratch),
        input_output_aliases=aliases or {},
        compiler_params=pltpu.CompilerParams(vmem_limit_bytes=megabytes * 2**20),
        cost_estimate=cost(microseconds),
        name=name,
    )


def edge_starts(core):
    last = SLAB - FRAME
    return (
        pl.multiple_of(jnp.where(core == 0, last, 0), 16),
        pl.multiple_of(jnp.where(core == 0, 0, last), 16),
    )


def prepare_kernel(place_ref, latent_ref, stale_ref, core_ref, chip_ref, o0, o1, o2, o3, sems):
    outs = (o0, o1, o2, o3)
    core_start, chip_start = edge_starts(place_ref[1])
    copies = [
        pltpu.make_async_copy(latent_ref.at[pl.ds(chip_start, FRAME), :], chip_ref, sems.at[8]),
        pltpu.make_async_copy(latent_ref.at[pl.ds(core_start, FRAME), :], core_ref, sems.at[9]),
    ]
    for k in range(RING):
        start = (place_ref[0] + k) % RING * WIDE
        for part in range(2):
            columns = pl.ds(pl.multiple_of(start + part * D, HEAD), WIDE)
            copies.append(
                pltpu.make_async_copy(
                    stale_ref.at[:, columns],
                    outs[k].at[:, part * WIDE : (part + 1) * WIDE],
                    sems.at[2 * k + part],
                )
            )
    for copy in copies:
        copy.start()
    for copy in copies:
        copy.wait()


def prepare(where, latent, stale_kv):
    edge = ((FRAME, D), bf16, VMEM)
    return call(
        prepare_kernel,
        "prepare",
        1,
        [SMEM, HBM, HBM],
        [edge, edge] + [((SLAB, 2 * WIDE), bf16, VMEM)] * RING,
        [pltpu.SemaphoreType.DMA((10,))],
    )(where, in_hbm(latent), in_hbm(stale_kv))


def mix_rows(place_ref, state_ref, core_ref, chip_ref, conv_ref, mod_ref, mixed_ref, normed_ref, row):
    first = place_ref[1] == 0
    state = state_ref[...].astype(f32)
    core_rows = core_ref[...].astype(f32)
    chip_rows = chip_ref[...].astype(f32)
    above = jnp.where(first, chip_rows, core_rows)
    below = jnp.where(first, core_rows, chip_rows)
    before = jnp.concatenate([above, state[: SLAB - FRAME]], 0)
    after_rows = jnp.concatenate([state[FRAME:], below], 0)
    mixed = (
        state
        + conv_ref[0:1, :] * before
        + conv_ref[1:2, :] * state
        + conv_ref[2:3, :] * after_rows
    )
    mixed_ref[...] = mixed
    shift = mod_ref[row : row + 1, :D]
    scale = mod_ref[row : row + 1, D : 2 * D]
    centred = mixed - jnp.mean(mixed, -1, keepdims=True)
    variance = jnp.mean(centred * centred, -1, keepdims=True)
    normed_ref[...] = (centred * lax.rsqrt(variance + epsilon) * (1.0 + scale) + shift).astype(bf16)


def embedding(moment):
    halfway = FREQ // 2
    index = lax.broadcasted_iota(jnp.int32, (halfway, 1), 0).astype(f32)
    angles = moment.astype(f32) * jnp.exp(-math.log(10000.0) * index / halfway)
    values = jnp.concatenate([jnp.cos(angles), jnp.sin(angles)], 0)
    return values / (1.0 + jnp.exp(-values))


def head_normed(block, gain):
    mean_square = jnp.mean(block * block, -1, keepdims=True)
    return (block * lax.rsqrt(mean_square + epsilon) * gain).astype(bf16)


def project_rows(normed, gain_ref, group, weights, out_ref):
    for part in range(3):
        block = jnp.dot(normed, weights[part], preferred_element_type=f32)
        if part < 2:
            gain = gain_ref[part : part + 1, pl.ds(group, WIDE)]
            for h in range(GROUP):
                here = slice(h * HEAD, (h + 1) * HEAD)
                out_ref[:, part * WIDE + h * HEAD : part * WIDE + (h + 1) * HEAD] = head_normed(
                    block[:, here], gain[:, here]
                )
        else:
            out_ref[:, part * WIDE :] = block.astype(bf16)


def open_kernel(
    place_ref, latent_ref, core_ref, chip_ref, taps_ref, q_gain_ref, k_gain_ref,
    w_mod_ref, w_qkv_ref, mod_ref, gains_ref, mixed_ref, o0, o1, o2, o3,
    mod_held, w_held, state_ref, conv_ref, normed_ref, sems
):
    outs = (o0, o1, o2, o3)
    tiles = mod_held.shape[0]
    tile = mod_held.shape[2]
    mods = [
        pltpu.make_async_copy(
            w_mod_ref.at[:, i * tile : (i + 1) * tile], mod_held.at[i], sems.at[i]
        )
        for i in range(tiles)
    ]
    rest = [
        pltpu.make_async_copy(latent_ref, state_ref, sems.at[tiles]),
        pltpu.make_async_copy(taps_ref, conv_ref, sems.at[tiles + 1]),
    ]
    groups, loads = {}, {}
    for k in range(RING):
        groups[k] = pl.multiple_of((place_ref[0] + k) % RING * WIDE, HEAD)
        loads[k] = [
            pltpu.make_async_copy(
                w_qkv_ref.at[:, pl.ds(pl.multiple_of(groups[k] + part * D, HEAD), WIDE)],
                w_held.at[3 * k + part],
                sems.at[tiles + 2 + 3 * k + part],
            )
            for part in range(3)
        ]
    for copy in (*rest, *mods, *loads[2]):
        copy.start()
    gains_ref[0:1, :] = (q_gain_ref[...] * (LOG2E / math.sqrt(HEAD))).reshape(1, D)
    gains_ref[1:2, :] = k_gain_ref[...].reshape(1, D)
    active = [embedding(place_ref[2 + s]) for s in range(STEPS)]
    for i, copy in enumerate(mods):
        copy.wait()
        if i == tiles // 2:
            for load in loads[1]:
                load.start()
        weights = mod_held[i]
        for s in range(STEPS):
            mod_ref[s : s + 1, i * tile : (i + 1) * tile] = jnp.sum(
                weights * active[s], 0, keepdims=True
            )
    for load in loads[3]:
        load.start()
    for copy in rest:
        copy.wait()
    mix_rows(place_ref, state_ref, core_ref, chip_ref, conv_ref, mod_ref, mixed_ref, normed_ref, 0)
    for k in (2, 1, 3, 0):
        if k == 2:
            for load in loads[0]:
                load.start()
        for load in loads[k]:
            load.wait()
        project_rows(
            normed_ref[...], gains_ref, groups[k], [w_held[3 * k + part] for part in range(3)], outs[k]
        )


def opening(where, state, core_rows, chip_rows, conv_weight, q_gain, k_gain, w_mod, w_qkv):
    tiles = 6
    return call(
        open_kernel,
        "opening",
        8,
        [SMEM, HBM, VMEM, VMEM, HBM, VMEM, VMEM, HBM, HBM],
        [((STEPS, w_mod.shape[1]), f32, VMEM), ((2, D), f32, VMEM), ((SLAB, D), f32, VMEM)]
        + [((SLAB, 3 * WIDE), bf16, VMEM)] * RING,
        [
            pltpu.VMEM((tiles, FREQ, w_mod.shape[1] // tiles), f32),
            pltpu.VMEM((3 * RING, D, WIDE), bf16),
            pltpu.VMEM((SLAB, D), bf16),
            pltpu.VMEM((3, D), f32),
            pltpu.VMEM((SLAB, D), bf16),
            pltpu.SemaphoreType.DMA((tiles + 2 + 3 * RING,)),
        ],
        megabytes=32,
    )(
        where, in_hbm(state), core_rows, chip_rows, in_hbm(conv_weight), q_gain, k_gain,
        in_hbm(w_mod), in_hbm(w_qkv),
    )


def mix_kernel(*refs, row):
    mix_rows(*refs, row)


def mix(where, state, core_rows, chip_rows, conv_weight, mod, row):
    return call(
        functools.partial(mix_kernel, row=row),
        "mix",
        1.2,
        [SMEM] + [VMEM] * 5,
        [((SLAB, D), f32, VMEM), ((SLAB, D), bf16, VMEM)],
    )(where, state, core_rows, chip_rows, conv_weight, mod)


def project_kernel(place_ref, normed_ref, gain_ref, w_ref, token_ref, out_ref, *, k):
    group = pl.multiple_of((place_ref[0] + k) % RING * WIDE, HEAD)
    weights = [
        w_ref[:, pl.ds(pl.multiple_of(group + part * D, HEAD), WIDE)] for part in range(3)
    ]
    project_rows(normed_ref[...], gain_ref, group, weights, out_ref)


def project(where, normed, gains, w_qkv, k, token):
    return call(
        functools.partial(project_kernel, k=k),
        "project",
        1.4,
        [SMEM] + [VMEM] * 3 + [ANY],
        [((SLAB, 3 * WIDE), bf16, VMEM)],
    )(where, normed, gains, w_qkv, token)[0]


def hold_kernel(*refs):
    pass


def held(array, tokens):
    return call(
        hold_kernel,
        "hold",
        0.1,
        [ANY] * (1 + len(tokens)),
        [(array.shape, array.dtype, ANY)],
        aliases={0: 0},
    )(array, *tokens)[0]


def stack_kernel(*refs):
    blocks, out_ref = refs[:RING], refs[-1]
    first = blocks[0].shape[1] - 2 * WIDE
    for k in range(RING):
        out_ref[k * SLAB : (k + 1) * SLAB, :] = blocks[k][:, first:]


def stack(blocks, token):
    return call(
        stack_kernel,
        "stack",
        1,
        [VMEM] * RING + [ANY],
        [((RING * SLAB, 2 * WIDE), bf16, VMEM)],
    )(*[blocks[k] for k in range(RING)], token)[0]


def join_kernel(place_ref, *refs):
    cache_ref = refs[-1]
    for k in range(RING):
        start = pl.multiple_of((place_ref[0] + k) % RING * WIDE, HEAD)
        cache_ref[:, pl.ds(start, WIDE)] = refs[k][:, WIDE : 2 * WIDE]
        cache_ref[:, pl.ds(pl.multiple_of(start + D, HEAD), WIDE)] = refs[k][:, 2 * WIDE :]


def join_cache(where, blocks, token):
    return call(
        join_kernel,
        "join_cache",
        1,
        [SMEM] + [VMEM] * RING + [ANY],
        [((SLAB, 2 * D), bf16, VMEM)],
    )(where, *[blocks[k] for k in range(RING)], token)[0]


def live_bias(place_ref, counts_ref):
    z, y, c = place_ref[0], place_ref[4], place_ref[1]
    index = lax.broadcasted_iota(jnp.int32, (1, SLAB), 1)
    rows = []
    for yy, cc in ((y, c), (y, 1 - c), (1 - y, c), (1 - y, 1 - c)):
        slabs = [8 * yy + 2 * ((z + RING - j) % RING) + cc for j in range(RING)]
        rows.append(
            jnp.concatenate(
                [jnp.where(index < counts_ref[slab], 0.0, masked_score) for slab in slabs], 1
            )
        )
    return rows


def attend_kernel(place_ref, counts_ref, *refs, slots, loads):
    n = len(slots)
    fresh, olds, outs = refs[:n], refs[n : n + 4], refs[n + 5 + loads :][:n]
    bias = live_bias(place_ref, counts_ref)
    if loads:
        load = pltpu.make_async_copy(refs[n + 5], refs[2 * n + 6], refs[2 * n + 7])
        load.start()
    rows = RING * SLAB
    ones = jnp.ones((rows, HEAD), bf16)

    def columns(part, h):
        return slice((part * GROUP + h) * HEAD, (part * GROUP + h + 1) * HEAD)

    for h in range(GROUP):
        for i, slot in enumerate(slots):
            queries = fresh[i][:, columns(0, h)]
            keys, values = [], []
            for a in range(4):
                for held, part in ((keys, 0), (values, 1)):
                    block = olds[a][:, columns(part, h)]
                    if a == 0:
                        pieces = [block[j * SLAB : (j + 1) * SLAB] for j in range(RING)]
                        pieces[slot] = fresh[i][:, columns(part + 1, h)]
                        block = jnp.concatenate(pieces, 0)
                    held.append(block)
            scores = [
                lax.dot_general(
                    queries, keys[a], (((1,), (1,)), ((), ())), preferred_element_type=f32
                )
                + bias[a]
                for a in range(4)
            ]
            highest = functools.reduce(
                jnp.maximum, [jnp.max(block, -1, keepdims=True) for block in scores]
            )
            summed = 0.0
            for a in range(4):
                probs = jnp.exp2(scores[a] - highest).astype(bf16)
                summed += jnp.dot(
                    probs, jnp.concatenate([values[a], ones], 1), preferred_element_type=f32
                )
            outs[i][:, columns(0, h)] = (summed[:, :HEAD] / summed[:, HEAD:]).astype(bf16)
    if loads:
        load.wait()


def attend(where, counts, fresh, olds, slots, token, weight=None):
    n = len(slots)
    loads = 0 if weight is None else 1
    return call(
        functools.partial(attend_kernel, slots=slots, loads=loads),
        "attend",
        2.4,
        [SMEM] * 2 + [VMEM] * (n + 4) + [ANY] + [HBM] * loads,
        [((SLAB, WIDE), bf16, VMEM)] * n + ([(weight.shape, bf16, KEPT)] if loads else []),
        [pltpu.SemaphoreType.DMA] if loads else [],
    )(
        where, counts, *[fresh[slot] for slot in slots], *olds, token,
        *([in_hbm(weight)] if loads else []),
    )


def output_kernel(
    place_ref, a0, a1, a2, a3, w_ref, mixed_ref, mod_ref, out_ref, core_ref, chip_ref, *, row
):
    total = 0.0
    for k, block in enumerate((a0, a1, a2, a3)):
        start = pl.multiple_of((place_ref[0] + k) % RING * WIDE, HEAD)
        total += jnp.dot(block[...], w_ref[pl.ds(start, WIDE), :], preferred_element_type=f32)
    gate = mod_ref[row : row + 1, 2 * D :]
    out_ref[...] = (mixed_ref[...] + gate * total).astype(bf16)
    core_start, chip_start = edge_starts(place_ref[1])
    core_ref[...] = out_ref[pl.ds(core_start, FRAME), :]
    chip_ref[...] = out_ref[pl.ds(chip_start, FRAME), :]


def output(where, attended, w_out, mixed, mod, row):
    edge = ((FRAME, D), bf16, VMEM)
    return call(
        functools.partial(output_kernel, row=row),
        "output",
        2,
        [SMEM] + [VMEM] * 7,
        [((SLAB, D), bf16, VMEM), edge, edge],
    )(where, *[attended[k] for k in range(RING)], in_vmem(w_out), mixed, mod)


def sent(block, k):
    return lax.ppermute(block, "patch", ring(k % RING)) if k % RING else block


def shards(latent, stale_kv, timesteps, counts, conv_weight, w_mod, w_qkv, q_gain, k_gain, w_out):
    own_slab = lax.axis_index("patch")
    y, z, c = own_slab // 8, (own_slab // 2) % RING, own_slab % 2
    where = jnp.stack([z, c, timesteps[0], timesteps[1], y]).astype(jnp.int32)
    state = latent
    to_core, to_chip, *pieces = prepare(where, latent, stale_kv)
    for step in range(STEPS):
        last = step + 1 == STEPS
        chip_rows = lax.ppermute(to_chip, "patch", NEXT_CHIP)
        core_rows = lax.ppermute(to_core, "patch", CORE)
        if step == 0:
            arrived = {k: sent(pieces[k], k) for k in (2, 1, 3, 0)}
            mod, gains, mixed, *blocks = opening(
                where, state, core_rows, chip_rows, conv_weight, q_gain, k_gain, w_mod, w_qkv
            )
            old = stack(arrived, blocks[2])
            old_y = lax.ppermute(old, "patch", ACROSS)
            old_core = lax.ppermute(old, "patch", CORE)
            fresh = {k: sent(blocks[k], k) for k in (2, 1, 3, 0)}
        else:
            mixed, normed = mix(where, state, core_rows, chip_rows, conv_weight, mod, step)
            blocks, fresh = {}, {}
            token = gains
            for k in (2, 1, 3):
                token = blocks[k] = project(where, normed, gains, w_qkv, k, token)
                fresh[k] = sent(token, k)
            blocks[0] = fresh[0] = project(where, normed, gains, w_qkv, 0, fresh[2])
        old_y = held(old_y, [fresh[k] for k in (2, 1, 3, 0)])
        olds = [old, old_core, old_y, lax.ppermute(old_y, "patch", CORE)]
        if step == 0:
            *far, w_out = attend(where, counts, fresh, olds, (2, 1), gains, w_out)
        else:
            far = attend(where, counts, fresh, olds, (2, 1), gains)
        returned = {2: sent(far[0], -2), 1: sent(far[1], -1)}
        near = attend(where, counts, fresh, olds, (3, 0), far[0])
        returned |= {3: sent(near[0], -3), 0: near[1]}
        if last:
            cache = join_cache(where, blocks, near[1])
        else:
            old = stack(fresh, returned[2])
            old_y = lax.ppermute(old, "patch", ACROSS)
            old_core = lax.ppermute(old, "patch", CORE)
        state, to_core, to_chip = output(where, returned, w_out, mixed, mod, step)
    return (state, cache)


def solution(mesh):
    rows = P(("req", "patch"), None)
    return jax.shard_map(
        shards,
        mesh=mesh,
        in_specs=(rows, rows, P("req"), P("req"), P(), P(), P(), P(), P(), P()),
        out_specs=(rows, rows),
        check_vma=False,
    )
```

time: 265 us -> 116 us (0.44)
  local copies, waits for them, and re-layouts: 65.4 us -> 1.42 us
  matrix products: 58.3 us -> 0 us
  waiting for transfers between devices: 90.4 us -> 32.2 us
  starting transfers between devices: 6.37 us -> 45 us
  Pallas kernels: 0 us -> 34.9 us
  other arithmetic: 26 us -> 0.73 us
  between operations: 16 us -> 0.92 us
    all_gather x2 -> x0, waiting for transfers between devices: 90.4 us -> none  [shards(): lax.all_gather(cache_rows, 'patch', axis=0, tiled=True)]
    dot_general x14 -> x0, matrix products: 58.3 us -> none  [the longest x4 17.3 us: attend(): jnp.einsum('qhk,khd->qhd', weights.astype(jnp.bfloat16), values_block, pr...]
    slice x16 -> x0, local copies, waits for them, and re-layouts: 48.4 us -> none  [the longest x3 27.3 us: cached_step(): block_rows[:, :head_total].reshape(count_rows, heads_count, HEAD)]
    ppermute x4 -> x25, starting transfers between devices: 6.29 us -> 45 us  [the longest x15 23.4 us: sent(): return lax.ppermute(block, 'patch', ring(k % RING)) if k % RING else block]
    pallas_call x0 -> x18, Pallas kernels: none -> 34.9 us  [the longest x4 12.4 us: attend(): call(functools.partial(attend_kernel, slots=slots, loads=loads), 'attend'...]
    ppermute x4 -> x25, waiting for transfers between devices: 0.01 us -> 32.2 us  [the longest x15 27.7 us: sent(): return lax.ppermute(block, 'patch', ring(k % RING)) if k % RING else block]
    reduce_sum x14 -> x0, other arithmetic: 16.1 us -> none  [the longest x4 11.2 us: attend(): denominator = denominator * factor + jnp.sum(weights, -1)]
    mul x4 -> x0, local copies, waits for them, and re-layouts: 6.47 us -> none  [head_normed(): split_rows * lax.rsqrt(mean_square + epsilon)]
  transfers between devices with their start and end apart: 6 -> 25, of which waited for: 2 -> 14; matrix products, arithmetic and copies ran while one was open for 34% -> 0% of each run, Pallas kernels for 0% -> 14%
where the time goes in v2:
time: 116 us; the launch traced here: 115 us
  starting transfers between devices  45 us (39%)
  Pallas kernels  34.9 us (30%)
  waiting for transfers between devices  32.2 us (28%)
  local copies, waits for them, and re-layouts  1.42 us (1%)
    ppermute x15, waiting for transfers between devices, sent(): return lax.ppermute(block, 'patch', ring(k % RING)) if k % RING else block  27.7 us
    ppermute x15, starting transfers between devices, sent(): return lax.ppermute(block, 'patch', ring(k % RING)) if k % RING else block  23.4 us
    pallas_call x4, Pallas kernels, attend(): call(functools.partial(attend_kernel, slots=slots, loads=loads), 'attend'...  12.4 us
    ppermute x2, starting transfers between devices, shards(): old_y = lax.ppermute(old, 'patch', ACROSS)  11.3 us
    pallas_call x1, Pallas kernels, opening(): call(open_kernel, 'opening', 8, [SMEM, HBM, VMEM, VMEM, HBM, VMEM, VMEM,...  8.36 us
    ppermute x2, starting transfers between devices, shards(): old_core = lax.ppermute(old, 'patch', CORE)  6.13 us
    pallas_call x4, Pallas kernels, project(): call(functools.partial(project_kernel, k=k), 'project', 1.4, [SMEM] + [VM...  5.37 us
    ppermute x2, waiting for transfers between devices, shards(): olds = [old, old_core, old_y, lax.ppermute(old_y, 'patch', CORE)]  4.08 us
  transfers between devices with their start and end apart: 25, of which 14 were waited for; matrix products, arithmetic and copies ran while one was open for 0% of the time, Pallas kernels for 14%

profile of v2, /device:TPU:0, one launch (start us, length us, event | category | flops | bytes accessed | tf_op | source)
XLA Modules:
  0.0 115.2 jit_solution(5169305677326789997)
XLA Ops:
  1.4 2.0 %prepare.1 = (bf16[80,1536]{1,0:T(8,128)(2,1)S(1)}, bf16[80,1536]{1,0:T(8,128)(2,1)S(1)}, bf16[128,768]{1,0:T(8,128)(2,1)S(1)}, bf16[128,768]{1,0:T(8,128)(2,1)S...) custom-call(s32[5]{0:T(128)S(1)} %pad_add_fusion.place_ref.refs_0_, bf16[128,1536]{1,0:T(8,128)(2,1)} %latent_ref.3, ...), custom_call_target="tpu_custom_call" | custom-call | flops 1000000000 | bytes 3000000 | tf_op jit(solution)/shard_map/prepare/pallas_call | solution.py:118
  4.2 3.4 %collective-permute-start.3 = (bf16[128,768]{1,0:T(8,128)(2,1)S(1)}, bf16[128,768]{1,0:T(8,128)(2,1)S(1)}, u32[]{:S(2)}, u32[]{:S(2)}) collective-permute-start(bf16[128,768]{1,0:T(8,128)(2,1)S(1)} %get-tuple-element.35), channel_id=1, source_target_pairs={{0,2},{1,3},{2,4},{3,5},{4,6},{5,7},{6,0},{7,1},{8,10},{9,11},{10,... | collective-permute-start | bytes 589832 | tf_op jit(solution)/shard_map/ppermute | solution.py:446
  7.6 4.0 %collective-permute-start.4 = (bf16[128,768]{1,0:T(8,128)(2,1)S(1)}, bf16[128,768]{1,0:T(8,128)(2,1)S(1)}, u32[]{:S(2)}, u32[]{:S(2)}) collective-permute-start(bf16[128,768]{1,0:T(8,128)(2,1)S(1)} %get-tuple-element.36), channel_id=1, source_target_pairs={{0,4},{1,5},{2,6},{3,7},{4,0},{5,1},{6,2},{7,3},{8,12},{9,13},{10,... | collective-permute-start | bytes 589832 | tf_op jit(solution)/shard_map/ppermute | solution.py:446
  13.7 8.4 %opening.1 = (f32[2,4608]{1,0:T(2,128)S(1)}, f32[2,1536]{1,0:T(2,128)S(1)}, f32[128,1536]{1,0:T(8,128)S(1)}, bf16[128,1152]{1,0:T(8,128)(2,1)S(1)}, bf16[128,115...) custom-call(s32[5]{0:T(128)S(1)} %pad_add_fusion.place_ref.refs_0_, ...), custom_call_target="tpu_custom_call" | custom-call | flops 8000000000 | bytes 24000000 | tf_op jit(solution)/shard_map/opening/pallas_call | solution.py:240
  22.8 5.2 %collective-permute-start.7 = (bf16[512,768]{1,0:T(8,128)(2,1)S(1)}, bf16[512,768]{1,0:T(8,128)(2,1)S(1)}, u32[]{:S(2)}, u32[]{:S(2)}) collective-permute-start(bf16[512,768]{1,0:T(8,128)(2,1)S(1)} %stack.18.refs_2_), channel_id=1, source_target_pairs={{0,8},{1,9},{2,10},{3,11},{4,12},{5,13},{6,14},{7,15},{8,0},{9,1},... | collective-permute-start | bytes 2359304 | tf_op jit(solution)/shard_map/ppermute | solution.py:465
  28.0 1.8 %collective-permute-start.2 = (bf16[128,1152]{1,0:T(8,128)(2,1)S(1)}, bf16[128,1152]{1,0:T(8,128)(2,1)S(1)}, u32[]{:S(2)}, u32[]{:S(2)}) collective-permute-start(bf16[128,1152]{1,0:T(8,128)(2,1)S(1)} %get-tuple-element.32), channel_id=1, source_target_pairs={{0,6},{1,7},{2,0},{3,1},{4,2},{5,3},{6,4},{7,5},{8,14},{9,15},{10,... | collective-permute-start | bytes 884744 | tf_op jit(solution)/shard_map/ppermute | solution.py:446
  30.0 1.9 %collective-permute-start.8 = (bf16[128,1152]{1,0:T(8,128)(2,1)S(1)}, bf16[128,1152]{1,0:T(8,128)(2,1)S(1)}, u32[]{:S(2)}, u32[]{:S(2)}) collective-permute-start(bf16[128,1152]{1,0:T(8,128)(2,1)S(1)} %get-tuple-element.38.refs_4_), channel_id=1, source_target_pairs={{0,4},{1,5},{2,6},{3,7},{4,0},{5,1},{6,2},{7,3},{8,12},{9,13},{10,... | collective-permute-start | bytes 884744 | tf_op jit(solution)/shard_map/ppermute | solution.py:446
  32.3 10.7 %collective-permute-done.2.refs_3_.refs_0_ = bf16[128,1152]{1,0:T(8,128)(2,1)S(1)} collective-permute-done((bf16[128,1152]{1,0:T(8,128)(2,1)S(1)}, bf16[128,1152]{1,0:T(8,128)(2,1)S(1)}, u32[]{:S(2)}, u32[]{:S(2)}) %collective-permute-start.2) | collective-permute-done | bytes 294944 | tf_op jit(solution)/shard_map/ppermute | solution.py:446
  43.0 3.9 %collective-permute-done.9.refs_2_.refs_1_ = bf16[128,1152]{1,0:T(8,128)(2,1)S(1)} collective-permute-done((bf16[128,1152]{1,0:T(8,128)(2,1)S(1)}, bf16[128,1152]{1,0:T(8,128)(2,1)S(1)}, u32[]{:S(2)}, u32[]{:S(2)}) %collective-permute-start.9) | collective-permute-done | bytes 294944 | tf_op jit(solution)/shard_map/ppermute | solution.py:446
  47.3 2.2 %collective-permute-done.10.refs_5_ = bf16[512,768]{1,0:T(8,128)(2,1)S(1)} collective-permute-done((bf16[512,768]{1,0:T(8,128)(2,1)S(1)}, bf16[512,768]{1,0:T(8,128)(2,1)S(1)}, u32[]{:S(2)}, u32[]{:S(2)}) %collective-permute-start.10) | collective-permute-done | bytes 786464 | tf_op jit(solution)/shard_map/ppermute | solution.py:477
  49.4 3.5 %attend.4 = (bf16[128,384]{1,0:T(8,128)(2,1)S(1)}, bf16[128,384]{1,0:T(8,128)(2,1)S(1)}, bf16[1536,1536]{1,0:T(8,128)(2,1)S(1)}) custom-call(s32[5]{0:T(128)S(1)} %pad_add_fusion.place_ref.refs_0_, s32[16]{0:T(128)S(1)} %copy-done.3, bf16[128,1152]{1,0:T(8,128)(2,1)S(1)} %collective-permute-done.8.refs_1_.refs_0_.refs_2_, ...), custom_call_target="tpu_custom_call" | custom-call | flops 2400000000 | bytes 7200000 | tf_op jit(solution)/shard_map/attend/pallas_call | solution.py:407
  53.0 2.9 %attend.5 = (bf16[128,384]{1,0:T(8,128)(2,1)S(1)}, bf16[128,384]{1,0:T(8,128)(2,1)S(1)}) custom-call(s32[5]{0:T(128)S(1)} %pad_add_fusion.place_ref.refs_0_, s32[16]{0:T(128)S(1)} %copy-done.3, bf16[128,1152]{1,0:T(8,128)(2,1)S(1)} %collective-permute-done.2.refs_3_.refs_0_, bf16[128,1152]{1,0:T(8,128)(2,1)S(1)} %get-tuple-element.33.refs_4_.refs_1_.refs_0_, ...), custom_call_target="tpu_custom_call" | custom-call | flops 2400000000 | bytes 7200000 | tf_op jit(solution)/shard_map/attend/pallas_call | solution.py:407
  56.0 3.2 %collective-permute-start.11 = (bf16[128,384]{1,0:T(8,128)(2,1)S(1)}, bf16[128,384]{1,0:T(8,128)(2,1)S(1)}, u32[]{:S(2)}, u32[]{:S(2)}) collective-permute-start(bf16[128,384]{1,0:T(8,128)(2,1)S(1)} %get-tuple-element.43), channel_id=1, source_target_pairs={{0,6},{1,7},{2,0},{3,1},{4,2},{5,3},{6,4},{7,5},{8,14},{9,15},{10,... | collective-permute-start | bytes 294920 | tf_op jit(solution)/shard_map/ppermute | solution.py:446
  59.2 2.8 %collective-permute-done.13.a3 = bf16[128,384]{1,0:T(8,128)(2,1)S(1)} collective-permute-done((bf16[128,384]{1,0:T(8,128)(2,1)S(1)}, bf16[128,384]{1,0:T(8,128)(2,1)S(1)}, u32[]{:S(2)}, u32[]{:S(2)}) %collective-permute-start.13) | collective-permute-done | bytes 98336 | tf_op jit(solution)/shard_map/ppermute | solution.py:446
  62.0 1.4 %collective-permute-done.11.a1 = bf16[128,384]{1,0:T(8,128)(2,1)S(1)} collective-permute-done((bf16[128,384]{1,0:T(8,128)(2,1)S(1)}, bf16[128,384]{1,0:T(8,128)(2,1)S(1)}, u32[]{:S(2)}, u32[]{:S(2)}) %collective-permute-start.11) | collective-permute-done | bytes 98336 | tf_op jit(solution)/shard_map/ppermute | solution.py:446
  63.4 1.9 %collective-permute-done.12.a2.refs_4_ = bf16[128,384]{1,0:T(8,128)(2,1)S(1)} collective-permute-done((bf16[128,384]{1,0:T(8,128)(2,1)S(1)}, bf16[128,384]{1,0:T(8,128)(2,1)S(1)}, u32[]{:S(2)}, u32[]{:S(2)}) %collective-permute-start.12) | collective-permute-done | bytes 98336 | tf_op jit(solution)/shard_map/ppermute | solution.py:446
  65.3 1.6 %output.2 = (bf16[128,1536]{1,0:T(8,128)(2,1)S(1)}, bf16[80,1536]{1,0:T(8,128)(2,1)S(1)}, bf16[80,1536]{1,0:T(8,128)(2,1)S(1)}) custom-call(s32[5]{0:T(128)S(1)} %pad_add_fusion.place_ref.refs_0_, bf16[128,384]{1,0:T(8,128)(2,1)S(1)} %get-tuple-element.42.a0, bf16[128,384]{1,0:T(8,128)(2,1)S(1)} %collective-permute-done.11.a1, ...), custom_call_target="tpu_custom_call" | custom-call | flops 2000000000 | bytes 6000000 | tf_op jit(solution)/shard_map/output/pallas_call | solution.py:436
  67.7 6.1 %collective-permute-start.19 = (bf16[512,768]{1,0:T(8,128)(2,1)S(1)}, bf16[512,768]{1,0:T(8,128)(2,1)S(1)}, u32[]{:S(2)}, u32[]{:S(2)}) collective-permute-start(bf16[512,768]{1,0:T(8,128)(2,1)S(1)} %stack.19.refs_2_), channel_id=1, source_target_pairs={{0,8},{1,9},{2,10},{3,11},{4,12},{5,13},{6,14},{7,15},{8,0},{9,1},... | collective-permute-start | bytes 2359304 | tf_op jit(solution)/shard_map/ppermute | solution.py:489
  75.0 1.4 %project.4.token_ref.refs_2_ = bf16[128,1152]{1,0:T(8,128)(2,1)S(1)} custom-call(s32[5]{0:T(128)S(1)} %pad_add_fusion.place_ref.refs_0_, bf16[128,1536]{1,0:T(8,128)(2,1)S(1)} %get-tuple-element.51.normed_ref, f32[2,1536]{1,0:T(2,128)S(1)} %get-tuple-element.40.refs_6_.gain_ref.token_ref, bf16[1536,4608]{1,0:T(8,128)(2,1)S(1)} %bitcast.4, ...), custom_call_target="tpu_custom_call" | custom-call | flops 1400000000 | bytes 4200000 | tf_op jit(solution)/shard_map/project/pallas_call | solution.py:285
  79.8 3.1 %collective-permute-start.16 = (bf16[128,1152]{1,0:T(8,128)(2,1)S(1)}, bf16[128,1152]{1,0:T(8,128)(2,1)S(1)}, u32[]{:S(2)}, u32[]{:S(2)}) collective-permute-start(bf16[128,1152]{1,0:T(8,128)(2,1)S(1)} %project.6.refs_3_), channel_id=1, source_target_pairs={{0,6},{1,7},{2,0},{3,1},{4,2},{5,3},{6,4},{7,5},{8,14},{9,15},{10,... | collective-permute-start | bytes 884744 | tf_op jit(solution)/shard_map/ppermute | solution.py:446
  82.9 5.8 %collective-permute-start.18 = (bf16[512,768]{1,0:T(8,128)(2,1)S(1)}, bf16[512,768]{1,0:T(8,128)(2,1)S(1)}, u32[]{:S(2)}, u32[]{:S(2)}) collective-permute-start(bf16[512,768]{1,0:T(8,128)(2,1)S(1)} %stack.19.refs_2_), channel_id=1, source_target_pairs={{0,1},{1,0},{2,3},{3,2},{4,5},{5,4},{6,7},{7,6},{8,9},{9,8},{10,11... | collective-permute-start | bytes 2359304 | tf_op jit(solution)/shard_map/ppermute | solution.py:490
  90.5 2.2 %collective-permute-done.20.refs_2_.refs_1_ = bf16[128,1152]{1,0:T(8,128)(2,1)S(1)} collective-permute-done((bf16[128,1152]{1,0:T(8,128)(2,1)S(1)}, bf16[128,1152]{1,0:T(8,128)(2,1)S(1)}, u32[]{:S(2)}, u32[]{:S(2)}) %collective-permute-start.20) | collective-permute-done | bytes 294944 | tf_op jit(solution)/shard_map/ppermute | solution.py:446
  93.1 2.3 %collective-permute-start.21 = (bf16[512,768]{1,0:T(8,128)(2,1)S(1)}, bf16[512,768]{1,0:T(8,128)(2,1)S(1)}, u32[]{:S(2)}, u32[]{:S(2)}) collective-permute-start(bf16[512,768]{1,0:T(8,128)(2,1)S(1)} %hold.3.refs_4_), channel_id=1, source_target_pairs={{0,1},{1,0},{2,3},{3,2},{4,5},{5,4},{6,7},{7,6},{8,9},{9,8},{10,11... | collective-permute-start | bytes 2359304 | tf_op jit(solution)/shard_map/ppermute | solution.py:477
  95.4 1.9 %collective-permute-done.21.refs_5_ = bf16[512,768]{1,0:T(8,128)(2,1)S(1)} collective-permute-done((bf16[512,768]{1,0:T(8,128)(2,1)S(1)}, bf16[512,768]{1,0:T(8,128)(2,1)S(1)}, u32[]{:S(2)}, u32[]{:S(2)}) %collective-permute-start.21) | collective-permute-done | bytes 786464 | tf_op jit(solution)/shard_map/ppermute | solution.py:477
  97.3 3.0 %attend.6 = (bf16[128,384]{1,0:T(8,128)(2,1)S(1)}, bf16[128,384]{1,0:T(8,128)(2,1)S(1)}) custom-call(s32[5]{0:T(128)S(1)} %pad_add_fusion.place_ref.refs_0_, s32[16]{0:T(128)S(1)} %copy-done.3, bf16[128,1152]{1,0:T(8,128)(2,1)S(1)} %collective-permute-done.17.token_ref.refs_1_.refs_0_, bf16[128,1152]{1,0:T(8,128)(2,1)S(1)} %collective-permute-done.20.refs_2_.refs_1_, ...), custom_call_target="tpu_custom_call" | custom-call | flops 2400000000 | bytes 7200000 | tf_op jit(solution)/shard_map/attend/pallas_call | solution.py:407
  100.3 3.0 %attend.7 = (bf16[128,384]{1,0:T(8,128)(2,1)S(1)}, bf16[128,384]{1,0:T(8,128)(2,1)S(1)}) custom-call(s32[5]{0:T(128)S(1)} %pad_add_fusion.place_ref.refs_0_, s32[16]{0:T(128)S(1)} %copy-done.3, bf16[128,1152]{1,0:T(8,128)(2,1)S(1)} %collective-permute-done.16.refs_3_.refs_0_, bf16[128,1152]{1,0:T(8,128)(2,1)S(1)} %project.7.refs_4_.refs_1_.refs_0_, ...), custom_call_target="tpu_custom_call" | custom-call | flops 2400000000 | bytes 7200000 | tf_op jit(solution)/shard_map/attend/pallas_call | solution.py:407
  103.3 1.4 %collective-permute-start.24 = (bf16[128,384]{1,0:T(8,128)(2,1)S(1)}, bf16[128,384]{1,0:T(8,128)(2,1)S(1)}, u32[]{:S(2)}, u32[]{:S(2)}) collective-permute-start(bf16[128,384]{1,0:T(8,128)(2,1)S(1)} %get-tuple-element.55), channel_id=1, source_target_pairs={{0,2},{1,3},{2,4},{3,5},{4,6},{5,7},{6,0},{7,1},{8,10},{9,11},{10,... | collective-permute-start | bytes 294920 | tf_op jit(solution)/shard_map/ppermute | solution.py:446
  104.6 2.0 %collective-permute-start.22 = (bf16[128,384]{1,0:T(8,128)(2,1)S(1)}, bf16[128,384]{1,0:T(8,128)(2,1)S(1)}, u32[]{:S(2)}, u32[]{:S(2)}) collective-permute-start(bf16[128,384]{1,0:T(8,128)(2,1)S(1)} %get-tuple-element.54), channel_id=1, source_target_pairs={{0,6},{1,7},{2,0},{3,1},{4,2},{5,3},{6,4},{7,5},{8,14},{9,15},{10,... | collective-permute-start | bytes 294920 | tf_op jit(solution)/shard_map/ppermute | solution.py:446
  107.4 1.5 %join_cache.1 = bf16[128,3072]{1,0:T(8,128)(2,1)} custom-call(s32[5]{0:T(128)S(1)} %pad_add_fusion.place_ref.refs_0_, bf16[128,1152]{1,0:T(8,128)(2,1)S(1)} %project.7.refs_4_.refs_1_.refs_0_, bf16[128,1152]{1,0:T(8,128)(2,1)S(1)} %project.5.token_ref.refs_1_, bf16[128,1152]{1,0:T(8,128)(2,1)S(1)} %project.4.token_ref.refs_2_, ...), custom_call_target="tpu_custom_call" | custom-call | flops 1000000000 | bytes 3000000 | tf_op jit(solution)/shard_map/join_cache/pallas_call | solution.py:335
  109.6 1.4 %collective-permute-done.22.a1 = bf16[128,384]{1,0:T(8,128)(2,1)S(1)} collective-permute-done((bf16[128,384]{1,0:T(8,128)(2,1)S(1)}, bf16[128,384]{1,0:T(8,128)(2,1)S(1)}, u32[]{:S(2)}, u32[]{:S(2)}) %collective-permute-start.22) | collective-permute-done | bytes 98336 | tf_op jit(solution)/shard_map/ppermute | solution.py:446
  111.0 1.7 %collective-permute-done.23.a2 = bf16[128,384]{1,0:T(8,128)(2,1)S(1)} collective-permute-done((bf16[128,384]{1,0:T(8,128)(2,1)S(1)}, bf16[128,384]{1,0:T(8,128)(2,1)S(1)}, u32[]{:S(2)}, u32[]{:S(2)}) %collective-permute-start.23) | collective-permute-done | bytes 98336 | tf_op jit(solution)/shard_map/ppermute | solution.py:446
  112.7 2.5 %output.3 = (bf16[128,1536]{1,0:T(8,128)(2,1)}, bf16[80,1536]{1,0:T(8,128)(2,1)}, bf16[80,1536]{1,0:T(8,128)(2,1)}) custom-call(s32[5]{0:T(128)S(1)} %pad_add_fusion.place_ref.refs_0_, bf16[128,384]{1,0:T(8,128)(2,1)S(1)} %get-tuple-element.53.a0.refs_4_, bf16[128,384]{1,0:T(8,128)(2,1)S(1)} %collective-permute-done.22.a1, ...), custom_call_target="tpu_custom_call" | custom-call | flops 2000000000 | bytes 6000000 | tf_op jit(solution)/shard_map/output/pallas_call | solution.py:436
  (54 shorter events, 14.4 us)
Async XLA Ops:
  3.4 8.9 %collective-permute-start = (bf16[80,1536]{1,0:T(8,128)(2,1)S(1)}, bf16[80,1536]{1,0:T(8,128)(2,1)S(1)}, u32[]{:S(2)}, u32[]{:S(2)}) collective-permute-start(bf16[80,1536]{1,0:T(8,128)(2,1)S(1)} %get-tuple-element.30), channel_id=1, source_target_pairs={{0,1},{1,0},{2,3},{3,2},{4,5},{5,4},{6,7},{7,6},{8,9},{9,8},{10,11... | collective-permute-start | bytes 737288 | tf_op jit(solution)/shard_map/ppermute | solution.py:458
  3.5 8.8 %collective-permute-start.1 = (bf16[80,1536]{1,0:T(8,128)(2,1)S(1)}, bf16[80,1536]{1,0:T(8,128)(2,1)S(1)}, u32[]{:S(2)}, u32[]{:S(2)}) collective-permute-start(bf16[80,1536]{1,0:T(8,128)(2,1)S(1)} %get-tuple-element.31), channel_id=1, source_target_pairs={{1,2},{3,4},{5,6},{7,8},{9,10},{11,12},{13,14},{2,1},{4,3},{6,5},{... | collective-permute-start | bytes 737288 | tf_op jit(solution)/shard_map/ppermute | solution.py:457
  4.2 17.9 %collective-permute-start.3 = (bf16[128,768]{1,0:T(8,128)(2,1)S(1)}, bf16[128,768]{1,0:T(8,128)(2,1)S(1)}, u32[]{:S(2)}, u32[]{:S(2)}) collective-permute-start(bf16[128,768]{1,0:T(8,128)(2,1)S(1)} %get-tuple-element.35), channel_id=1, source_target_pairs={{0,2},{1,3},{2,4},{3,5},{4,6},{5,7},{6,0},{7,1},{8,10},{9,11},{10,... | collective-permute-start | bytes 589832 | tf_op jit(solution)/shard_map/ppermute | solution.py:446
  7.6 14.5 %collective-permute-start.4 = (bf16[128,768]{1,0:T(8,128)(2,1)S(1)}, bf16[128,768]{1,0:T(8,128)(2,1)S(1)}, u32[]{:S(2)}, u32[]{:S(2)}) collective-permute-start(bf16[128,768]{1,0:T(8,128)(2,1)S(1)} %get-tuple-element.36), channel_id=1, source_target_pairs={{0,4},{1,5},{2,6},{3,7},{4,0},{5,1},{6,2},{7,3},{8,12},{9,13},{10,... | collective-permute-start | bytes 589832 | tf_op jit(solution)/shard_map/ppermute | solution.py:446
  11.6 11.1 %collective-permute-start.5 = (bf16[128,768]{1,0:T(8,128)(2,1)S(1)}, bf16[128,768]{1,0:T(8,128)(2,1)S(1)}, u32[]{:S(2)}, u32[]{:S(2)}) collective-permute-start(bf16[128,768]{1,0:T(8,128)(2,1)S(1)} %get-tuple-element.37), channel_id=1, source_target_pairs={{0,6},{1,7},{2,0},{3,1},{4,2},{5,3},{6,4},{7,5},{8,14},{9,15},{10,... | collective-permute-start | bytes 589832 | tf_op jit(solution)/shard_map/ppermute | solution.py:446
  12.3 0.7 copy-start.1
  22.1 27.4 %copy-start.3 = (s32[16]{0:T(128)S(1)}, s32[16]{0:T(128)}, u32[]{:S(2)}) copy-start(s32[16]{0:T(128)} %counts_ref.7) | copy-start | bytes 196
  22.8 24.1 %collective-permute-start.7 = (bf16[512,768]{1,0:T(8,128)(2,1)S(1)}, bf16[512,768]{1,0:T(8,128)(2,1)S(1)}, u32[]{:S(2)}, u32[]{:S(2)}) collective-permute-start(bf16[512,768]{1,0:T(8,128)(2,1)S(1)} %stack.18.refs_2_), channel_id=1, source_target_pairs={{0,8},{1,9},{2,10},{3,11},{4,12},{5,13},{6,14},{7,15},{8,0},{9,1},... | collective-permute-start | bytes 2359304 | tf_op jit(solution)/shard_map/ppermute | solution.py:465
  28.0 15.0 %collective-permute-start.2 = (bf16[128,1152]{1,0:T(8,128)(2,1)S(1)}, bf16[128,1152]{1,0:T(8,128)(2,1)S(1)}, u32[]{:S(2)}, u32[]{:S(2)}) collective-permute-start(bf16[128,1152]{1,0:T(8,128)(2,1)S(1)} %get-tuple-element.32), channel_id=1, source_target_pairs={{0,6},{1,7},{2,0},{3,1},{4,2},{5,3},{6,4},{7,5},{8,14},{9,15},{10,... | collective-permute-start | bytes 884744 | tf_op jit(solution)/shard_map/ppermute | solution.py:446
  29.7 17.1 %collective-permute-start.9 = (bf16[128,1152]{1,0:T(8,128)(2,1)S(1)}, bf16[128,1152]{1,0:T(8,128)(2,1)S(1)}, u32[]{:S(2)}, u32[]{:S(2)}) collective-permute-start(bf16[128,1152]{1,0:T(8,128)(2,1)S(1)} %get-tuple-element.39), channel_id=1, source_target_pairs={{0,2},{1,3},{2,4},{3,5},{4,6},{5,7},{6,0},{7,1},{8,10},{9,11},{10,... | collective-permute-start | bytes 884744 | tf_op jit(solution)/shard_map/ppermute | solution.py:446
  30.0 16.9 %collective-permute-start.8 = (bf16[128,1152]{1,0:T(8,128)(2,1)S(1)}, bf16[128,1152]{1,0:T(8,128)(2,1)S(1)}, u32[]{:S(2)}, u32[]{:S(2)}) collective-permute-start(bf16[128,1152]{1,0:T(8,128)(2,1)S(1)} %get-tuple-element.38.refs_4_), channel_id=1, source_target_pairs={{0,4},{1,5},{2,6},{3,7},{4,0},{5,1},{6,2},{7,3},{8,12},{9,13},{10,... | collective-permute-start | bytes 884744 | tf_op jit(solution)/shard_map/ppermute | solution.py:446
  31.9 15.3 %collective-permute-start.6 = (bf16[512,768]{1,0:T(8,128)(2,1)S(1)}, bf16[512,768]{1,0:T(8,128)(2,1)S(1)}, u32[]{:S(2)}, u32[]{:S(2)}) collective-permute-start(bf16[512,768]{1,0:T(8,128)(2,1)S(1)} %stack.18.refs_2_), channel_id=1, source_target_pairs={{0,1},{1,0},{2,3},{3,2},{4,5},{5,4},{6,7},{7,6},{8,9},{9,8},{10,11... | collective-permute-start | bytes 2359304 | tf_op jit(solution)/shard_map/ppermute | solution.py:466
  46.9 2.5 %collective-permute-start.10 = (bf16[512,768]{1,0:T(8,128)(2,1)S(1)}, bf16[512,768]{1,0:T(8,128)(2,1)S(1)}, u32[]{:S(2)}, u32[]{:S(2)}) collective-permute-start(bf16[512,768]{1,0:T(8,128)(2,1)S(1)} %hold.2.refs_4_), channel_id=1, source_target_pairs={{0,1},{1,0},{2,3},{3,2},{4,5},{5,4},{6,7},{7,6},{8,9},{9,8},{10,11... | collective-permute-start | bytes 2359304 | tf_op jit(solution)/shard_map/ppermute | solution.py:477
  49.4 25.5 %slice-start = ((s8[14155776]{0:T(1024)(128)(4,1)}), s8[4194304]{0:T(1024)(128)(4,1)S(1)}, s32[]{:S(2)}) async-start(s8[14155776]{0:T(1024)(128)(4,1)} %bitcast.3), calls=%async_computation | async-start | bytes 8388608
  49.4 25.5 %slice-start.1 = ((s8[14155776]{0:T(1024)(128)(4,1)}), s8[4194304]{0:T(1024)(128)(4,1)S(1)}, s32[]{:S(2)}) async-start(s8[14155776]{0:T(1024)(128)(4,1)} %bitcast.3), calls=%async_computation.1 | async-start | bytes 8388608
  53.0 22.0 %slice-start.2 = ((s8[14155776]{0:T(1024)(128)(4,1)}), s8[4194304]{0:T(1024)(128)(4,1)S(1)}, s32[]{:S(2)}) async-start(s8[14155776]{0:T(1024)(128)(4,1)} %bitcast.3), calls=%async_computation.2 | async-start | bytes 8388608
  55.9 6.1 %collective-permute-start.13 = (bf16[128,384]{1,0:T(8,128)(2,1)S(1)}, bf16[128,384]{1,0:T(8,128)(2,1)S(1)}, u32[]{:S(2)}, u32[]{:S(2)}) collective-permute-start(bf16[128,384]{1,0:T(8,128)(2,1)S(1)} %get-tuple-element.44), channel_id=1, source_target_pairs={{0,2},{1,3},{2,4},{3,5},{4,6},{5,7},{6,0},{7,1},{8,10},{9,11},{10,... | collective-permute-start | bytes 294920 | tf_op jit(solution)/shard_map/ppermute | solution.py:446
  56.0 7.4 %collective-permute-start.11 = (bf16[128,384]{1,0:T(8,128)(2,1)S(1)}, bf16[128,384]{1,0:T(8,128)(2,1)S(1)}, u32[]{:S(2)}, u32[]{:S(2)}) collective-permute-start(bf16[128,384]{1,0:T(8,128)(2,1)S(1)} %get-tuple-element.43), channel_id=1, source_target_pairs={{0,6},{1,7},{2,0},{3,1},{4,2},{5,3},{6,4},{7,5},{8,14},{9,15},{10,... | collective-permute-start | bytes 294920 | tf_op jit(solution)/shard_map/ppermute | solution.py:446
  59.2 6.1 %collective-permute-start.12 = (bf16[128,384]{1,0:T(8,128)(2,1)S(1)}, bf16[128,384]{1,0:T(8,128)(2,1)S(1)}, u32[]{:S(2)}, u32[]{:S(2)}) collective-permute-start(bf16[128,384]{1,0:T(8,128)(2,1)S(1)} %get-tuple-element.41.refs_6_), channel_id=1, source_target_pairs={{0,4},{1,5},{2,6},{3,7},{4,0},{5,1},{6,2},{7,3},{8,12},{9,13},{10,... | collective-permute-start | bytes 294920 | tf_op jit(solution)/shard_map/ppermute | solution.py:446
  65.3 8.5 %copy-start = (f32[3,1536]{1,0:T(4,128)S(1)}, f32[3,1536]{1,0:T(4,128)}, u32[]{:S(2)}) copy-start(f32[3,1536]{1,0:T(4,128)} %refs_4_.1) | copy-start | bytes 55300
  65.3 9.7 %slice-start.3 = ((s8[14155776]{0:T(1024)(128)(4,1)}), s8[1572864]{0:T(1024)(128)(4,1)S(1)}, s32[]{:S(2)}) async-start(s8[14155776]{0:T(1024)(128)(4,1)} %bitcast.3), calls=%async_computation.3 | async-start | bytes 3145728
  66.9 7.0 %collective-permute-start.14 = (bf16[80,1536]{1,0:T(8,128)(2,1)S(1)}, bf16[80,1536]{1,0:T(8,128)(2,1)S(1)}, u32[]{:S(2)}, u32[]{:S(2)}) collective-permute-start(bf16[80,1536]{1,0:T(8,128)(2,1)S(1)} %get-tuple-element.49), channel_id=1, source_target_pairs={{0,1},{1,0},{2,3},{3,2},{4,5},{5,4},{6,7},{7,6},{8,9},{9,8},{10,11... | collective-permute-start | bytes 737288 | tf_op jit(solution)/shard_map/ppermute | solution.py:458
  67.0 6.9 %collective-permute-start.15 = (bf16[80,1536]{1,0:T(8,128)(2,1)S(1)}, bf16[80,1536]{1,0:T(8,128)(2,1)S(1)}, u32[]{:S(2)}, u32[]{:S(2)}) collective-permute-start(bf16[80,1536]{1,0:T(8,128)(2,1)S(1)} %get-tuple-element.50), channel_id=1, source_target_pairs={{1,2},{3,4},{5,6},{7,8},{9,10},{11,12},{13,14},{2,1},{4,3},{6,5},{... | collective-permute-start | bytes 737288 | tf_op jit(solution)/shard_map/ppermute | solution.py:457
  67.7 25.4 %collective-permute-start.19 = (bf16[512,768]{1,0:T(8,128)(2,1)S(1)}, bf16[512,768]{1,0:T(8,128)(2,1)S(1)}, u32[]{:S(2)}, u32[]{:S(2)}) collective-permute-start(bf16[512,768]{1,0:T(8,128)(2,1)S(1)} %stack.19.refs_2_), channel_id=1, source_target_pairs={{0,8},{1,9},{2,10},{3,11},{4,12},{5,13},{6,14},{7,15},{8,0},{9,1},... | collective-permute-start | bytes 2359304 | tf_op jit(solution)/shard_map/ppermute | solution.py:489
  77.7 11.4 %collective-permute-start.17 = (bf16[128,1152]{1,0:T(8,128)(2,1)S(1)}, bf16[128,1152]{1,0:T(8,128)(2,1)S(1)}, u32[]{:S(2)}, u32[]{:S(2)}) collective-permute-start(bf16[128,1152]{1,0:T(8,128)(2,1)S(1)} %project.4.token_ref.refs_2_), channel_id=1, source_target_pairs={{0,4},{1,5},{2,6},{3,7},{4,0},{5,1},{6,2},{7,3},{8,12},{9,13},{10,... | collective-permute-start | bytes 884744 | tf_op jit(solution)/shard_map/ppermute | solution.py:446
  79.8 10.6 %collective-permute-start.16 = (bf16[128,1152]{1,0:T(8,128)(2,1)S(1)}, bf16[128,1152]{1,0:T(8,128)(2,1)S(1)}, u32[]{:S(2)}, u32[]{:S(2)}) collective-permute-start(bf16[128,1152]{1,0:T(8,128)(2,1)S(1)} %project.6.refs_3_), channel_id=1, source_target_pairs={{0,6},{1,7},{2,0},{3,1},{4,2},{5,3},{6,4},{7,5},{8,14},{9,15},{10,... | collective-permute-start | bytes 884744 | tf_op jit(solution)/shard_map/ppermute | solution.py:446
  82.9 9.8 %collective-permute-start.20 = (bf16[128,1152]{1,0:T(8,128)(2,1)S(1)}, bf16[128,1152]{1,0:T(8,128)(2,1)S(1)}, u32[]{:S(2)}, u32[]{:S(2)}) collective-permute-start(bf16[128,1152]{1,0:T(8,128)(2,1)S(1)} %project.5.token_ref.refs_1_), channel_id=1, source_target_pairs={{0,2},{1,3},{2,4},{3,5},{4,6},{5,7},{6,0},{7,1},{8,10},{9,11},{10,... | collective-permute-start | bytes 884744 | tf_op jit(solution)/shard_map/ppermute | solution.py:446
  82.9 12.5 %collective-permute-start.18 = (bf16[512,768]{1,0:T(8,128)(2,1)S(1)}, bf16[512,768]{1,0:T(8,128)(2,1)S(1)}, u32[]{:S(2)}, u32[]{:S(2)}) collective-permute-start(bf16[512,768]{1,0:T(8,128)(2,1)S(1)} %stack.19.refs_2_), channel_id=1, source_target_pairs={{0,1},{1,0},{2,3},{3,2},{4,5},{5,4},{6,7},{7,6},{8,9},{9,8},{10,11... | collective-permute-start | bytes 2359304 | tf_op jit(solution)/shard_map/ppermute | solution.py:490
  93.1 4.2 %collective-permute-start.21 = (bf16[512,768]{1,0:T(8,128)(2,1)S(1)}, bf16[512,768]{1,0:T(8,128)(2,1)S(1)}, u32[]{:S(2)}, u32[]{:S(2)}) collective-permute-start(bf16[512,768]{1,0:T(8,128)(2,1)S(1)} %hold.3.refs_4_), channel_id=1, source_target_pairs={{0,1},{1,0},{2,3},{3,2},{4,5},{5,4},{6,7},{7,6},{8,9},{9,8},{10,11... | collective-permute-start | bytes 2359304 | tf_op jit(solution)/shard_map/ppermute | solution.py:477
  103.3 6.4 %collective-permute-start.24 = (bf16[128,384]{1,0:T(8,128)(2,1)S(1)}, bf16[128,384]{1,0:T(8,128)(2,1)S(1)}, u32[]{:S(2)}, u32[]{:S(2)}) collective-permute-start(bf16[128,384]{1,0:T(8,128)(2,1)S(1)} %get-tuple-element.55), channel_id=1, source_target_pairs={{0,2},{1,3},{2,4},{3,5},{4,6},{5,7},{6,0},{7,1},{8,10},{9,11},{10,... | collective-permute-start | bytes 294920 | tf_op jit(solution)/shard_map/ppermute | solution.py:446
  104.6 6.4 %collective-permute-start.22 = (bf16[128,384]{1,0:T(8,128)(2,1)S(1)}, bf16[128,384]{1,0:T(8,128)(2,1)S(1)}, u32[]{:S(2)}, u32[]{:S(2)}) collective-permute-start(bf16[128,384]{1,0:T(8,128)(2,1)S(1)} %get-tuple-element.54), channel_id=1, source_target_pairs={{0,6},{1,7},{2,0},{3,1},{4,2},{5,3},{6,4},{7,5},{8,14},{9,15},{10,... | collective-permute-start | bytes 294920 | tf_op jit(solution)/shard_map/ppermute | solution.py:446
  106.6 6.1 %collective-permute-start.23 = (bf16[128,384]{1,0:T(8,128)(2,1)S(1)}, bf16[128,384]{1,0:T(8,128)(2,1)S(1)}, u32[]{:S(2)}, u32[]{:S(2)}) collective-permute-start(bf16[128,384]{1,0:T(8,128)(2,1)S(1)} %get-tuple-element.52.refs_6_), channel_id=1, source_target_pairs={{0,4},{1,5},{2,6},{3,7},{4,0},{5,1},{6,2},{7,3},{8,12},{9,13},{10,... | collective-permute-start | bytes 294920 | tf_op jit(solution)/shard_map/ppermute | solution.py:446
  (1 other events, 0.7 us)

commit v3 on v2

v3 whole, which is shorter than its diff:
```python
import functools
import math

import jax
import jax.numpy as jnp
from jax import lax
from jax.experimental import pallas as pl
from jax.experimental.pallas import tpu as pltpu
from jax.sharding import PartitionSpec as P

HEAD = 128
FREQ = 256
FRAME = 80
STEPS = 2
SLAB = 128
D = 1536
GROUP = 3
WIDE = GROUP * HEAD
RING = 4
LOG2E = math.log2(math.e)
ORDER = (2, 1, 3, 0)

epsilon = 1e-06
masked_score = -1e30
f32 = jnp.float32
bf16 = jnp.bfloat16


def place(y, z, c):
    return 8 * y + 2 * z + c


DEVICES = [(y, z, c) for y in range(2) for z in range(RING) for c in range(2)]
CORE = [(place(y, z, c), place(y, z, 1 - c)) for y, z, c in DEVICES]
ACROSS = [(place(y, z, c), place(1 - y, z, c)) for y, z, c in DEVICES]


def ring(k):
    return [(place(y, z, c), place(y, (z + k) % RING, c)) for y, z, c in DEVICES]


NEXT_CHIP = [(p, p + 1) for p in range(1, 15, 2)] + [(p + 1, p) for p in range(1, 15, 2)]


VMEM = pl.BlockSpec(memory_space=pltpu.VMEM)
SMEM = pl.BlockSpec(memory_space=pltpu.SMEM)
ANY = pl.BlockSpec(memory_space=pl.ANY)
HBM = pl.BlockSpec(memory_space=pltpu.HBM)


def cost(microseconds):
    return pl.CostEstimate(
        flops=int(microseconds * 1e9), bytes_accessed=int(microseconds * 1e6), transcendentals=0
    )


KEPT = "kept"


def in_vmem(array):
    return pltpu.with_memory_space_constraint(array, pltpu.VMEM)


def in_hbm(array):
    return pltpu.with_memory_space_constraint(array, pltpu.HBM)


def call(body, name, in_specs, outs, scratch=(), aliases=None, megabytes=12, us=0.1):
    return pl.pallas_call(
        body,
        in_specs=in_specs,
        out_specs=[VMEM if spec is KEPT else spec for _, _, spec in outs],
        out_shape=[
            (pltpu.VMEM if spec is KEPT else jax.ShapeDtypeStruct)(shape, dtype)
            for shape, dtype, spec in outs
        ],
        scratch_shapes=list(scratch),
        input_output_aliases=aliases or {},
        compiler_params=pltpu.CompilerParams(vmem_limit_bytes=megabytes * 2**20),
        cost_estimate=cost(us),
        name=name,
    )


def edge_starts(core):
    last = SLAB - FRAME
    return (
        pl.multiple_of(jnp.where(core == 0, last, 0), 16),
        pl.multiple_of(jnp.where(core == 0, 0, last), 16),
    )


def prepare_kernel(place_ref, latent_ref, stale_ref, core_ref, chip_ref, o0, o1, o2, o3, sems):
    outs = (o0, o1, o2, o3)
    core_start, chip_start = edge_starts(place_ref[1])
    copies = [
        pltpu.make_async_copy(latent_ref.at[pl.ds(chip_start, FRAME), :], chip_ref, sems.at[8]),
        pltpu.make_async_copy(latent_ref.at[pl.ds(core_start, FRAME), :], core_ref, sems.at[9]),
    ]
    for k in range(RING):
        start = (place_ref[0] + k) % RING * WIDE
        for part in range(2):
            columns = pl.ds(pl.multiple_of(start + part * D, HEAD), WIDE)
            copies.append(
                pltpu.make_async_copy(
                    stale_ref.at[:, columns],
                    outs[k].at[:, part * WIDE : (part + 1) * WIDE],
                    sems.at[2 * k + part],
                )
            )
    for copy in copies:
        copy.start()
    for copy in copies:
        copy.wait()


def prepare(where, latent, stale_kv):
    edge = ((FRAME, D), bf16, VMEM)
    return call(
        prepare_kernel,
        "prepare",
        [SMEM, HBM, HBM],
        [edge, edge] + [((SLAB, 2 * WIDE), bf16, VMEM)] * RING,
        [pltpu.SemaphoreType.DMA((10,))],
    )(where, in_hbm(latent), in_hbm(stale_kv))


def mix_rows(place_ref, state_ref, core_ref, chip_ref, conv_ref, mod_ref, mixed_ref, normed_ref, row):
    first = place_ref[1] == 0
    state = state_ref[...].astype(f32)
    core_rows = core_ref[...].astype(f32)
    chip_rows = chip_ref[...].astype(f32)
    above = jnp.where(first, chip_rows, core_rows)
    below = jnp.where(first, core_rows, chip_rows)
    before = jnp.concatenate([above, state[: SLAB - FRAME]], 0)
    after_rows = jnp.concatenate([state[FRAME:], below], 0)
    mixed = (
        state
        + conv_ref[0:1, :] * before
        + conv_ref[1:2, :] * state
        + conv_ref[2:3, :] * after_rows
    )
    mixed_ref[...] = mixed
    shift = mod_ref[row : row + 1, :D]
    scale = mod_ref[row : row + 1, D : 2 * D]
    centred = mixed - jnp.mean(mixed, -1, keepdims=True)
    variance = jnp.mean(centred * centred, -1, keepdims=True)
    normed_ref[...] = (centred * lax.rsqrt(variance + epsilon) * (1.0 + scale) + shift).astype(bf16)


def embedding(moment):
    halfway = FREQ // 2
    index = lax.broadcasted_iota(jnp.int32, (halfway, 1), 0).astype(f32)
    angles = moment.astype(f32) * jnp.exp(-math.log(10000.0) * index / halfway)
    values = jnp.concatenate([jnp.cos(angles), jnp.sin(angles)], 0)
    return values / (1.0 + jnp.exp(-values))


def head_normed(block, gain):
    mean_square = jnp.mean(block * block, -1, keepdims=True)
    return (block * lax.rsqrt(mean_square + epsilon) * gain).astype(bf16)


def normed_heads(normed, weight, gain_ref, row, group, out_ref, start):
    block = jnp.dot(normed, weight, preferred_element_type=f32)
    gain = gain_ref[row : row + 1, pl.ds(group, WIDE)]
    for h in range(GROUP):
        here = slice(h * HEAD, (h + 1) * HEAD)
        out_ref[:, start + h * HEAD : start + (h + 1) * HEAD] = head_normed(
            block[:, here], gain[:, here]
        )


def group_start(place_ref, k):
    return pl.multiple_of((place_ref[0] + k) % RING * WIDE, HEAD)


def weight_copies(place_ref, w_ref, held, sems, parts):
    copies = {}
    for k in range(RING):
        copies[k] = []
        for i, part in enumerate(parts):
            columns = pl.ds(pl.multiple_of(group_start(place_ref, k) + part * D, HEAD), WIDE)
            slot = k * len(parts) + i
            copies[k].append(
                pltpu.make_async_copy(w_ref.at[:, columns], held.at[slot], sems.at[slot])
            )
    return copies


def project_queries(place_ref, normed_ref, gains_ref, copies, held, outs):
    for k in ORDER:
        for copy in copies[k]:
            copy.wait()
        normed_heads(
            normed_ref[...], held[k], gains_ref, 0, group_start(place_ref, k), outs[k], 0
        )


def fill_bias(place_ref, counts_ref, bias_ref):
    z, c, y = place_ref[0], place_ref[1], place_ref[4]
    index = lax.broadcasted_iota(jnp.int32, (1, SLAB), 1)
    for a, (yy, cc) in enumerate(((y, c), (y, 1 - c), (1 - y, c), (1 - y, 1 - c))):
        for j in range(RING):
            slab = 8 * yy + 2 * ((z + RING - j) % RING) + cc
            here = slice(j * SLAB, (j + 1) * SLAB)
            row = jnp.where(index < counts_ref[slab], 0.0, masked_score)
            bias_ref[a : a + 1, here] = row
            if a == 0:
                for slot in range(RING):
                    bias_ref[4 + slot : 5 + slot, here] = (
                        jnp.full((1, SLAB), masked_score, f32) if slot == j else row
                    )
                if j == 0:
                    bias_ref[8:9, here] = row


def open_kernel(
    place_ref, counts_ref, latent_ref, core_ref, chip_ref, taps_ref, q_gain_ref, k_gain_ref,
    w_mod_ref, w_qkv_ref, mod_ref, gains_ref, bias_ref, mixed_ref, o0, o1, o2, o3,
    mod_held, w_held, state_ref, conv_ref, q_held, k_held, normed_ref, sems, w_sems
):
    outs = (o0, o1, o2, o3)
    tiles = mod_held.shape[0]
    tile = mod_held.shape[2]
    mods = [
        pltpu.make_async_copy(
            w_mod_ref.at[:, i * tile : (i + 1) * tile], mod_held.at[i], sems.at[i]
        )
        for i in range(tiles)
    ]
    rest = [
        pltpu.make_async_copy(latent_ref, state_ref, sems.at[tiles]),
        pltpu.make_async_copy(taps_ref, conv_ref, sems.at[tiles + 1]),
        pltpu.make_async_copy(q_gain_ref, q_held, sems.at[tiles + 2]),
        pltpu.make_async_copy(k_gain_ref, k_held, sems.at[tiles + 3]),
    ]
    loads = weight_copies(place_ref, w_qkv_ref, w_held, w_sems, (0, 1, 2))
    for copy in (*rest, *mods, *loads[ORDER[0]]):
        copy.start()
    active = [embedding(place_ref[2 + s]) for s in range(STEPS)]
    fill_bias(place_ref, counts_ref, bias_ref)
    for copy in rest:
        copy.wait()
    gains_ref[0:1, :] = (q_held[...] * (LOG2E / math.sqrt(HEAD))).reshape(1, D)
    gains_ref[1:2, :] = k_held[...].reshape(1, D)
    for i, copy in enumerate(mods):
        copy.wait()
        if i == tiles // 2:
            for load in loads[ORDER[1]]:
                load.start()
        weights = mod_held[i]
        for s in range(STEPS):
            mod_ref[s : s + 1, i * tile : (i + 1) * tile] = jnp.sum(
                weights * active[s], 0, keepdims=True
            )
    for k in ORDER[2:]:
        for load in loads[k]:
            load.start()
    mix_rows(place_ref, state_ref, core_ref, chip_ref, conv_ref, mod_ref, mixed_ref, normed_ref, 0)
    for k in ORDER:
        for load in loads[k]:
            load.wait()
        group = group_start(place_ref, k)
        for part in range(2):
            normed_heads(
                normed_ref[...], w_held[3 * k + part], gains_ref, part, group, outs[k], part * WIDE
            )
        outs[k][:, 2 * WIDE :] = jnp.dot(
            normed_ref[...], w_held[3 * k + 2], preferred_element_type=f32
        ).astype(bf16)


def opening(where, counts, state, core_rows, chip_rows, conv_weight, q_gain, k_gain, w_mod, w_qkv):
    tiles = 6
    return call(
        open_kernel,
        "opening",
        [SMEM, SMEM, HBM, VMEM, VMEM] + [HBM] * 5,
        [
            ((STEPS, w_mod.shape[1]), f32, VMEM),
            ((2, D), f32, VMEM),
            ((16, RING * SLAB), f32, VMEM),
            ((SLAB, D), f32, VMEM),
        ]
        + [((SLAB, 3 * WIDE), bf16, VMEM)] * RING,
        [
            pltpu.VMEM((tiles, FREQ, w_mod.shape[1] // tiles), f32),
            pltpu.VMEM((3 * RING, D, WIDE), bf16),
            pltpu.VMEM((SLAB, D), bf16),
            pltpu.VMEM((3, D), f32),
            pltpu.VMEM((D,), f32),
            pltpu.VMEM((D,), f32),
            pltpu.VMEM((SLAB, D), bf16),
            pltpu.SemaphoreType.DMA((tiles + 4,)),
            pltpu.SemaphoreType.DMA((3 * RING,)),
        ],
        megabytes=32,
    )(
        where, counts, in_hbm(state), core_rows, chip_rows, in_hbm(conv_weight), in_hbm(q_gain),
        in_hbm(k_gain), in_hbm(w_mod), in_hbm(w_qkv),
    )


def next_kernel(
    place_ref, state_ref, core_ref, chip_ref, conv_ref, mod_ref, gains_ref, w_qkv_ref,
    mixed_ref, normed_ref, o0, o1, o2, o3, w_held, w_sems, *, row
):
    loads = weight_copies(place_ref, w_qkv_ref, w_held, w_sems, (0,))
    for k in ORDER:
        for copy in loads[k]:
            copy.start()
    mix_rows(
        place_ref, state_ref, core_ref, chip_ref, conv_ref, mod_ref, mixed_ref, normed_ref, row
    )
    project_queries(place_ref, normed_ref, gains_ref, loads, w_held, (o0, o1, o2, o3))


def next_queries(where, state, core_rows, chip_rows, conv_weight, mod, gains, w_qkv, row):
    return call(
        functools.partial(next_kernel, row=row),
        "next_queries",
        [SMEM] + [VMEM] * 6 + [HBM],
        [((SLAB, D), f32, VMEM), ((SLAB, D), bf16, VMEM)] + [((SLAB, WIDE), bf16, VMEM)] * RING,
        [pltpu.VMEM((RING, D, WIDE), bf16), pltpu.SemaphoreType.DMA((RING,))],
    )(where, state, core_rows, chip_rows, conv_weight, mod, gains, in_hbm(w_qkv))


def dots(queries, keys):
    return lax.dot_general(queries, keys, (((1,), (1,)), ((), ())), preferred_element_type=f32)


def home_kernel(bias_ref, *refs):
    queries, keys, values = refs[:RING], refs[RING : 2 * RING], refs[2 * RING : 3 * RING]
    summed_ref, lse_ref = refs[-2:]
    bias = bias_ref[8:9, :SLAB]
    lanes = lax.broadcasted_iota(jnp.int32, (SLAB, HEAD), 1)
    ones = jnp.ones((SLAB, HEAD), bf16)
    heads = [slice(h * HEAD, (h + 1) * HEAD) for h in range(GROUP)]
    for pair in ((0, 1), (2, 3)):
        places = [(k, here) for k in pair for here in heads]
        first = keys[0].shape[1] - 2 * WIDE
        scores = [
            dots(queries[k][:, here], keys[k][:, first + here.start : first + here.stop]) + bias
            for k, here in places
        ]
        highest = [jnp.max(block, -1, keepdims=True) for block in scores]
        probs = [jnp.exp2(block - top).astype(bf16) for block, top in zip(scores, highest)]
        start = values[0].shape[1] - WIDE
        both = [
            jnp.dot(
                block,
                jnp.concatenate([values[k][:, start + here.start : start + here.stop], ones], 1),
                preferred_element_type=f32,
            )
            for block, (k, here) in zip(probs, places)
        ]
        for block, (k, here) in zip(both, places):
            summed_ref[:, k * WIDE + here.start : k * WIDE + here.stop] = (
                block[:, :HEAD] / block[:, HEAD:]
            )
        for i, k in enumerate(pair):
            lse = jnp.zeros((SLAB, HEAD), f32)
            for h in range(GROUP):
                n = i * GROUP + h
                lse = jnp.where(lanes == h, highest[n] + jnp.log2(both[n][:, HEAD:]), lse)
            lse_ref[:, k * HEAD : (k + 1) * HEAD] = lse


def at_home(bias, queries, keys, values, token):
    return call(
        home_kernel,
        "at_home",
        [VMEM] * (3 * RING + 1) + [ANY],
        [((SLAB, D), f32, VMEM), ((SLAB, RING * HEAD), f32, VMEM)],
    )(bias, *queries, *keys, *values, token)


def last_keys_kernel(
    place_ref, normed_ref, gains_ref, w_ref, token_ref, o0, o1, o2, o3, cache_ref, w_held, w_sems
):
    outs = (o0, o1, o2, o3)
    loads = weight_copies(place_ref, w_ref, w_held, w_sems, (1, 2))
    for k in ORDER:
        for copy in loads[k]:
            copy.start()
    for k in ORDER:
        for copy in loads[k]:
            copy.wait()
        group = group_start(place_ref, k)
        normed_heads(normed_ref[...], w_held[2 * k], gains_ref, 1, group, outs[k], 0)
        values = jnp.dot(
            normed_ref[...], w_held[2 * k + 1], preferred_element_type=f32
        ).astype(bf16)
        outs[k][:, WIDE:] = values
        cache_ref[:, pl.ds(group, WIDE)] = outs[k][:, :WIDE]
        cache_ref[:, pl.ds(pl.multiple_of(group + D, HEAD), WIDE)] = values


def last_keys(where, normed, gains, w_qkv, token):
    return call(
        last_keys_kernel,
        "last_keys",
        [SMEM] + [VMEM] * 2 + [HBM, ANY],
        [((SLAB, 2 * WIDE), bf16, VMEM)] * RING + [((SLAB, 2 * D), bf16, VMEM)],
        [pltpu.VMEM((2 * RING, D, WIDE), bf16), pltpu.SemaphoreType.DMA((2 * RING,))],
        megabytes=24,
    )(where, normed, gains, in_hbm(w_qkv), token)


def hold_kernel(*refs):
    pass


def held(array, tokens):
    return call(
        hold_kernel,
        "hold",
        [ANY] * (1 + len(tokens)),
        [(array.shape, array.dtype, ANY)],
        aliases={0: 0},
    )(array, *tokens)[0]


def stack_kernel(*refs):
    blocks, out_ref = refs[:RING], refs[-1]
    first = blocks[0].shape[1] - 2 * WIDE
    for k in range(RING):
        out_ref[k * SLAB : (k + 1) * SLAB, :] = blocks[k][:, first:]


def stack(blocks, token):
    return call(
        stack_kernel,
        "stack",
        [VMEM] * RING + [ANY],
        [((RING * SLAB, 2 * WIDE), bf16, VMEM)],
    )(*[blocks[k] for k in range(RING)], token)[0]


def attend_kernel(q0, q1, q2, q3, a0, a1, a2, a3, bias_ref, token_ref, *outs):
    queries = (q0, q1, q2, q3)
    olds = (a0, a1, a2, a3)
    lanes = lax.broadcasted_iota(jnp.int32, (SLAB, HEAD), 1)
    ones = jnp.ones((RING * SLAB, HEAD), bf16)
    lse = [jnp.zeros((SLAB, HEAD), f32)] * RING
    for h in range(GROUP):
        here = slice(h * HEAD, (h + 1) * HEAD)
        there = slice(WIDE + h * HEAD, WIDE + (h + 1) * HEAD)
        keys = [old[:, here] for old in olds]
        values = [jnp.concatenate([old[:, there], ones], 1) for old in olds]
        for pair in ((0, 1), (2, 3)):
            joined = jnp.concatenate([queries[slot][:, here] for slot in pair], 0)
            products = [dots(joined, keys[a]) for a in range(4)]
            for i, slot in enumerate(pair):
                scores = []
                for a in range(4):
                    row = a if a else 4 + slot
                    scores.append(
                        products[a][i * SLAB : (i + 1) * SLAB] + bias_ref[row : row + 1, :]
                    )
                highest = functools.reduce(
                    jnp.maximum, [jnp.max(block, -1, keepdims=True) for block in scores]
                )
                both = 0.0
                for a in range(4):
                    probs = jnp.exp2(scores[a] - highest).astype(bf16)
                    both += jnp.dot(probs, values[a], preferred_element_type=f32)
                total = both[:, HEAD:]
                outs[slot][:, here] = (both[:, :HEAD] / total).astype(bf16)
                lse[slot] = jnp.where(lanes == h, highest + jnp.log2(total), lse[slot])
    for slot in range(RING):
        rest = lse[slot]
        packed = 0.0
        for part in range(3):
            piece = rest.astype(bf16).astype(f32)
            rest = rest - piece
            packed += pltpu.roll(piece, part * GROUP, 1) if part else piece
        outs[slot][:, WIDE:] = packed.astype(bf16)


def attend(queries, olds, bias, token):
    return call(
        attend_kernel,
        "attend",
        [VMEM] * 9 + [ANY],
        [((SLAB, WIDE + HEAD), bf16, VMEM)] * RING,
        us=6,
    )(*[queries[k] for k in range(RING)], *olds, bias, token)


def output_kernel(
    place_ref, a0, a1, a2, a3, w_ref, summed_ref, lse_ref, mixed_ref, mod_ref,
    out_ref, core_ref, chip_ref, *, row
):
    total = 0.0
    for k, away in enumerate((a0, a1, a2, a3)):
        pieces = away[:, WIDE:].astype(f32)
        lse = (
            pieces
            + pltpu.roll(pieces, HEAD - GROUP, 1)
            + pltpu.roll(pieces, HEAD - 2 * GROUP, 1)
        )
        home = lse_ref[:, k * HEAD : (k + 1) * HEAD]
        share = 1.0 / (1.0 + jnp.exp2(home - lse))
        merged = []
        for h in range(GROUP):
            here = slice(k * WIDE + h * HEAD, k * WIDE + (h + 1) * HEAD)
            part = share[:, h : h + 1]
            merged.append(
                part * away[:, h * HEAD : (h + 1) * HEAD].astype(f32)
                + (1.0 - part) * summed_ref[:, here]
            )
        attended = jnp.concatenate(merged, 1).astype(bf16)
        start = group_start(place_ref, k)
        total += jnp.dot(attended, w_ref[pl.ds(start, WIDE), :], preferred_element_type=f32)
    gate = mod_ref[row : row + 1, 2 * D :]
    out_ref[...] = (mixed_ref[...] + gate * total).astype(bf16)
    core_start, chip_start = edge_starts(place_ref[1])
    core_ref[...] = out_ref[pl.ds(core_start, FRAME), :]
    chip_ref[...] = out_ref[pl.ds(chip_start, FRAME), :]


def output(where, away, summed, lse, w_out, mixed, mod, row):
    edge = ((FRAME, D), bf16, VMEM)
    return call(
        functools.partial(output_kernel, row=row),
        "output",
        [SMEM] + [VMEM] * 9,
        [((SLAB, D), bf16, VMEM), edge, edge],
    )(
        where, *[away[k] for k in range(RING)], w_out, summed, lse, mixed, mod
    )


def sent(block, k):
    return lax.ppermute(block, "patch", ring(k % RING)) if k % RING else block


def shards(latent, stale_kv, timesteps, counts, conv_weight, w_mod, w_qkv, q_gain, k_gain, w_out):
    own_slab = lax.axis_index("patch")
    y, z, c = own_slab // 8, (own_slab // 2) % RING, own_slab % 2
    where = jnp.stack([z, c, timesteps[0], timesteps[1], y]).astype(jnp.int32)
    to_core, to_chip, *pieces = prepare(where, latent, stale_kv)
    chip_rows = lax.ppermute(to_chip, "patch", NEXT_CHIP)
    core_rows = lax.ppermute(to_core, "patch", CORE)
    arrived = {k: sent(pieces[k], k) for k in ORDER}
    mod, gains, bias, mixed, *blocks = opening(
        where, counts, latent, core_rows, chip_rows, conv_weight, q_gain, k_gain, w_mod, w_qkv
    )
    old = stack(arrived, mixed)
    old_y = lax.ppermute(old, "patch", ACROSS)
    old_core = lax.ppermute(old, "patch", CORE)
    fresh = {k: sent(blocks[k], k) for k in ORDER}
    summed, lse = at_home(bias, blocks, blocks, blocks, old)
    new = stack(fresh, lse)
    new_y = lax.ppermute(new, "patch", ACROSS)
    new_core = lax.ppermute(new, "patch", CORE)
    old_y = held(old_y, [new])
    olds = [old, old_core, old_y, lax.ppermute(old_y, "patch", CORE)]
    found = attend(fresh, olds, bias, new)
    away = {k: sent(found[k], -k) for k in ORDER}
    state, to_core, to_chip = output(where, away, summed, lse, w_out, mixed, mod, 0)

    chip_rows = lax.ppermute(to_chip, "patch", NEXT_CHIP)
    core_rows = lax.ppermute(to_core, "patch", CORE)
    mixed, normed, *own = next_queries(
        where, state, core_rows, chip_rows, conv_weight, mod, gains, w_qkv, 1
    )
    queries = {k: sent(own[k], k) for k in ORDER}
    new_y = held(new_y, own[:1])
    olds = [new, new_core, new_y, lax.ppermute(new_y, "patch", CORE)]
    *pairs, cache = last_keys(where, normed, gains, w_qkv, normed)
    found = attend(queries, olds, bias, pairs[0])
    away = {k: sent(found[k], -k) for k in ORDER}
    summed, lse = at_home(bias, own, pairs, pairs, found[0])
    state, _, _ = output(where, away, summed, lse, w_out, mixed, mod, 1)
    return (state, cache)


def solution(mesh):
    rows = P(("req", "patch"), None)
    return jax.shard_map(
        shards,
        mesh=mesh,
        in_specs=(rows, rows, P("req"), P("req"), P(), P(), P(), P(), P(), P()),
        out_specs=(rows, rows),
        check_vma=False,
    )
```

time: 116 us -> 109 us (0.940)
  waiting for transfers between devices: 32.2 us -> 27.1 us
  starting transfers between devices: 45 us -> 43.2 us
  Pallas kernels: 34.9 us -> 36.3 us
    ppermute x0 -> x3, starting transfers between devices: none -> 9.76 us  [the longest x1 5.57 us: shards(): olds = [new, new_core, new_y, lax.ppermute(new_y, 'patch', CORE)]]
    ppermute x2 -> x1, starting transfers between devices: 11.3 us -> 4.56 us  [shards(): old_y = lax.ppermute(old, 'patch', ACROSS)]
    ppermute x2 -> x1, starting transfers between devices: 6.13 us -> 0.01 us  [shards(): old_core = lax.ppermute(old, 'patch', CORE)]
    ppermute x2 -> x1, waiting for transfers between devices: 4.08 us -> 0.01 us  [shards(): olds = [old, old_core, old_y, lax.ppermute(old_y, 'patch', CORE)]]
    ppermute x15, starting transfers between devices: 23.4 us -> 27.3 us  [sent(): return lax.ppermute(block, 'patch', ring(k % RING)) if k % RING else block]
    ppermute x2 -> x1, starting transfers between devices: 2.64 us -> 0.09 us  [shards(): olds = [old, old_core, old_y, lax.ppermute(old_y, 'patch', CORE)]]
    pallas_call x18 -> x14, Pallas kernels: 34.9 us -> 36.3 us  [the longest x2 9.36 us: attend(): call(attend_kernel, 'attend', [VMEM] * 9 + [ANY], [((SLAB, WIDE + HEAD),...]
  transfers between devices with their start and end apart: 25 -> 25, of which waited for: 14 -> 11; matrix products, arithmetic and copies ran while one was open for 0% -> 0% of each run, Pallas kernels for 14% -> 25%
where the time goes in v3:
time: 109 us
  starting transfers between devices  43.2 us (40%)
  Pallas kernels  36.3 us (33%)
  waiting for transfers between devices  27.1 us (25%)
    ppermute x15, starting transfers between devices, sent(): return lax.ppermute(block, 'patch', ring(k % RING)) if k % RING else block  27.3 us
    ppermute x15, waiting for transfers between devices, sent(): return lax.ppermute(block, 'patch', ring(k % RING)) if k % RING else block  27.1 us
    pallas_call x2, Pallas kernels, attend(): call(attend_kernel, 'attend', [VMEM] * 9 + [ANY], [((SLAB, WIDE + HEAD),...  9.36 us
    pallas_call x1, Pallas kernels, opening(): call(open_kernel, 'opening', [SMEM, SMEM, HBM, VMEM, VMEM] + [HBM] * 5, [...  8.45 us
    pallas_call x1, Pallas kernels, last_keys(): call(last_keys_kernel, 'last_keys', [SMEM] + [VMEM] * 2 + [HBM, ANY], [((...  5.91 us
    ppermute x1, starting transfers between devices, shards(): olds = [new, new_core, new_y, lax.ppermute(new_y, 'patch', CORE)]  5.57 us
    pallas_call x2, Pallas kernels, output(): call(functools.partial(output_kernel, row=row), 'output', [SMEM] + [VMEM]...  4.57 us
    ppermute x1, starting transfers between devices, shards(): old_y = lax.ppermute(old, 'patch', ACROSS)  4.56 us
  transfers between devices with their start and end apart: 25, of which 11 were waited for; matrix products, arithmetic and copies ran while one was open for 0% of the time, Pallas kernels for 25%

profile of v3, /device:TPU:0, one launch (start us, length us, event | category | flops | bytes accessed | tf_op | source)
XLA Modules:
  0.0 109.0 jit_solution(11074076582822275813)
XLA Ops:
  1.4 2.0 %prepare.1 = (bf16[80,1536]{1,0:T(8,128)(2,1)S(1)}, bf16[80,1536]{1,0:T(8,128)(2,1)S(1)}, bf16[128,768]{1,0:T(8,128)(2,1)S(1)}, bf16[128,768]{1,0:T(8,128)(2,1)S...) custom-call(s32[5]{0:T(128)S(1)} %pad_add_fusion.place_ref, bf16[128,1536]{1,0:T(8,128)(2,1)} %latent_ref.3, ...), custom_call_target="tpu_custom_call" | custom-call | flops 100000000 | bytes 100000 | tf_op jit(solution)/shard_map/prepare/pallas_call | solution.py:119
  4.2 3.4 %collective-permute-start.5 = (bf16[128,768]{1,0:T(8,128)(2,1)S(1)}, bf16[128,768]{1,0:T(8,128)(2,1)S(1)}, u32[]{:S(2)}, u32[]{:S(2)}) collective-permute-start(bf16[128,768]{1,0:T(8,128)(2,1)S(1)} %get-tuple-element.50), channel_id=1, source_target_pairs={{0,2},{1,3},{2,4},{3,5},{4,6},{5,7},{6,0},{7,1},{8,10},{9,11},{10,... | collective-permute-start | bytes 589832 | tf_op jit(solution)/shard_map/ppermute | solution.py:537
  7.6 4.0 %collective-permute-start.6 = (bf16[128,768]{1,0:T(8,128)(2,1)S(1)}, bf16[128,768]{1,0:T(8,128)(2,1)S(1)}, u32[]{:S(2)}, u32[]{:S(2)}) collective-permute-start(bf16[128,768]{1,0:T(8,128)(2,1)S(1)} %get-tuple-element.51), channel_id=1, source_target_pairs={{0,4},{1,5},{2,6},{3,7},{4,0},{5,1},{6,2},{7,3},{8,12},{9,13},{10,... | collective-permute-start | bytes 589832 | tf_op jit(solution)/shard_map/ppermute | solution.py:537
  13.0 8.5 %opening.1 = (f32[2,4608]{1,0:T(2,128)S(1)}, f32[2,1536]{1,0:T(2,128)S(1)}, f32[16,512]{1,0:T(8,128)S(1)}, f32[128,1536]{1,0:T(8,128)S(1)}, bf16[128,1152]{1,0:T...) custom-call(s32[5]{0:T(128)S(1)} %pad_add_fusion.place_ref, ...), custom_call_target="tpu_custom_call" | custom-call | flops 100000000 | bytes 100000 | tf_op jit(solution)/shard_map/opening/pallas_call | solution.py:276
  21.6 1.1 %collective-permute-done.7.refs_3_ = bf16[128,768]{1,0:T(8,128)(2,1)S(1)} collective-permute-done((bf16[128,768]{1,0:T(8,128)(2,1)S(1)}, bf16[128,768]{1,0:T(8,128)(2,1)S(1)}, u32[]{:S(2)}, u32[]{:S(2)}) %collective-permute-start.7) | collective-permute-done | bytes 196640 | tf_op jit(solution)/shard_map/ppermute | solution.py:537
  22.8 4.6 %collective-permute-start.9 = (bf16[512,768]{1,0:T(8,128)(2,1)S(1)}, bf16[512,768]{1,0:T(8,128)(2,1)S(1)}, u32[]{:S(2)}, u32[]{:S(2)}) collective-permute-start(bf16[512,768]{1,0:T(8,128)(2,1)S(1)} %stack.18.refs_12_.a0), channel_id=1, source_target_pairs={{0,8},{1,9},{2,10},{3,11},{4,12},{5,13},{6,14},{7,15},{8,0},{9,1},... | collective-permute-start | bytes 2359304 | tf_op jit(solution)/shard_map/ppermute | solution.py:552
  27.3 3.2 %collective-permute-start.3 = (bf16[128,1152]{1,0:T(8,128)(2,1)S(1)}, bf16[128,1152]{1,0:T(8,128)(2,1)S(1)}, u32[]{:S(2)}, u32[]{:S(2)}) collective-permute-start(bf16[128,1152]{1,0:T(8,128)(2,1)S(1)} %get-tuple-element.47.refs_2_.refs_6_.refs_10_), channel_id=1, source_target_pairs={{0,4},{1,5},{2,6},{3,7},{4,0},{5,1},{6,2},{7,3},{8,12},{9,13},{10,... | collective-permute-start | bytes 884744 | tf_op jit(solution)/shard_map/ppermute | solution.py:537
  30.5 1.3 %collective-permute-start.4 = (bf16[128,1152]{1,0:T(8,128)(2,1)S(1)}, bf16[128,1152]{1,0:T(8,128)(2,1)S(1)}, u32[]{:S(2)}, u32[]{:S(2)}) collective-permute-start(bf16[128,1152]{1,0:T(8,128)(2,1)S(1)} %get-tuple-element.48.refs_3_.refs_7_.refs_11_), channel_id=1, source_target_pairs={{0,6},{1,7},{2,0},{3,1},{4,2},{5,3},{6,4},{7,5},{8,14},{9,15},{10,... | collective-permute-start | bytes 884744 | tf_op jit(solution)/shard_map/ppermute | solution.py:537
  31.9 0.9 at_home.2
  32.8 5.0 %collective-permute-done.2.refs_1_.q1 = bf16[128,1152]{1,0:T(8,128)(2,1)S(1)} collective-permute-done((bf16[128,1152]{1,0:T(8,128)(2,1)S(1)}, bf16[128,1152]{1,0:T(8,128)(2,1)S(1)}, u32[]{:S(2)}, u32[]{:S(2)}) %collective-permute-start.2) | collective-permute-done | bytes 294944 | tf_op jit(solution)/shard_map/ppermute | solution.py:537
  37.8 6.4 %collective-permute-done.3.refs_2_.q2 = bf16[128,1152]{1,0:T(8,128)(2,1)S(1)} collective-permute-done((bf16[128,1152]{1,0:T(8,128)(2,1)S(1)}, bf16[128,1152]{1,0:T(8,128)(2,1)S(1)}, u32[]{:S(2)}, u32[]{:S(2)}) %collective-permute-start.3) | collective-permute-done | bytes 294944 | tf_op jit(solution)/shard_map/ppermute | solution.py:537
  45.0 2.4 %collective-permute-start.20 = (bf16[512,768]{1,0:T(8,128)(2,1)S(1)}, bf16[512,768]{1,0:T(8,128)(2,1)S(1)}, u32[]{:S(2)}, u32[]{:S(2)}) collective-permute-start(bf16[512,768]{1,0:T(8,128)(2,1)S(1)} %stack.19.refs_1_.token_ref.a0), channel_id=1, source_target_pairs={{0,8},{1,9},{2,10},{3,11},{4,12},{5,13},{6,14},{7,15},{8,0},{9,1},... | collective-permute-start | bytes 2359304 | tf_op jit(solution)/shard_map/ppermute | solution.py:557
  47.4 4.7 %attend.2 = (bf16[128,512]{1,0:T(8,128)(2,1)S(1)}, bf16[128,512]{1,0:T(8,128)(2,1)S(1)}, bf16[128,512]{1,0:T(8,128)(2,1)S(1)}, bf16[128,512]{1,0:T(8,128)(2,1)S(1)}) custom-call(bf16[128,1152]{1,0:T(8,128)(2,1)S(1)} %get-tuple-element.45.refs_0_.refs_4_.refs_8_.q0, bf16[128,1152]{1,0:T(8,128)(2,1)S(1)} %collective-permute-done.2.refs_1_.q1, ...), custom_call_target="tpu_custom_call" | custom-call | flops 6000000000 | bytes 6000000 | tf_op jit(solution)/shard_map/attend/pallas_call | solution.py:483
  52.1 3.5 %collective-permute-start.11 = (bf16[128,512]{1,0:T(8,128)(2,1)S(1)}, bf16[128,512]{1,0:T(8,128)(2,1)S(1)}, u32[]{:S(2)}, u32[]{:S(2)}) collective-permute-start(bf16[128,512]{1,0:T(8,128)(2,1)S(1)} %get-tuple-element.57), channel_id=1, source_target_pairs={{0,6},{1,7},{2,0},{3,1},{4,2},{5,3},{6,4},{7,5},{8,14},{9,15},{10,... | collective-permute-start | bytes 393224 | tf_op jit(solution)/shard_map/ppermute | solution.py:537
  55.6 0.9 collective-permute-start.13
  56.6 4.8 %collective-permute-done.11.a1 = bf16[128,512]{1,0:T(8,128)(2,1)S(1)} collective-permute-done((bf16[128,512]{1,0:T(8,128)(2,1)S(1)}, bf16[128,512]{1,0:T(8,128)(2,1)S(1)}, u32[]{:S(2)}, u32[]{:S(2)}) %collective-permute-start.11) | collective-permute-done | bytes 131104 | tf_op jit(solution)/shard_map/ppermute | solution.py:537
  61.3 2.2 %collective-permute-done.12.a2 = bf16[128,512]{1,0:T(8,128)(2,1)S(1)} collective-permute-done((bf16[128,512]{1,0:T(8,128)(2,1)S(1)}, bf16[128,512]{1,0:T(8,128)(2,1)S(1)}, u32[]{:S(2)}, u32[]{:S(2)}) %collective-permute-start.12) | collective-permute-done | bytes 131104 | tf_op jit(solution)/shard_map/ppermute | solution.py:537
  63.5 1.2 %collective-permute-done.13.a3 = bf16[128,512]{1,0:T(8,128)(2,1)S(1)} collective-permute-done((bf16[128,512]{1,0:T(8,128)(2,1)S(1)}, bf16[128,512]{1,0:T(8,128)(2,1)S(1)}, u32[]{:S(2)}, u32[]{:S(2)}) %collective-permute-start.13) | collective-permute-done | bytes 131104 | tf_op jit(solution)/shard_map/ppermute | solution.py:537
  64.7 1.8 %output.2 = (bf16[128,1536]{1,0:T(8,128)(2,1)S(1)}, bf16[80,1536]{1,0:T(8,128)(2,1)S(1)}, bf16[80,1536]{1,0:T(8,128)(2,1)S(1)}) custom-call(s32[5]{0:T(128)S(1)} %pad_add_fusion.place_ref, bf16[128,512]{1,0:T(8,128)(2,1)S(1)} %get-tuple-element.56.a0, bf16[128,512]{1,0:T(8,128)(2,1)S(1)} %collective-permute-done.11.a1, ...), custom_call_target="tpu_custom_call" | custom-call | flops 100000000 | bytes 100000 | tf_op jit(solution)/shard_map/output/pallas_call | solution.py:526
  67.3 1.8 %collective-permute-start.19 = (bf16[512,768]{1,0:T(8,128)(2,1)S(1)}, bf16[512,768]{1,0:T(8,128)(2,1)S(1)}, u32[]{:S(2)}, u32[]{:S(2)}) collective-permute-start(bf16[512,768]{1,0:T(8,128)(2,1)S(1)} %stack.19.refs_1_.token_ref.a0), channel_id=1, source_target_pairs={{0,1},{1,0},{2,3},{3,2},{4,5},{5,4},{6,7},{7,6},{8,9},{9,8},{10,11... | collective-permute-start | bytes 2359304 | tf_op jit(solution)/shard_map/ppermute | solution.py:558
  69.2 4.2 %next_queries.1 = (f32[128,1536]{1,0:T(8,128)S(1)}, bf16[128,1536]{1,0:T(8,128)(2,1)S(1)}, bf16[128,384]{1,0:T(8,128)(2,1)S(1)}, bf16[128,384]{1,0:T(8,128)(2,1)...) custom-call(s32[5]{0:T(128)S(1)} %pad_add_fusion.place_ref, ...), custom_call_target="tpu_custom_call" | custom-call | flops 100000000 | bytes 100000 | tf_op jit(solution)/shard_map/next_queries/pallas_call | solution.py:320
  73.4 5.6 %collective-permute-start.21 = (bf16[512,768]{1,0:T(8,128)(2,1)S(1)}, bf16[512,768]{1,0:T(8,128)(2,1)S(1)}, u32[]{:S(2)}, u32[]{:S(2)}) collective-permute-start(bf16[512,768]{1,0:T(8,128)(2,1)S(1)} %hold.3.a2), channel_id=1, source_target_pairs={{0,1},{1,0},{2,3},{3,2},{4,5},{5,4},{6,7},{7,6},{8,9},{9,8},{10,11... | collective-permute-start | bytes 2359304 | tf_op jit(solution)/shard_map/ppermute | solution.py:572
  78.9 6.0 %collective-permute-start.17 = (bf16[128,384]{1,0:T(8,128)(2,1)S(1)}, bf16[128,384]{1,0:T(8,128)(2,1)S(1)}, u32[]{:S(2)}, u32[]{:S(2)}) collective-permute-start(bf16[128,384]{1,0:T(8,128)(2,1)S(1)} %get-tuple-element.68.refs_2_), channel_id=1, source_target_pairs={{0,4},{1,5},{2,6},{3,7},{4,0},{5,1},{6,2},{7,3},{8,12},{9,13},{10,... | collective-permute-start | bytes 294920 | tf_op jit(solution)/shard_map/ppermute | solution.py:537
  84.9 5.9 %last_keys.1 = (bf16[128,768]{1,0:T(8,128)(2,1)S(1)}, bf16[128,768]{1,0:T(8,128)(2,1)S(1)}, bf16[128,768]{1,0:T(8,128)(2,1)S(1)}, bf16[128,768]{1,0:T(8,128)(2,1)S(1)}, bf16[128,3072]{1,0:T(8,128)(2,1)}) custom-call(s32[5]{0:T(128)S(1)} %pad_add_fusion.place_ref, bf16[128,1536]{1,0:T(8,128)(2,1)S(1)} %get-tuple-element.70.normed_ref.token_ref, ...), custom_call_target="tpu_custom_call" | custom-call | flops 100000000 | bytes 100000 | tf_op jit(solution)/shard_map/last_keys/pallas_call | solution.py:401
  90.9 4.7 %attend.3 = (bf16[128,512]{1,0:T(8,128)(2,1)S(1)}, bf16[128,512]{1,0:T(8,128)(2,1)S(1)}, bf16[128,512]{1,0:T(8,128)(2,1)S(1)}, bf16[128,512]{1,0:T(8,128)(2,1)S(1)}) custom-call(bf16[128,384]{1,0:T(8,128)(2,1)S(1)} %get-tuple-element.66.refs_1_.q0.refs_0_, bf16[128,384]{1,0:T(8,128)(2,1)S(1)} %collective-permute-done.16.q1, ...), custom_call_target="tpu_custom_call" | custom-call | flops 6000000000 | bytes 6000000 | tf_op jit(solution)/shard_map/attend/pallas_call | solution.py:483
  95.6 1.1 %collective-permute-start.22 = (bf16[128,512]{1,0:T(8,128)(2,1)S(1)}, bf16[128,512]{1,0:T(8,128)(2,1)S(1)}, u32[]{:S(2)}, u32[]{:S(2)}) collective-permute-start(bf16[128,512]{1,0:T(8,128)(2,1)S(1)} %get-tuple-element.73), channel_id=1, source_target_pairs={{0,6},{1,7},{2,0},{3,1},{4,2},{5,3},{6,4},{7,5},{8,14},{9,15},{10,... | collective-permute-start | bytes 393224 | tf_op jit(solution)/shard_map/ppermute | solution.py:537
  96.7 3.0 %collective-permute-start.23 = (bf16[128,512]{1,0:T(8,128)(2,1)S(1)}, bf16[128,512]{1,0:T(8,128)(2,1)S(1)}, u32[]{:S(2)}, u32[]{:S(2)}) collective-permute-start(bf16[128,512]{1,0:T(8,128)(2,1)S(1)} %get-tuple-element.74), channel_id=1, source_target_pairs={{0,4},{1,5},{2,6},{3,7},{4,0},{5,1},{6,2},{7,3},{8,12},{9,13},{10,... | collective-permute-start | bytes 393224 | tf_op jit(solution)/shard_map/ppermute | solution.py:537
  99.8 0.9 at_home.3
  100.6 1.4 %collective-permute-done.22.a1 = bf16[128,512]{1,0:T(8,128)(2,1)S(1)} collective-permute-done((bf16[128,512]{1,0:T(8,128)(2,1)S(1)}, bf16[128,512]{1,0:T(8,128)(2,1)S(1)}, u32[]{:S(2)}, u32[]{:S(2)}) %collective-permute-start.22) | collective-permute-done | bytes 131104 | tf_op jit(solution)/shard_map/ppermute | solution.py:537
  102.0 2.6 %collective-permute-done.23.a2 = bf16[128,512]{1,0:T(8,128)(2,1)S(1)} collective-permute-done((bf16[128,512]{1,0:T(8,128)(2,1)S(1)}, bf16[128,512]{1,0:T(8,128)(2,1)S(1)}, u32[]{:S(2)}, u32[]{:S(2)}) %collective-permute-start.23) | collective-permute-done | bytes 131104 | tf_op jit(solution)/shard_map/ppermute | solution.py:537
  104.6 1.6 %collective-permute-done.24.a3 = bf16[128,512]{1,0:T(8,128)(2,1)S(1)} collective-permute-done((bf16[128,512]{1,0:T(8,128)(2,1)S(1)}, bf16[128,512]{1,0:T(8,128)(2,1)S(1)}, u32[]{:S(2)}, u32[]{:S(2)}) %collective-permute-start.24) | collective-permute-done | bytes 131104 | tf_op jit(solution)/shard_map/ppermute | solution.py:537
  106.2 2.7 %output.3 = (bf16[128,1536]{1,0:T(8,128)(2,1)}, bf16[80,1536]{1,0:T(8,128)(2,1)}, bf16[80,1536]{1,0:T(8,128)(2,1)}) custom-call(s32[5]{0:T(128)S(1)} %pad_add_fusion.place_ref, bf16[128,512]{1,0:T(8,128)(2,1)S(1)} %get-tuple-element.72.refs_12_.a0, bf16[128,512]{1,0:T(8,128)(2,1)S(1)} %collective-permute-done.22.a1, ...), custom_call_target="tpu_custom_call" | custom-call | flops 100000000 | bytes 100000 | tf_op jit(solution)/shard_map/output/pallas_call | solution.py:526
  (42 shorter events, 4.6 us)
Async XLA Ops:
  3.4 8.9 %collective-permute-start = (bf16[80,1536]{1,0:T(8,128)(2,1)S(1)}, bf16[80,1536]{1,0:T(8,128)(2,1)S(1)}, u32[]{:S(2)}, u32[]{:S(2)}) collective-permute-start(bf16[80,1536]{1,0:T(8,128)(2,1)S(1)} %get-tuple-element.43), channel_id=1, source_target_pairs={{0,1},{1,0},{2,3},{3,2},{4,5},{5,4},{6,7},{7,6},{8,9},{9,8},{10,11... | collective-permute-start | bytes 737288 | tf_op jit(solution)/shard_map/ppermute | solution.py:546
  3.5 8.8 %collective-permute-start.1 = (bf16[80,1536]{1,0:T(8,128)(2,1)S(1)}, bf16[80,1536]{1,0:T(8,128)(2,1)S(1)}, u32[]{:S(2)}, u32[]{:S(2)}) collective-permute-start(bf16[80,1536]{1,0:T(8,128)(2,1)S(1)} %get-tuple-element.44), channel_id=1, source_target_pairs={{1,2},{3,4},{5,6},{7,8},{9,10},{11,12},{13,14},{2,1},{4,3},{6,5},{... | collective-permute-start | bytes 737288 | tf_op jit(solution)/shard_map/ppermute | solution.py:545
  4.2 17.2 %collective-permute-start.5 = (bf16[128,768]{1,0:T(8,128)(2,1)S(1)}, bf16[128,768]{1,0:T(8,128)(2,1)S(1)}, u32[]{:S(2)}, u32[]{:S(2)}) collective-permute-start(bf16[128,768]{1,0:T(8,128)(2,1)S(1)} %get-tuple-element.50), channel_id=1, source_target_pairs={{0,2},{1,3},{2,4},{3,5},{4,6},{5,7},{6,0},{7,1},{8,10},{9,11},{10,... | collective-permute-start | bytes 589832 | tf_op jit(solution)/shard_map/ppermute | solution.py:537
  7.6 13.9 %collective-permute-start.6 = (bf16[128,768]{1,0:T(8,128)(2,1)S(1)}, bf16[128,768]{1,0:T(8,128)(2,1)S(1)}, u32[]{:S(2)}, u32[]{:S(2)}) collective-permute-start(bf16[128,768]{1,0:T(8,128)(2,1)S(1)} %get-tuple-element.51), channel_id=1, source_target_pairs={{0,4},{1,5},{2,6},{3,7},{4,0},{5,1},{6,2},{7,3},{8,12},{9,13},{10,... | collective-permute-start | bytes 589832 | tf_op jit(solution)/shard_map/ppermute | solution.py:537
  11.6 11.1 %collective-permute-start.7 = (bf16[128,768]{1,0:T(8,128)(2,1)S(1)}, bf16[128,768]{1,0:T(8,128)(2,1)S(1)}, u32[]{:S(2)}, u32[]{:S(2)}) collective-permute-start(bf16[128,768]{1,0:T(8,128)(2,1)S(1)} %get-tuple-element.52), channel_id=1, source_target_pairs={{0,6},{1,7},{2,0},{3,1},{4,2},{5,3},{6,4},{7,5},{8,14},{9,15},{10,... | collective-permute-start | bytes 589832 | tf_op jit(solution)/shard_map/ppermute | solution.py:537
  12.3 0.7 copy-start.1
  22.8 22.1 %collective-permute-start.9 = (bf16[512,768]{1,0:T(8,128)(2,1)S(1)}, bf16[512,768]{1,0:T(8,128)(2,1)S(1)}, u32[]{:S(2)}, u32[]{:S(2)}) collective-permute-start(bf16[512,768]{1,0:T(8,128)(2,1)S(1)} %stack.18.refs_12_.a0), channel_id=1, source_target_pairs={{0,8},{1,9},{2,10},{3,11},{4,12},{5,13},{6,14},{7,15},{8,0},{9,1},... | collective-permute-start | bytes 2359304 | tf_op jit(solution)/shard_map/ppermute | solution.py:552
  27.3 10.5 %collective-permute-start.2 = (bf16[128,1152]{1,0:T(8,128)(2,1)S(1)}, bf16[128,1152]{1,0:T(8,128)(2,1)S(1)}, u32[]{:S(2)}, u32[]{:S(2)}) collective-permute-start(bf16[128,1152]{1,0:T(8,128)(2,1)S(1)} %get-tuple-element.46.refs_1_.refs_5_.refs_9_), channel_id=1, source_target_pairs={{0,2},{1,3},{2,4},{3,5},{4,6},{5,7},{6,0},{7,1},{8,10},{9,11},{10,... | collective-permute-start | bytes 884744 | tf_op jit(solution)/shard_map/ppermute | solution.py:537
  27.3 16.9 %collective-permute-start.3 = (bf16[128,1152]{1,0:T(8,128)(2,1)S(1)}, bf16[128,1152]{1,0:T(8,128)(2,1)S(1)}, u32[]{:S(2)}, u32[]{:S(2)}) collective-permute-start(bf16[128,1152]{1,0:T(8,128)(2,1)S(1)} %get-tuple-element.47.refs_2_.refs_6_.refs_10_), channel_id=1, source_target_pairs={{0,4},{1,5},{2,6},{3,7},{4,0},{5,1},{6,2},{7,3},{8,12},{9,13},{10,... | collective-permute-start | bytes 884744 | tf_op jit(solution)/shard_map/ppermute | solution.py:537
  30.5 14.3 %collective-permute-start.4 = (bf16[128,1152]{1,0:T(8,128)(2,1)S(1)}, bf16[128,1152]{1,0:T(8,128)(2,1)S(1)}, u32[]{:S(2)}, u32[]{:S(2)}) collective-permute-start(bf16[128,1152]{1,0:T(8,128)(2,1)S(1)} %get-tuple-element.48.refs_3_.refs_7_.refs_11_), channel_id=1, source_target_pairs={{0,6},{1,7},{2,0},{3,1},{4,2},{5,3},{6,4},{7,5},{8,14},{9,15},{10,... | collective-permute-start | bytes 884744 | tf_op jit(solution)/shard_map/ppermute | solution.py:537
  31.9 15.5 %collective-permute-start.8 = (bf16[512,768]{1,0:T(8,128)(2,1)S(1)}, bf16[512,768]{1,0:T(8,128)(2,1)S(1)}, u32[]{:S(2)}, u32[]{:S(2)}) collective-permute-start(bf16[512,768]{1,0:T(8,128)(2,1)S(1)} %stack.18.refs_12_.a0), channel_id=1, source_target_pairs={{0,1},{1,0},{2,3},{3,2},{4,5},{5,4},{6,7},{7,6},{8,9},{9,8},{10,11... | collective-permute-start | bytes 2359304 | tf_op jit(solution)/shard_map/ppermute | solution.py:553
  44.9 19.9 %slice-start = ((s8[4718592]{0:T(1024)(128)(4,1)}), s8[4194304]{0:T(1024)(128)(4,1)S(1)}, s32[]{:S(2)}) async-start(s8[4718592]{0:T(1024)(128)(4,1)} %bitcast.3), calls=%async_computation | async-start | bytes 8388608
  44.9 19.8 %slice-start.1 = ((s8[4718592]{0:T(1024)(128)(4,1)}), s8[524288]{0:T(1024)(128)(4,1)S(1)}, s32[]{:S(2)}) async-start(s8[4718592]{0:T(1024)(128)(4,1)} %bitcast.3), calls=%async_computation.1 | async-start | bytes 1048576
  44.9 2.5 %collective-permute-start.10 = (bf16[512,768]{1,0:T(8,128)(2,1)S(1)}, bf16[512,768]{1,0:T(8,128)(2,1)S(1)}, u32[]{:S(2)}, u32[]{:S(2)}) collective-permute-start(bf16[512,768]{1,0:T(8,128)(2,1)S(1)} %hold.2.a2), channel_id=1, source_target_pairs={{0,1},{1,0},{2,3},{3,2},{4,5},{5,4},{6,7},{7,6},{8,9},{9,8},{10,11... | collective-permute-start | bytes 2359304 | tf_op jit(solution)/shard_map/ppermute | solution.py:560
  45.0 28.3 %collective-permute-start.20 = (bf16[512,768]{1,0:T(8,128)(2,1)S(1)}, bf16[512,768]{1,0:T(8,128)(2,1)S(1)}, u32[]{:S(2)}, u32[]{:S(2)}) collective-permute-start(bf16[512,768]{1,0:T(8,128)(2,1)S(1)} %stack.19.refs_1_.token_ref.a0), channel_id=1, source_target_pairs={{0,8},{1,9},{2,10},{3,11},{4,12},{5,13},{6,14},{7,15},{8,0},{9,1},... | collective-permute-start | bytes 2359304 | tf_op jit(solution)/shard_map/ppermute | solution.py:557
  52.1 17.1 %copy-start = (f32[3,1536]{1,0:T(4,128)S(1)}, f32[3,1536]{1,0:T(4,128)}, u32[]{:S(2)}) copy-start(f32[3,1536]{1,0:T(4,128)} %conv_ref.1) | copy-start | bytes 55300
  52.1 9.2 %collective-permute-start.11 = (bf16[128,512]{1,0:T(8,128)(2,1)S(1)}, bf16[128,512]{1,0:T(8,128)(2,1)S(1)}, u32[]{:S(2)}, u32[]{:S(2)}) collective-permute-start(bf16[128,512]{1,0:T(8,128)(2,1)S(1)} %get-tuple-element.57), channel_id=1, source_target_pairs={{0,6},{1,7},{2,0},{3,1},{4,2},{5,3},{6,4},{7,5},{8,14},{9,15},{10,... | collective-permute-start | bytes 393224 | tf_op jit(solution)/shard_map/ppermute | solution.py:537
  55.6 7.9 %collective-permute-start.12 = (bf16[128,512]{1,0:T(8,128)(2,1)S(1)}, bf16[128,512]{1,0:T(8,128)(2,1)S(1)}, u32[]{:S(2)}, u32[]{:S(2)}) collective-permute-start(bf16[128,512]{1,0:T(8,128)(2,1)S(1)} %get-tuple-element.58), channel_id=1, source_target_pairs={{0,4},{1,5},{2,6},{3,7},{4,0},{5,1},{6,2},{7,3},{8,12},{9,13},{10,... | collective-permute-start | bytes 393224 | tf_op jit(solution)/shard_map/ppermute | solution.py:537
  55.6 9.1 %collective-permute-start.13 = (bf16[128,512]{1,0:T(8,128)(2,1)S(1)}, bf16[128,512]{1,0:T(8,128)(2,1)S(1)}, u32[]{:S(2)}, u32[]{:S(2)}) collective-permute-start(bf16[128,512]{1,0:T(8,128)(2,1)S(1)} %get-tuple-element.59), channel_id=1, source_target_pairs={{0,2},{1,3},{2,4},{3,5},{4,6},{5,7},{6,0},{7,1},{8,10},{9,11},{10,... | collective-permute-start | bytes 393224 | tf_op jit(solution)/shard_map/ppermute | solution.py:537
  66.6 2.6 %collective-permute-start.14 = (bf16[80,1536]{1,0:T(8,128)(2,1)S(1)}, bf16[80,1536]{1,0:T(8,128)(2,1)S(1)}, u32[]{:S(2)}, u32[]{:S(2)}) collective-permute-start(bf16[80,1536]{1,0:T(8,128)(2,1)S(1)} %get-tuple-element.63), channel_id=1, source_target_pairs={{0,1},{1,0},{2,3},{3,2},{4,5},{5,4},{6,7},{7,6},{8,9},{9,8},{10,11... | collective-permute-start | bytes 737288 | tf_op jit(solution)/shard_map/ppermute | solution.py:566
  66.7 2.5 %collective-permute-start.15 = (bf16[80,1536]{1,0:T(8,128)(2,1)S(1)}, bf16[80,1536]{1,0:T(8,128)(2,1)S(1)}, u32[]{:S(2)}, u32[]{:S(2)}) collective-permute-start(bf16[80,1536]{1,0:T(8,128)(2,1)S(1)} %get-tuple-element.64), channel_id=1, source_target_pairs={{1,2},{3,4},{5,6},{7,8},{9,10},{11,12},{13,14},{2,1},{4,3},{6,5},{... | collective-permute-start | bytes 737288 | tf_op jit(solution)/shard_map/ppermute | solution.py:565
  67.3 23.5 %collective-permute-start.19 = (bf16[512,768]{1,0:T(8,128)(2,1)S(1)}, bf16[512,768]{1,0:T(8,128)(2,1)S(1)}, u32[]{:S(2)}, u32[]{:S(2)}) collective-permute-start(bf16[512,768]{1,0:T(8,128)(2,1)S(1)} %stack.19.refs_1_.token_ref.a0), channel_id=1, source_target_pairs={{0,1},{1,0},{2,3},{3,2},{4,5},{5,4},{6,7},{7,6},{8,9},{9,8},{10,11... | collective-permute-start | bytes 2359304 | tf_op jit(solution)/shard_map/ppermute | solution.py:558
  73.4 17.5 %collective-permute-start.21 = (bf16[512,768]{1,0:T(8,128)(2,1)S(1)}, bf16[512,768]{1,0:T(8,128)(2,1)S(1)}, u32[]{:S(2)}, u32[]{:S(2)}) collective-permute-start(bf16[512,768]{1,0:T(8,128)(2,1)S(1)} %hold.3.a2), channel_id=1, source_target_pairs={{0,1},{1,0},{2,3},{3,2},{4,5},{5,4},{6,7},{7,6},{8,9},{9,8},{10,11... | collective-permute-start | bytes 2359304 | tf_op jit(solution)/shard_map/ppermute | solution.py:572
  78.9 11.9 %collective-permute-start.16 = (bf16[128,384]{1,0:T(8,128)(2,1)S(1)}, bf16[128,384]{1,0:T(8,128)(2,1)S(1)}, u32[]{:S(2)}, u32[]{:S(2)}) collective-permute-start(bf16[128,384]{1,0:T(8,128)(2,1)S(1)} %get-tuple-element.67.refs_1_), channel_id=1, source_target_pairs={{0,2},{1,3},{2,4},{3,5},{4,6},{5,7},{6,0},{7,1},{8,10},{9,11},{10,... | collective-permute-start | bytes 294920 | tf_op jit(solution)/shard_map/ppermute | solution.py:537
  78.9 11.9 %collective-permute-start.17 = (bf16[128,384]{1,0:T(8,128)(2,1)S(1)}, bf16[128,384]{1,0:T(8,128)(2,1)S(1)}, u32[]{:S(2)}, u32[]{:S(2)}) collective-permute-start(bf16[128,384]{1,0:T(8,128)(2,1)S(1)} %get-tuple-element.68.refs_2_), channel_id=1, source_target_pairs={{0,4},{1,5},{2,6},{3,7},{4,0},{5,1},{6,2},{7,3},{8,12},{9,13},{10,... | collective-permute-start | bytes 294920 | tf_op jit(solution)/shard_map/ppermute | solution.py:537
  84.9 6.0 %collective-permute-start.18 = (bf16[128,384]{1,0:T(8,128)(2,1)S(1)}, bf16[128,384]{1,0:T(8,128)(2,1)S(1)}, u32[]{:S(2)}, u32[]{:S(2)}) collective-permute-start(bf16[128,384]{1,0:T(8,128)(2,1)S(1)} %get-tuple-element.69.refs_3_), channel_id=1, source_target_pairs={{0,6},{1,7},{2,0},{3,1},{4,2},{5,3},{6,4},{7,5},{8,14},{9,15},{10,... | collective-permute-start | bytes 294920 | tf_op jit(solution)/shard_map/ppermute | solution.py:537
  95.6 6.4 %collective-permute-start.22 = (bf16[128,512]{1,0:T(8,128)(2,1)S(1)}, bf16[128,512]{1,0:T(8,128)(2,1)S(1)}, u32[]{:S(2)}, u32[]{:S(2)}) collective-permute-start(bf16[128,512]{1,0:T(8,128)(2,1)S(1)} %get-tuple-element.73), channel_id=1, source_target_pairs={{0,6},{1,7},{2,0},{3,1},{4,2},{5,3},{6,4},{7,5},{8,14},{9,15},{10,... | collective-permute-start | bytes 393224 | tf_op jit(solution)/shard_map/ppermute | solution.py:537
  96.7 7.9 %collective-permute-start.23 = (bf16[128,512]{1,0:T(8,128)(2,1)S(1)}, bf16[128,512]{1,0:T(8,128)(2,1)S(1)}, u32[]{:S(2)}, u32[]{:S(2)}) collective-permute-start(bf16[128,512]{1,0:T(8,128)(2,1)S(1)} %get-tuple-element.74), channel_id=1, source_target_pairs={{0,4},{1,5},{2,6},{3,7},{4,0},{5,1},{6,2},{7,3},{8,12},{9,13},{10,... | collective-permute-start | bytes 393224 | tf_op jit(solution)/shard_map/ppermute | solution.py:537
  99.7 6.5 %collective-permute-start.24 = (bf16[128,512]{1,0:T(8,128)(2,1)S(1)}, bf16[128,512]{1,0:T(8,128)(2,1)S(1)}, u32[]{:S(2)}, u32[]{:S(2)}) collective-permute-start(bf16[128,512]{1,0:T(8,128)(2,1)S(1)} %get-tuple-element.75), channel_id=1, source_target_pairs={{0,2},{1,3},{2,4},{3,5},{4,6},{5,7},{6,0},{7,1},{8,10},{9,11},{10,... | collective-permute-start | bytes 393224 | tf_op jit(solution)/shard_map/ppermute | solution.py:537

commit v4 on v3

v4 whole, which is shorter than its diff:
```python
import functools
import math

import jax
import jax.numpy as jnp
from jax import lax
from jax.experimental import pallas as pl
from jax.experimental.pallas import tpu as pltpu
from jax.sharding import PartitionSpec as P

HEAD = 128
FREQ = 256
FRAME = 80
STEPS = 2
SLAB = 128
D = 1536
GROUP = 3
WIDE = GROUP * HEAD
RING = 4
LOG2E = math.log2(math.e)
ORDER = (2, 1, 3, 0)

epsilon = 1e-06
masked_score = -1e30
f32 = jnp.float32
bf16 = jnp.bfloat16


def place(y, z, c):
    return 8 * y + 2 * z + c


DEVICES = [(y, z, c) for y in range(2) for z in range(RING) for c in range(2)]
CORE = [(place(y, z, c), place(y, z, 1 - c)) for y, z, c in DEVICES]
ACROSS = [(place(y, z, c), place(1 - y, z, c)) for y, z, c in DEVICES]


def ring(k):
    return [(place(y, z, c), place(y, (z + k) % RING, c)) for y, z, c in DEVICES]


NEXT_CHIP = [(p, p + 1) for p in range(1, 15, 2)] + [(p + 1, p) for p in range(1, 15, 2)]


VMEM = pl.BlockSpec(memory_space=pltpu.VMEM)
SMEM = pl.BlockSpec(memory_space=pltpu.SMEM)
ANY = pl.BlockSpec(memory_space=pl.ANY)
HBM = pl.BlockSpec(memory_space=pltpu.HBM)


def cost(microseconds):
    return pl.CostEstimate(
        flops=int(microseconds * 1e9), bytes_accessed=int(microseconds * 1e6), transcendentals=0
    )


KEPT = "kept"


def in_vmem(array):
    return pltpu.with_memory_space_constraint(array, pltpu.VMEM)


def in_hbm(array):
    return pltpu.with_memory_space_constraint(array, pltpu.HBM)


def call(body, name, in_specs, outs, scratch=(), aliases=None, megabytes=10, us=0.1):
    return pl.pallas_call(
        body,
        in_specs=in_specs,
        out_specs=[VMEM if spec is KEPT else spec for _, _, spec in outs],
        out_shape=[
            (pltpu.VMEM if spec is KEPT else jax.ShapeDtypeStruct)(shape, dtype)
            for shape, dtype, spec in outs
        ],
        scratch_shapes=list(scratch),
        input_output_aliases=aliases or {},
        compiler_params=pltpu.CompilerParams(vmem_limit_bytes=megabytes * 2**20),
        cost_estimate=cost(us),
        name=name,
    )


def edge_starts(core):
    last = SLAB - FRAME
    return (
        pl.multiple_of(jnp.where(core == 0, last, 0), 16),
        pl.multiple_of(jnp.where(core == 0, 0, last), 16),
    )


def prepare_kernel(place_ref, latent_ref, stale_ref, core_ref, chip_ref, o0, o1, o2, o3, sems):
    outs = (o0, o1, o2, o3)
    core_start, chip_start = edge_starts(place_ref[1])
    copies = [
        pltpu.make_async_copy(latent_ref.at[pl.ds(chip_start, FRAME), :], chip_ref, sems.at[8]),
        pltpu.make_async_copy(latent_ref.at[pl.ds(core_start, FRAME), :], core_ref, sems.at[9]),
    ]
    for k in range(RING):
        start = (place_ref[0] + k) % RING * WIDE
        for part in range(2):
            columns = pl.ds(pl.multiple_of(start + part * D, HEAD), WIDE)
            copies.append(
                pltpu.make_async_copy(
                    stale_ref.at[:, columns],
                    outs[k].at[:, part * WIDE : (part + 1) * WIDE],
                    sems.at[2 * k + part],
                )
            )
    for copy in copies:
        copy.start()
    for copy in copies:
        copy.wait()


def prepare(where, latent, stale_kv):
    edge = ((FRAME, D), bf16, VMEM)
    return call(
        prepare_kernel,
        "prepare",
        [SMEM, HBM, HBM],
        [edge, edge] + [((SLAB, 2 * WIDE), bf16, VMEM)] * RING,
        [pltpu.SemaphoreType.DMA((10,))],
        us=8,
    )(where, in_hbm(latent), in_hbm(stale_kv))


def mix_rows(place_ref, state_ref, core_ref, chip_ref, conv_ref, mod_ref, mixed_ref, normed_ref, row):
    first = place_ref[1] == 0
    state = state_ref[...].astype(f32)
    core_rows = core_ref[...].astype(f32)
    chip_rows = chip_ref[...].astype(f32)
    above = jnp.where(first, chip_rows, core_rows)
    below = jnp.where(first, core_rows, chip_rows)
    before = jnp.concatenate([above, state[: SLAB - FRAME]], 0)
    after_rows = jnp.concatenate([state[FRAME:], below], 0)
    mixed = (
        state
        + conv_ref[0:1, :] * before
        + conv_ref[1:2, :] * state
        + conv_ref[2:3, :] * after_rows
    )
    mixed_ref[...] = mixed
    shift = mod_ref[row : row + 1, :D]
    scale = mod_ref[row : row + 1, D : 2 * D]
    centred = mixed - jnp.mean(mixed, -1, keepdims=True)
    variance = jnp.mean(centred * centred, -1, keepdims=True)
    normed_ref[...] = (centred * lax.rsqrt(variance + epsilon) * (1.0 + scale) + shift).astype(bf16)


def embedding(moment):
    halfway = FREQ // 2
    index = lax.broadcasted_iota(jnp.int32, (halfway, 1), 0).astype(f32)
    angles = moment.astype(f32) * jnp.exp(-math.log(10000.0) * index / halfway)
    values = jnp.concatenate([jnp.cos(angles), jnp.sin(angles)], 0)
    return values / (1.0 + jnp.exp(-values))


def head_normed(block, gain):
    mean_square = jnp.mean(block * block, -1, keepdims=True)
    return (block * lax.rsqrt(mean_square + epsilon) * gain).astype(bf16)


def normed_heads(normed, weight, gain_ref, row, group, out_ref, start):
    block = jnp.dot(normed, weight, preferred_element_type=f32)
    gain = gain_ref[row : row + 1, pl.ds(group, WIDE)]
    for h in range(GROUP):
        here = slice(h * HEAD, (h + 1) * HEAD)
        out_ref[:, start + h * HEAD : start + (h + 1) * HEAD] = head_normed(
            block[:, here], gain[:, here]
        )


def group_start(place_ref, k):
    return pl.multiple_of((place_ref[0] + k) % RING * WIDE, HEAD)


def project(normed, w_ref, gains_ref, part, held_ref, first):
    block = jnp.dot(normed, w_ref[:, part * D : (part + 1) * D], preferred_element_type=f32)
    if part == 2:
        held_ref[:, first : first + D] = block.astype(bf16)
        return
    for h in range(D // HEAD):
        here = slice(h * HEAD, (h + 1) * HEAD)
        held_ref[:, first + here.start : first + here.stop] = head_normed(
            block[:, here], gains_ref[part : part + 1, here]
        )


def dealt(place_ref, held_ref, parts, outs):
    for k, out_ref in enumerate(outs):
        for i in range(parts):
            start = pl.multiple_of(group_start(place_ref, k) + i * D, HEAD)
            out_ref[:, i * WIDE : (i + 1) * WIDE] = held_ref[:, pl.ds(start, WIDE)]


def modulated(active, weights):
    return [jnp.sum(weights * active[s], 0, keepdims=True) for s in range(STEPS)]


def open_kernel(
    place_ref, latent_ref, core_ref, chip_ref, taps_ref, q_gain_ref, k_gain_ref, w_mod_ref,
    w_qkv_ref, token_ref, mod_ref, gains_ref, mixed_ref, o0, o1, o2, o3,
    state_ref, conv_ref, q_held, k_held, normed_ref, held_ref, sems
):
    copies = [
        pltpu.make_async_copy(latent_ref, state_ref, sems.at[0]),
        pltpu.make_async_copy(taps_ref, conv_ref, sems.at[1]),
        pltpu.make_async_copy(q_gain_ref, q_held, sems.at[2]),
        pltpu.make_async_copy(k_gain_ref, k_held, sems.at[3]),
    ]
    for copy in copies:
        copy.start()
    active = [embedding(place_ref[2 + s]) for s in range(STEPS)]
    for i in range(4):
        here = slice(i * 2 * D // 4, (i + 1) * 2 * D // 4)
        for s, row in enumerate(modulated(active, w_mod_ref[:, here])):
            mod_ref[s : s + 1, here] = row
    for copy in copies:
        copy.wait()
    gains_ref[0:1, :] = (q_held[...] * (LOG2E / math.sqrt(HEAD))).reshape(1, D)
    gains_ref[1:2, :] = k_held[...].reshape(1, D)
    mix_rows(place_ref, state_ref, core_ref, chip_ref, conv_ref, mod_ref, mixed_ref, normed_ref, 0)
    for part in range(3):
        project(normed_ref[...], w_qkv_ref, gains_ref, part, held_ref, part * D)
    dealt(place_ref, held_ref, 3, (o0, o1, o2, o3))


def opening(where, state, core_rows, chip_rows, conv_weight, q_gain, k_gain, w_mod, w_qkv, token):
    return call(
        open_kernel,
        "opening",
        [SMEM, HBM, VMEM, VMEM] + [HBM] * 3 + [VMEM] * 2 + [ANY],
        [((STEPS, 2 * D), f32, VMEM), ((2, D), f32, VMEM), ((SLAB, D), f32, VMEM)]
        + [((SLAB, 3 * WIDE), bf16, VMEM)] * RING,
        [
            pltpu.VMEM((SLAB, D), bf16),
            pltpu.VMEM((3, D), f32),
            pltpu.VMEM((D,), f32),
            pltpu.VMEM((D,), f32),
            pltpu.VMEM((SLAB, D), bf16),
            pltpu.VMEM((SLAB, 3 * D), bf16),
            pltpu.SemaphoreType.DMA((4,)),
        ],
        us=10,
    )(
        where, in_hbm(state), core_rows, chip_rows, in_hbm(conv_weight), in_hbm(q_gain),
        in_hbm(k_gain), w_mod, w_qkv, token,
    )


def fill_bias(place_ref, counts_ref, bias_ref):
    z, c, y = place_ref[0], place_ref[1], place_ref[4]
    index = lax.broadcasted_iota(jnp.int32, (1, SLAB), 1)
    for a, (yy, cc) in enumerate(((y, c), (y, 1 - c), (1 - y, c), (1 - y, 1 - c))):
        for j in range(RING):
            slab = 8 * yy + 2 * ((z + RING - j) % RING) + cc
            here = slice(j * SLAB, (j + 1) * SLAB)
            row = jnp.where(index < counts_ref[slab], 0.0, masked_score)
            bias_ref[a : a + 1, here] = row
            if a == 0:
                for slot in range(RING):
                    bias_ref[4 + slot : 5 + slot, here] = (
                        jnp.full((1, SLAB), masked_score, f32) if slot == j else row
                    )
                if j == 0:
                    bias_ref[8:9, here] = row


def aside_kernel(place_ref, counts_ref, w_mod_ref, token_ref, gates_ref, bias_ref, held, sem):
    load = pltpu.make_async_copy(w_mod_ref.at[:, 2 * D :], held, sem)
    load.start()
    active = [embedding(place_ref[2 + s]) for s in range(STEPS)]
    fill_bias(place_ref, counts_ref, bias_ref)
    load.wait()
    for s, row in enumerate(modulated(active, held[...])):
        gates_ref[s : s + 1, :] = row


def aside(where, counts, w_mod, token):
    return call(
        aside_kernel,
        "aside",
        [SMEM, SMEM, HBM, ANY],
        [((STEPS, D), f32, VMEM), ((16, RING * SLAB), f32, VMEM)],
        [pltpu.VMEM((FREQ, D), f32), pltpu.SemaphoreType.DMA],
    )(where, counts, in_hbm(w_mod), token)


def next_kernel(
    place_ref, state_ref, core_ref, chip_ref, conv_ref, mod_ref, gains_ref, w_qkv_ref,
    mixed_ref, normed_ref, o0, o1, o2, o3, held_ref, *, row
):
    mix_rows(
        place_ref, state_ref, core_ref, chip_ref, conv_ref, mod_ref, mixed_ref, normed_ref, row
    )
    project(normed_ref[...], w_qkv_ref, gains_ref, 0, held_ref, 0)
    dealt(place_ref, held_ref, 1, (o0, o1, o2, o3))


def next_queries(where, state, core_rows, chip_rows, conv_weight, mod, gains, w_qkv, row):
    return call(
        functools.partial(next_kernel, row=row),
        "next_queries",
        [SMEM] + [VMEM] * 7,
        [((SLAB, D), f32, VMEM), ((SLAB, D), bf16, VMEM)] + [((SLAB, WIDE), bf16, VMEM)] * RING,
        [pltpu.VMEM((SLAB, D), bf16)],
    )(where, state, core_rows, chip_rows, conv_weight, mod, gains, w_qkv)


def dots(queries, keys):
    return lax.dot_general(queries, keys, (((1,), (1,)), ((), ())), preferred_element_type=f32)


def home_kernel(bias_ref, *refs):
    queries, keys, values = refs[:RING], refs[RING : 2 * RING], refs[2 * RING : 3 * RING]
    summed_ref, lse_ref = refs[-2:]
    bias = bias_ref[8:9, :SLAB]
    lanes = lax.broadcasted_iota(jnp.int32, (SLAB, HEAD), 1)
    ones = jnp.ones((SLAB, HEAD), bf16)
    heads = [slice(h * HEAD, (h + 1) * HEAD) for h in range(GROUP)]
    for pair in ((0, 1), (2, 3)):
        places = [(k, here) for k in pair for here in heads]
        first = keys[0].shape[1] - 2 * WIDE
        scores = [
            dots(queries[k][:, here], keys[k][:, first + here.start : first + here.stop]) + bias
            for k, here in places
        ]
        highest = [jnp.max(block, -1, keepdims=True) for block in scores]
        probs = [jnp.exp2(block - top).astype(bf16) for block, top in zip(scores, highest)]
        start = values[0].shape[1] - WIDE
        both = [
            jnp.dot(
                block,
                jnp.concatenate([values[k][:, start + here.start : start + here.stop], ones], 1),
                preferred_element_type=f32,
            )
            for block, (k, here) in zip(probs, places)
        ]
        for block, (k, here) in zip(both, places):
            summed_ref[:, k * WIDE + here.start : k * WIDE + here.stop] = (
                block[:, :HEAD] / block[:, HEAD:]
            )
        for i, k in enumerate(pair):
            lse = jnp.zeros((SLAB, HEAD), f32)
            for h in range(GROUP):
                n = i * GROUP + h
                lse = jnp.where(lanes == h, highest[n] + jnp.log2(both[n][:, HEAD:]), lse)
            lse_ref[:, k * HEAD : (k + 1) * HEAD] = lse


def at_home(bias, queries, keys, values, token):
    return call(
        home_kernel,
        "at_home",
        [VMEM] * (3 * RING + 1) + [ANY],
        [((SLAB, D), f32, VMEM), ((SLAB, RING * HEAD), f32, VMEM)],
    )(bias, *queries, *keys, *values, token)


def last_keys_kernel(
    place_ref, normed_ref, gains_ref, w_ref, token_ref, o0, o1, o2, o3, cache_ref, held_ref, sems
):
    writes = []
    for part in (1, 2):
        project(normed_ref[...], w_ref, gains_ref, part, held_ref, (part - 1) * D)
        columns = pl.ds((part - 1) * D, D)
        writes.append(
            pltpu.make_async_copy(
                held_ref.at[:, columns], cache_ref.at[:, columns], sems.at[part - 1]
            )
        )
        writes[-1].start()
    dealt(place_ref, held_ref, 2, (o0, o1, o2, o3))
    for write in writes:
        write.wait()


def last_keys(where, normed, gains, w_qkv, token):
    return call(
        last_keys_kernel,
        "last_keys",
        [SMEM] + [VMEM] * 3 + [ANY],
        [((SLAB, 2 * WIDE), bf16, VMEM)] * RING + [((SLAB, 2 * D), bf16, HBM)],
        [pltpu.VMEM((SLAB, 2 * D), bf16), pltpu.SemaphoreType.DMA((2,))],
    )(where, normed, gains, w_qkv, token)


def hold_kernel(*refs):
    pass


def held(array, tokens):
    return call(
        hold_kernel,
        "hold",
        [ANY] * (1 + len(tokens)),
        [(array.shape, array.dtype, ANY)],
        aliases={0: 0},
    )(array, *tokens)[0]


def stack_kernel(*refs):
    blocks, out_ref = refs[:RING], refs[-1]
    first = blocks[0].shape[1] - 2 * WIDE
    for k in range(RING):
        out_ref[k * SLAB : (k + 1) * SLAB, :] = blocks[k][:, first:]


def stack(blocks, token, us=0.1):
    return call(
        stack_kernel,
        "stack",
        [VMEM] * RING + [ANY],
        [((RING * SLAB, 2 * WIDE), bf16, VMEM)],
        us=us,
    )(*[blocks[k] for k in range(RING)], token)[0]


def attend_kernel(q0, q1, a0, a1, a2, a3, bias_ref, token_ref, *outs, slots):
    queries = (q0, q1)
    olds = (a0, a1, a2, a3)
    lanes = lax.broadcasted_iota(jnp.int32, (SLAB, HEAD), 1)
    ones = jnp.ones((RING * SLAB, HEAD), bf16)
    lse = [jnp.zeros((SLAB, HEAD), f32)] * 2
    for h in range(GROUP):
        here = slice(h * HEAD, (h + 1) * HEAD)
        there = slice(WIDE + h * HEAD, WIDE + (h + 1) * HEAD)
        keys = [old[:, here] for old in olds]
        values = [jnp.concatenate([old[:, there], ones], 1) for old in olds]
        joined = jnp.concatenate([query[:, here] for query in queries], 0)
        products = [dots(joined, keys[a]) for a in range(4)]
        for i, slot in enumerate(slots):
            scores = []
            for a in range(4):
                row = a if a else 4 + slot
                scores.append(products[a][i * SLAB : (i + 1) * SLAB] + bias_ref[row : row + 1, :])
            highest = functools.reduce(
                jnp.maximum, [jnp.max(block, -1, keepdims=True) for block in scores]
            )
            both = 0.0
            for a in range(4):
                probs = jnp.exp2(scores[a] - highest).astype(bf16)
                both += jnp.dot(probs, values[a], preferred_element_type=f32)
            total = both[:, HEAD:]
            outs[i][:, here] = (both[:, :HEAD] / total).astype(bf16)
            lse[i] = jnp.where(lanes == h, highest + jnp.log2(total), lse[i])
    for i in range(2):
        rest = lse[i]
        packed = 0.0
        for part in range(3):
            piece = rest.astype(bf16).astype(f32)
            rest = rest - piece
            packed += pltpu.roll(piece, part * GROUP, 1) if part else piece
        outs[i][:, WIDE:] = packed.astype(bf16)


def attend(queries, olds, bias, slots, token):
    return call(
        functools.partial(attend_kernel, slots=slots),
        "attend",
        [VMEM] * 7 + [ANY],
        [((SLAB, WIDE + HEAD), bf16, VMEM)] * 2,
        us=4,
    )(*[queries[k] for k in slots], *olds, bias, token)


def merged(away, summed_ref, lse_ref, k):
    pieces = away[:, WIDE:].astype(f32)
    lse = (
        pieces + pltpu.roll(pieces, HEAD - GROUP, 1) + pltpu.roll(pieces, HEAD - 2 * GROUP, 1)
    )
    share = 1.0 / (1.0 + jnp.exp2(lse_ref[:, k * HEAD : (k + 1) * HEAD] - lse))
    heads = []
    for h in range(GROUP):
        here = slice(k * WIDE + h * HEAD, k * WIDE + (h + 1) * HEAD)
        part = share[:, h : h + 1]
        heads.append(
            part * away[:, h * HEAD : (h + 1) * HEAD].astype(f32)
            + (1.0 - part) * summed_ref[:, here]
        )
    return jnp.concatenate(heads, 1).astype(bf16)


def early_output_kernel(place_ref, a0, a1, a2, w_ref, summed_ref, lse_ref, out_ref):
    total = 0.0
    for k, away in enumerate((a0, a1, a2)):
        weight = w_ref[pl.ds(group_start(place_ref, k), WIDE), :]
        total += jnp.dot(
            merged(away, summed_ref, lse_ref, k), weight, preferred_element_type=f32
        )
    out_ref[...] = total


def early_output(where, away, summed, lse, w_out):
    return call(
        early_output_kernel,
        "early_output",
        [SMEM] + [VMEM] * 6,
        [((SLAB, D), f32, VMEM)],
        us=3,
    )(where, away[0], away[1], away[2], w_out, summed, lse)[0]


def output_kernel(
    place_ref, away, w_ref, summed_ref, lse_ref, early_ref, mixed_ref, gates_ref, out_ref, *edges, row
):
    weight = w_ref[pl.ds(group_start(place_ref, 3), WIDE), :]
    total = early_ref[...] + jnp.dot(
        merged(away, summed_ref, lse_ref, 3), weight, preferred_element_type=f32
    )
    gate = gates_ref[row : row + 1, :]
    out_ref[...] = (mixed_ref[...] + gate * total).astype(bf16)
    if edges:
        for edge_ref, start in zip(edges, edge_starts(place_ref[1])):
            edge_ref[...] = out_ref[pl.ds(start, FRAME), :]


def output(where, away, summed, lse, w_out, early, mixed, gates, row):
    edge = ((FRAME, D), bf16, VMEM)
    return call(
        functools.partial(output_kernel, row=row),
        "output",
        [SMEM] + [VMEM] * 7,
        [((SLAB, D), bf16, VMEM)] + ([edge, edge] if row + 1 < STEPS else []),
    )(where, away[3], w_out, summed, lse, early, mixed, gates)


def sent(block, k):
    return lax.ppermute(block, "patch", ring(k % RING)) if k % RING else block


def shards(latent, stale_kv, timesteps, counts, conv_weight, w_mod, w_qkv, q_gain, k_gain, w_out):
    own_slab = lax.axis_index("patch")
    y, z, c = own_slab // 8, (own_slab // 2) % RING, own_slab % 2
    where = jnp.stack([z, c, timesteps[0], timesteps[1], y]).astype(jnp.int32)
    to_core, to_chip, *pieces = prepare(where, latent, stale_kv)
    chip_rows = lax.ppermute(to_chip, "patch", NEXT_CHIP)
    core_rows = lax.ppermute(to_core, "patch", CORE)
    arrived = {k: sent(pieces[k], k) for k in ORDER}
    old = stack(arrived, arrived[0], us=8)
    old_y = lax.ppermute(old, "patch", ACROSS)
    old_core = lax.ppermute(old, "patch", CORE)
    mod, gains, mixed, *blocks = opening(
        where, latent, core_rows, chip_rows, conv_weight, q_gain, k_gain, w_mod, w_qkv, old
    )
    fresh = {k: sent(blocks[k], k) for k in ORDER}
    gates, bias = aside(where, counts, w_mod, mixed)
    summed, lse = at_home(bias, blocks, blocks, blocks, mixed)
    new = stack(fresh, lse)
    new_y = lax.ppermute(new, "patch", ACROSS)
    new_core = lax.ppermute(new, "patch", CORE)
    old_y = held(old_y, [new])
    olds = [old, old_core, old_y, lax.ppermute(old_y, "patch", CORE)]
    far = attend(fresh, olds, bias, (2, 1), new)
    near = attend(fresh, olds, bias, (3, 0), far[0])
    away = {2: sent(far[0], -2), 1: sent(far[1], -1), 3: sent(near[0], -3), 0: near[1]}
    early = early_output(where, away, summed, lse, w_out)
    state, to_core, to_chip = output(where, away, summed, lse, w_out, early, mixed, gates, 0)

    chip_rows = lax.ppermute(to_chip, "patch", NEXT_CHIP)
    core_rows = lax.ppermute(to_core, "patch", CORE)
    mixed, normed, *own = next_queries(
        where, state, core_rows, chip_rows, conv_weight, mod, gains, w_qkv, 1
    )
    queries = {k: sent(own[k], k) for k in ORDER}
    new_y = held(new_y, own[:1])
    olds = [new, new_core, new_y, lax.ppermute(new_y, "patch", CORE)]
    *pairs, cache = last_keys(where, normed, gains, w_qkv, normed)
    far = attend(queries, olds, bias, (2, 1), pairs[1])
    near = attend(queries, olds, bias, (3, 0), far[0])
    away = {2: sent(far[0], -2), 1: sent(far[1], -1), 3: sent(near[0], -3), 0: near[1]}
    summed, lse = at_home(bias, own, pairs, pairs, normed)
    early = early_output(where, away, summed, lse, w_out)
    (state,) = output(where, away, summed, lse, w_out, early, mixed, gates, 1)
    return (state, cache)


def solution(mesh):
    rows = P(("req", "patch"), None)
    return jax.shard_map(
        shards,
        mesh=mesh,
        in_specs=(rows, rows, P("req"), P("req"), P(), P(), P(), P(), P(), P()),
        out_specs=(rows, rows),
        check_vma=False,
    )
```

time: 109 us -> 99.3 us (0.911)
  starting transfers between devices: 43.2 us -> 36.9 us
  Pallas kernels: 36.3 us -> 31.2 us
  waiting for transfers between devices: 27.1 us -> 29.1 us
    ppermute x15, starting transfers between devices: 27.3 us -> 22.7 us  [sent(): return lax.ppermute(block, 'patch', ring(k % RING)) if k % RING else block]
    pallas_call x1, Pallas kernels: 4.16 us -> 2 us  [next_queries(): call(functools.partial(next_kernel, row=row), 'next_queries', [SMEM] + [V...]
    pallas_call x4 -> x9, Pallas kernels: 23.7 us -> 22.1 us  [the longest x4 9.77 us: attend(): call(functools.partial(attend_kernel, slots=slots), 'attend', [VMEM] * 7...]
    pallas_call x2, Pallas kernels: 4.57 us -> 3.01 us  [output(): call(functools.partial(output_kernel, row=row), 'output', [SMEM] + [VMEM]...]
    ppermute x15, waiting for transfers between devices: 27.1 us -> 28.6 us  [sent(): return lax.ppermute(block, 'patch', ring(k % RING)) if k % RING else block]
    ppermute x1, starting transfers between devices: 4.56 us -> 3.44 us  [shards(): old_y = lax.ppermute(old, 'patch', ACROSS)]
  transfers between devices with their start and end apart: 25 -> 25, of which waited for: 11 -> 12; matrix products, arithmetic and copies ran while one was open for 0% -> 0% of each run, Pallas kernels for 25% -> 27%
where the time goes in v4:
time: 99.3 us; the launch traced here: 99.1 us
  starting transfers between devices  36.9 us (37%)
  Pallas kernels  31.2 us (31%)
  waiting for transfers between devices  29.1 us (29%)
    ppermute x15, waiting for transfers between devices, sent(): return lax.ppermute(block, 'patch', ring(k % RING)) if k % RING else block  28.6 us
    ppermute x15, starting transfers between devices, sent(): return lax.ppermute(block, 'patch', ring(k % RING)) if k % RING else block  22.7 us
    pallas_call x4, Pallas kernels, attend(): call(functools.partial(attend_kernel, slots=slots), 'attend', [VMEM] * 7...  9.77 us
    ppermute x1, starting transfers between devices, shards(): olds = [new, new_core, new_y, lax.ppermute(new_y, 'patch', CORE)]  5.15 us
    pallas_call x1, Pallas kernels, opening(): call(open_kernel, 'opening', [SMEM, HBM, VMEM, VMEM] + [HBM] * 3 + [VMEM]...  4.26 us
    ppermute x1, starting transfers between devices, shards(): old_y = lax.ppermute(old, 'patch', ACROSS)  3.44 us
    pallas_call x2, Pallas kernels, early_output(): call(early_output_kernel, 'early_output', [SMEM] + [VMEM] * 6, [((SLAB, D...  3.12 us
    pallas_call x2, Pallas kernels, output(): call(functools.partial(output_kernel, row=row), 'output', [SMEM] + [VMEM]...  3.01 us
  transfers between devices with their start and end apart: 25, of which 12 were waited for; matrix products, arithmetic and copies ran while one was open for 0% of the time, Pallas kernels for 27%

profile of v4, /device:TPU:0, one launch (start us, length us, event | category | flops | bytes accessed | tf_op | source)
XLA Modules:
  0.0 99.1 jit_solution(13287451509583854392)
XLA Ops:
  1.4 2.3 %prepare.1 = (bf16[80,1536]{1,0:T(8,128)(2,1)S(1)}, bf16[80,1536]{1,0:T(8,128)(2,1)S(1)}, bf16[128,768]{1,0:T(8,128)(2,1)S(1)}, bf16[128,768]{1,0:T(8,128)(2,1)S...) custom-call(s32[5]{0:T(128)S(1)} %pad_add_fusion.place_ref, bf16[128,1536]{1,0:T(8,128)(2,1)} %latent_ref.3, ...), custom_call_target="tpu_custom_call" | custom-call | flops 8000000000 | bytes 8000000 | tf_op jit(solution)/shard_map/prepare/pallas_call | solution.py:119
  3.7 2.1 %collective-permute-start.2 = (bf16[128,768]{1,0:T(8,128)(2,1)S(1)}, bf16[128,768]{1,0:T(8,128)(2,1)S(1)}, u32[]{:S(2)}, u32[]{:S(2)}) collective-permute-start(bf16[128,768]{1,0:T(8,128)(2,1)S(1)} %get-tuple-element.46), channel_id=1, source_target_pairs={{0,2},{1,3},{2,4},{3,5},{4,6},{5,7},{6,0},{7,1},{8,10},{9,11},{10,... | collective-permute-start | bytes 589832 | tf_op jit(solution)/shard_map/ppermute | solution.py:531
  5.8 3.6 %collective-permute-start.3 = (bf16[128,768]{1,0:T(8,128)(2,1)S(1)}, bf16[128,768]{1,0:T(8,128)(2,1)S(1)}, u32[]{:S(2)}, u32[]{:S(2)}) collective-permute-start(bf16[128,768]{1,0:T(8,128)(2,1)S(1)} %get-tuple-element.47), channel_id=1, source_target_pairs={{0,4},{1,5},{2,6},{3,7},{4,0},{5,1},{6,2},{7,3},{8,12},{9,13},{10,... | collective-permute-start | bytes 589832 | tf_op jit(solution)/shard_map/ppermute | solution.py:531
  11.2 1.6 %collective-permute-done.2.refs_1_ = bf16[128,768]{1,0:T(8,128)(2,1)S(1)} collective-permute-done((bf16[128,768]{1,0:T(8,128)(2,1)S(1)}, bf16[128,768]{1,0:T(8,128)(2,1)S(1)}, u32[]{:S(2)}, u32[]{:S(2)}) %collective-permute-start.2) | collective-permute-done | bytes 196640 | tf_op jit(solution)/shard_map/ppermute | solution.py:531
  12.8 6.5 %collective-permute-done.3.refs_2_ = bf16[128,768]{1,0:T(8,128)(2,1)S(1)} collective-permute-done((bf16[128,768]{1,0:T(8,128)(2,1)S(1)}, bf16[128,768]{1,0:T(8,128)(2,1)S(1)}, u32[]{:S(2)}, u32[]{:S(2)}) %collective-permute-start.3) | collective-permute-done | bytes 196640 | tf_op jit(solution)/shard_map/ppermute | solution.py:531
  19.4 3.4 %collective-permute-start.7 = (bf16[512,768]{1,0:T(8,128)(2,1)S(1)}, bf16[512,768]{1,0:T(8,128)(2,1)S(1)}, u32[]{:S(2)}, u32[]{:S(2)}) collective-permute-start(bf16[512,768]{1,0:T(8,128)(2,1)S(1)} %stack.18.token_ref.a0), channel_id=1, source_target_pairs={{0,8},{1,9},{2,10},{3,11},{4,12},{5,13},{6,14},{7,15},{8,0},{9,1},... | collective-permute-start | bytes 2359304 | tf_op jit(solution)/shard_map/ppermute | solution.py:543
  22.9 4.3 %opening.1 = (f32[2,3072]{1,0:T(2,128)S(1)}, f32[2,1536]{1,0:T(2,128)S(1)}, f32[128,1536]{1,0:T(8,128)S(1)}, bf16[128,1152]{1,0:T(8,128)(2,1)S(1)}, bf16[128,115...) custom-call(s32[5]{0:T(128)S(1)} %pad_add_fusion.place_ref, ...), custom_call_target="tpu_custom_call" | custom-call | flops 10000000000 | bytes 10000000 | tf_op jit(solution)/shard_map/opening/pallas_call | solution.py:231
  27.2 1.5 %collective-permute-start.5 = (bf16[128,1152]{1,0:T(8,128)(2,1)S(1)}, bf16[128,1152]{1,0:T(8,128)(2,1)S(1)}, u32[]{:S(2)}, u32[]{:S(2)}) collective-permute-start(bf16[128,1152]{1,0:T(8,128)(2,1)S(1)} %get-tuple-element.49.refs_3_.refs_7_.refs_11_), channel_id=1, source_target_pairs={{0,6},{1,7},{2,0},{3,1},{4,2},{5,3},{6,4},{7,5},{8,14},{9,15},{10,... | collective-permute-start | bytes 884744 | tf_op jit(solution)/shard_map/ppermute | solution.py:531
  30.2 2.3 %aside.1 = (f32[2,1536]{1,0:T(2,128)S(1)}, f32[16,512]{1,0:T(8,128)S(1)}) custom-call(s32[5]{0:T(128)S(1)} %pad_add_fusion.place_ref, s32[16]{0:T(128)S(1)} %copy-done.1, f32[256,4608]{1,0:T(8,128)} %w_mod_ref.3, f32[128,1536]{1,0:T(8,128)S(1)} %get-tuple-element.53.token_ref.refs_12_.mixed_ref), custom_call_target="tpu_custom_call" | custom-call | flops 100000000 | bytes 100000 | tf_op jit(solution)/shard_map/aside/pallas_call | solution.py:282
  33.4 8.1 %collective-permute-done.5.refs_3_.q0 = bf16[128,1152]{1,0:T(8,128)(2,1)S(1)} collective-permute-done((bf16[128,1152]{1,0:T(8,128)(2,1)S(1)}, bf16[128,1152]{1,0:T(8,128)(2,1)S(1)}, u32[]{:S(2)}, u32[]{:S(2)}) %collective-permute-start.5) | collective-permute-done | bytes 294944 | tf_op jit(solution)/shard_map/ppermute | solution.py:531
  41.5 3.4 %collective-permute-done.8.refs_1_.q1 = bf16[128,1152]{1,0:T(8,128)(2,1)S(1)} collective-permute-done((bf16[128,1152]{1,0:T(8,128)(2,1)S(1)}, bf16[128,1152]{1,0:T(8,128)(2,1)S(1)}, u32[]{:S(2)}, u32[]{:S(2)}) %collective-permute-start.8) | collective-permute-done | bytes 294944 | tf_op jit(solution)/shard_map/ppermute | solution.py:531
  45.0 2.2 %collective-permute-start.18 = (bf16[512,768]{1,0:T(8,128)(2,1)S(1)}, bf16[512,768]{1,0:T(8,128)(2,1)S(1)}, u32[]{:S(2)}, u32[]{:S(2)}) collective-permute-start(bf16[512,768]{1,0:T(8,128)(2,1)S(1)} %stack.19.refs_1_.token_ref.a0), channel_id=1, source_target_pairs={{0,8},{1,9},{2,10},{3,11},{4,12},{5,13},{6,14},{7,15},{8,0},{9,1},... | collective-permute-start | bytes 2359304 | tf_op jit(solution)/shard_map/ppermute | solution.py:552
  47.3 2.4 %attend.4 = (bf16[128,512]{1,0:T(8,128)(2,1)S(1)}, bf16[128,512]{1,0:T(8,128)(2,1)S(1)}) custom-call(bf16[128,1152]{1,0:T(8,128)(2,1)S(1)} %collective-permute-done.9.refs_2_.q0, bf16[128,1152]{1,0:T(8,128)(2,1)S(1)} %collective-permute-done.8.refs_1_.q1, bf16[512,768]{1,0:T(8,128)(2,1)S(1)} %stack.18.token_ref.a0, ...), custom_call_target="tpu_custom_call" | custom-call | flops 4000000000 | bytes 4000000 | tf_op jit(solution)/shard_map/attend/pallas_call | solution.py:460
  50.7 2.5 %attend.5 = (bf16[128,512]{1,0:T(8,128)(2,1)S(1)}, bf16[128,512]{1,0:T(8,128)(2,1)S(1)}) custom-call(bf16[128,1152]{1,0:T(8,128)(2,1)S(1)} %collective-permute-done.5.refs_3_.q0, bf16[128,1152]{1,0:T(8,128)(2,1)S(1)} %get-tuple-element.50.refs_0_.refs_4_.refs_8_.q1, bf16[512,768]{1,0:T(8,128)(2,1)S(1)} %stack.18.token_ref.a0, ...), custom_call_target="tpu_custom_call" | custom-call | flops 4000000000 | bytes 4000000 | tf_op jit(solution)/shard_map/attend/pallas_call | solution.py:460
  53.2 1.2 %collective-permute-start.11 = (bf16[128,512]{1,0:T(8,128)(2,1)S(1)}, bf16[128,512]{1,0:T(8,128)(2,1)S(1)}, u32[]{:S(2)}, u32[]{:S(2)}) collective-permute-start(bf16[128,512]{1,0:T(8,128)(2,1)S(1)} %get-tuple-element.57), channel_id=1, source_target_pairs={{0,2},{1,3},{2,4},{3,5},{4,6},{5,7},{6,0},{7,1},{8,10},{9,11},{10,... | collective-permute-start | bytes 393224 | tf_op jit(solution)/shard_map/ppermute | solution.py:531
  54.4 1.8 %collective-permute-done.12.a1 = bf16[128,512]{1,0:T(8,128)(2,1)S(1)} collective-permute-done((bf16[128,512]{1,0:T(8,128)(2,1)S(1)}, bf16[128,512]{1,0:T(8,128)(2,1)S(1)}, u32[]{:S(2)}, u32[]{:S(2)}) %collective-permute-start.12) | collective-permute-done | bytes 131104 | tf_op jit(solution)/shard_map/ppermute | solution.py:531
  57.2 1.6 %early_output.2.early_ref = f32[128,1536]{1,0:T(8,128)S(1)} custom-call(s32[5]{0:T(128)S(1)} %pad_add_fusion.place_ref, bf16[128,512]{1,0:T(8,128)(2,1)S(1)} %get-tuple-element.59.a0, bf16[128,512]{1,0:T(8,128)(2,1)S(1)} %collective-permute-done.12.a1, bf16[128,512]{1,0:T(8,128)(2,1)S(1)} %collective-permute-done.13.a2, bf16[1536,1536]{1,0:T(8,128)(2,1)S(1)} %bitcast.6, ...), custom_call_target="tpu_custom_call" | custom-call | flops 3000000000 | bytes 3000000 | tf_op jit(solution)/shard_map/early_output/pallas_call | solution.py:497
  58.8 1.5 %collective-permute-done.11.away = bf16[128,512]{1,0:T(8,128)(2,1)S(1)} collective-permute-done((bf16[128,512]{1,0:T(8,128)(2,1)S(1)}, bf16[128,512]{1,0:T(8,128)(2,1)S(1)}, u32[]{:S(2)}, u32[]{:S(2)}) %collective-permute-start.11) | collective-permute-done | bytes 131104 | tf_op jit(solution)/shard_map/ppermute | solution.py:531
  62.2 1.8 %collective-permute-start.17 = (bf16[512,768]{1,0:T(8,128)(2,1)S(1)}, bf16[512,768]{1,0:T(8,128)(2,1)S(1)}, u32[]{:S(2)}, u32[]{:S(2)}) collective-permute-start(bf16[512,768]{1,0:T(8,128)(2,1)S(1)} %stack.19.refs_1_.token_ref.a0), channel_id=1, source_target_pairs={{0,1},{1,0},{2,3},{3,2},{4,5},{5,4},{6,7},{7,6},{8,9},{9,8},{10,11... | collective-permute-start | bytes 2359304 | tf_op jit(solution)/shard_map/ppermute | solution.py:553
  64.1 2.0 %next_queries.1 = (f32[128,1536]{1,0:T(8,128)S(1)}, bf16[128,1536]{1,0:T(8,128)(2,1)S(1)}, bf16[128,384]{1,0:T(8,128)(2,1)S(1)}, bf16[128,384]{1,0:T(8,128)(2,1)...) custom-call(s32[5]{0:T(128)S(1)} %pad_add_fusion.place_ref, ...), custom_call_target="tpu_custom_call" | custom-call | flops 100000000 | bytes 100000 | tf_op jit(solution)/shard_map/next_queries/pallas_call | solution.py:303
  66.5 5.2 %collective-permute-start.19 = (bf16[512,768]{1,0:T(8,128)(2,1)S(1)}, bf16[512,768]{1,0:T(8,128)(2,1)S(1)}, u32[]{:S(2)}, u32[]{:S(2)}) collective-permute-start(bf16[512,768]{1,0:T(8,128)(2,1)S(1)} %hold.3.a2), channel_id=1, source_target_pairs={{0,1},{1,0},{2,3},{3,2},{4,5},{5,4},{6,7},{7,6},{8,9},{9,8},{10,11... | collective-permute-start | bytes 2359304 | tf_op jit(solution)/shard_map/ppermute | solution.py:569
  71.7 1.5 %collective-permute-start.20 = (bf16[128,384]{1,0:T(8,128)(2,1)S(1)}, bf16[128,384]{1,0:T(8,128)(2,1)S(1)}, u32[]{:S(2)}, u32[]{:S(2)}) collective-permute-start(bf16[128,384]{1,0:T(8,128)(2,1)S(1)} %get-tuple-element.69.refs_2_), channel_id=1, source_target_pairs={{0,4},{1,5},{2,6},{3,7},{4,0},{5,1},{6,2},{7,3},{8,12},{9,13},{10,... | collective-permute-start | bytes 294920 | tf_op jit(solution)/shard_map/ppermute | solution.py:531
  73.2 5.1 %collective-permute-start.21 = (bf16[128,384]{1,0:T(8,128)(2,1)S(1)}, bf16[128,384]{1,0:T(8,128)(2,1)S(1)}, u32[]{:S(2)}, u32[]{:S(2)}) collective-permute-start(bf16[128,384]{1,0:T(8,128)(2,1)S(1)} %get-tuple-element.70.refs_1_), channel_id=1, source_target_pairs={{0,2},{1,3},{2,4},{3,5},{4,6},{5,7},{6,0},{7,1},{8,10},{9,11},{10,... | collective-permute-start | bytes 294920 | tf_op jit(solution)/shard_map/ppermute | solution.py:531
  78.3 2.7 %last_keys.1 = (bf16[128,768]{1,0:T(8,128)(2,1)S(1)}, bf16[128,768]{1,0:T(8,128)(2,1)S(1)}, bf16[128,768]{1,0:T(8,128)(2,1)S(1)}, bf16[128,768]{1,0:T(8,128)(2,1)S(1)}, bf16[128,3072]{1,0:T(8,128)(2,1)}) custom-call(s32[5]{0:T(128)S(1)} %pad_add_fusion.place_ref, bf16[128,1536]{1,0:T(8,128)(2,1)S(1)} %get-tuple-element.71.normed_ref.token_ref.refs_12_, ...), custom_call_target="tpu_custom_call" | custom-call | flops 100000000 | bytes 100000 | tf_op jit(solution)/shard_map/last_keys/pallas_call | solution.py:381
  81.9 2.4 %attend.6 = (bf16[128,512]{1,0:T(8,128)(2,1)S(1)}, bf16[128,512]{1,0:T(8,128)(2,1)S(1)}) custom-call(bf16[128,384]{1,0:T(8,128)(2,1)S(1)} %collective-permute-done.20.q0, bf16[128,384]{1,0:T(8,128)(2,1)S(1)} %collective-permute-done.21.q1, bf16[512,768]{1,0:T(8,128)(2,1)S(1)} %stack.19.refs_1_.token_ref.a0, bf16[512,768]{1,0:T(8,128)(2,1)S(1)} %collective-permute-done.17.a1, ...), custom_call_target="tpu_custom_call" | custom-call | flops 4000000000 | bytes 4000000 | tf_op jit(solution)/shard_map/attend/pallas_call | solution.py:460
  84.3 2.6 %collective-permute-start.23 = (bf16[128,512]{1,0:T(8,128)(2,1)S(1)}, bf16[128,512]{1,0:T(8,128)(2,1)S(1)}, u32[]{:S(2)}, u32[]{:S(2)}) collective-permute-start(bf16[128,512]{1,0:T(8,128)(2,1)S(1)} %get-tuple-element.81), channel_id=1, source_target_pairs={{0,6},{1,7},{2,0},{3,1},{4,2},{5,3},{6,4},{7,5},{8,14},{9,15},{10,... | collective-permute-start | bytes 393224 | tf_op jit(solution)/shard_map/ppermute | solution.py:531
  86.9 1.6 %collective-permute-start.24 = (bf16[128,512]{1,0:T(8,128)(2,1)S(1)}, bf16[128,512]{1,0:T(8,128)(2,1)S(1)}, u32[]{:S(2)}, u32[]{:S(2)}) collective-permute-start(bf16[128,512]{1,0:T(8,128)(2,1)S(1)} %get-tuple-element.73.token_ref), channel_id=1, source_target_pairs={{0,4},{1,5},{2,6},{3,7},{4,0},{5,1},{6,2},{7,3},{8,12},{9,13},{10,... | collective-permute-start | bytes 393224 | tf_op jit(solution)/shard_map/ppermute | solution.py:531
  88.5 2.4 %attend.7 = (bf16[128,512]{1,0:T(8,128)(2,1)S(1)}, bf16[128,512]{1,0:T(8,128)(2,1)S(1)}) custom-call(bf16[128,384]{1,0:T(8,128)(2,1)S(1)} %collective-permute-done.16.q0, bf16[128,384]{1,0:T(8,128)(2,1)S(1)} %get-tuple-element.68.refs_1_.q1.refs_0_, bf16[512,768]{1,0:T(8,128)(2,1)S(1)} %stack.19.refs_1_.token_ref.a0, ...), custom_call_target="tpu_custom_call" | custom-call | flops 4000000000 | bytes 4000000 | tf_op jit(solution)/shard_map/attend/pallas_call | solution.py:460
  91.7 2.2 %collective-permute-done.24.a2 = bf16[128,512]{1,0:T(8,128)(2,1)S(1)} collective-permute-done((bf16[128,512]{1,0:T(8,128)(2,1)S(1)}, bf16[128,512]{1,0:T(8,128)(2,1)S(1)}, u32[]{:S(2)}, u32[]{:S(2)}) %collective-permute-start.24) | collective-permute-done | bytes 131104 | tf_op jit(solution)/shard_map/ppermute | solution.py:531
  93.9 1.6 %early_output.3.early_ref = f32[128,1536]{1,0:T(8,128)S(1)} custom-call(s32[5]{0:T(128)S(1)} %pad_add_fusion.place_ref, bf16[128,512]{1,0:T(8,128)(2,1)S(1)} %get-tuple-element.80.a0, bf16[128,512]{1,0:T(8,128)(2,1)S(1)} %collective-permute-done.23.a1, bf16[128,512]{1,0:T(8,128)(2,1)S(1)} %collective-permute-done.24.a2, bf16[1536,1536]{1,0:T(8,128)(2,1)S(1)} %bitcast.6, ...), custom_call_target="tpu_custom_call" | custom-call | flops 3000000000 | bytes 3000000 | tf_op jit(solution)/shard_map/early_output/pallas_call | solution.py:497
  95.4 1.8 %collective-permute-done.22.away = bf16[128,512]{1,0:T(8,128)(2,1)S(1)} collective-permute-done((bf16[128,512]{1,0:T(8,128)(2,1)S(1)}, bf16[128,512]{1,0:T(8,128)(2,1)S(1)}, u32[]{:S(2)}, u32[]{:S(2)}) %collective-permute-start.22) | collective-permute-done | bytes 131104 | tf_op jit(solution)/shard_map/ppermute | solution.py:531
  97.2 1.9 %output.3 = bf16[128,1536]{1,0:T(8,128)(2,1)} custom-call(s32[5]{0:T(128)S(1)} %pad_add_fusion.place_ref, bf16[128,512]{1,0:T(8,128)(2,1)S(1)} %collective-permute-done.22.away, bf16[1536,1536]{1,0:T(8,128)(2,1)S(1)} %bitcast.6, f32[128,1536]{1,0:T(8,128)S(1)} %get-tuple-element.78.summed_ref, f32[128,512]{1,0:T(8,128)S(1)} %get-tuple-element.79.lse_ref, ...), custom_call_target="tpu_custom_call" | custom-call | flops 100000000 | bytes 100000 | tf_op jit(solution)/shard_map/output/pallas_call | solution.py:522
  (61 shorter events, 11.2 us)
Async XLA Ops:
  1.4 21.4 %slice-start = ((s8[14155776]{0:T(1024)(128)(4,1)}), s8[4194304]{0:T(1024)(128)(4,1)S(1)}, s32[]{:S(2)}) async-start(s8[14155776]{0:T(1024)(128)(4,1)} %bitcast.3), calls=%async_computation | async-start | bytes 8388608
  1.4 21.4 %slice-start.1 = ((s8[14155776]{0:T(1024)(128)(4,1)}), s8[4194304]{0:T(1024)(128)(4,1)S(1)}, s32[]{:S(2)}) async-start(s8[14155776]{0:T(1024)(128)(4,1)} %bitcast.3), calls=%async_computation.1 | async-start | bytes 8388608
  1.4 21.4 %slice-start.6 = ((s8[4718592]{0:T(1024)(128)(4,1)}), s8[4194304]{0:T(1024)(128)(4,1)S(1)}, s32[]{:S(2)}) async-start(s8[4718592]{0:T(1024)(128)(4,1)} %bitcast.7), calls=%async_computation.6 | async-start | bytes 8388608
  3.7 9.1 %collective-permute-start.2 = (bf16[128,768]{1,0:T(8,128)(2,1)S(1)}, bf16[128,768]{1,0:T(8,128)(2,1)S(1)}, u32[]{:S(2)}, u32[]{:S(2)}) collective-permute-start(bf16[128,768]{1,0:T(8,128)(2,1)S(1)} %get-tuple-element.46), channel_id=1, source_target_pairs={{0,2},{1,3},{2,4},{3,5},{4,6},{5,7},{6,0},{7,1},{8,10},{9,11},{10,... | collective-permute-start | bytes 589832 | tf_op jit(solution)/shard_map/ppermute | solution.py:531
  5.8 13.6 %collective-permute-start.3 = (bf16[128,768]{1,0:T(8,128)(2,1)S(1)}, bf16[128,768]{1,0:T(8,128)(2,1)S(1)}, u32[]{:S(2)}, u32[]{:S(2)}) collective-permute-start(bf16[128,768]{1,0:T(8,128)(2,1)S(1)} %get-tuple-element.47), channel_id=1, source_target_pairs={{0,4},{1,5},{2,6},{3,7},{4,0},{5,1},{6,2},{7,3},{8,12},{9,13},{10,... | collective-permute-start | bytes 589832 | tf_op jit(solution)/shard_map/ppermute | solution.py:531
  9.3 13.5 %slice-start.2 = ((s8[14155776]{0:T(1024)(128)(4,1)}), s8[4194304]{0:T(1024)(128)(4,1)S(1)}, s32[]{:S(2)}) async-start(s8[14155776]{0:T(1024)(128)(4,1)} %bitcast.3), calls=%async_computation.2 | async-start | bytes 8388608
  9.3 13.5 %slice-start.7 = ((s8[4718592]{0:T(1024)(128)(4,1)}), s8[524288]{0:T(1024)(128)(4,1)S(1)}, s32[]{:S(2)}) async-start(s8[4718592]{0:T(1024)(128)(4,1)} %bitcast.7), calls=%async_computation.7 | async-start | bytes 1048576
  9.3 10.0 %collective-permute-start.4 = (bf16[128,768]{1,0:T(8,128)(2,1)S(1)}, bf16[128,768]{1,0:T(8,128)(2,1)S(1)}, u32[]{:S(2)}, u32[]{:S(2)}) collective-permute-start(bf16[128,768]{1,0:T(8,128)(2,1)S(1)} %get-tuple-element.48), channel_id=1, source_target_pairs={{0,6},{1,7},{2,0},{3,1},{4,2},{5,3},{6,4},{7,5},{8,14},{9,15},{10,... | collective-permute-start | bytes 589832 | tf_op jit(solution)/shard_map/ppermute | solution.py:531
  10.4 12.5 %collective-permute-start = (bf16[80,1536]{1,0:T(8,128)(2,1)S(1)}, bf16[80,1536]{1,0:T(8,128)(2,1)S(1)}, u32[]{:S(2)}, u32[]{:S(2)}) collective-permute-start(bf16[80,1536]{1,0:T(8,128)(2,1)S(1)} %get-tuple-element.43), channel_id=1, source_target_pairs={{0,1},{1,0},{2,3},{3,2},{4,5},{5,4},{6,7},{7,6},{8,9},{9,8},{10,11... | collective-permute-start | bytes 737288 | tf_op jit(solution)/shard_map/ppermute | solution.py:540
  10.4 12.5 %collective-permute-start.1 = (bf16[80,1536]{1,0:T(8,128)(2,1)S(1)}, bf16[80,1536]{1,0:T(8,128)(2,1)S(1)}, u32[]{:S(2)}, u32[]{:S(2)}) collective-permute-start(bf16[80,1536]{1,0:T(8,128)(2,1)S(1)} %get-tuple-element.44), channel_id=1, source_target_pairs={{1,2},{3,4},{5,6},{7,8},{9,10},{11,12},{13,14},{2,1},{4,3},{6,5},{... | collective-permute-start | bytes 737288 | tf_op jit(solution)/shard_map/ppermute | solution.py:539
  19.4 10.9 %copy-start.1 = (s32[16]{0:T(128)S(1)}, s32[16]{0:T(128)}, u32[]{:S(2)}) copy-start(s32[16]{0:T(128)} %counts_ref.1) | copy-start | bytes 196
  19.4 25.5 %collective-permute-start.7 = (bf16[512,768]{1,0:T(8,128)(2,1)S(1)}, bf16[512,768]{1,0:T(8,128)(2,1)S(1)}, u32[]{:S(2)}, u32[]{:S(2)}) collective-permute-start(bf16[512,768]{1,0:T(8,128)(2,1)S(1)} %stack.18.token_ref.a0), channel_id=1, source_target_pairs={{0,8},{1,9},{2,10},{3,11},{4,12},{5,13},{6,14},{7,15},{8,0},{9,1},... | collective-permute-start | bytes 2359304 | tf_op jit(solution)/shard_map/ppermute | solution.py:543
  27.2 14.3 %collective-permute-start.5 = (bf16[128,1152]{1,0:T(8,128)(2,1)S(1)}, bf16[128,1152]{1,0:T(8,128)(2,1)S(1)}, u32[]{:S(2)}, u32[]{:S(2)}) collective-permute-start(bf16[128,1152]{1,0:T(8,128)(2,1)S(1)} %get-tuple-element.49.refs_3_.refs_7_.refs_11_), channel_id=1, source_target_pairs={{0,6},{1,7},{2,0},{3,1},{4,2},{5,3},{6,4},{7,5},{8,14},{9,15},{10,... | collective-permute-start | bytes 884744 | tf_op jit(solution)/shard_map/ppermute | solution.py:531
  28.7 16.2 %collective-permute-start.8 = (bf16[128,1152]{1,0:T(8,128)(2,1)S(1)}, bf16[128,1152]{1,0:T(8,128)(2,1)S(1)}, u32[]{:S(2)}, u32[]{:S(2)}) collective-permute-start(bf16[128,1152]{1,0:T(8,128)(2,1)S(1)} %get-tuple-element.51.refs_1_.refs_5_.refs_9_), channel_id=1, source_target_pairs={{0,2},{1,3},{2,4},{3,5},{4,6},{5,7},{6,0},{7,1},{8,10},{9,11},{10,... | collective-permute-start | bytes 884744 | tf_op jit(solution)/shard_map/ppermute | solution.py:531
  29.3 15.6 %collective-permute-start.9 = (bf16[128,1152]{1,0:T(8,128)(2,1)S(1)}, bf16[128,1152]{1,0:T(8,128)(2,1)S(1)}, u32[]{:S(2)}, u32[]{:S(2)}) collective-permute-start(bf16[128,1152]{1,0:T(8,128)(2,1)S(1)} %get-tuple-element.52.refs_2_.refs_6_.refs_10_), channel_id=1, source_target_pairs={{0,4},{1,5},{2,6},{3,7},{4,0},{5,1},{6,2},{7,3},{8,12},{9,13},{10,... | collective-permute-start | bytes 884744 | tf_op jit(solution)/shard_map/ppermute | solution.py:531
  30.2 17.0 %collective-permute-start.6 = (bf16[512,768]{1,0:T(8,128)(2,1)S(1)}, bf16[512,768]{1,0:T(8,128)(2,1)S(1)}, u32[]{:S(2)}, u32[]{:S(2)}) collective-permute-start(bf16[512,768]{1,0:T(8,128)(2,1)S(1)} %stack.18.token_ref.a0), channel_id=1, source_target_pairs={{0,1},{1,0},{2,3},{3,2},{4,5},{5,4},{6,7},{7,6},{8,9},{9,8},{10,11... | collective-permute-start | bytes 2359304 | tf_op jit(solution)/shard_map/ppermute | solution.py:544
  45.0 2.4 %collective-permute-start.10 = (bf16[512,768]{1,0:T(8,128)(2,1)S(1)}, bf16[512,768]{1,0:T(8,128)(2,1)S(1)}, u32[]{:S(2)}, u32[]{:S(2)}) collective-permute-start(bf16[512,768]{1,0:T(8,128)(2,1)S(1)} %hold.2.a2), channel_id=1, source_target_pairs={{0,1},{1,0},{2,3},{3,2},{4,5},{5,4},{6,7},{7,6},{8,9},{9,8},{10,11... | collective-permute-start | bytes 2359304 | tf_op jit(solution)/shard_map/ppermute | solution.py:555
  45.0 21.5 %collective-permute-start.18 = (bf16[512,768]{1,0:T(8,128)(2,1)S(1)}, bf16[512,768]{1,0:T(8,128)(2,1)S(1)}, u32[]{:S(2)}, u32[]{:S(2)}) collective-permute-start(bf16[512,768]{1,0:T(8,128)(2,1)S(1)} %stack.19.refs_1_.token_ref.a0), channel_id=1, source_target_pairs={{0,8},{1,9},{2,10},{3,11},{4,12},{5,13},{6,14},{7,15},{8,0},{9,1},... | collective-permute-start | bytes 2359304 | tf_op jit(solution)/shard_map/ppermute | solution.py:552
  49.8 6.4 %collective-permute-start.12 = (bf16[128,512]{1,0:T(8,128)(2,1)S(1)}, bf16[128,512]{1,0:T(8,128)(2,1)S(1)}, u32[]{:S(2)}, u32[]{:S(2)}) collective-permute-start(bf16[128,512]{1,0:T(8,128)(2,1)S(1)} %get-tuple-element.60), channel_id=1, source_target_pairs={{0,6},{1,7},{2,0},{3,1},{4,2},{5,3},{6,4},{7,5},{8,14},{9,15},{10,... | collective-permute-start | bytes 393224 | tf_op jit(solution)/shard_map/ppermute | solution.py:531
  50.1 7.1 %slice-start.5 = ((s8[4718592]{0:T(1024)(128)(4,1)}), s8[524288]{0:T(1024)(128)(4,1)S(1)}, s32[]{:S(2)}) async-start(s8[4718592]{0:T(1024)(128)(4,1)} %bitcast.5), calls=%async_computation.5 | async-start | bytes 1048576
  50.1 7.1 %collective-permute-start.13 = (bf16[128,512]{1,0:T(8,128)(2,1)S(1)}, bf16[128,512]{1,0:T(8,128)(2,1)S(1)}, u32[]{:S(2)}, u32[]{:S(2)}) collective-permute-start(bf16[128,512]{1,0:T(8,128)(2,1)S(1)} %get-tuple-element.56.token_ref), channel_id=1, source_target_pairs={{0,4},{1,5},{2,6},{3,7},{4,0},{5,1},{6,2},{7,3},{8,12},{9,13},{10,... | collective-permute-start | bytes 393224 | tf_op jit(solution)/shard_map/ppermute | solution.py:531
  53.2 7.1 %collective-permute-start.11 = (bf16[128,512]{1,0:T(8,128)(2,1)S(1)}, bf16[128,512]{1,0:T(8,128)(2,1)S(1)}, u32[]{:S(2)}, u32[]{:S(2)}) collective-permute-start(bf16[128,512]{1,0:T(8,128)(2,1)S(1)} %get-tuple-element.57), channel_id=1, source_target_pairs={{0,2},{1,3},{2,4},{3,5},{4,6},{5,7},{6,0},{7,1},{8,10},{9,11},{10,... | collective-permute-start | bytes 393224 | tf_op jit(solution)/shard_map/ppermute | solution.py:531
  61.5 2.6 %collective-permute-start.14 = (bf16[80,1536]{1,0:T(8,128)(2,1)S(1)}, bf16[80,1536]{1,0:T(8,128)(2,1)S(1)}, u32[]{:S(2)}, u32[]{:S(2)}) collective-permute-start(bf16[80,1536]{1,0:T(8,128)(2,1)S(1)} %get-tuple-element.63), channel_id=1, source_target_pairs={{0,1},{1,0},{2,3},{3,2},{4,5},{5,4},{6,7},{7,6},{8,9},{9,8},{10,11... | collective-permute-start | bytes 737288 | tf_op jit(solution)/shard_map/ppermute | solution.py:563
  61.6 2.5 %collective-permute-start.15 = (bf16[80,1536]{1,0:T(8,128)(2,1)S(1)}, bf16[80,1536]{1,0:T(8,128)(2,1)S(1)}, u32[]{:S(2)}, u32[]{:S(2)}) collective-permute-start(bf16[80,1536]{1,0:T(8,128)(2,1)S(1)} %get-tuple-element.64), channel_id=1, source_target_pairs={{1,2},{3,4},{5,6},{7,8},{9,10},{11,12},{13,14},{2,1},{4,3},{6,5},{... | collective-permute-start | bytes 737288 | tf_op jit(solution)/shard_map/ppermute | solution.py:562
  62.2 19.6 %collective-permute-start.17 = (bf16[512,768]{1,0:T(8,128)(2,1)S(1)}, bf16[512,768]{1,0:T(8,128)(2,1)S(1)}, u32[]{:S(2)}, u32[]{:S(2)}) collective-permute-start(bf16[512,768]{1,0:T(8,128)(2,1)S(1)} %stack.19.refs_1_.token_ref.a0), channel_id=1, source_target_pairs={{0,1},{1,0},{2,3},{3,2},{4,5},{5,4},{6,7},{7,6},{8,9},{9,8},{10,11... | collective-permute-start | bytes 2359304 | tf_op jit(solution)/shard_map/ppermute | solution.py:553
  66.5 15.4 %collective-permute-start.19 = (bf16[512,768]{1,0:T(8,128)(2,1)S(1)}, bf16[512,768]{1,0:T(8,128)(2,1)S(1)}, u32[]{:S(2)}, u32[]{:S(2)}) collective-permute-start(bf16[512,768]{1,0:T(8,128)(2,1)S(1)} %hold.3.a2), channel_id=1, source_target_pairs={{0,1},{1,0},{2,3},{3,2},{4,5},{5,4},{6,7},{7,6},{8,9},{9,8},{10,11... | collective-permute-start | bytes 2359304 | tf_op jit(solution)/shard_map/ppermute | solution.py:569
  71.7 10.2 %collective-permute-start.20 = (bf16[128,384]{1,0:T(8,128)(2,1)S(1)}, bf16[128,384]{1,0:T(8,128)(2,1)S(1)}, u32[]{:S(2)}, u32[]{:S(2)}) collective-permute-start(bf16[128,384]{1,0:T(8,128)(2,1)S(1)} %get-tuple-element.69.refs_2_), channel_id=1, source_target_pairs={{0,4},{1,5},{2,6},{3,7},{4,0},{5,1},{6,2},{7,3},{8,12},{9,13},{10,... | collective-permute-start | bytes 294920 | tf_op jit(solution)/shard_map/ppermute | solution.py:531
  73.2 8.7 %collective-permute-start.21 = (bf16[128,384]{1,0:T(8,128)(2,1)S(1)}, bf16[128,384]{1,0:T(8,128)(2,1)S(1)}, u32[]{:S(2)}, u32[]{:S(2)}) collective-permute-start(bf16[128,384]{1,0:T(8,128)(2,1)S(1)} %get-tuple-element.70.refs_1_), channel_id=1, source_target_pairs={{0,2},{1,3},{2,4},{3,5},{4,6},{5,7},{6,0},{7,1},{8,10},{9,11},{10,... | collective-permute-start | bytes 294920 | tf_op jit(solution)/shard_map/ppermute | solution.py:531
  78.3 10.2 %collective-permute-start.16 = (bf16[128,384]{1,0:T(8,128)(2,1)S(1)}, bf16[128,384]{1,0:T(8,128)(2,1)S(1)}, u32[]{:S(2)}, u32[]{:S(2)}) collective-permute-start(bf16[128,384]{1,0:T(8,128)(2,1)S(1)} %get-tuple-element.67.refs_3_), channel_id=1, source_target_pairs={{0,6},{1,7},{2,0},{3,1},{4,2},{5,3},{6,4},{7,5},{8,14},{9,15},{10,... | collective-permute-start | bytes 294920 | tf_op jit(solution)/shard_map/ppermute | solution.py:531
  84.3 7.4 %collective-permute-start.23 = (bf16[128,512]{1,0:T(8,128)(2,1)S(1)}, bf16[128,512]{1,0:T(8,128)(2,1)S(1)}, u32[]{:S(2)}, u32[]{:S(2)}) collective-permute-start(bf16[128,512]{1,0:T(8,128)(2,1)S(1)} %get-tuple-element.81), channel_id=1, source_target_pairs={{0,6},{1,7},{2,0},{3,1},{4,2},{5,3},{6,4},{7,5},{8,14},{9,15},{10,... | collective-permute-start | bytes 393224 | tf_op jit(solution)/shard_map/ppermute | solution.py:531
  86.9 6.9 %collective-permute-start.24 = (bf16[128,512]{1,0:T(8,128)(2,1)S(1)}, bf16[128,512]{1,0:T(8,128)(2,1)S(1)}, u32[]{:S(2)}, u32[]{:S(2)}) collective-permute-start(bf16[128,512]{1,0:T(8,128)(2,1)S(1)} %get-tuple-element.73.token_ref), channel_id=1, source_target_pairs={{0,4},{1,5},{2,6},{3,7},{4,0},{5,1},{6,2},{7,3},{8,12},{9,13},{10,... | collective-permute-start | bytes 393224 | tf_op jit(solution)/shard_map/ppermute | solution.py:531
  90.9 6.2 %collective-permute-start.22 = (bf16[128,512]{1,0:T(8,128)(2,1)S(1)}, bf16[128,512]{1,0:T(8,128)(2,1)S(1)}, u32[]{:S(2)}, u32[]{:S(2)}) collective-permute-start(bf16[128,512]{1,0:T(8,128)(2,1)S(1)} %get-tuple-element.74), channel_id=1, source_target_pairs={{0,2},{1,3},{2,4},{3,5},{4,6},{5,7},{6,0},{7,1},{8,10},{9,11},{10,... | collective-permute-start | bytes 393224 | tf_op jit(solution)/shard_map/ppermute | solution.py:531
  (3 other events, 15.9 us)

commit v5 on v4

--- a/solution.py
+++ b/solution.py
@@ -404,8 +404,8 @@
 def stack_kernel(*refs):
     blocks, out_ref = refs[:RING], refs[-1]
     first = blocks[0].shape[1] - 2 * WIDE
-    for k in range(RING):
-        out_ref[k * SLAB : (k + 1) * SLAB, :] = blocks[k][:, first:]
+    for k, block in zip(ORDER, blocks):
+        out_ref[k * SLAB : (k + 1) * SLAB, :] = block[:, first:]
 
 
 def stack(blocks, token, us=0.1):
@@ -415,10 +415,10 @@
         [VMEM] * RING + [ANY],
         [((RING * SLAB, 2 * WIDE), bf16, VMEM)],
         us=us,
-    )(*[blocks[k] for k in range(RING)], token)[0]
-
-
-def attend_kernel(q0, q1, a0, a1, a2, a3, bias_ref, token_ref, *outs, slots):
+    )(*[blocks[k] for k in ORDER], token)[0]
+
+
+def attend_kernel(token_ref, q0, q1, a0, a1, a2, a3, bias_ref, *outs, slots):
     queries = (q0, q1)
     olds = (a0, a1, a2, a3)
     lanes = lax.broadcasted_iota(jnp.int32, (SLAB, HEAD), 1)
@@ -460,10 +460,10 @@
     return call(
         functools.partial(attend_kernel, slots=slots),
         "attend",
-        [VMEM] * 7 + [ANY],
+        [ANY] + [VMEM] * 7,
         [((SLAB, WIDE + HEAD), bf16, VMEM)] * 2,
         us=4,
-    )(*[queries[k] for k in slots], *olds, bias, token)
+    )(token, *[queries[k] for k in slots], *olds, bias)
 
 
 def merged(away, summed_ref, lse_ref, k):
@@ -483,7 +483,7 @@
     return jnp.concatenate(heads, 1).astype(bf16)
 
 
-def early_output_kernel(place_ref, a0, a1, a2, w_ref, summed_ref, lse_ref, out_ref):
+def early_output_kernel(place_ref, a2, a1, a0, w_ref, summed_ref, lse_ref, out_ref):
     total = 0.0
     for k, away in enumerate((a0, a1, a2)):
         weight = w_ref[pl.ds(group_start(place_ref, k), WIDE), :]
@@ -500,7 +500,7 @@
         [SMEM] + [VMEM] * 6,
         [((SLAB, D), f32, VMEM)],
         us=3,
-    )(where, away[0], away[1], away[2], w_out, summed, lse)[0]
+    )(where, away[2], away[1], away[0], w_out, summed, lse)[0]
 
 
 def output_kernel(

time: 99.3 us -> 97.9 us (0.986)
  waiting for transfers between devices: 29.1 us -> 22.3 us
  starting transfers between devices: 36.9 us -> 42.5 us
    ppermute x15, waiting for transfers between devices: 28.6 us -> 22.2 us  [sent(): return lax.ppermute(block, 'patch', ring(k % RING)) if k % RING else block]
    ppermute x15, starting transfers between devices: 22.7 us -> 27 us  [sent(): return lax.ppermute(block, 'patch', ring(k % RING)) if k % RING else block]
    ppermute x1, starting transfers between devices: 2.16 us -> 3.28 us  [shards(): new_y = lax.ppermute(new, 'patch', ACROSS)]
  transfers between devices with their start and end apart: 25 -> 25, of which waited for: 12 -> 11; matrix products, arithmetic and copies ran while one was open for 0% -> 0% of each run, Pallas kernels for 27% -> 28%
where the time goes in v5:
time: 97.9 us; the launch traced here: 97.8 us
  starting transfers between devices  42.5 us (43%)
  Pallas kernels  31.2 us (32%)
  waiting for transfers between devices  22.3 us (23%)
  between operations  1 us (1%)
    ppermute x15, starting transfers between devices, sent(): return lax.ppermute(block, 'patch', ring(k % RING)) if k % RING else block  27 us
    ppermute x15, waiting for transfers between devices, sent(): return lax.ppermute(block, 'patch', ring(k % RING)) if k % RING else block  22.2 us
    pallas_call x4, Pallas kernels, attend(): call(functools.partial(attend_kernel, slots=slots), 'attend', [ANY] + [VM...  9.78 us
    ppermute x1, starting transfers between devices, shards(): olds = [new, new_core, new_y, lax.ppermute(new_y, 'patch', CORE)]  5.57 us
    pallas_call x1, Pallas kernels, opening(): call(open_kernel, 'opening', [SMEM, HBM, VMEM, VMEM] + [HBM] * 3 + [VMEM]...  4.26 us
    ppermute x1, starting transfers between devices, shards(): new_y = lax.ppermute(new, 'patch', ACROSS)  3.28 us
    ppermute x1, starting transfers between devices, shards(): old_y = lax.ppermute(old, 'patch', ACROSS)  3.27 us
    pallas_call x2, Pallas kernels, early_output(): call(early_output_kernel, 'early_output', [SMEM] + [VMEM] * 6, [((SLAB, D...  3.12 us
  transfers between devices with their start and end apart: 25, of which 11 were waited for; matrix products, arithmetic and copies ran while one was open for 0% of the time, Pallas kernels for 28%

profile of v5, /device:TPU:0, one launch (start us, length us, event | category | flops | bytes accessed | tf_op | source)
XLA Modules:
  0.0 97.8 jit_solution(10526095638563503413)
XLA Ops:
  1.4 2.3 %prepare.1 = (bf16[80,1536]{1,0:T(8,128)(2,1)S(1)}, bf16[80,1536]{1,0:T(8,128)(2,1)S(1)}, bf16[128,768]{1,0:T(8,128)(2,1)S(1)}, bf16[128,768]{1,0:T(8,128)(2,1)S...) custom-call(s32[5]{0:T(128)S(1)} %pad_add_fusion.place_ref, bf16[128,1536]{1,0:T(8,128)(2,1)} %latent_ref.3, ...), custom_call_target="tpu_custom_call" | custom-call | flops 8000000000 | bytes 8000000 | tf_op jit(solution)/shard_map/prepare/pallas_call | solution.py:119
  3.7 4.0 %collective-permute-start.2 = (bf16[128,768]{1,0:T(8,128)(2,1)S(1)}, bf16[128,768]{1,0:T(8,128)(2,1)S(1)}, u32[]{:S(2)}, u32[]{:S(2)}) collective-permute-start(bf16[128,768]{1,0:T(8,128)(2,1)S(1)} %get-tuple-element.45), channel_id=1, source_target_pairs={{0,4},{1,5},{2,6},{3,7},{4,0},{5,1},{6,2},{7,3},{8,12},{9,13},{10,... | collective-permute-start | bytes 589832 | tf_op jit(solution)/shard_map/ppermute | solution.py:531
  8.8 2.2 %collective-permute-start.4 = (bf16[128,768]{1,0:T(8,128)(2,1)S(1)}, bf16[128,768]{1,0:T(8,128)(2,1)S(1)}, u32[]{:S(2)}, u32[]{:S(2)}) collective-permute-start(bf16[128,768]{1,0:T(8,128)(2,1)S(1)} %get-tuple-element.47), channel_id=1, source_target_pairs={{0,6},{1,7},{2,0},{3,1},{4,2},{5,3},{6,4},{7,5},{8,14},{9,15},{10,... | collective-permute-start | bytes 589832 | tf_op jit(solution)/shard_map/ppermute | solution.py:531
  11.6 1.8 %collective-permute-done.2.refs_0_ = bf16[128,768]{1,0:T(8,128)(2,1)S(1)} collective-permute-done((bf16[128,768]{1,0:T(8,128)(2,1)S(1)}, bf16[128,768]{1,0:T(8,128)(2,1)S(1)}, u32[]{:S(2)}, u32[]{:S(2)}) %collective-permute-start.2) | collective-permute-done | bytes 196640 | tf_op jit(solution)/shard_map/ppermute | solution.py:531
  13.5 3.8 %collective-permute-done.3.refs_1_ = bf16[128,768]{1,0:T(8,128)(2,1)S(1)} collective-permute-done((bf16[128,768]{1,0:T(8,128)(2,1)S(1)}, bf16[128,768]{1,0:T(8,128)(2,1)S(1)}, u32[]{:S(2)}, u32[]{:S(2)}) %collective-permute-start.3) | collective-permute-done | bytes 196640 | tf_op jit(solution)/shard_map/ppermute | solution.py:531
  17.6 3.3 %collective-permute-start.9 = (bf16[512,768]{1,0:T(8,128)(2,1)S(1)}, bf16[512,768]{1,0:T(8,128)(2,1)S(1)}, u32[]{:S(2)}, u32[]{:S(2)}) collective-permute-start(bf16[512,768]{1,0:T(8,128)(2,1)S(1)} %stack.18.token_ref.a0), channel_id=1, source_target_pairs={{0,8},{1,9},{2,10},{3,11},{4,12},{5,13},{6,14},{7,15},{8,0},{9,1},... | collective-permute-start | bytes 2359304 | tf_op jit(solution)/shard_map/ppermute | solution.py:543
  21.0 4.3 %opening.1 = (f32[2,3072]{1,0:T(2,128)S(1)}, f32[2,1536]{1,0:T(2,128)S(1)}, f32[128,1536]{1,0:T(8,128)S(1)}, bf16[128,1152]{1,0:T(8,128)(2,1)S(1)}, bf16[128,115...) custom-call(s32[5]{0:T(128)S(1)} %pad_add_fusion.place_ref, ...), custom_call_target="tpu_custom_call" | custom-call | flops 10000000000 | bytes 10000000 | tf_op jit(solution)/shard_map/opening/pallas_call | solution.py:231
  25.3 2.7 %collective-permute-start.5 = (bf16[128,1152]{1,0:T(8,128)(2,1)S(1)}, bf16[128,1152]{1,0:T(8,128)(2,1)S(1)}, u32[]{:S(2)}, u32[]{:S(2)}) collective-permute-start(bf16[128,1152]{1,0:T(8,128)(2,1)S(1)} %get-tuple-element.49.refs_2_.refs_6_.refs_10_), channel_id=1, source_target_pairs={{0,4},{1,5},{2,6},{3,7},{4,0},{5,1},{6,2},{7,3},{8,12},{9,13},{10,... | collective-permute-start | bytes 884744 | tf_op jit(solution)/shard_map/ppermute | solution.py:531
  28.9 2.3 %collective-permute-start.7 = (bf16[128,1152]{1,0:T(8,128)(2,1)S(1)}, bf16[128,1152]{1,0:T(8,128)(2,1)S(1)}, u32[]{:S(2)}, u32[]{:S(2)}) collective-permute-start(bf16[128,1152]{1,0:T(8,128)(2,1)S(1)} %get-tuple-element.51.refs_3_.refs_7_.refs_11_), channel_id=1, source_target_pairs={{0,6},{1,7},{2,0},{3,1},{4,2},{5,3},{6,4},{7,5},{8,14},{9,15},{10,... | collective-permute-start | bytes 884744 | tf_op jit(solution)/shard_map/ppermute | solution.py:531
  31.2 2.3 %aside.1 = (f32[2,1536]{1,0:T(2,128)S(1)}, f32[16,512]{1,0:T(8,128)S(1)}) custom-call(s32[5]{0:T(128)S(1)} %pad_add_fusion.place_ref, s32[16]{0:T(128)S(1)} %copy-done.1, f32[256,4608]{1,0:T(8,128)} %w_mod_ref.3, f32[128,1536]{1,0:T(8,128)S(1)} %get-tuple-element.53.token_ref.refs_12_.mixed_ref), custom_call_target="tpu_custom_call" | custom-call | flops 100000000 | bytes 100000 | tf_op jit(solution)/shard_map/aside/pallas_call | solution.py:282
  34.4 2.5 %collective-permute-done.5.refs_0_.q0 = bf16[128,1152]{1,0:T(8,128)(2,1)S(1)} collective-permute-done((bf16[128,1152]{1,0:T(8,128)(2,1)S(1)}, bf16[128,1152]{1,0:T(8,128)(2,1)S(1)}, u32[]{:S(2)}, u32[]{:S(2)}) %collective-permute-start.5) | collective-permute-done | bytes 294944 | tf_op jit(solution)/shard_map/ppermute | solution.py:531
  36.8 4.3 %collective-permute-done.6.refs_1_.q1 = bf16[128,1152]{1,0:T(8,128)(2,1)S(1)} collective-permute-done((bf16[128,1152]{1,0:T(8,128)(2,1)S(1)}, bf16[128,1152]{1,0:T(8,128)(2,1)S(1)}, u32[]{:S(2)}, u32[]{:S(2)}) %collective-permute-start.6) | collective-permute-done | bytes 294944 | tf_op jit(solution)/shard_map/ppermute | solution.py:531
  41.6 3.3 %collective-permute-start.19 = (bf16[512,768]{1,0:T(8,128)(2,1)S(1)}, bf16[512,768]{1,0:T(8,128)(2,1)S(1)}, u32[]{:S(2)}, u32[]{:S(2)}) collective-permute-start(bf16[512,768]{1,0:T(8,128)(2,1)S(1)} %stack.19.refs_1_.token_ref.a0), channel_id=1, source_target_pairs={{0,8},{1,9},{2,10},{3,11},{4,12},{5,13},{6,14},{7,15},{8,0},{9,1},... | collective-permute-start | bytes 2359304 | tf_op jit(solution)/shard_map/ppermute | solution.py:552
  44.9 2.5 %attend.4 = (bf16[128,512]{1,0:T(8,128)(2,1)S(1)}, bf16[128,512]{1,0:T(8,128)(2,1)S(1)}) custom-call(bf16[512,768]{1,0:T(8,128)(2,1)S(1)} %stack.19.refs_1_.token_ref.a0, bf16[128,1152]{1,0:T(8,128)(2,1)S(1)} %collective-permute-done.5.refs_0_.q0, bf16[128,1152]{1,0:T(8,128)(2,1)S(1)} %collective-permute-done.6.refs_1_.q1, ...), custom_call_target="tpu_custom_call" | custom-call | flops 4000000000 | bytes 4000000 | tf_op jit(solution)/shard_map/attend/pallas_call | solution.py:460
  48.7 2.0 %collective-permute-start.13 = (bf16[128,512]{1,0:T(8,128)(2,1)S(1)}, bf16[128,512]{1,0:T(8,128)(2,1)S(1)}, u32[]{:S(2)}, u32[]{:S(2)}) collective-permute-start(bf16[128,512]{1,0:T(8,128)(2,1)S(1)} %get-tuple-element.59), channel_id=1, source_target_pairs={{0,6},{1,7},{2,0},{3,1},{4,2},{5,3},{6,4},{7,5},{8,14},{9,15},{10,... | collective-permute-start | bytes 393224 | tf_op jit(solution)/shard_map/ppermute | solution.py:531
  50.7 2.4 %attend.5 = (bf16[128,512]{1,0:T(8,128)(2,1)S(1)}, bf16[128,512]{1,0:T(8,128)(2,1)S(1)}) custom-call(bf16[128,512]{1,0:T(8,128)(2,1)S(1)} %get-tuple-element.56.token_ref, bf16[128,1152]{1,0:T(8,128)(2,1)S(1)} %collective-permute-done.7.refs_2_.q0, bf16[128,1152]{1,0:T(8,128)(2,1)S(1)} %get-tuple-element.52.refs_0_.refs_4_.refs_8_.refs_3_.q1, ...), custom_call_target="tpu_custom_call" | custom-call | flops 4000000000 | bytes 4000000 | tf_op jit(solution)/shard_map/attend/pallas_call | solution.py:460
  53.2 1.3 %collective-permute-done.12.a2 = bf16[128,512]{1,0:T(8,128)(2,1)S(1)} collective-permute-done((bf16[128,512]{1,0:T(8,128)(2,1)S(1)}, bf16[128,512]{1,0:T(8,128)(2,1)S(1)}, u32[]{:S(2)}, u32[]{:S(2)}) %collective-permute-start.12) | collective-permute-done | bytes 131104 | tf_op jit(solution)/shard_map/ppermute | solution.py:531
  54.5 1.7 %collective-permute-done.13.a1 = bf16[128,512]{1,0:T(8,128)(2,1)S(1)} collective-permute-done((bf16[128,512]{1,0:T(8,128)(2,1)S(1)}, bf16[128,512]{1,0:T(8,128)(2,1)S(1)}, u32[]{:S(2)}, u32[]{:S(2)}) %collective-permute-start.13) | collective-permute-done | bytes 131104 | tf_op jit(solution)/shard_map/ppermute | solution.py:531
  56.3 1.6 %early_output.2.early_ref = f32[128,1536]{1,0:T(8,128)S(1)} custom-call(s32[5]{0:T(128)S(1)} %pad_add_fusion.place_ref, bf16[128,512]{1,0:T(8,128)(2,1)S(1)} %collective-permute-done.12.a2, bf16[128,512]{1,0:T(8,128)(2,1)S(1)} %collective-permute-done.13.a1, bf16[128,512]{1,0:T(8,128)(2,1)S(1)} %get-tuple-element.60.a0, bf16[1536,1536]{1,0:T(8,128)(2,1)S(1)} %bitcast.6, ...), custom_call_target="tpu_custom_call" | custom-call | flops 3000000000 | bytes 3000000 | tf_op jit(solution)/shard_map/early_output/pallas_call | solution.py:497
  57.8 1.6 %collective-permute-done.11.away = bf16[128,512]{1,0:T(8,128)(2,1)S(1)} collective-permute-done((bf16[128,512]{1,0:T(8,128)(2,1)S(1)}, bf16[128,512]{1,0:T(8,128)(2,1)S(1)}, u32[]{:S(2)}, u32[]{:S(2)}) %collective-permute-start.11) | collective-permute-done | bytes 131104 | tf_op jit(solution)/shard_map/ppermute | solution.py:531
  61.3 1.8 %collective-permute-start.18 = (bf16[512,768]{1,0:T(8,128)(2,1)S(1)}, bf16[512,768]{1,0:T(8,128)(2,1)S(1)}, u32[]{:S(2)}, u32[]{:S(2)}) collective-permute-start(bf16[512,768]{1,0:T(8,128)(2,1)S(1)} %stack.19.refs_1_.token_ref.a0), channel_id=1, source_target_pairs={{0,1},{1,0},{2,3},{3,2},{4,5},{5,4},{6,7},{7,6},{8,9},{9,8},{10,11... | collective-permute-start | bytes 2359304 | tf_op jit(solution)/shard_map/ppermute | solution.py:553
  63.2 2.0 %next_queries.1 = (f32[128,1536]{1,0:T(8,128)S(1)}, bf16[128,1536]{1,0:T(8,128)(2,1)S(1)}, bf16[128,384]{1,0:T(8,128)(2,1)S(1)}, bf16[128,384]{1,0:T(8,128)(2,1)...) custom-call(s32[5]{0:T(128)S(1)} %pad_add_fusion.place_ref, ...), custom_call_target="tpu_custom_call" | custom-call | flops 100000000 | bytes 100000 | tf_op jit(solution)/shard_map/next_queries/pallas_call | solution.py:303
  65.2 5.6 %collective-permute-start.20 = (bf16[512,768]{1,0:T(8,128)(2,1)S(1)}, bf16[512,768]{1,0:T(8,128)(2,1)S(1)}, u32[]{:S(2)}, u32[]{:S(2)}) collective-permute-start(bf16[512,768]{1,0:T(8,128)(2,1)S(1)} %hold.3.a2), channel_id=1, source_target_pairs={{0,1},{1,0},{2,3},{3,2},{4,5},{5,4},{6,7},{7,6},{8,9},{9,8},{10,11... | collective-permute-start | bytes 2359304 | tf_op jit(solution)/shard_map/ppermute | solution.py:569
  71.5 4.9 %collective-permute-start.17 = (bf16[128,384]{1,0:T(8,128)(2,1)S(1)}, bf16[128,384]{1,0:T(8,128)(2,1)S(1)}, u32[]{:S(2)}, u32[]{:S(2)}) collective-permute-start(bf16[128,384]{1,0:T(8,128)(2,1)S(1)} %get-tuple-element.70.refs_1_), channel_id=1, source_target_pairs={{0,2},{1,3},{2,4},{3,5},{4,6},{5,7},{6,0},{7,1},{8,10},{9,11},{10,... | collective-permute-start | bytes 294920 | tf_op jit(solution)/shard_map/ppermute | solution.py:531
  76.4 2.7 %last_keys.1 = (bf16[128,768]{1,0:T(8,128)(2,1)S(1)}, bf16[128,768]{1,0:T(8,128)(2,1)S(1)}, bf16[128,768]{1,0:T(8,128)(2,1)S(1)}, bf16[128,768]{1,0:T(8,128)(2,1)S(1)}, bf16[128,3072]{1,0:T(8,128)(2,1)}) custom-call(s32[5]{0:T(128)S(1)} %pad_add_fusion.place_ref, bf16[128,1536]{1,0:T(8,128)(2,1)S(1)} %get-tuple-element.67.normed_ref.token_ref.refs_12_, ...), custom_call_target="tpu_custom_call" | custom-call | flops 100000000 | bytes 100000 | tf_op jit(solution)/shard_map/last_keys/pallas_call | solution.py:381
  80.0 2.4 %attend.6 = (bf16[128,512]{1,0:T(8,128)(2,1)S(1)}, bf16[128,512]{1,0:T(8,128)(2,1)S(1)}) custom-call(bf16[128,768]{1,0:T(8,128)(2,1)S(1)} %get-tuple-element.68.token_ref.refs_5_.refs_9_, bf16[128,384]{1,0:T(8,128)(2,1)S(1)} %collective-permute-done.16.q0, bf16[128,384]{1,0:T(8,128)(2,1)S(1)} %collective-permute-done.17.q1, ...), custom_call_target="tpu_custom_call" | custom-call | flops 4000000000 | bytes 4000000 | tf_op jit(solution)/shard_map/attend/pallas_call | solution.py:460
  82.4 2.1 %collective-permute-start.23 = (bf16[128,512]{1,0:T(8,128)(2,1)S(1)}, bf16[128,512]{1,0:T(8,128)(2,1)S(1)}, u32[]{:S(2)}, u32[]{:S(2)}) collective-permute-start(bf16[128,512]{1,0:T(8,128)(2,1)S(1)} %get-tuple-element.72.token_ref), channel_id=1, source_target_pairs={{0,4},{1,5},{2,6},{3,7},{4,0},{5,1},{6,2},{7,3},{8,12},{9,13},{10,... | collective-permute-start | bytes 393224 | tf_op jit(solution)/shard_map/ppermute | solution.py:531
  84.6 2.6 %collective-permute-start.24 = (bf16[128,512]{1,0:T(8,128)(2,1)S(1)}, bf16[128,512]{1,0:T(8,128)(2,1)S(1)}, u32[]{:S(2)}, u32[]{:S(2)}) collective-permute-start(bf16[128,512]{1,0:T(8,128)(2,1)S(1)} %get-tuple-element.80), channel_id=1, source_target_pairs={{0,6},{1,7},{2,0},{3,1},{4,2},{5,3},{6,4},{7,5},{8,14},{9,15},{10,... | collective-permute-start | bytes 393224 | tf_op jit(solution)/shard_map/ppermute | solution.py:531
  87.2 2.4 %attend.7 = (bf16[128,512]{1,0:T(8,128)(2,1)S(1)}, bf16[128,512]{1,0:T(8,128)(2,1)S(1)}) custom-call(bf16[128,512]{1,0:T(8,128)(2,1)S(1)} %get-tuple-element.72.token_ref, bf16[128,384]{1,0:T(8,128)(2,1)S(1)} %collective-permute-done.21.q0, bf16[128,384]{1,0:T(8,128)(2,1)S(1)} %get-tuple-element.71.refs_1_.q1.refs_0_, ...), custom_call_target="tpu_custom_call" | custom-call | flops 4000000000 | bytes 4000000 | tf_op jit(solution)/shard_map/attend/pallas_call | solution.py:460
  90.7 1.6 %early_output.3.early_ref = f32[128,1536]{1,0:T(8,128)S(1)} custom-call(s32[5]{0:T(128)S(1)} %pad_add_fusion.place_ref, bf16[128,512]{1,0:T(8,128)(2,1)S(1)} %collective-permute-done.23.a2, bf16[128,512]{1,0:T(8,128)(2,1)S(1)} %collective-permute-done.24.a1, bf16[128,512]{1,0:T(8,128)(2,1)S(1)} %get-tuple-element.81.a0, bf16[1536,1536]{1,0:T(8,128)(2,1)S(1)} %bitcast.6, ...), custom_call_target="tpu_custom_call" | custom-call | flops 3000000000 | bytes 3000000 | tf_op jit(solution)/shard_map/early_output/pallas_call | solution.py:497
  92.2 3.6 %collective-permute-done.22.away = bf16[128,512]{1,0:T(8,128)(2,1)S(1)} collective-permute-done((bf16[128,512]{1,0:T(8,128)(2,1)S(1)}, bf16[128,512]{1,0:T(8,128)(2,1)S(1)}, u32[]{:S(2)}, u32[]{:S(2)}) %collective-permute-start.22) | collective-permute-done | bytes 131104 | tf_op jit(solution)/shard_map/ppermute | solution.py:531
  95.9 1.9 %output.3 = bf16[128,1536]{1,0:T(8,128)(2,1)} custom-call(s32[5]{0:T(128)S(1)} %pad_add_fusion.place_ref, bf16[128,512]{1,0:T(8,128)(2,1)S(1)} %collective-permute-done.22.away, bf16[1536,1536]{1,0:T(8,128)(2,1)S(1)} %bitcast.6, f32[128,1536]{1,0:T(8,128)S(1)} %get-tuple-element.78.summed_ref, f32[128,512]{1,0:T(8,128)S(1)} %get-tuple-element.79.lse_ref, ...), custom_call_target="tpu_custom_call" | custom-call | flops 100000000 | bytes 100000 | tf_op jit(solution)/shard_map/output/pallas_call | solution.py:522
  (61 shorter events, 11.0 us)
Async XLA Ops:
  1.4 19.5 %slice-start = ((s8[14155776]{0:T(1024)(128)(4,1)}), s8[4194304]{0:T(1024)(128)(4,1)S(1)}, s32[]{:S(2)}) async-start(s8[14155776]{0:T(1024)(128)(4,1)} %bitcast.3), calls=%async_computation | async-start | bytes 8388608
  1.4 19.5 %slice-start.1 = ((s8[14155776]{0:T(1024)(128)(4,1)}), s8[4194304]{0:T(1024)(128)(4,1)S(1)}, s32[]{:S(2)}) async-start(s8[14155776]{0:T(1024)(128)(4,1)} %bitcast.3), calls=%async_computation.1 | async-start | bytes 8388608
  1.4 19.5 %slice-start.6 = ((s8[4718592]{0:T(1024)(128)(4,1)}), s8[4194304]{0:T(1024)(128)(4,1)S(1)}, s32[]{:S(2)}) async-start(s8[4718592]{0:T(1024)(128)(4,1)} %bitcast.7), calls=%async_computation.6 | async-start | bytes 8388608
  3.7 9.8 %collective-permute-start.2 = (bf16[128,768]{1,0:T(8,128)(2,1)S(1)}, bf16[128,768]{1,0:T(8,128)(2,1)S(1)}, u32[]{:S(2)}, u32[]{:S(2)}) collective-permute-start(bf16[128,768]{1,0:T(8,128)(2,1)S(1)} %get-tuple-element.45), channel_id=1, source_target_pairs={{0,4},{1,5},{2,6},{3,7},{4,0},{5,1},{6,2},{7,3},{8,12},{9,13},{10,... | collective-permute-start | bytes 589832 | tf_op jit(solution)/shard_map/ppermute | solution.py:531
  7.7 9.5 %collective-permute-start.3 = (bf16[128,768]{1,0:T(8,128)(2,1)S(1)}, bf16[128,768]{1,0:T(8,128)(2,1)S(1)}, u32[]{:S(2)}, u32[]{:S(2)}) collective-permute-start(bf16[128,768]{1,0:T(8,128)(2,1)S(1)} %get-tuple-element.46), channel_id=1, source_target_pairs={{0,2},{1,3},{2,4},{3,5},{4,6},{5,7},{6,0},{7,1},{8,10},{9,11},{10,... | collective-permute-start | bytes 589832 | tf_op jit(solution)/shard_map/ppermute | solution.py:531
  8.7 12.2 %slice-start.2 = ((s8[14155776]{0:T(1024)(128)(4,1)}), s8[4194304]{0:T(1024)(128)(4,1)S(1)}, s32[]{:S(2)}) async-start(s8[14155776]{0:T(1024)(128)(4,1)} %bitcast.3), calls=%async_computation.2 | async-start | bytes 8388608
  8.7 12.2 %slice-start.7 = ((s8[4718592]{0:T(1024)(128)(4,1)}), s8[524288]{0:T(1024)(128)(4,1)S(1)}, s32[]{:S(2)}) async-start(s8[4718592]{0:T(1024)(128)(4,1)} %bitcast.7), calls=%async_computation.7 | async-start | bytes 1048576
  8.8 8.8 %collective-permute-start.4 = (bf16[128,768]{1,0:T(8,128)(2,1)S(1)}, bf16[128,768]{1,0:T(8,128)(2,1)S(1)}, u32[]{:S(2)}, u32[]{:S(2)}) collective-permute-start(bf16[128,768]{1,0:T(8,128)(2,1)S(1)} %get-tuple-element.47), channel_id=1, source_target_pairs={{0,6},{1,7},{2,0},{3,1},{4,2},{5,3},{6,4},{7,5},{8,14},{9,15},{10,... | collective-permute-start | bytes 589832 | tf_op jit(solution)/shard_map/ppermute | solution.py:531
  11.0 10.0 %collective-permute-start = (bf16[80,1536]{1,0:T(8,128)(2,1)S(1)}, bf16[80,1536]{1,0:T(8,128)(2,1)S(1)}, u32[]{:S(2)}, u32[]{:S(2)}) collective-permute-start(bf16[80,1536]{1,0:T(8,128)(2,1)S(1)} %get-tuple-element.43), channel_id=1, source_target_pairs={{0,1},{1,0},{2,3},{3,2},{4,5},{5,4},{6,7},{7,6},{8,9},{9,8},{10,11... | collective-permute-start | bytes 737288 | tf_op jit(solution)/shard_map/ppermute | solution.py:540
  11.0 10.0 %collective-permute-start.1 = (bf16[80,1536]{1,0:T(8,128)(2,1)S(1)}, bf16[80,1536]{1,0:T(8,128)(2,1)S(1)}, u32[]{:S(2)}, u32[]{:S(2)}) collective-permute-start(bf16[80,1536]{1,0:T(8,128)(2,1)S(1)} %get-tuple-element.44), channel_id=1, source_target_pairs={{1,2},{3,4},{5,6},{7,8},{9,10},{11,12},{13,14},{2,1},{4,3},{6,5},{... | collective-permute-start | bytes 737288 | tf_op jit(solution)/shard_map/ppermute | solution.py:539
  17.6 13.6 %copy-start.1 = (s32[16]{0:T(128)S(1)}, s32[16]{0:T(128)}, u32[]{:S(2)}) copy-start(s32[16]{0:T(128)} %counts_ref.1) | copy-start | bytes 196
  17.6 23.9 %collective-permute-start.9 = (bf16[512,768]{1,0:T(8,128)(2,1)S(1)}, bf16[512,768]{1,0:T(8,128)(2,1)S(1)}, u32[]{:S(2)}, u32[]{:S(2)}) collective-permute-start(bf16[512,768]{1,0:T(8,128)(2,1)S(1)} %stack.18.token_ref.a0), channel_id=1, source_target_pairs={{0,8},{1,9},{2,10},{3,11},{4,12},{5,13},{6,14},{7,15},{8,0},{9,1},... | collective-permute-start | bytes 2359304 | tf_op jit(solution)/shard_map/ppermute | solution.py:543
  25.3 11.6 %collective-permute-start.5 = (bf16[128,1152]{1,0:T(8,128)(2,1)S(1)}, bf16[128,1152]{1,0:T(8,128)(2,1)S(1)}, u32[]{:S(2)}, u32[]{:S(2)}) collective-permute-start(bf16[128,1152]{1,0:T(8,128)(2,1)S(1)} %get-tuple-element.49.refs_2_.refs_6_.refs_10_), channel_id=1, source_target_pairs={{0,4},{1,5},{2,6},{3,7},{4,0},{5,1},{6,2},{7,3},{8,12},{9,13},{10,... | collective-permute-start | bytes 884744 | tf_op jit(solution)/shard_map/ppermute | solution.py:531
  28.0 13.2 %collective-permute-start.6 = (bf16[128,1152]{1,0:T(8,128)(2,1)S(1)}, bf16[128,1152]{1,0:T(8,128)(2,1)S(1)}, u32[]{:S(2)}, u32[]{:S(2)}) collective-permute-start(bf16[128,1152]{1,0:T(8,128)(2,1)S(1)} %get-tuple-element.50.refs_1_.refs_5_.refs_9_), channel_id=1, source_target_pairs={{0,2},{1,3},{2,4},{3,5},{4,6},{5,7},{6,0},{7,1},{8,10},{9,11},{10,... | collective-permute-start | bytes 884744 | tf_op jit(solution)/shard_map/ppermute | solution.py:531
  28.9 12.6 %collective-permute-start.7 = (bf16[128,1152]{1,0:T(8,128)(2,1)S(1)}, bf16[128,1152]{1,0:T(8,128)(2,1)S(1)}, u32[]{:S(2)}, u32[]{:S(2)}) collective-permute-start(bf16[128,1152]{1,0:T(8,128)(2,1)S(1)} %get-tuple-element.51.refs_3_.refs_7_.refs_11_), channel_id=1, source_target_pairs={{0,6},{1,7},{2,0},{3,1},{4,2},{5,3},{6,4},{7,5},{8,14},{9,15},{10,... | collective-permute-start | bytes 884744 | tf_op jit(solution)/shard_map/ppermute | solution.py:531
  31.2 13.7 %collective-permute-start.8 = (bf16[512,768]{1,0:T(8,128)(2,1)S(1)}, bf16[512,768]{1,0:T(8,128)(2,1)S(1)}, u32[]{:S(2)}, u32[]{:S(2)}) collective-permute-start(bf16[512,768]{1,0:T(8,128)(2,1)S(1)} %stack.18.token_ref.a0), channel_id=1, source_target_pairs={{0,1},{1,0},{2,3},{3,2},{4,5},{5,4},{6,7},{7,6},{8,9},{9,8},{10,11... | collective-permute-start | bytes 2359304 | tf_op jit(solution)/shard_map/ppermute | solution.py:544
  41.5 3.4 %collective-permute-start.10 = (bf16[512,768]{1,0:T(8,128)(2,1)S(1)}, bf16[512,768]{1,0:T(8,128)(2,1)S(1)}, u32[]{:S(2)}, u32[]{:S(2)}) collective-permute-start(bf16[512,768]{1,0:T(8,128)(2,1)S(1)} %hold.2.a2), channel_id=1, source_target_pairs={{0,1},{1,0},{2,3},{3,2},{4,5},{5,4},{6,7},{7,6},{8,9},{9,8},{10,11... | collective-permute-start | bytes 2359304 | tf_op jit(solution)/shard_map/ppermute | solution.py:555
  41.6 23.5 %collective-permute-start.19 = (bf16[512,768]{1,0:T(8,128)(2,1)S(1)}, bf16[512,768]{1,0:T(8,128)(2,1)S(1)}, u32[]{:S(2)}, u32[]{:S(2)}) collective-permute-start(bf16[512,768]{1,0:T(8,128)(2,1)S(1)} %stack.19.refs_1_.token_ref.a0), channel_id=1, source_target_pairs={{0,8},{1,9},{2,10},{3,11},{4,12},{5,13},{6,14},{7,15},{8,0},{9,1},... | collective-permute-start | bytes 2359304 | tf_op jit(solution)/shard_map/ppermute | solution.py:552
  47.4 7.1 %collective-permute-start.12 = (bf16[128,512]{1,0:T(8,128)(2,1)S(1)}, bf16[128,512]{1,0:T(8,128)(2,1)S(1)}, u32[]{:S(2)}, u32[]{:S(2)}) collective-permute-start(bf16[128,512]{1,0:T(8,128)(2,1)S(1)} %get-tuple-element.56.token_ref), channel_id=1, source_target_pairs={{0,4},{1,5},{2,6},{3,7},{4,0},{5,1},{6,2},{7,3},{8,12},{9,13},{10,... | collective-permute-start | bytes 393224 | tf_op jit(solution)/shard_map/ppermute | solution.py:531
  48.7 7.6 %slice-start.5 = ((s8[4718592]{0:T(1024)(128)(4,1)}), s8[524288]{0:T(1024)(128)(4,1)S(1)}, s32[]{:S(2)}) async-start(s8[4718592]{0:T(1024)(128)(4,1)} %bitcast.5), calls=%async_computation.5 | async-start | bytes 1048576
  48.7 7.6 %collective-permute-start.13 = (bf16[128,512]{1,0:T(8,128)(2,1)S(1)}, bf16[128,512]{1,0:T(8,128)(2,1)S(1)}, u32[]{:S(2)}, u32[]{:S(2)}) collective-permute-start(bf16[128,512]{1,0:T(8,128)(2,1)S(1)} %get-tuple-element.59), channel_id=1, source_target_pairs={{0,6},{1,7},{2,0},{3,1},{4,2},{5,3},{6,4},{7,5},{8,14},{9,15},{10,... | collective-permute-start | bytes 393224 | tf_op jit(solution)/shard_map/ppermute | solution.py:531
  53.1 6.3 %collective-permute-start.11 = (bf16[128,512]{1,0:T(8,128)(2,1)S(1)}, bf16[128,512]{1,0:T(8,128)(2,1)S(1)}, u32[]{:S(2)}, u32[]{:S(2)}) collective-permute-start(bf16[128,512]{1,0:T(8,128)(2,1)S(1)} %get-tuple-element.57), channel_id=1, source_target_pairs={{0,2},{1,3},{2,4},{3,5},{4,6},{5,7},{6,0},{7,1},{8,10},{9,11},{10,... | collective-permute-start | bytes 393224 | tf_op jit(solution)/shard_map/ppermute | solution.py:531
  60.6 2.6 %collective-permute-start.14 = (bf16[80,1536]{1,0:T(8,128)(2,1)S(1)}, bf16[80,1536]{1,0:T(8,128)(2,1)S(1)}, u32[]{:S(2)}, u32[]{:S(2)}) collective-permute-start(bf16[80,1536]{1,0:T(8,128)(2,1)S(1)} %get-tuple-element.63), channel_id=1, source_target_pairs={{0,1},{1,0},{2,3},{3,2},{4,5},{5,4},{6,7},{7,6},{8,9},{9,8},{10,11... | collective-permute-start | bytes 737288 | tf_op jit(solution)/shard_map/ppermute | solution.py:563
  60.7 2.5 %collective-permute-start.15 = (bf16[80,1536]{1,0:T(8,128)(2,1)S(1)}, bf16[80,1536]{1,0:T(8,128)(2,1)S(1)}, u32[]{:S(2)}, u32[]{:S(2)}) collective-permute-start(bf16[80,1536]{1,0:T(8,128)(2,1)S(1)} %get-tuple-element.64), channel_id=1, source_target_pairs={{1,2},{3,4},{5,6},{7,8},{9,10},{11,12},{13,14},{2,1},{4,3},{6,5},{... | collective-permute-start | bytes 737288 | tf_op jit(solution)/shard_map/ppermute | solution.py:562
  61.3 18.6 %collective-permute-start.18 = (bf16[512,768]{1,0:T(8,128)(2,1)S(1)}, bf16[512,768]{1,0:T(8,128)(2,1)S(1)}, u32[]{:S(2)}, u32[]{:S(2)}) collective-permute-start(bf16[512,768]{1,0:T(8,128)(2,1)S(1)} %stack.19.refs_1_.token_ref.a0), channel_id=1, source_target_pairs={{0,1},{1,0},{2,3},{3,2},{4,5},{5,4},{6,7},{7,6},{8,9},{9,8},{10,11... | collective-permute-start | bytes 2359304 | tf_op jit(solution)/shard_map/ppermute | solution.py:553
  65.2 14.8 %collective-permute-start.20 = (bf16[512,768]{1,0:T(8,128)(2,1)S(1)}, bf16[512,768]{1,0:T(8,128)(2,1)S(1)}, u32[]{:S(2)}, u32[]{:S(2)}) collective-permute-start(bf16[512,768]{1,0:T(8,128)(2,1)S(1)} %hold.3.a2), channel_id=1, source_target_pairs={{0,1},{1,0},{2,3},{3,2},{4,5},{5,4},{6,7},{7,6},{8,9},{9,8},{10,11... | collective-permute-start | bytes 2359304 | tf_op jit(solution)/shard_map/ppermute | solution.py:569
  70.8 9.2 %collective-permute-start.16 = (bf16[128,384]{1,0:T(8,128)(2,1)S(1)}, bf16[128,384]{1,0:T(8,128)(2,1)S(1)}, u32[]{:S(2)}, u32[]{:S(2)}) collective-permute-start(bf16[128,384]{1,0:T(8,128)(2,1)S(1)} %get-tuple-element.69.refs_2_), channel_id=1, source_target_pairs={{0,4},{1,5},{2,6},{3,7},{4,0},{5,1},{6,2},{7,3},{8,12},{9,13},{10,... | collective-permute-start | bytes 294920 | tf_op jit(solution)/shard_map/ppermute | solution.py:531
  71.5 8.5 %collective-permute-start.17 = (bf16[128,384]{1,0:T(8,128)(2,1)S(1)}, bf16[128,384]{1,0:T(8,128)(2,1)S(1)}, u32[]{:S(2)}, u32[]{:S(2)}) collective-permute-start(bf16[128,384]{1,0:T(8,128)(2,1)S(1)} %get-tuple-element.70.refs_1_), channel_id=1, source_target_pairs={{0,2},{1,3},{2,4},{3,5},{4,6},{5,7},{6,0},{7,1},{8,10},{9,11},{10,... | collective-permute-start | bytes 294920 | tf_op jit(solution)/shard_map/ppermute | solution.py:531
  76.3 10.8 %collective-permute-start.21 = (bf16[128,384]{1,0:T(8,128)(2,1)S(1)}, bf16[128,384]{1,0:T(8,128)(2,1)S(1)}, u32[]{:S(2)}, u32[]{:S(2)}) collective-permute-start(bf16[128,384]{1,0:T(8,128)(2,1)S(1)} %get-tuple-element.73.refs_3_), channel_id=1, source_target_pairs={{0,6},{1,7},{2,0},{3,1},{4,2},{5,3},{6,4},{7,5},{8,14},{9,15},{10,... | collective-permute-start | bytes 294920 | tf_op jit(solution)/shard_map/ppermute | solution.py:531
  82.4 7.3 %collective-permute-start.23 = (bf16[128,512]{1,0:T(8,128)(2,1)S(1)}, bf16[128,512]{1,0:T(8,128)(2,1)S(1)}, u32[]{:S(2)}, u32[]{:S(2)}) collective-permute-start(bf16[128,512]{1,0:T(8,128)(2,1)S(1)} %get-tuple-element.72.token_ref), channel_id=1, source_target_pairs={{0,4},{1,5},{2,6},{3,7},{4,0},{5,1},{6,2},{7,3},{8,12},{9,13},{10,... | collective-permute-start | bytes 393224 | tf_op jit(solution)/shard_map/ppermute | solution.py:531
  84.6 6.1 %collective-permute-start.24 = (bf16[128,512]{1,0:T(8,128)(2,1)S(1)}, bf16[128,512]{1,0:T(8,128)(2,1)S(1)}, u32[]{:S(2)}, u32[]{:S(2)}) collective-permute-start(bf16[128,512]{1,0:T(8,128)(2,1)S(1)} %get-tuple-element.80), channel_id=1, source_target_pairs={{0,6},{1,7},{2,0},{3,1},{4,2},{5,3},{6,4},{7,5},{8,14},{9,15},{10,... | collective-permute-start | bytes 393224 | tf_op jit(solution)/shard_map/ppermute | solution.py:531
  89.6 6.2 %collective-permute-start.22 = (bf16[128,512]{1,0:T(8,128)(2,1)S(1)}, bf16[128,512]{1,0:T(8,128)(2,1)S(1)}, u32[]{:S(2)}, u32[]{:S(2)}) collective-permute-start(bf16[128,512]{1,0:T(8,128)(2,1)S(1)} %get-tuple-element.74), channel_id=1, source_target_pairs={{0,2},{1,3},{2,4},{3,5},{4,6},{5,7},{6,0},{7,1},{8,10},{9,11},{10,... | collective-permute-start | bytes 393224 | tf_op jit(solution)/shard_map/ppermute | solution.py:531
  (3 other events, 16.3 us)

commit v6 on v5

--- a/solution.py
+++ b/solution.py
@@ -418,18 +418,19 @@
     )(*[blocks[k] for k in ORDER], token)[0]
 
 
-def attend_kernel(token_ref, q0, q1, a0, a1, a2, a3, bias_ref, *outs, slots):
-    queries = (q0, q1)
-    olds = (a0, a1, a2, a3)
+def attend_kernel(token_ref, *refs, slots):
+    n = len(slots)
+    queries, olds, bias_ref, outs = refs[:n], refs[n : n + 4], refs[n + 4], refs[n + 5 :]
     lanes = lax.broadcasted_iota(jnp.int32, (SLAB, HEAD), 1)
     ones = jnp.ones((RING * SLAB, HEAD), bf16)
-    lse = [jnp.zeros((SLAB, HEAD), f32)] * 2
+    lse = [jnp.zeros((SLAB, HEAD), f32)] * n
     for h in range(GROUP):
         here = slice(h * HEAD, (h + 1) * HEAD)
         there = slice(WIDE + h * HEAD, WIDE + (h + 1) * HEAD)
         keys = [old[:, here] for old in olds]
         values = [jnp.concatenate([old[:, there], ones], 1) for old in olds]
-        joined = jnp.concatenate([query[:, here] for query in queries], 0)
+        joined = [query[:, here] for query in queries]
+        joined = jnp.concatenate(joined, 0) if n > 1 else joined[0]
         products = [dots(joined, keys[a]) for a in range(4)]
         for i, slot in enumerate(slots):
             scores = []
@@ -446,7 +447,7 @@
             total = both[:, HEAD:]
             outs[i][:, here] = (both[:, :HEAD] / total).astype(bf16)
             lse[i] = jnp.where(lanes == h, highest + jnp.log2(total), lse[i])
-    for i in range(2):
+    for i in range(n):
         rest = lse[i]
         packed = 0.0
         for part in range(3):
@@ -460,8 +461,8 @@
     return call(
         functools.partial(attend_kernel, slots=slots),
         "attend",
-        [ANY] + [VMEM] * 7,
-        [((SLAB, WIDE + HEAD), bf16, VMEM)] * 2,
+        [ANY] + [VMEM] * (len(slots) + 5),
+        [((SLAB, WIDE + HEAD), bf16, VMEM)] * len(slots),
         us=4,
     )(token, *[queries[k] for k in slots], *olds, bias)
 
@@ -554,8 +555,9 @@
     old_y = held(old_y, [new])
     olds = [old, old_core, old_y, lax.ppermute(old_y, "patch", CORE)]
     far = attend(fresh, olds, bias, (2, 1), new)
-    near = attend(fresh, olds, bias, (3, 0), far[0])
-    away = {2: sent(far[0], -2), 1: sent(far[1], -1), 3: sent(near[0], -3), 0: near[1]}
+    (near,) = attend(fresh, olds, bias, (3,), far[0])
+    (here,) = attend(fresh, olds, bias, (0,), near)
+    away = {2: sent(far[0], -2), 1: sent(far[1], -1), 3: sent(near, -3), 0: here}
     early = early_output(where, away, summed, lse, w_out)
     state, to_core, to_chip = output(where, away, summed, lse, w_out, early, mixed, gates, 0)
 
@@ -569,8 +571,9 @@
     olds = [new, new_core, new_y, lax.ppermute(new_y, "patch", CORE)]
     *pairs, cache = last_keys(where, normed, gains, w_qkv, normed)
     far = attend(queries, olds, bias, (2, 1), pairs[1])
-    near = attend(queries, olds, bias, (3, 0), far[0])
-    away = {2: sent(far[0], -2), 1: sent(far[1], -1), 3: sent(near[0], -3), 0: near[1]}
+    (near,) = attend(queries, olds, bias, (3,), far[0])
+    (here,) = attend(queries, olds, bias, (0,), near)
+    away = {2: sent(far[0], -2), 1: sent(far[1], -1), 3: sent(near, -3), 0: here}
     summed, lse = at_home(bias, own, pairs, pairs, normed)
     early = early_output(where, away, summed, lse, w_out)
     (state,) = output(where, away, summed, lse, w_out, early, mixed, gates, 1)

time: 97.9 us -> 97.2 us (level)
  waiting for transfers between devices: 22.3 us -> 19.2 us
  Pallas kernels: 31.2 us -> 32.4 us
  starting transfers between devices: 42.5 us -> 43.6 us
    ppermute x15, waiting for transfers between devices: 22.2 us -> 19.2 us  [sent(): return lax.ppermute(block, 'patch', ring(k % RING)) if k % RING else block]
    pallas_call x4 -> x6, Pallas kernels: 9.78 us -> 10.9 us  [attend(): call(functools.partial(attend_kernel, slots=slots), 'attend', [ANY] + [VM...]
    ppermute x15, starting transfers between devices: 27 us -> 28.2 us  [sent(): return lax.ppermute(block, 'patch', ring(k % RING)) if k % RING else block]
  transfers between devices with their start and end apart: 25 -> 25, of which waited for: 11 -> 11; matrix products, arithmetic and copies ran while one was open for 0% -> 0% of each run, Pallas kernels for 28% -> 29%
where the time goes in v6:
time: 97.2 us; the launch traced here: 97 us
  starting transfers between devices  43.6 us (45%)
  Pallas kernels  32.4 us (33%)
  waiting for transfers between devices  19.2 us (20%)
  between operations  1.01 us (1%)
    ppermute x15, starting transfers between devices, sent(): return lax.ppermute(block, 'patch', ring(k % RING)) if k % RING else block  28.2 us
    ppermute x15, waiting for transfers between devices, sent(): return lax.ppermute(block, 'patch', ring(k % RING)) if k % RING else block  19.2 us
    pallas_call x6, Pallas kernels, attend(): call(functools.partial(attend_kernel, slots=slots), 'attend', [ANY] + [VM...  10.9 us
    ppermute x1, starting transfers between devices, shards(): olds = [new, new_core, new_y, lax.ppermute(new_y, 'patch', CORE)]  4.99 us
    pallas_call x1, Pallas kernels, opening(): call(open_kernel, 'opening', [SMEM, HBM, VMEM, VMEM] + [HBM] * 3 + [VMEM]...  4.26 us
    ppermute x1, starting transfers between devices, shards(): new_y = lax.ppermute(new, 'patch', ACROSS)  3.28 us
    ppermute x1, starting transfers between devices, shards(): old_y = lax.ppermute(old, 'patch', ACROSS)  3.27 us
    pallas_call x2, Pallas kernels, early_output(): call(early_output_kernel, 'early_output', [SMEM] + [VMEM] * 6, [((SLAB, D...  3.12 us
  transfers between devices with their start and end apart: 25, of which 11 were waited for; matrix products, arithmetic and copies ran while one was open for 0% of the time, Pallas kernels for 29%

profile of v6, /device:TPU:0, one launch (start us, length us, event | category | flops | bytes accessed | tf_op | source)
XLA Modules:
  0.0 97.0 jit_solution(12813914325892930612)
XLA Ops:
  1.4 2.3 %prepare.1 = (bf16[80,1536]{1,0:T(8,128)(2,1)S(1)}, bf16[80,1536]{1,0:T(8,128)(2,1)S(1)}, bf16[128,768]{1,0:T(8,128)(2,1)S(1)}, bf16[128,768]{1,0:T(8,128)(2,1)S...) custom-call(s32[5]{0:T(128)S(1)} %pad_add_fusion.place_ref, bf16[128,1536]{1,0:T(8,128)(2,1)} %latent_ref.3, ...), custom_call_target="tpu_custom_call" | custom-call | flops 8000000000 | bytes 8000000 | tf_op jit(solution)/shard_map/prepare/pallas_call | solution.py:119
  3.7 4.0 %collective-permute-start.2 = (bf16[128,768]{1,0:T(8,128)(2,1)S(1)}, bf16[128,768]{1,0:T(8,128)(2,1)S(1)}, u32[]{:S(2)}, u32[]{:S(2)}) collective-permute-start(bf16[128,768]{1,0:T(8,128)(2,1)S(1)} %get-tuple-element.41), channel_id=1, source_target_pairs={{0,4},{1,5},{2,6},{3,7},{4,0},{5,1},{6,2},{7,3},{8,12},{9,13},{10,... | collective-permute-start | bytes 589832 | tf_op jit(solution)/shard_map/ppermute | solution.py:532
  8.8 2.2 %collective-permute-start.4 = (bf16[128,768]{1,0:T(8,128)(2,1)S(1)}, bf16[128,768]{1,0:T(8,128)(2,1)S(1)}, u32[]{:S(2)}, u32[]{:S(2)}) collective-permute-start(bf16[128,768]{1,0:T(8,128)(2,1)S(1)} %get-tuple-element.43), channel_id=1, source_target_pairs={{0,6},{1,7},{2,0},{3,1},{4,2},{5,3},{6,4},{7,5},{8,14},{9,15},{10,... | collective-permute-start | bytes 589832 | tf_op jit(solution)/shard_map/ppermute | solution.py:532
  11.6 1.8 %collective-permute-done.2.refs_0_ = bf16[128,768]{1,0:T(8,128)(2,1)S(1)} collective-permute-done((bf16[128,768]{1,0:T(8,128)(2,1)S(1)}, bf16[128,768]{1,0:T(8,128)(2,1)S(1)}, u32[]{:S(2)}, u32[]{:S(2)}) %collective-permute-start.2) | collective-permute-done | bytes 196640 | tf_op jit(solution)/shard_map/ppermute | solution.py:532
  13.5 3.8 %collective-permute-done.3.refs_1_ = bf16[128,768]{1,0:T(8,128)(2,1)S(1)} collective-permute-done((bf16[128,768]{1,0:T(8,128)(2,1)S(1)}, bf16[128,768]{1,0:T(8,128)(2,1)S(1)}, u32[]{:S(2)}, u32[]{:S(2)}) %collective-permute-start.3) | collective-permute-done | bytes 196640 | tf_op jit(solution)/shard_map/ppermute | solution.py:532
  17.6 3.3 %collective-permute-start.9 = (bf16[512,768]{1,0:T(8,128)(2,1)S(1)}, bf16[512,768]{1,0:T(8,128)(2,1)S(1)}, u32[]{:S(2)}, u32[]{:S(2)}) collective-permute-start(bf16[512,768]{1,0:T(8,128)(2,1)S(1)} %stack.18.token_ref.refs_2_.refs_1_), channel_id=1, source_target_pairs={{0,8},{1,9},{2,10},{3,11},{4,12},{5,13},{6,14},{7,15},{8,0},{9,1},... | collective-permute-start | bytes 2359304 | tf_op jit(solution)/shard_map/ppermute | solution.py:544
  21.0 4.3 %opening.1 = (f32[2,3072]{1,0:T(2,128)S(1)}, f32[2,1536]{1,0:T(2,128)S(1)}, f32[128,1536]{1,0:T(8,128)S(1)}, bf16[128,1152]{1,0:T(8,128)(2,1)S(1)}, bf16[128,115...) custom-call(s32[5]{0:T(128)S(1)} %pad_add_fusion.place_ref, ...), custom_call_target="tpu_custom_call" | custom-call | flops 10000000000 | bytes 10000000 | tf_op jit(solution)/shard_map/opening/pallas_call | solution.py:231
  25.3 2.7 %collective-permute-start.5 = (bf16[128,1152]{1,0:T(8,128)(2,1)S(1)}, bf16[128,1152]{1,0:T(8,128)(2,1)S(1)}, u32[]{:S(2)}, u32[]{:S(2)}) collective-permute-start(bf16[128,1152]{1,0:T(8,128)(2,1)S(1)} %get-tuple-element.45.refs_2_.refs_6_.refs_10_), channel_id=1, source_target_pairs={{0,4},{1,5},{2,6},{3,7},{4,0},{5,1},{6,2},{7,3},{8,12},{9,13},{10,... | collective-permute-start | bytes 884744 | tf_op jit(solution)/shard_map/ppermute | solution.py:532
  28.9 2.3 %collective-permute-start.7 = (bf16[128,1152]{1,0:T(8,128)(2,1)S(1)}, bf16[128,1152]{1,0:T(8,128)(2,1)S(1)}, u32[]{:S(2)}, u32[]{:S(2)}) collective-permute-start(bf16[128,1152]{1,0:T(8,128)(2,1)S(1)} %get-tuple-element.47.refs_3_.refs_7_.refs_11_), channel_id=1, source_target_pairs={{0,6},{1,7},{2,0},{3,1},{4,2},{5,3},{6,4},{7,5},{8,14},{9,15},{10,... | collective-permute-start | bytes 884744 | tf_op jit(solution)/shard_map/ppermute | solution.py:532
  31.2 2.3 %aside.1 = (f32[2,1536]{1,0:T(2,128)S(1)}, f32[16,512]{1,0:T(8,128)S(1)}) custom-call(s32[5]{0:T(128)S(1)} %pad_add_fusion.place_ref, s32[16]{0:T(128)S(1)} %copy-done.1, f32[256,4608]{1,0:T(8,128)} %w_mod_ref.3, f32[128,1536]{1,0:T(8,128)S(1)} %get-tuple-element.49.token_ref.refs_12_.mixed_ref), custom_call_target="tpu_custom_call" | custom-call | flops 100000000 | bytes 100000 | tf_op jit(solution)/shard_map/aside/pallas_call | solution.py:282
  34.4 2.5 %collective-permute-done.5.refs_0_ = bf16[128,1152]{1,0:T(8,128)(2,1)S(1)} collective-permute-done((bf16[128,1152]{1,0:T(8,128)(2,1)S(1)}, bf16[128,1152]{1,0:T(8,128)(2,1)S(1)}, u32[]{:S(2)}, u32[]{:S(2)}) %collective-permute-start.5) | collective-permute-done | bytes 294944 | tf_op jit(solution)/shard_map/ppermute | solution.py:532
  36.8 4.3 %collective-permute-done.6.refs_1_ = bf16[128,1152]{1,0:T(8,128)(2,1)S(1)} collective-permute-done((bf16[128,1152]{1,0:T(8,128)(2,1)S(1)}, bf16[128,1152]{1,0:T(8,128)(2,1)S(1)}, u32[]{:S(2)}, u32[]{:S(2)}) %collective-permute-start.6) | collective-permute-done | bytes 294944 | tf_op jit(solution)/shard_map/ppermute | solution.py:532
  41.6 3.3 %collective-permute-start.19 = (bf16[512,768]{1,0:T(8,128)(2,1)S(1)}, bf16[512,768]{1,0:T(8,128)(2,1)S(1)}, u32[]{:S(2)}, u32[]{:S(2)}) collective-permute-start(bf16[512,768]{1,0:T(8,128)(2,1)S(1)} %stack.19.refs_1_.token_ref.refs_2_), channel_id=1, source_target_pairs={{0,8},{1,9},{2,10},{3,11},{4,12},{5,13},{6,14},{7,15},{8,0},{9,1},... | collective-permute-start | bytes 2359304 | tf_op jit(solution)/shard_map/ppermute | solution.py:553
  44.9 2.5 %attend.6 = (bf16[128,512]{1,0:T(8,128)(2,1)S(1)}, bf16[128,512]{1,0:T(8,128)(2,1)S(1)}) custom-call(bf16[512,768]{1,0:T(8,128)(2,1)S(1)} %stack.19.refs_1_.token_ref.refs_2_, bf16[128,1152]{1,0:T(8,128)(2,1)S(1)} %collective-permute-done.5.refs_0_, bf16[128,1152]{1,0:T(8,128)(2,1)S(1)} %collective-permute-done.6.refs_1_, ...), custom_call_target="tpu_custom_call" | custom-call | flops 4000000000 | bytes 4000000 | tf_op jit(solution)/shard_map/attend/pallas_call | solution.py:461
  48.7 2.0 %collective-permute-start.13 = (bf16[128,512]{1,0:T(8,128)(2,1)S(1)}, bf16[128,512]{1,0:T(8,128)(2,1)S(1)}, u32[]{:S(2)}, u32[]{:S(2)}) collective-permute-start(bf16[128,512]{1,0:T(8,128)(2,1)S(1)} %get-tuple-element.54), channel_id=1, source_target_pairs={{0,6},{1,7},{2,0},{3,1},{4,2},{5,3},{6,4},{7,5},{8,14},{9,15},{10,... | collective-permute-start | bytes 393224 | tf_op jit(solution)/shard_map/ppermute | solution.py:532
  50.7 1.5 %attend.7.token_ref = bf16[128,512]{1,0:T(8,128)(2,1)S(1)} custom-call(bf16[128,512]{1,0:T(8,128)(2,1)S(1)} %get-tuple-element.52.token_ref, bf16[128,1152]{1,0:T(8,128)(2,1)S(1)} %collective-permute-done.7.refs_2_.refs_0_, bf16[512,768]{1,0:T(8,128)(2,1)S(1)} %stack.18.token_ref.refs_2_.refs_1_, ...), custom_call_target="tpu_custom_call" | custom-call | flops 4000000000 | bytes 4000000 | tf_op jit(solution)/shard_map/attend/pallas_call | solution.py:461
  52.3 1.5 %attend.8.a0 = bf16[128,512]{1,0:T(8,128)(2,1)S(1)} custom-call(bf16[128,512]{1,0:T(8,128)(2,1)S(1)} %attend.7.token_ref, bf16[128,1152]{1,0:T(8,128)(2,1)S(1)} %get-tuple-element.48.refs_0_.refs_4_.refs_8_.refs_3_, bf16[512,768]{1,0:T(8,128)(2,1)S(1)} %stack.18.token_ref.refs_2_.refs_1_, bf16[512,768]{1,0:T(8,128)(2,1)S(1)} %collective-permute-done.8.refs_3_.refs_2_, ...), custom_call_target="tpu_custom_call" | custom-call | flops 4000000000 | bytes 4000000 | tf_op jit(solution)/shard_map/attend/pallas_call | solution.py:461
  54.5 1.7 %collective-permute-done.13.a1 = bf16[128,512]{1,0:T(8,128)(2,1)S(1)} collective-permute-done((bf16[128,512]{1,0:T(8,128)(2,1)S(1)}, bf16[128,512]{1,0:T(8,128)(2,1)S(1)}, u32[]{:S(2)}, u32[]{:S(2)}) %collective-permute-start.13) | collective-permute-done | bytes 131104 | tf_op jit(solution)/shard_map/ppermute | solution.py:532
  56.3 1.6 %early_output.2.early_ref = f32[128,1536]{1,0:T(8,128)S(1)} custom-call(s32[5]{0:T(128)S(1)} %pad_add_fusion.place_ref, bf16[128,512]{1,0:T(8,128)(2,1)S(1)} %collective-permute-done.12.a2, bf16[128,512]{1,0:T(8,128)(2,1)S(1)} %collective-permute-done.13.a1, bf16[128,512]{1,0:T(8,128)(2,1)S(1)} %attend.8.a0, bf16[1536,1536]{1,0:T(8,128)(2,1)S(1)} %bitcast.6, ...), custom_call_target="tpu_custom_call" | custom-call | flops 3000000000 | bytes 3000000 | tf_op jit(solution)/shard_map/early_output/pallas_call | solution.py:498
  60.4 2.4 %collective-permute-start.18 = (bf16[512,768]{1,0:T(8,128)(2,1)S(1)}, bf16[512,768]{1,0:T(8,128)(2,1)S(1)}, u32[]{:S(2)}, u32[]{:S(2)}) collective-permute-start(bf16[512,768]{1,0:T(8,128)(2,1)S(1)} %stack.19.refs_1_.token_ref.refs_2_), channel_id=1, source_target_pairs={{0,1},{1,0},{2,3},{3,2},{4,5},{5,4},{6,7},{7,6},{8,9},{9,8},{10,11... | collective-permute-start | bytes 2359304 | tf_op jit(solution)/shard_map/ppermute | solution.py:554
  62.8 2.0 %next_queries.1 = (f32[128,1536]{1,0:T(8,128)S(1)}, bf16[128,1536]{1,0:T(8,128)(2,1)S(1)}, bf16[128,384]{1,0:T(8,128)(2,1)S(1)}, bf16[128,384]{1,0:T(8,128)(2,1)...) custom-call(s32[5]{0:T(128)S(1)} %pad_add_fusion.place_ref, ...), custom_call_target="tpu_custom_call" | custom-call | flops 100000000 | bytes 100000 | tf_op jit(solution)/shard_map/next_queries/pallas_call | solution.py:303
  64.9 5.0 %collective-permute-start.20 = (bf16[512,768]{1,0:T(8,128)(2,1)S(1)}, bf16[512,768]{1,0:T(8,128)(2,1)S(1)}, u32[]{:S(2)}, u32[]{:S(2)}) collective-permute-start(bf16[512,768]{1,0:T(8,128)(2,1)S(1)} %hold.3.refs_4_.refs_3_), channel_id=1, source_target_pairs={{0,1},{1,0},{2,3},{3,2},{4,5},{5,4},{6,7},{7,6},{8,9},{9,8},{10,11... | collective-permute-start | bytes 2359304 | tf_op jit(solution)/shard_map/ppermute | solution.py:571
  69.8 1.6 %collective-permute-start.16 = (bf16[128,384]{1,0:T(8,128)(2,1)S(1)}, bf16[128,384]{1,0:T(8,128)(2,1)S(1)}, u32[]{:S(2)}, u32[]{:S(2)}) collective-permute-start(bf16[128,384]{1,0:T(8,128)(2,1)S(1)} %get-tuple-element.63.refs_2_), channel_id=1, source_target_pairs={{0,4},{1,5},{2,6},{3,7},{4,0},{5,1},{6,2},{7,3},{8,12},{9,13},{10,... | collective-permute-start | bytes 294920 | tf_op jit(solution)/shard_map/ppermute | solution.py:532
  71.5 4.9 %collective-permute-start.17 = (bf16[128,384]{1,0:T(8,128)(2,1)S(1)}, bf16[128,384]{1,0:T(8,128)(2,1)S(1)}, u32[]{:S(2)}, u32[]{:S(2)}) collective-permute-start(bf16[128,384]{1,0:T(8,128)(2,1)S(1)} %get-tuple-element.64.refs_1_), channel_id=1, source_target_pairs={{0,2},{1,3},{2,4},{3,5},{4,6},{5,7},{6,0},{7,1},{8,10},{9,11},{10,... | collective-permute-start | bytes 294920 | tf_op jit(solution)/shard_map/ppermute | solution.py:532
  76.3 2.7 %last_keys.1 = (bf16[128,768]{1,0:T(8,128)(2,1)S(1)}, bf16[128,768]{1,0:T(8,128)(2,1)S(1)}, bf16[128,768]{1,0:T(8,128)(2,1)S(1)}, bf16[128,768]{1,0:T(8,128)(2,1)S(1)}, bf16[128,3072]{1,0:T(8,128)(2,1)}) custom-call(s32[5]{0:T(128)S(1)} %pad_add_fusion.place_ref, bf16[128,1536]{1,0:T(8,128)(2,1)S(1)} %get-tuple-element.61.normed_ref.token_ref.refs_12_, ...), custom_call_target="tpu_custom_call" | custom-call | flops 100000000 | bytes 100000 | tf_op jit(solution)/shard_map/last_keys/pallas_call | solution.py:381
  80.0 2.4 %attend.9 = (bf16[128,512]{1,0:T(8,128)(2,1)S(1)}, bf16[128,512]{1,0:T(8,128)(2,1)S(1)}) custom-call(bf16[128,768]{1,0:T(8,128)(2,1)S(1)} %get-tuple-element.62.token_ref.refs_5_.refs_9_, bf16[128,384]{1,0:T(8,128)(2,1)S(1)} %collective-permute-done.16.refs_0_, bf16[128,384]{1,0:T(8,128)(2,1)S(1)} %collective-permute-done.17.refs_1_, ...), custom_call_target="tpu_custom_call" | custom-call | flops 4000000000 | bytes 4000000 | tf_op jit(solution)/shard_map/attend/pallas_call | solution.py:461
  82.4 2.4 %collective-permute-start.23 = (bf16[128,512]{1,0:T(8,128)(2,1)S(1)}, bf16[128,512]{1,0:T(8,128)(2,1)S(1)}, u32[]{:S(2)}, u32[]{:S(2)}) collective-permute-start(bf16[128,512]{1,0:T(8,128)(2,1)S(1)} %get-tuple-element.66.token_ref), channel_id=1, source_target_pairs={{0,4},{1,5},{2,6},{3,7},{4,0},{5,1},{6,2},{7,3},{8,12},{9,13},{10,... | collective-permute-start | bytes 393224 | tf_op jit(solution)/shard_map/ppermute | solution.py:532
  84.8 2.6 %collective-permute-start.24 = (bf16[128,512]{1,0:T(8,128)(2,1)S(1)}, bf16[128,512]{1,0:T(8,128)(2,1)S(1)}, u32[]{:S(2)}, u32[]{:S(2)}) collective-permute-start(bf16[128,512]{1,0:T(8,128)(2,1)S(1)} %get-tuple-element.73), channel_id=1, source_target_pairs={{0,6},{1,7},{2,0},{3,1},{4,2},{5,3},{6,4},{7,5},{8,14},{9,15},{10,... | collective-permute-start | bytes 393224 | tf_op jit(solution)/shard_map/ppermute | solution.py:532
  89.0 1.5 %attend.11.a0 = bf16[128,512]{1,0:T(8,128)(2,1)S(1)} custom-call(bf16[128,512]{1,0:T(8,128)(2,1)S(1)} %attend.10.token_ref, bf16[128,384]{1,0:T(8,128)(2,1)S(1)} %get-tuple-element.65.refs_1_.refs_0_, bf16[512,768]{1,0:T(8,128)(2,1)S(1)} %stack.19.refs_1_.token_ref.refs_2_, bf16[512,768]{1,0:T(8,128)(2,1)S(1)} %collective-permute-done.18.refs_3_.refs_2_, ...), custom_call_target="tpu_custom_call" | custom-call | flops 4000000000 | bytes 4000000 | tf_op jit(solution)/shard_map/attend/pallas_call | solution.py:461
  90.9 1.6 %early_output.3.early_ref = f32[128,1536]{1,0:T(8,128)S(1)} custom-call(s32[5]{0:T(128)S(1)} %pad_add_fusion.place_ref, bf16[128,512]{1,0:T(8,128)(2,1)S(1)} %collective-permute-done.23.a2, bf16[128,512]{1,0:T(8,128)(2,1)S(1)} %collective-permute-done.24.a1, bf16[128,512]{1,0:T(8,128)(2,1)S(1)} %attend.11.a0, bf16[1536,1536]{1,0:T(8,128)(2,1)S(1)} %bitcast.6, ...), custom_call_target="tpu_custom_call" | custom-call | flops 3000000000 | bytes 3000000 | tf_op jit(solution)/shard_map/early_output/pallas_call | solution.py:498
  92.4 2.7 %collective-permute-done.22.away = bf16[128,512]{1,0:T(8,128)(2,1)S(1)} collective-permute-done((bf16[128,512]{1,0:T(8,128)(2,1)S(1)}, bf16[128,512]{1,0:T(8,128)(2,1)S(1)}, u32[]{:S(2)}, u32[]{:S(2)}) %collective-permute-start.22) | collective-permute-done | bytes 131104 | tf_op jit(solution)/shard_map/ppermute | solution.py:532
  95.2 1.9 %output.3 = bf16[128,1536]{1,0:T(8,128)(2,1)} custom-call(s32[5]{0:T(128)S(1)} %pad_add_fusion.place_ref, bf16[128,512]{1,0:T(8,128)(2,1)S(1)} %collective-permute-done.22.away, bf16[1536,1536]{1,0:T(8,128)(2,1)S(1)} %bitcast.6, f32[128,1536]{1,0:T(8,128)S(1)} %get-tuple-element.71.summed_ref, f32[128,512]{1,0:T(8,128)S(1)} %get-tuple-element.72.lse_ref, ...), custom_call_target="tpu_custom_call" | custom-call | flops 100000000 | bytes 100000 | tf_op jit(solution)/shard_map/output/pallas_call | solution.py:523
  (63 shorter events, 12.5 us)
Async XLA Ops:
  1.4 19.5 %slice-start = ((s8[14155776]{0:T(1024)(128)(4,1)}), s8[4194304]{0:T(1024)(128)(4,1)S(1)}, s32[]{:S(2)}) async-start(s8[14155776]{0:T(1024)(128)(4,1)} %bitcast.3), calls=%async_computation | async-start | bytes 8388608
  1.4 19.5 %slice-start.1 = ((s8[14155776]{0:T(1024)(128)(4,1)}), s8[4194304]{0:T(1024)(128)(4,1)S(1)}, s32[]{:S(2)}) async-start(s8[14155776]{0:T(1024)(128)(4,1)} %bitcast.3), calls=%async_computation.1 | async-start | bytes 8388608
  1.4 19.5 %slice-start.6 = ((s8[4718592]{0:T(1024)(128)(4,1)}), s8[4194304]{0:T(1024)(128)(4,1)S(1)}, s32[]{:S(2)}) async-start(s8[4718592]{0:T(1024)(128)(4,1)} %bitcast.7), calls=%async_computation.6 | async-start | bytes 8388608
  3.7 9.8 %collective-permute-start.2 = (bf16[128,768]{1,0:T(8,128)(2,1)S(1)}, bf16[128,768]{1,0:T(8,128)(2,1)S(1)}, u32[]{:S(2)}, u32[]{:S(2)}) collective-permute-start(bf16[128,768]{1,0:T(8,128)(2,1)S(1)} %get-tuple-element.41), channel_id=1, source_target_pairs={{0,4},{1,5},{2,6},{3,7},{4,0},{5,1},{6,2},{7,3},{8,12},{9,13},{10,... | collective-permute-start | bytes 589832 | tf_op jit(solution)/shard_map/ppermute | solution.py:532
  7.7 9.5 %collective-permute-start.3 = (bf16[128,768]{1,0:T(8,128)(2,1)S(1)}, bf16[128,768]{1,0:T(8,128)(2,1)S(1)}, u32[]{:S(2)}, u32[]{:S(2)}) collective-permute-start(bf16[128,768]{1,0:T(8,128)(2,1)S(1)} %get-tuple-element.42), channel_id=1, source_target_pairs={{0,2},{1,3},{2,4},{3,5},{4,6},{5,7},{6,0},{7,1},{8,10},{9,11},{10,... | collective-permute-start | bytes 589832 | tf_op jit(solution)/shard_map/ppermute | solution.py:532
  8.7 12.2 %slice-start.2 = ((s8[14155776]{0:T(1024)(128)(4,1)}), s8[4194304]{0:T(1024)(128)(4,1)S(1)}, s32[]{:S(2)}) async-start(s8[14155776]{0:T(1024)(128)(4,1)} %bitcast.3), calls=%async_computation.2 | async-start | bytes 8388608
  8.7 12.2 %slice-start.7 = ((s8[4718592]{0:T(1024)(128)(4,1)}), s8[524288]{0:T(1024)(128)(4,1)S(1)}, s32[]{:S(2)}) async-start(s8[4718592]{0:T(1024)(128)(4,1)} %bitcast.7), calls=%async_computation.7 | async-start | bytes 1048576
  8.8 8.8 %collective-permute-start.4 = (bf16[128,768]{1,0:T(8,128)(2,1)S(1)}, bf16[128,768]{1,0:T(8,128)(2,1)S(1)}, u32[]{:S(2)}, u32[]{:S(2)}) collective-permute-start(bf16[128,768]{1,0:T(8,128)(2,1)S(1)} %get-tuple-element.43), channel_id=1, source_target_pairs={{0,6},{1,7},{2,0},{3,1},{4,2},{5,3},{6,4},{7,5},{8,14},{9,15},{10,... | collective-permute-start | bytes 589832 | tf_op jit(solution)/shard_map/ppermute | solution.py:532
  11.0 10.0 %collective-permute-start = (bf16[80,1536]{1,0:T(8,128)(2,1)S(1)}, bf16[80,1536]{1,0:T(8,128)(2,1)S(1)}, u32[]{:S(2)}, u32[]{:S(2)}) collective-permute-start(bf16[80,1536]{1,0:T(8,128)(2,1)S(1)} %get-tuple-element.39), channel_id=1, source_target_pairs={{0,1},{1,0},{2,3},{3,2},{4,5},{5,4},{6,7},{7,6},{8,9},{9,8},{10,11... | collective-permute-start | bytes 737288 | tf_op jit(solution)/shard_map/ppermute | solution.py:541
  11.0 10.0 %collective-permute-start.1 = (bf16[80,1536]{1,0:T(8,128)(2,1)S(1)}, bf16[80,1536]{1,0:T(8,128)(2,1)S(1)}, u32[]{:S(2)}, u32[]{:S(2)}) collective-permute-start(bf16[80,1536]{1,0:T(8,128)(2,1)S(1)} %get-tuple-element.40), channel_id=1, source_target_pairs={{1,2},{3,4},{5,6},{7,8},{9,10},{11,12},{13,14},{2,1},{4,3},{6,5},{... | collective-permute-start | bytes 737288 | tf_op jit(solution)/shard_map/ppermute | solution.py:540
  17.6 13.6 %copy-start.1 = (s32[16]{0:T(128)S(1)}, s32[16]{0:T(128)}, u32[]{:S(2)}) copy-start(s32[16]{0:T(128)} %counts_ref.1) | copy-start | bytes 196
  17.6 23.9 %collective-permute-start.9 = (bf16[512,768]{1,0:T(8,128)(2,1)S(1)}, bf16[512,768]{1,0:T(8,128)(2,1)S(1)}, u32[]{:S(2)}, u32[]{:S(2)}) collective-permute-start(bf16[512,768]{1,0:T(8,128)(2,1)S(1)} %stack.18.token_ref.refs_2_.refs_1_), channel_id=1, source_target_pairs={{0,8},{1,9},{2,10},{3,11},{4,12},{5,13},{6,14},{7,15},{8,0},{9,1},... | collective-permute-start | bytes 2359304 | tf_op jit(solution)/shard_map/ppermute | solution.py:544
  25.3 11.6 %collective-permute-start.5 = (bf16[128,1152]{1,0:T(8,128)(2,1)S(1)}, bf16[128,1152]{1,0:T(8,128)(2,1)S(1)}, u32[]{:S(2)}, u32[]{:S(2)}) collective-permute-start(bf16[128,1152]{1,0:T(8,128)(2,1)S(1)} %get-tuple-element.45.refs_2_.refs_6_.refs_10_), channel_id=1, source_target_pairs={{0,4},{1,5},{2,6},{3,7},{4,0},{5,1},{6,2},{7,3},{8,12},{9,13},{10,... | collective-permute-start | bytes 884744 | tf_op jit(solution)/shard_map/ppermute | solution.py:532
  28.0 13.2 %collective-permute-start.6 = (bf16[128,1152]{1,0:T(8,128)(2,1)S(1)}, bf16[128,1152]{1,0:T(8,128)(2,1)S(1)}, u32[]{:S(2)}, u32[]{:S(2)}) collective-permute-start(bf16[128,1152]{1,0:T(8,128)(2,1)S(1)} %get-tuple-element.46.refs_1_.refs_5_.refs_9_), channel_id=1, source_target_pairs={{0,2},{1,3},{2,4},{3,5},{4,6},{5,7},{6,0},{7,1},{8,10},{9,11},{10,... | collective-permute-start | bytes 884744 | tf_op jit(solution)/shard_map/ppermute | solution.py:532
  28.9 12.6 %collective-permute-start.7 = (bf16[128,1152]{1,0:T(8,128)(2,1)S(1)}, bf16[128,1152]{1,0:T(8,128)(2,1)S(1)}, u32[]{:S(2)}, u32[]{:S(2)}) collective-permute-start(bf16[128,1152]{1,0:T(8,128)(2,1)S(1)} %get-tuple-element.47.refs_3_.refs_7_.refs_11_), channel_id=1, source_target_pairs={{0,6},{1,7},{2,0},{3,1},{4,2},{5,3},{6,4},{7,5},{8,14},{9,15},{10,... | collective-permute-start | bytes 884744 | tf_op jit(solution)/shard_map/ppermute | solution.py:532
  31.2 13.7 %collective-permute-start.8 = (bf16[512,768]{1,0:T(8,128)(2,1)S(1)}, bf16[512,768]{1,0:T(8,128)(2,1)S(1)}, u32[]{:S(2)}, u32[]{:S(2)}) collective-permute-start(bf16[512,768]{1,0:T(8,128)(2,1)S(1)} %stack.18.token_ref.refs_2_.refs_1_), channel_id=1, source_target_pairs={{0,1},{1,0},{2,3},{3,2},{4,5},{5,4},{6,7},{7,6},{8,9},{9,8},{10,11... | collective-permute-start | bytes 2359304 | tf_op jit(solution)/shard_map/ppermute | solution.py:545
  41.5 3.4 %collective-permute-start.10 = (bf16[512,768]{1,0:T(8,128)(2,1)S(1)}, bf16[512,768]{1,0:T(8,128)(2,1)S(1)}, u32[]{:S(2)}, u32[]{:S(2)}) collective-permute-start(bf16[512,768]{1,0:T(8,128)(2,1)S(1)} %hold.2.refs_4_.refs_3_), channel_id=1, source_target_pairs={{0,1},{1,0},{2,3},{3,2},{4,5},{5,4},{6,7},{7,6},{8,9},{9,8},{10,11... | collective-permute-start | bytes 2359304 | tf_op jit(solution)/shard_map/ppermute | solution.py:556
  41.6 23.2 %collective-permute-start.19 = (bf16[512,768]{1,0:T(8,128)(2,1)S(1)}, bf16[512,768]{1,0:T(8,128)(2,1)S(1)}, u32[]{:S(2)}, u32[]{:S(2)}) collective-permute-start(bf16[512,768]{1,0:T(8,128)(2,1)S(1)} %stack.19.refs_1_.token_ref.refs_2_), channel_id=1, source_target_pairs={{0,8},{1,9},{2,10},{3,11},{4,12},{5,13},{6,14},{7,15},{8,0},{9,1},... | collective-permute-start | bytes 2359304 | tf_op jit(solution)/shard_map/ppermute | solution.py:553
  47.4 7.1 %collective-permute-start.12 = (bf16[128,512]{1,0:T(8,128)(2,1)S(1)}, bf16[128,512]{1,0:T(8,128)(2,1)S(1)}, u32[]{:S(2)}, u32[]{:S(2)}) collective-permute-start(bf16[128,512]{1,0:T(8,128)(2,1)S(1)} %get-tuple-element.52.token_ref), channel_id=1, source_target_pairs={{0,4},{1,5},{2,6},{3,7},{4,0},{5,1},{6,2},{7,3},{8,12},{9,13},{10,... | collective-permute-start | bytes 393224 | tf_op jit(solution)/shard_map/ppermute | solution.py:532
  48.7 7.6 %collective-permute-start.13 = (bf16[128,512]{1,0:T(8,128)(2,1)S(1)}, bf16[128,512]{1,0:T(8,128)(2,1)S(1)}, u32[]{:S(2)}, u32[]{:S(2)}) collective-permute-start(bf16[128,512]{1,0:T(8,128)(2,1)S(1)} %get-tuple-element.54), channel_id=1, source_target_pairs={{0,6},{1,7},{2,0},{3,1},{4,2},{5,3},{6,4},{7,5},{8,14},{9,15},{10,... | collective-permute-start | bytes 393224 | tf_op jit(solution)/shard_map/ppermute | solution.py:532
  50.7 5.6 %slice-start.4 = ((s8[4718592]{0:T(1024)(128)(4,1)}), s8[4194304]{0:T(1024)(128)(4,1)S(1)}, s32[]{:S(2)}) async-start(s8[4718592]{0:T(1024)(128)(4,1)} %bitcast.5), calls=%async_computation.4 | async-start | bytes 8388608
  52.2 6.3 %collective-permute-start.11 = (bf16[128,512]{1,0:T(8,128)(2,1)S(1)}, bf16[128,512]{1,0:T(8,128)(2,1)S(1)}, u32[]{:S(2)}, u32[]{:S(2)}) collective-permute-start(bf16[128,512]{1,0:T(8,128)(2,1)S(1)} %attend.7.token_ref), channel_id=1, source_target_pairs={{0,2},{1,3},{2,4},{3,5},{4,6},{5,7},{6,0},{7,1},{8,10},{9,11},{10,... | collective-permute-start | bytes 393224 | tf_op jit(solution)/shard_map/ppermute | solution.py:532
  59.6 3.2 %collective-permute-start.14 = (bf16[80,1536]{1,0:T(8,128)(2,1)S(1)}, bf16[80,1536]{1,0:T(8,128)(2,1)S(1)}, u32[]{:S(2)}, u32[]{:S(2)}) collective-permute-start(bf16[80,1536]{1,0:T(8,128)(2,1)S(1)} %get-tuple-element.57), channel_id=1, source_target_pairs={{0,1},{1,0},{2,3},{3,2},{4,5},{5,4},{6,7},{7,6},{8,9},{9,8},{10,11... | collective-permute-start | bytes 737288 | tf_op jit(solution)/shard_map/ppermute | solution.py:565
  59.7 3.1 %collective-permute-start.15 = (bf16[80,1536]{1,0:T(8,128)(2,1)S(1)}, bf16[80,1536]{1,0:T(8,128)(2,1)S(1)}, u32[]{:S(2)}, u32[]{:S(2)}) collective-permute-start(bf16[80,1536]{1,0:T(8,128)(2,1)S(1)} %get-tuple-element.58), channel_id=1, source_target_pairs={{1,2},{3,4},{5,6},{7,8},{9,10},{11,12},{13,14},{2,1},{4,3},{6,5},{... | collective-permute-start | bytes 737288 | tf_op jit(solution)/shard_map/ppermute | solution.py:564
  60.4 19.5 %collective-permute-start.18 = (bf16[512,768]{1,0:T(8,128)(2,1)S(1)}, bf16[512,768]{1,0:T(8,128)(2,1)S(1)}, u32[]{:S(2)}, u32[]{:S(2)}) collective-permute-start(bf16[512,768]{1,0:T(8,128)(2,1)S(1)} %stack.19.refs_1_.token_ref.refs_2_), channel_id=1, source_target_pairs={{0,1},{1,0},{2,3},{3,2},{4,5},{5,4},{6,7},{7,6},{8,9},{9,8},{10,11... | collective-permute-start | bytes 2359304 | tf_op jit(solution)/shard_map/ppermute | solution.py:554
  64.9 15.1 %collective-permute-start.20 = (bf16[512,768]{1,0:T(8,128)(2,1)S(1)}, bf16[512,768]{1,0:T(8,128)(2,1)S(1)}, u32[]{:S(2)}, u32[]{:S(2)}) collective-permute-start(bf16[512,768]{1,0:T(8,128)(2,1)S(1)} %hold.3.refs_4_.refs_3_), channel_id=1, source_target_pairs={{0,1},{1,0},{2,3},{3,2},{4,5},{5,4},{6,7},{7,6},{8,9},{9,8},{10,11... | collective-permute-start | bytes 2359304 | tf_op jit(solution)/shard_map/ppermute | solution.py:571
  69.8 10.1 %collective-permute-start.16 = (bf16[128,384]{1,0:T(8,128)(2,1)S(1)}, bf16[128,384]{1,0:T(8,128)(2,1)S(1)}, u32[]{:S(2)}, u32[]{:S(2)}) collective-permute-start(bf16[128,384]{1,0:T(8,128)(2,1)S(1)} %get-tuple-element.63.refs_2_), channel_id=1, source_target_pairs={{0,4},{1,5},{2,6},{3,7},{4,0},{5,1},{6,2},{7,3},{8,12},{9,13},{10,... | collective-permute-start | bytes 294920 | tf_op jit(solution)/shard_map/ppermute | solution.py:532
  71.5 8.5 %collective-permute-start.17 = (bf16[128,384]{1,0:T(8,128)(2,1)S(1)}, bf16[128,384]{1,0:T(8,128)(2,1)S(1)}, u32[]{:S(2)}, u32[]{:S(2)}) collective-permute-start(bf16[128,384]{1,0:T(8,128)(2,1)S(1)} %get-tuple-element.64.refs_1_), channel_id=1, source_target_pairs={{0,2},{1,3},{2,4},{3,5},{4,6},{5,7},{6,0},{7,1},{8,10},{9,11},{10,... | collective-permute-start | bytes 294920 | tf_op jit(solution)/shard_map/ppermute | solution.py:532
  76.3 11.1 %collective-permute-start.21 = (bf16[128,384]{1,0:T(8,128)(2,1)S(1)}, bf16[128,384]{1,0:T(8,128)(2,1)S(1)}, u32[]{:S(2)}, u32[]{:S(2)}) collective-permute-start(bf16[128,384]{1,0:T(8,128)(2,1)S(1)} %get-tuple-element.67.refs_3_), channel_id=1, source_target_pairs={{0,6},{1,7},{2,0},{3,1},{4,2},{5,3},{6,4},{7,5},{8,14},{9,15},{10,... | collective-permute-start | bytes 294920 | tf_op jit(solution)/shard_map/ppermute | solution.py:532
  82.4 8.1 %collective-permute-start.23 = (bf16[128,512]{1,0:T(8,128)(2,1)S(1)}, bf16[128,512]{1,0:T(8,128)(2,1)S(1)}, u32[]{:S(2)}, u32[]{:S(2)}) collective-permute-start(bf16[128,512]{1,0:T(8,128)(2,1)S(1)} %get-tuple-element.66.token_ref), channel_id=1, source_target_pairs={{0,4},{1,5},{2,6},{3,7},{4,0},{5,1},{6,2},{7,3},{8,12},{9,13},{10,... | collective-permute-start | bytes 393224 | tf_op jit(solution)/shard_map/ppermute | solution.py:532
  84.8 6.1 %collective-permute-start.24 = (bf16[128,512]{1,0:T(8,128)(2,1)S(1)}, bf16[128,512]{1,0:T(8,128)(2,1)S(1)}, u32[]{:S(2)}, u32[]{:S(2)}) collective-permute-start(bf16[128,512]{1,0:T(8,128)(2,1)S(1)} %get-tuple-element.73), channel_id=1, source_target_pairs={{0,6},{1,7},{2,0},{3,1},{4,2},{5,3},{6,4},{7,5},{8,14},{9,15},{10,... | collective-permute-start | bytes 393224 | tf_op jit(solution)/shard_map/ppermute | solution.py:532
  88.9 6.2 %collective-permute-start.22 = (bf16[128,512]{1,0:T(8,128)(2,1)S(1)}, bf16[128,512]{1,0:T(8,128)(2,1)S(1)}, u32[]{:S(2)}, u32[]{:S(2)}) collective-permute-start(bf16[128,512]{1,0:T(8,128)(2,1)S(1)} %attend.10.token_ref), channel_id=1, source_target_pairs={{0,2},{1,3},{2,4},{3,5},{4,6},{5,7},{6,0},{7,1},{8,10},{9,11},{10,... | collective-permute-start | bytes 393224 | tf_op jit(solution)/shard_map/ppermute | solution.py:532
  (3 other events, 12.5 us)

commit v7 on v6

--- a/solution.py
+++ b/solution.py
@@ -513,9 +513,8 @@
     )
     gate = gates_ref[row : row + 1, :]
     out_ref[...] = (mixed_ref[...] + gate * total).astype(bf16)
-    if edges:
-        for edge_ref, start in zip(edges, edge_starts(place_ref[1])):
-            edge_ref[...] = out_ref[pl.ds(start, FRAME), :]
+    for edge_ref, start in zip(edges, edge_starts(place_ref[1])):
+        edge_ref[...] = out_ref[pl.ds(start, FRAME), :]
 
 
 def output(where, away, summed, lse, w_out, early, mixed, gates, row):
@@ -524,8 +523,41 @@
         functools.partial(output_kernel, row=row),
         "output",
         [SMEM] + [VMEM] * 7,
-        [((SLAB, D), bf16, VMEM)] + ([edge, edge] if row + 1 < STEPS else []),
+        [((SLAB, D), bf16, VMEM), edge, edge],
     )(where, away[3], w_out, summed, lse, early, mixed, gates)
+
+
+def last_output_kernel(
+    place_ref, away, w_ref, summed_ref, lse_ref, early_ref, mixed_ref, gates_ref, out_ref,
+    held_ref, sems, *, row
+):
+    attended = merged(away, summed_ref, lse_ref, 3)
+    rows = pl.ds(group_start(place_ref, 3), WIDE)
+    width = D // 3
+    writes = []
+    for i in range(3):
+        here = slice(i * width, (i + 1) * width)
+        total = early_ref[:, here] + jnp.dot(
+            attended, w_ref[rows, here], preferred_element_type=f32
+        )
+        gate = gates_ref[row : row + 1, here]
+        held_ref[:, here] = (mixed_ref[:, here] + gate * total).astype(bf16)
+        writes.append(
+            pltpu.make_async_copy(held_ref.at[:, here], out_ref.at[:, here], sems.at[i])
+        )
+        writes[-1].start()
+    for write in writes:
+        write.wait()
+
+
+def last_output(where, away, summed, lse, w_out, early, mixed, gates, row):
+    return call(
+        functools.partial(last_output_kernel, row=row),
+        "last_output",
+        [SMEM] + [VMEM] * 7,
+        [((SLAB, D), bf16, HBM)],
+        [pltpu.VMEM((SLAB, D), bf16), pltpu.SemaphoreType.DMA((3,))],
+    )(where, away[3], w_out, summed, lse, early, mixed, gates)[0]
 
 
 def sent(block, k):
@@ -552,7 +584,7 @@
     new = stack(fresh, lse)
     new_y = lax.ppermute(new, "patch", ACROSS)
     new_core = lax.ppermute(new, "patch", CORE)
-    old_y = held(old_y, [new])
+    old_y = held(old_y, [fresh[2], fresh[1], fresh[3], lse])
     olds = [old, old_core, old_y, lax.ppermute(old_y, "patch", CORE)]
     far = attend(fresh, olds, bias, (2, 1), new)
     (near,) = attend(fresh, olds, bias, (3,), far[0])
@@ -576,7 +608,7 @@
     away = {2: sent(far[0], -2), 1: sent(far[1], -1), 3: sent(near, -3), 0: here}
     summed, lse = at_home(bias, own, pairs, pairs, normed)
     early = early_output(where, away, summed, lse, w_out)
-    (state,) = output(where, away, summed, lse, w_out, early, mixed, gates, 1)
+    state = last_output(where, away, summed, lse, w_out, early, mixed, gates, 1)
     return (state, cache)
 
 

time: 97.2 us -> 97.2 us (level)
    pallas_call x2 -> x1, Pallas kernels: 3 us -> 1.14 us  [output(): call(functools.partial(output_kernel, row=row), 'output', [SMEM] + [VMEM]...]
    pallas_call x0 -> x1, Pallas kernels: none -> 1.79 us  [last_output(): call(functools.partial(last_output_kernel, row=row), 'last_output', [SMEM...]
where the time goes in v7:
time: 97.2 us; the launch traced here: 97 us
  starting transfers between devices  43.5 us (45%)
  Pallas kernels  32.3 us (33%)
  waiting for transfers between devices  19.2 us (20%)
  between operations  1.16 us (1%)
    ppermute x15, starting transfers between devices, sent(): return lax.ppermute(block, 'patch', ring(k % RING)) if k % RING else block  28 us
    ppermute x15, waiting for transfers between devices, sent(): return lax.ppermute(block, 'patch', ring(k % RING)) if k % RING else block  19.2 us
    pallas_call x6, Pallas kernels, attend(): call(functools.partial(attend_kernel, slots=slots), 'attend', [ANY] + [VM...  10.9 us
    ppermute x1, starting transfers between devices, shards(): olds = [new, new_core, new_y, lax.ppermute(new_y, 'patch', CORE)]  4.98 us
    pallas_call x1, Pallas kernels, opening(): call(open_kernel, 'opening', [SMEM, HBM, VMEM, VMEM] + [HBM] * 3 + [VMEM]...  4.26 us
    ppermute x1, starting transfers between devices, shards(): new_y = lax.ppermute(new, 'patch', ACROSS)  3.36 us
    ppermute x1, starting transfers between devices, shards(): old_y = lax.ppermute(old, 'patch', ACROSS)  3.27 us
    pallas_call x2, Pallas kernels, early_output(): call(early_output_kernel, 'early_output', [SMEM] + [VMEM] * 6, [((SLAB, D...  3.14 us
  transfers between devices with their start and end apart: 25, of which 11 were waited for; matrix products, arithmetic and copies ran while one was open for 0% of the time, Pallas kernels for 29%

profile of v7, /device:TPU:0, one launch (start us, length us, event | category | flops | bytes accessed | tf_op | source)
XLA Modules:
  0.0 97.0 jit_solution(14566079667955686440)
XLA Ops:
  1.4 2.3 %prepare.1 = (bf16[80,1536]{1,0:T(8,128)(2,1)S(1)}, bf16[80,1536]{1,0:T(8,128)(2,1)S(1)}, bf16[128,768]{1,0:T(8,128)(2,1)S(1)}, bf16[128,768]{1,0:T(8,128)(2,1)S...) custom-call(s32[5]{0:T(128)S(1)} %pad_add_fusion.place_ref, bf16[128,1536]{1,0:T(8,128)(2,1)} %latent_ref.3, ...), custom_call_target="tpu_custom_call" | custom-call | flops 8000000000 | bytes 8000000 | tf_op jit(solution)/shard_map/prepare/pallas_call | solution.py:119
  3.7 4.0 %collective-permute-start.2 = (bf16[128,768]{1,0:T(8,128)(2,1)S(1)}, bf16[128,768]{1,0:T(8,128)(2,1)S(1)}, u32[]{:S(2)}, u32[]{:S(2)}) collective-permute-start(bf16[128,768]{1,0:T(8,128)(2,1)S(1)} %get-tuple-element.41), channel_id=1, source_target_pairs={{0,4},{1,5},{2,6},{3,7},{4,0},{5,1},{6,2},{7,3},{8,12},{9,13},{10,... | collective-permute-start | bytes 589832 | tf_op jit(solution)/shard_map/ppermute | solution.py:564
  8.8 2.2 %collective-permute-start.4 = (bf16[128,768]{1,0:T(8,128)(2,1)S(1)}, bf16[128,768]{1,0:T(8,128)(2,1)S(1)}, u32[]{:S(2)}, u32[]{:S(2)}) collective-permute-start(bf16[128,768]{1,0:T(8,128)(2,1)S(1)} %get-tuple-element.43), channel_id=1, source_target_pairs={{0,6},{1,7},{2,0},{3,1},{4,2},{5,3},{6,4},{7,5},{8,14},{9,15},{10,... | collective-permute-start | bytes 589832 | tf_op jit(solution)/shard_map/ppermute | solution.py:564
  11.6 1.8 %collective-permute-done.2.refs_0_ = bf16[128,768]{1,0:T(8,128)(2,1)S(1)} collective-permute-done((bf16[128,768]{1,0:T(8,128)(2,1)S(1)}, bf16[128,768]{1,0:T(8,128)(2,1)S(1)}, u32[]{:S(2)}, u32[]{:S(2)}) %collective-permute-start.2) | collective-permute-done | bytes 196640 | tf_op jit(solution)/shard_map/ppermute | solution.py:564
  13.5 3.8 %collective-permute-done.3.refs_1_ = bf16[128,768]{1,0:T(8,128)(2,1)S(1)} collective-permute-done((bf16[128,768]{1,0:T(8,128)(2,1)S(1)}, bf16[128,768]{1,0:T(8,128)(2,1)S(1)}, u32[]{:S(2)}, u32[]{:S(2)}) %collective-permute-start.3) | collective-permute-done | bytes 196640 | tf_op jit(solution)/shard_map/ppermute | solution.py:564
  17.6 3.3 %collective-permute-start.9 = (bf16[512,768]{1,0:T(8,128)(2,1)S(1)}, bf16[512,768]{1,0:T(8,128)(2,1)S(1)}, u32[]{:S(2)}, u32[]{:S(2)}) collective-permute-start(bf16[512,768]{1,0:T(8,128)(2,1)S(1)} %stack.18.token_ref.refs_2_.refs_1_), channel_id=1, source_target_pairs={{0,8},{1,9},{2,10},{3,11},{4,12},{5,13},{6,14},{7,15},{8,0},{9,1},... | collective-permute-start | bytes 2359304 | tf_op jit(solution)/shard_map/ppermute | solution.py:576
  21.0 4.3 %opening.1 = (f32[2,3072]{1,0:T(2,128)S(1)}, f32[2,1536]{1,0:T(2,128)S(1)}, f32[128,1536]{1,0:T(8,128)S(1)}, bf16[128,1152]{1,0:T(8,128)(2,1)S(1)}, bf16[128,115...) custom-call(s32[5]{0:T(128)S(1)} %pad_add_fusion.place_ref, ...), custom_call_target="tpu_custom_call" | custom-call | flops 10000000000 | bytes 10000000 | tf_op jit(solution)/shard_map/opening/pallas_call | solution.py:231
  25.3 2.7 %collective-permute-start.5 = (bf16[128,1152]{1,0:T(8,128)(2,1)S(1)}, bf16[128,1152]{1,0:T(8,128)(2,1)S(1)}, u32[]{:S(2)}, u32[]{:S(2)}) collective-permute-start(bf16[128,1152]{1,0:T(8,128)(2,1)S(1)} %get-tuple-element.45.refs_2_.refs_6_.refs_10_), channel_id=1, source_target_pairs={{0,4},{1,5},{2,6},{3,7},{4,0},{5,1},{6,2},{7,3},{8,12},{9,13},{10,... | collective-permute-start | bytes 884744 | tf_op jit(solution)/shard_map/ppermute | solution.py:564
  28.9 2.3 %collective-permute-start.7 = (bf16[128,1152]{1,0:T(8,128)(2,1)S(1)}, bf16[128,1152]{1,0:T(8,128)(2,1)S(1)}, u32[]{:S(2)}, u32[]{:S(2)}) collective-permute-start(bf16[128,1152]{1,0:T(8,128)(2,1)S(1)} %get-tuple-element.47.refs_3_.refs_7_.refs_11_), channel_id=1, source_target_pairs={{0,6},{1,7},{2,0},{3,1},{4,2},{5,3},{6,4},{7,5},{8,14},{9,15},{10,... | collective-permute-start | bytes 884744 | tf_op jit(solution)/shard_map/ppermute | solution.py:564
  31.2 2.3 %aside.1 = (f32[2,1536]{1,0:T(2,128)S(1)}, f32[16,512]{1,0:T(8,128)S(1)}) custom-call(s32[5]{0:T(128)S(1)} %pad_add_fusion.place_ref, s32[16]{0:T(128)S(1)} %copy-done.1, f32[256,4608]{1,0:T(8,128)} %w_mod_ref.3, f32[128,1536]{1,0:T(8,128)S(1)} %get-tuple-element.49.token_ref.refs_12_.mixed_ref), custom_call_target="tpu_custom_call" | custom-call | flops 100000000 | bytes 100000 | tf_op jit(solution)/shard_map/aside/pallas_call | solution.py:282
  34.4 2.5 %collective-permute-done.5.refs_0_.refs_1_ = bf16[128,1152]{1,0:T(8,128)(2,1)S(1)} collective-permute-done((bf16[128,1152]{1,0:T(8,128)(2,1)S(1)}, bf16[128,1152]{1,0:T(8,128)(2,1)S(1)}, u32[]{:S(2)}, u32[]{:S(2)}) %collective-permute-start.5) | collective-permute-done | bytes 294944 | tf_op jit(solution)/shard_map/ppermute | solution.py:564
  36.8 4.3 %collective-permute-done.6.refs_1_.refs_2_ = bf16[128,1152]{1,0:T(8,128)(2,1)S(1)} collective-permute-done((bf16[128,1152]{1,0:T(8,128)(2,1)S(1)}, bf16[128,1152]{1,0:T(8,128)(2,1)S(1)}, u32[]{:S(2)}, u32[]{:S(2)}) %collective-permute-start.6) | collective-permute-done | bytes 294944 | tf_op jit(solution)/shard_map/ppermute | solution.py:564
  41.5 3.4 %collective-permute-start.19 = (bf16[512,768]{1,0:T(8,128)(2,1)S(1)}, bf16[512,768]{1,0:T(8,128)(2,1)S(1)}, u32[]{:S(2)}, u32[]{:S(2)}) collective-permute-start(bf16[512,768]{1,0:T(8,128)(2,1)S(1)} %stack.19.token_ref.refs_2_.refs_1_), channel_id=1, source_target_pairs={{0,8},{1,9},{2,10},{3,11},{4,12},{5,13},{6,14},{7,15},{8,0},{9,1},... | collective-permute-start | bytes 2359304 | tf_op jit(solution)/shard_map/ppermute | solution.py:585
  44.9 2.5 %attend.6 = (bf16[128,512]{1,0:T(8,128)(2,1)S(1)}, bf16[128,512]{1,0:T(8,128)(2,1)S(1)}) custom-call(bf16[512,768]{1,0:T(8,128)(2,1)S(1)} %stack.19.token_ref.refs_2_.refs_1_, bf16[128,1152]{1,0:T(8,128)(2,1)S(1)} %collective-permute-done.5.refs_0_.refs_1_, bf16[128,1152]{1,0:T(8,128)(2,1)S(1)} %collective-permute-done.6.refs_1_.refs_2_, ...), custom_call_target="tpu_custom_call" | custom-call | flops 4000000000 | bytes 4000000 | tf_op jit(solution)/shard_map/attend/pallas_call | solution.py:461
  48.6 1.9 %collective-permute-start.13 = (bf16[128,512]{1,0:T(8,128)(2,1)S(1)}, bf16[128,512]{1,0:T(8,128)(2,1)S(1)}, u32[]{:S(2)}, u32[]{:S(2)}) collective-permute-start(bf16[128,512]{1,0:T(8,128)(2,1)S(1)} %get-tuple-element.54), channel_id=1, source_target_pairs={{0,6},{1,7},{2,0},{3,1},{4,2},{5,3},{6,4},{7,5},{8,14},{9,15},{10,... | collective-permute-start | bytes 393224 | tf_op jit(solution)/shard_map/ppermute | solution.py:564
  50.6 1.5 %attend.7.token_ref = bf16[128,512]{1,0:T(8,128)(2,1)S(1)} custom-call(bf16[128,512]{1,0:T(8,128)(2,1)S(1)} %get-tuple-element.52.token_ref, bf16[128,1152]{1,0:T(8,128)(2,1)S(1)} %collective-permute-done.7.refs_2_.refs_3_.refs_0_, bf16[512,768]{1,0:T(8,128)(2,1)S(1)} %stack.18.token_ref.refs_2_.refs_1_, ...), custom_call_target="tpu_custom_call" | custom-call | flops 4000000000 | bytes 4000000 | tf_op jit(solution)/shard_map/attend/pallas_call | solution.py:461
  52.3 1.5 %attend.8.a0 = bf16[128,512]{1,0:T(8,128)(2,1)S(1)} custom-call(bf16[128,512]{1,0:T(8,128)(2,1)S(1)} %attend.7.token_ref, bf16[128,1152]{1,0:T(8,128)(2,1)S(1)} %get-tuple-element.48.refs_0_.refs_4_.refs_8_.refs_3_, bf16[512,768]{1,0:T(8,128)(2,1)S(1)} %stack.18.token_ref.refs_2_.refs_1_, bf16[512,768]{1,0:T(8,128)(2,1)S(1)} %collective-permute-done.8.refs_3_.refs_2_, ...), custom_call_target="tpu_custom_call" | custom-call | flops 4000000000 | bytes 4000000 | tf_op jit(solution)/shard_map/attend/pallas_call | solution.py:461
  54.6 1.5 %collective-permute-done.13.a1 = bf16[128,512]{1,0:T(8,128)(2,1)S(1)} collective-permute-done((bf16[128,512]{1,0:T(8,128)(2,1)S(1)}, bf16[128,512]{1,0:T(8,128)(2,1)S(1)}, u32[]{:S(2)}, u32[]{:S(2)}) %collective-permute-start.13) | collective-permute-done | bytes 131104 | tf_op jit(solution)/shard_map/ppermute | solution.py:564
  56.1 1.6 %early_output.2.early_ref = f32[128,1536]{1,0:T(8,128)S(1)} custom-call(s32[5]{0:T(128)S(1)} %pad_add_fusion.place_ref, bf16[128,512]{1,0:T(8,128)(2,1)S(1)} %collective-permute-done.12.a2, bf16[128,512]{1,0:T(8,128)(2,1)S(1)} %collective-permute-done.13.a1, bf16[128,512]{1,0:T(8,128)(2,1)S(1)} %attend.8.a0, bf16[1536,1536]{1,0:T(8,128)(2,1)S(1)} %bitcast.6, ...), custom_call_target="tpu_custom_call" | custom-call | flops 3000000000 | bytes 3000000 | tf_op jit(solution)/shard_map/early_output/pallas_call | solution.py:498
  60.4 2.4 %collective-permute-start.18 = (bf16[512,768]{1,0:T(8,128)(2,1)S(1)}, bf16[512,768]{1,0:T(8,128)(2,1)S(1)}, u32[]{:S(2)}, u32[]{:S(2)}) collective-permute-start(bf16[512,768]{1,0:T(8,128)(2,1)S(1)} %stack.19.token_ref.refs_2_.refs_1_), channel_id=1, source_target_pairs={{0,1},{1,0},{2,3},{3,2},{4,5},{5,4},{6,7},{7,6},{8,9},{9,8},{10,11... | collective-permute-start | bytes 2359304 | tf_op jit(solution)/shard_map/ppermute | solution.py:586
  62.8 2.0 %next_queries.1 = (f32[128,1536]{1,0:T(8,128)S(1)}, bf16[128,1536]{1,0:T(8,128)(2,1)S(1)}, bf16[128,384]{1,0:T(8,128)(2,1)S(1)}, bf16[128,384]{1,0:T(8,128)(2,1)...) custom-call(s32[5]{0:T(128)S(1)} %pad_add_fusion.place_ref, ...), custom_call_target="tpu_custom_call" | custom-call | flops 100000000 | bytes 100000 | tf_op jit(solution)/shard_map/next_queries/pallas_call | solution.py:303
  64.8 5.0 %collective-permute-start.20 = (bf16[512,768]{1,0:T(8,128)(2,1)S(1)}, bf16[512,768]{1,0:T(8,128)(2,1)S(1)}, u32[]{:S(2)}, u32[]{:S(2)}) collective-permute-start(bf16[512,768]{1,0:T(8,128)(2,1)S(1)} %hold.3.refs_4_.refs_3_), channel_id=1, source_target_pairs={{0,1},{1,0},{2,3},{3,2},{4,5},{5,4},{6,7},{7,6},{8,9},{9,8},{10,11... | collective-permute-start | bytes 2359304 | tf_op jit(solution)/shard_map/ppermute | solution.py:603
  69.8 1.6 %collective-permute-start.16 = (bf16[128,384]{1,0:T(8,128)(2,1)S(1)}, bf16[128,384]{1,0:T(8,128)(2,1)S(1)}, u32[]{:S(2)}, u32[]{:S(2)}) collective-permute-start(bf16[128,384]{1,0:T(8,128)(2,1)S(1)} %get-tuple-element.63.refs_2_), channel_id=1, source_target_pairs={{0,4},{1,5},{2,6},{3,7},{4,0},{5,1},{6,2},{7,3},{8,12},{9,13},{10,... | collective-permute-start | bytes 294920 | tf_op jit(solution)/shard_map/ppermute | solution.py:564
  71.4 4.8 %collective-permute-start.17 = (bf16[128,384]{1,0:T(8,128)(2,1)S(1)}, bf16[128,384]{1,0:T(8,128)(2,1)S(1)}, u32[]{:S(2)}, u32[]{:S(2)}) collective-permute-start(bf16[128,384]{1,0:T(8,128)(2,1)S(1)} %get-tuple-element.64.refs_1_), channel_id=1, source_target_pairs={{0,2},{1,3},{2,4},{3,5},{4,6},{5,7},{6,0},{7,1},{8,10},{9,11},{10,... | collective-permute-start | bytes 294920 | tf_op jit(solution)/shard_map/ppermute | solution.py:564
  76.2 2.7 %last_keys.1 = (bf16[128,768]{1,0:T(8,128)(2,1)S(1)}, bf16[128,768]{1,0:T(8,128)(2,1)S(1)}, bf16[128,768]{1,0:T(8,128)(2,1)S(1)}, bf16[128,768]{1,0:T(8,128)(2,1)S(1)}, bf16[128,3072]{1,0:T(8,128)(2,1)}) custom-call(s32[5]{0:T(128)S(1)} %pad_add_fusion.place_ref, bf16[128,1536]{1,0:T(8,128)(2,1)S(1)} %get-tuple-element.61.normed_ref.token_ref.refs_12_, ...), custom_call_target="tpu_custom_call" | custom-call | flops 100000000 | bytes 100000 | tf_op jit(solution)/shard_map/last_keys/pallas_call | solution.py:381
  79.8 2.4 %attend.9 = (bf16[128,512]{1,0:T(8,128)(2,1)S(1)}, bf16[128,512]{1,0:T(8,128)(2,1)S(1)}) custom-call(bf16[128,768]{1,0:T(8,128)(2,1)S(1)} %get-tuple-element.62.token_ref.refs_5_.refs_9_, bf16[128,384]{1,0:T(8,128)(2,1)S(1)} %collective-permute-done.16.refs_0_, bf16[128,384]{1,0:T(8,128)(2,1)S(1)} %collective-permute-done.17.refs_1_, ...), custom_call_target="tpu_custom_call" | custom-call | flops 4000000000 | bytes 4000000 | tf_op jit(solution)/shard_map/attend/pallas_call | solution.py:461
  82.3 2.4 %collective-permute-start.23 = (bf16[128,512]{1,0:T(8,128)(2,1)S(1)}, bf16[128,512]{1,0:T(8,128)(2,1)S(1)}, u32[]{:S(2)}, u32[]{:S(2)}) collective-permute-start(bf16[128,512]{1,0:T(8,128)(2,1)S(1)} %get-tuple-element.66.token_ref), channel_id=1, source_target_pairs={{0,4},{1,5},{2,6},{3,7},{4,0},{5,1},{6,2},{7,3},{8,12},{9,13},{10,... | collective-permute-start | bytes 393224 | tf_op jit(solution)/shard_map/ppermute | solution.py:564
  84.6 2.6 %collective-permute-start.24 = (bf16[128,512]{1,0:T(8,128)(2,1)S(1)}, bf16[128,512]{1,0:T(8,128)(2,1)S(1)}, u32[]{:S(2)}, u32[]{:S(2)}) collective-permute-start(bf16[128,512]{1,0:T(8,128)(2,1)S(1)} %get-tuple-element.73), channel_id=1, source_target_pairs={{0,6},{1,7},{2,0},{3,1},{4,2},{5,3},{6,4},{7,5},{8,14},{9,15},{10,... | collective-permute-start | bytes 393224 | tf_op jit(solution)/shard_map/ppermute | solution.py:564
  88.9 1.5 %attend.11.a0 = bf16[128,512]{1,0:T(8,128)(2,1)S(1)} custom-call(bf16[128,512]{1,0:T(8,128)(2,1)S(1)} %attend.10.token_ref, bf16[128,384]{1,0:T(8,128)(2,1)S(1)} %get-tuple-element.65.refs_1_.refs_0_, bf16[512,768]{1,0:T(8,128)(2,1)S(1)} %stack.19.token_ref.refs_2_.refs_1_, bf16[512,768]{1,0:T(8,128)(2,1)S(1)} %collective-permute-done.18.refs_3_.refs_2_, ...), custom_call_target="tpu_custom_call" | custom-call | flops 4000000000 | bytes 4000000 | tf_op jit(solution)/shard_map/attend/pallas_call | solution.py:461
  90.7 1.6 %early_output.3.early_ref = f32[128,1536]{1,0:T(8,128)S(1)} custom-call(s32[5]{0:T(128)S(1)} %pad_add_fusion.place_ref, bf16[128,512]{1,0:T(8,128)(2,1)S(1)} %collective-permute-done.23.a2, bf16[128,512]{1,0:T(8,128)(2,1)S(1)} %collective-permute-done.24.a1, bf16[128,512]{1,0:T(8,128)(2,1)S(1)} %attend.11.a0, bf16[1536,1536]{1,0:T(8,128)(2,1)S(1)} %bitcast.6, ...), custom_call_target="tpu_custom_call" | custom-call | flops 3000000000 | bytes 3000000 | tf_op jit(solution)/shard_map/early_output/pallas_call | solution.py:498
  92.3 2.7 %collective-permute-done.22.away = bf16[128,512]{1,0:T(8,128)(2,1)S(1)} collective-permute-done((bf16[128,512]{1,0:T(8,128)(2,1)S(1)}, bf16[128,512]{1,0:T(8,128)(2,1)S(1)}, u32[]{:S(2)}, u32[]{:S(2)}) %collective-permute-start.22) | collective-permute-done | bytes 131104 | tf_op jit(solution)/shard_map/ppermute | solution.py:564
  95.0 1.8 %last_output.1 = bf16[128,1536]{1,0:T(8,128)(2,1)} custom-call(s32[5]{0:T(128)S(1)} %pad_add_fusion.place_ref, bf16[128,512]{1,0:T(8,128)(2,1)S(1)} %collective-permute-done.22.away, bf16[1536,1536]{1,0:T(8,128)(2,1)S(1)} %bitcast.6, f32[128,1536]{1,0:T(8,128)S(1)} %get-tuple-element.71.summed_ref, f32[128,512]{1,0:T(8,128)S(1)} %get-tuple-element.72.lse_ref, ...), custom_call_target="tpu_custom_call" | custom-call | flops 100000000 | bytes 100000 | tf_op jit(solution)/shard_map/last_output/pallas_call | solution.py:554
  (63 shorter events, 12.7 us)
Async XLA Ops:
  1.4 19.5 %slice-start = ((s8[14155776]{0:T(1024)(128)(4,1)}), s8[4194304]{0:T(1024)(128)(4,1)S(1)}, s32[]{:S(2)}) async-start(s8[14155776]{0:T(1024)(128)(4,1)} %bitcast.3), calls=%async_computation | async-start | bytes 8388608
  1.4 19.5 %slice-start.1 = ((s8[14155776]{0:T(1024)(128)(4,1)}), s8[4194304]{0:T(1024)(128)(4,1)S(1)}, s32[]{:S(2)}) async-start(s8[14155776]{0:T(1024)(128)(4,1)} %bitcast.3), calls=%async_computation.1 | async-start | bytes 8388608
  1.4 19.5 %slice-start.6 = ((s8[4718592]{0:T(1024)(128)(4,1)}), s8[4194304]{0:T(1024)(128)(4,1)S(1)}, s32[]{:S(2)}) async-start(s8[4718592]{0:T(1024)(128)(4,1)} %bitcast.7), calls=%async_computation.6 | async-start | bytes 8388608
  3.7 9.8 %collective-permute-start.2 = (bf16[128,768]{1,0:T(8,128)(2,1)S(1)}, bf16[128,768]{1,0:T(8,128)(2,1)S(1)}, u32[]{:S(2)}, u32[]{:S(2)}) collective-permute-start(bf16[128,768]{1,0:T(8,128)(2,1)S(1)} %get-tuple-element.41), channel_id=1, source_target_pairs={{0,4},{1,5},{2,6},{3,7},{4,0},{5,1},{6,2},{7,3},{8,12},{9,13},{10,... | collective-permute-start | bytes 589832 | tf_op jit(solution)/shard_map/ppermute | solution.py:564
  7.7 9.5 %collective-permute-start.3 = (bf16[128,768]{1,0:T(8,128)(2,1)S(1)}, bf16[128,768]{1,0:T(8,128)(2,1)S(1)}, u32[]{:S(2)}, u32[]{:S(2)}) collective-permute-start(bf16[128,768]{1,0:T(8,128)(2,1)S(1)} %get-tuple-element.42), channel_id=1, source_target_pairs={{0,2},{1,3},{2,4},{3,5},{4,6},{5,7},{6,0},{7,1},{8,10},{9,11},{10,... | collective-permute-start | bytes 589832 | tf_op jit(solution)/shard_map/ppermute | solution.py:564
  8.7 12.2 %slice-start.2 = ((s8[14155776]{0:T(1024)(128)(4,1)}), s8[4194304]{0:T(1024)(128)(4,1)S(1)}, s32[]{:S(2)}) async-start(s8[14155776]{0:T(1024)(128)(4,1)} %bitcast.3), calls=%async_computation.2 | async-start | bytes 8388608
  8.7 12.2 %slice-start.7 = ((s8[4718592]{0:T(1024)(128)(4,1)}), s8[524288]{0:T(1024)(128)(4,1)S(1)}, s32[]{:S(2)}) async-start(s8[4718592]{0:T(1024)(128)(4,1)} %bitcast.7), calls=%async_computation.7 | async-start | bytes 1048576
  8.8 8.8 %collective-permute-start.4 = (bf16[128,768]{1,0:T(8,128)(2,1)S(1)}, bf16[128,768]{1,0:T(8,128)(2,1)S(1)}, u32[]{:S(2)}, u32[]{:S(2)}) collective-permute-start(bf16[128,768]{1,0:T(8,128)(2,1)S(1)} %get-tuple-element.43), channel_id=1, source_target_pairs={{0,6},{1,7},{2,0},{3,1},{4,2},{5,3},{6,4},{7,5},{8,14},{9,15},{10,... | collective-permute-start | bytes 589832 | tf_op jit(solution)/shard_map/ppermute | solution.py:564
  11.0 10.0 %collective-permute-start = (bf16[80,1536]{1,0:T(8,128)(2,1)S(1)}, bf16[80,1536]{1,0:T(8,128)(2,1)S(1)}, u32[]{:S(2)}, u32[]{:S(2)}) collective-permute-start(bf16[80,1536]{1,0:T(8,128)(2,1)S(1)} %get-tuple-element.39), channel_id=1, source_target_pairs={{0,1},{1,0},{2,3},{3,2},{4,5},{5,4},{6,7},{7,6},{8,9},{9,8},{10,11... | collective-permute-start | bytes 737288 | tf_op jit(solution)/shard_map/ppermute | solution.py:573
  11.0 10.0 %collective-permute-start.1 = (bf16[80,1536]{1,0:T(8,128)(2,1)S(1)}, bf16[80,1536]{1,0:T(8,128)(2,1)S(1)}, u32[]{:S(2)}, u32[]{:S(2)}) collective-permute-start(bf16[80,1536]{1,0:T(8,128)(2,1)S(1)} %get-tuple-element.40), channel_id=1, source_target_pairs={{1,2},{3,4},{5,6},{7,8},{9,10},{11,12},{13,14},{2,1},{4,3},{6,5},{... | collective-permute-start | bytes 737288 | tf_op jit(solution)/shard_map/ppermute | solution.py:572
  17.6 13.6 %copy-start.1 = (s32[16]{0:T(128)S(1)}, s32[16]{0:T(128)}, u32[]{:S(2)}) copy-start(s32[16]{0:T(128)} %counts_ref.1) | copy-start | bytes 196
  17.6 23.8 %collective-permute-start.9 = (bf16[512,768]{1,0:T(8,128)(2,1)S(1)}, bf16[512,768]{1,0:T(8,128)(2,1)S(1)}, u32[]{:S(2)}, u32[]{:S(2)}) collective-permute-start(bf16[512,768]{1,0:T(8,128)(2,1)S(1)} %stack.18.token_ref.refs_2_.refs_1_), channel_id=1, source_target_pairs={{0,8},{1,9},{2,10},{3,11},{4,12},{5,13},{6,14},{7,15},{8,0},{9,1},... | collective-permute-start | bytes 2359304 | tf_op jit(solution)/shard_map/ppermute | solution.py:576
  25.3 11.6 %collective-permute-start.5 = (bf16[128,1152]{1,0:T(8,128)(2,1)S(1)}, bf16[128,1152]{1,0:T(8,128)(2,1)S(1)}, u32[]{:S(2)}, u32[]{:S(2)}) collective-permute-start(bf16[128,1152]{1,0:T(8,128)(2,1)S(1)} %get-tuple-element.45.refs_2_.refs_6_.refs_10_), channel_id=1, source_target_pairs={{0,4},{1,5},{2,6},{3,7},{4,0},{5,1},{6,2},{7,3},{8,12},{9,13},{10,... | collective-permute-start | bytes 884744 | tf_op jit(solution)/shard_map/ppermute | solution.py:564
  28.0 13.2 %collective-permute-start.6 = (bf16[128,1152]{1,0:T(8,128)(2,1)S(1)}, bf16[128,1152]{1,0:T(8,128)(2,1)S(1)}, u32[]{:S(2)}, u32[]{:S(2)}) collective-permute-start(bf16[128,1152]{1,0:T(8,128)(2,1)S(1)} %get-tuple-element.46.refs_1_.refs_5_.refs_9_), channel_id=1, source_target_pairs={{0,2},{1,3},{2,4},{3,5},{4,6},{5,7},{6,0},{7,1},{8,10},{9,11},{10,... | collective-permute-start | bytes 884744 | tf_op jit(solution)/shard_map/ppermute | solution.py:564
  28.9 12.6 %collective-permute-start.7 = (bf16[128,1152]{1,0:T(8,128)(2,1)S(1)}, bf16[128,1152]{1,0:T(8,128)(2,1)S(1)}, u32[]{:S(2)}, u32[]{:S(2)}) collective-permute-start(bf16[128,1152]{1,0:T(8,128)(2,1)S(1)} %get-tuple-element.47.refs_3_.refs_7_.refs_11_), channel_id=1, source_target_pairs={{0,6},{1,7},{2,0},{3,1},{4,2},{5,3},{6,4},{7,5},{8,14},{9,15},{10,... | collective-permute-start | bytes 884744 | tf_op jit(solution)/shard_map/ppermute | solution.py:564
  31.2 13.7 %collective-permute-start.8 = (bf16[512,768]{1,0:T(8,128)(2,1)S(1)}, bf16[512,768]{1,0:T(8,128)(2,1)S(1)}, u32[]{:S(2)}, u32[]{:S(2)}) collective-permute-start(bf16[512,768]{1,0:T(8,128)(2,1)S(1)} %stack.18.token_ref.refs_2_.refs_1_), channel_id=1, source_target_pairs={{0,1},{1,0},{2,3},{3,2},{4,5},{5,4},{6,7},{7,6},{8,9},{9,8},{10,11... | collective-permute-start | bytes 2359304 | tf_op jit(solution)/shard_map/ppermute | solution.py:577
  41.5 3.4 %collective-permute-start.10 = (bf16[512,768]{1,0:T(8,128)(2,1)S(1)}, bf16[512,768]{1,0:T(8,128)(2,1)S(1)}, u32[]{:S(2)}, u32[]{:S(2)}) collective-permute-start(bf16[512,768]{1,0:T(8,128)(2,1)S(1)} %hold.2.refs_4_.refs_3_), channel_id=1, source_target_pairs={{0,1},{1,0},{2,3},{3,2},{4,5},{5,4},{6,7},{7,6},{8,9},{9,8},{10,11... | collective-permute-start | bytes 2359304 | tf_op jit(solution)/shard_map/ppermute | solution.py:588
  41.5 23.3 %collective-permute-start.19 = (bf16[512,768]{1,0:T(8,128)(2,1)S(1)}, bf16[512,768]{1,0:T(8,128)(2,1)S(1)}, u32[]{:S(2)}, u32[]{:S(2)}) collective-permute-start(bf16[512,768]{1,0:T(8,128)(2,1)S(1)} %stack.19.token_ref.refs_2_.refs_1_), channel_id=1, source_target_pairs={{0,8},{1,9},{2,10},{3,11},{4,12},{5,13},{6,14},{7,15},{8,0},{9,1},... | collective-permute-start | bytes 2359304 | tf_op jit(solution)/shard_map/ppermute | solution.py:585
  47.4 7.2 %collective-permute-start.12 = (bf16[128,512]{1,0:T(8,128)(2,1)S(1)}, bf16[128,512]{1,0:T(8,128)(2,1)S(1)}, u32[]{:S(2)}, u32[]{:S(2)}) collective-permute-start(bf16[128,512]{1,0:T(8,128)(2,1)S(1)} %get-tuple-element.52.token_ref), channel_id=1, source_target_pairs={{0,4},{1,5},{2,6},{3,7},{4,0},{5,1},{6,2},{7,3},{8,12},{9,13},{10,... | collective-permute-start | bytes 393224 | tf_op jit(solution)/shard_map/ppermute | solution.py:564
  48.6 7.5 %collective-permute-start.13 = (bf16[128,512]{1,0:T(8,128)(2,1)S(1)}, bf16[128,512]{1,0:T(8,128)(2,1)S(1)}, u32[]{:S(2)}, u32[]{:S(2)}) collective-permute-start(bf16[128,512]{1,0:T(8,128)(2,1)S(1)} %get-tuple-element.54), channel_id=1, source_target_pairs={{0,6},{1,7},{2,0},{3,1},{4,2},{5,3},{6,4},{7,5},{8,14},{9,15},{10,... | collective-permute-start | bytes 393224 | tf_op jit(solution)/shard_map/ppermute | solution.py:564
  50.6 5.5 %slice-start.4 = ((s8[4718592]{0:T(1024)(128)(4,1)}), s8[4194304]{0:T(1024)(128)(4,1)S(1)}, s32[]{:S(2)}) async-start(s8[4718592]{0:T(1024)(128)(4,1)} %bitcast.5), calls=%async_computation.4 | async-start | bytes 8388608
  52.1 6.3 %collective-permute-start.11 = (bf16[128,512]{1,0:T(8,128)(2,1)S(1)}, bf16[128,512]{1,0:T(8,128)(2,1)S(1)}, u32[]{:S(2)}, u32[]{:S(2)}) collective-permute-start(bf16[128,512]{1,0:T(8,128)(2,1)S(1)} %attend.7.token_ref), channel_id=1, source_target_pairs={{0,2},{1,3},{2,4},{3,5},{4,6},{5,7},{6,0},{7,1},{8,10},{9,11},{10,... | collective-permute-start | bytes 393224 | tf_op jit(solution)/shard_map/ppermute | solution.py:564
  59.6 3.2 %collective-permute-start.14 = (bf16[80,1536]{1,0:T(8,128)(2,1)S(1)}, bf16[80,1536]{1,0:T(8,128)(2,1)S(1)}, u32[]{:S(2)}, u32[]{:S(2)}) collective-permute-start(bf16[80,1536]{1,0:T(8,128)(2,1)S(1)} %get-tuple-element.57), channel_id=1, source_target_pairs={{0,1},{1,0},{2,3},{3,2},{4,5},{5,4},{6,7},{7,6},{8,9},{9,8},{10,11... | collective-permute-start | bytes 737288 | tf_op jit(solution)/shard_map/ppermute | solution.py:597
  59.7 3.1 %collective-permute-start.15 = (bf16[80,1536]{1,0:T(8,128)(2,1)S(1)}, bf16[80,1536]{1,0:T(8,128)(2,1)S(1)}, u32[]{:S(2)}, u32[]{:S(2)}) collective-permute-start(bf16[80,1536]{1,0:T(8,128)(2,1)S(1)} %get-tuple-element.58), channel_id=1, source_target_pairs={{1,2},{3,4},{5,6},{7,8},{9,10},{11,12},{13,14},{2,1},{4,3},{6,5},{... | collective-permute-start | bytes 737288 | tf_op jit(solution)/shard_map/ppermute | solution.py:596
  60.4 19.4 %collective-permute-start.18 = (bf16[512,768]{1,0:T(8,128)(2,1)S(1)}, bf16[512,768]{1,0:T(8,128)(2,1)S(1)}, u32[]{:S(2)}, u32[]{:S(2)}) collective-permute-start(bf16[512,768]{1,0:T(8,128)(2,1)S(1)} %stack.19.token_ref.refs_2_.refs_1_), channel_id=1, source_target_pairs={{0,1},{1,0},{2,3},{3,2},{4,5},{5,4},{6,7},{7,6},{8,9},{9,8},{10,11... | collective-permute-start | bytes 2359304 | tf_op jit(solution)/shard_map/ppermute | solution.py:586
  64.8 15.0 %collective-permute-start.20 = (bf16[512,768]{1,0:T(8,128)(2,1)S(1)}, bf16[512,768]{1,0:T(8,128)(2,1)S(1)}, u32[]{:S(2)}, u32[]{:S(2)}) collective-permute-start(bf16[512,768]{1,0:T(8,128)(2,1)S(1)} %hold.3.refs_4_.refs_3_), channel_id=1, source_target_pairs={{0,1},{1,0},{2,3},{3,2},{4,5},{5,4},{6,7},{7,6},{8,9},{9,8},{10,11... | collective-permute-start | bytes 2359304 | tf_op jit(solution)/shard_map/ppermute | solution.py:603
  69.8 10.0 %collective-permute-start.16 = (bf16[128,384]{1,0:T(8,128)(2,1)S(1)}, bf16[128,384]{1,0:T(8,128)(2,1)S(1)}, u32[]{:S(2)}, u32[]{:S(2)}) collective-permute-start(bf16[128,384]{1,0:T(8,128)(2,1)S(1)} %get-tuple-element.63.refs_2_), channel_id=1, source_target_pairs={{0,4},{1,5},{2,6},{3,7},{4,0},{5,1},{6,2},{7,3},{8,12},{9,13},{10,... | collective-permute-start | bytes 294920 | tf_op jit(solution)/shard_map/ppermute | solution.py:564
  71.4 8.4 %collective-permute-start.17 = (bf16[128,384]{1,0:T(8,128)(2,1)S(1)}, bf16[128,384]{1,0:T(8,128)(2,1)S(1)}, u32[]{:S(2)}, u32[]{:S(2)}) collective-permute-start(bf16[128,384]{1,0:T(8,128)(2,1)S(1)} %get-tuple-element.64.refs_1_), channel_id=1, source_target_pairs={{0,2},{1,3},{2,4},{3,5},{4,6},{5,7},{6,0},{7,1},{8,10},{9,11},{10,... | collective-permute-start | bytes 294920 | tf_op jit(solution)/shard_map/ppermute | solution.py:564
  76.2 11.1 %collective-permute-start.21 = (bf16[128,384]{1,0:T(8,128)(2,1)S(1)}, bf16[128,384]{1,0:T(8,128)(2,1)S(1)}, u32[]{:S(2)}, u32[]{:S(2)}) collective-permute-start(bf16[128,384]{1,0:T(8,128)(2,1)S(1)} %get-tuple-element.67.refs_3_), channel_id=1, source_target_pairs={{0,6},{1,7},{2,0},{3,1},{4,2},{5,3},{6,4},{7,5},{8,14},{9,15},{10,... | collective-permute-start | bytes 294920 | tf_op jit(solution)/shard_map/ppermute | solution.py:564
  82.3 8.1 %collective-permute-start.23 = (bf16[128,512]{1,0:T(8,128)(2,1)S(1)}, bf16[128,512]{1,0:T(8,128)(2,1)S(1)}, u32[]{:S(2)}, u32[]{:S(2)}) collective-permute-start(bf16[128,512]{1,0:T(8,128)(2,1)S(1)} %get-tuple-element.66.token_ref), channel_id=1, source_target_pairs={{0,4},{1,5},{2,6},{3,7},{4,0},{5,1},{6,2},{7,3},{8,12},{9,13},{10,... | collective-permute-start | bytes 393224 | tf_op jit(solution)/shard_map/ppermute | solution.py:564
  84.6 6.1 %collective-permute-start.24 = (bf16[128,512]{1,0:T(8,128)(2,1)S(1)}, bf16[128,512]{1,0:T(8,128)(2,1)S(1)}, u32[]{:S(2)}, u32[]{:S(2)}) collective-permute-start(bf16[128,512]{1,0:T(8,128)(2,1)S(1)} %get-tuple-element.73), channel_id=1, source_target_pairs={{0,6},{1,7},{2,0},{3,1},{4,2},{5,3},{6,4},{7,5},{8,14},{9,15},{10,... | collective-permute-start | bytes 393224 | tf_op jit(solution)/shard_map/ppermute | solution.py:564
  88.8 6.2 %collective-permute-start.22 = (bf16[128,512]{1,0:T(8,128)(2,1)S(1)}, bf16[128,512]{1,0:T(8,128)(2,1)S(1)}, u32[]{:S(2)}, u32[]{:S(2)}) collective-permute-start(bf16[128,512]{1,0:T(8,128)(2,1)S(1)} %attend.10.token_ref), channel_id=1, source_target_pairs={{0,2},{1,3},{2,4},{3,5},{4,6},{5,7},{6,0},{7,1},{8,10},{9,11},{10,... | collective-permute-start | bytes 393224 | tf_op jit(solution)/shard_map/ppermute | solution.py:564
  (3 other events, 12.5 us)

commit v8 on v6

--- a/solution.py
+++ b/solution.py
@@ -18,6 +18,7 @@
 WIDE = GROUP * HEAD
 RING = 4
 LOG2E = math.log2(math.e)
+EXTRA = 16
 ORDER = (2, 1, 3, 0)
 
 epsilon = 1e-06
@@ -445,7 +446,7 @@
                 probs = jnp.exp2(scores[a] - highest).astype(bf16)
                 both += jnp.dot(probs, values[a], preferred_element_type=f32)
             total = both[:, HEAD:]
-            outs[i][:, here] = (both[:, :HEAD] / total).astype(bf16)
+            outs[i][:SLAB, here] = (both[:, :HEAD] / total).astype(bf16)
             lse[i] = jnp.where(lanes == h, highest + jnp.log2(total), lse[i])
     for i in range(n):
         rest = lse[i]
@@ -454,7 +455,8 @@
             piece = rest.astype(bf16).astype(f32)
             rest = rest - piece
             packed += pltpu.roll(piece, part * GROUP, 1) if part else piece
-        outs[i][:, WIDE:] = packed.astype(bf16)
+        outs[i][SLAB:, :HEAD] = packed.T[:EXTRA].astype(bf16)
+        outs[i][SLAB:, HEAD:] = jnp.zeros((EXTRA, WIDE - HEAD), bf16)
 
 
 def attend(queries, olds, bias, slots, token):
@@ -462,13 +464,14 @@
         functools.partial(attend_kernel, slots=slots),
         "attend",
         [ANY] + [VMEM] * (len(slots) + 5),
-        [((SLAB, WIDE + HEAD), bf16, VMEM)] * len(slots),
+        [((SLAB + EXTRA, WIDE), bf16, VMEM)] * len(slots),
         us=4,
     )(token, *[queries[k] for k in slots], *olds, bias)
 
 
 def merged(away, summed_ref, lse_ref, k):
-    pieces = away[:, WIDE:].astype(f32)
+    rows = away[SLAB:, :HEAD].astype(f32)
+    pieces = jnp.concatenate([rows, jnp.zeros((HEAD - EXTRA, HEAD), f32)], 0).T
     lse = (
         pieces + pltpu.roll(pieces, HEAD - GROUP, 1) + pltpu.roll(pieces, HEAD - 2 * GROUP, 1)
     )
@@ -478,7 +481,7 @@
         here = slice(k * WIDE + h * HEAD, k * WIDE + (h + 1) * HEAD)
         part = share[:, h : h + 1]
         heads.append(
-            part * away[:, h * HEAD : (h + 1) * HEAD].astype(f32)
+            part * away[:SLAB, h * HEAD : (h + 1) * HEAD].astype(f32)
             + (1.0 - part) * summed_ref[:, here]
         )
     return jnp.concatenate(heads, 1).astype(bf16)

time: 97.2 us -> 96.4 us (level)
  Pallas kernels: 32.4 us -> 33.4 us
  waiting for transfers between devices: 19.2 us -> 18.2 us
    ppermute x15, waiting for transfers between devices: 19.2 us -> 18.2 us  [sent(): return lax.ppermute(block, 'patch', ring(k % RING)) if k % RING else block]
  transfers between devices with their start and end apart: 25 -> 25, of which waited for: 11 -> 10; matrix products, arithmetic and copies ran while one was open for 0% -> 0% of each run, Pallas kernels for 29% -> 30%
where the time goes in v8:
time: 96.4 us; the launch traced here: 96.3 us
  starting transfers between devices  42.9 us (45%)
  Pallas kernels  33.4 us (35%)
  waiting for transfers between devices  18.2 us (19%)
  between operations  0.98 us (1%)
    ppermute x15, starting transfers between devices, sent(): return lax.ppermute(block, 'patch', ring(k % RING)) if k % RING else block  27.5 us
    ppermute x15, waiting for transfers between devices, sent(): return lax.ppermute(block, 'patch', ring(k % RING)) if k % RING else block  18.2 us
    pallas_call x6, Pallas kernels, attend(): call(functools.partial(attend_kernel, slots=slots), 'attend', [ANY] + [VM...  11.3 us
    ppermute x1, starting transfers between devices, shards(): olds = [new, new_core, new_y, lax.ppermute(new_y, 'patch', CORE)]  5.37 us
    pallas_call x1, Pallas kernels, opening(): call(open_kernel, 'opening', [SMEM, HBM, VMEM, VMEM] + [HBM] * 3 + [VMEM]...  4.3 us
    pallas_call x2, Pallas kernels, early_output(): call(early_output_kernel, 'early_output', [SMEM] + [VMEM] * 6, [((SLAB, D...  3.58 us
    ppermute x1, starting transfers between devices, shards(): old_y = lax.ppermute(old, 'patch', ACROSS)  3.27 us
    ppermute x1, starting transfers between devices, shards(): new_y = lax.ppermute(new, 'patch', ACROSS)  3.27 us
  transfers between devices with their start and end apart: 25, of which 10 were waited for; matrix products, arithmetic and copies ran while one was open for 0% of the time, Pallas kernels for 30%

profile of v8, /device:TPU:0, one launch (start us, length us, event | category | flops | bytes accessed | tf_op | source)
XLA Modules:
  0.0 96.3 jit_solution(1631903601778498583)
XLA Ops:
  1.4 2.3 %prepare.1 = (bf16[80,1536]{1,0:T(8,128)(2,1)S(1)}, bf16[80,1536]{1,0:T(8,128)(2,1)S(1)}, bf16[128,768]{1,0:T(8,128)(2,1)S(1)}, bf16[128,768]{1,0:T(8,128)(2,1)S...) custom-call(s32[5]{0:T(128)S(1)} %pad_add_fusion.place_ref, bf16[128,1536]{1,0:T(8,128)(2,1)} %latent_ref.3, ...), custom_call_target="tpu_custom_call" | custom-call | flops 8000000000 | bytes 8000000 | tf_op jit(solution)/shard_map/prepare/pallas_call | solution.py:120
  3.7 4.0 %collective-permute-start.2 = (bf16[128,768]{1,0:T(8,128)(2,1)S(1)}, bf16[128,768]{1,0:T(8,128)(2,1)S(1)}, u32[]{:S(2)}, u32[]{:S(2)}) collective-permute-start(bf16[128,768]{1,0:T(8,128)(2,1)S(1)} %get-tuple-element.41), channel_id=1, source_target_pairs={{0,4},{1,5},{2,6},{3,7},{4,0},{5,1},{6,2},{7,3},{8,12},{9,13},{10,... | collective-permute-start | bytes 589832 | tf_op jit(solution)/shard_map/ppermute | solution.py:535
  8.8 2.2 %collective-permute-start.4 = (bf16[128,768]{1,0:T(8,128)(2,1)S(1)}, bf16[128,768]{1,0:T(8,128)(2,1)S(1)}, u32[]{:S(2)}, u32[]{:S(2)}) collective-permute-start(bf16[128,768]{1,0:T(8,128)(2,1)S(1)} %get-tuple-element.43), channel_id=1, source_target_pairs={{0,6},{1,7},{2,0},{3,1},{4,2},{5,3},{6,4},{7,5},{8,14},{9,15},{10,... | collective-permute-start | bytes 589832 | tf_op jit(solution)/shard_map/ppermute | solution.py:535
  11.6 1.8 %collective-permute-done.2.refs_0_ = bf16[128,768]{1,0:T(8,128)(2,1)S(1)} collective-permute-done((bf16[128,768]{1,0:T(8,128)(2,1)S(1)}, bf16[128,768]{1,0:T(8,128)(2,1)S(1)}, u32[]{:S(2)}, u32[]{:S(2)}) %collective-permute-start.2) | collective-permute-done | bytes 196640 | tf_op jit(solution)/shard_map/ppermute | solution.py:535
  13.5 3.8 %collective-permute-done.3.refs_1_ = bf16[128,768]{1,0:T(8,128)(2,1)S(1)} collective-permute-done((bf16[128,768]{1,0:T(8,128)(2,1)S(1)}, bf16[128,768]{1,0:T(8,128)(2,1)S(1)}, u32[]{:S(2)}, u32[]{:S(2)}) %collective-permute-start.3) | collective-permute-done | bytes 196640 | tf_op jit(solution)/shard_map/ppermute | solution.py:535
  17.6 3.3 %collective-permute-start.9 = (bf16[512,768]{1,0:T(8,128)(2,1)S(1)}, bf16[512,768]{1,0:T(8,128)(2,1)S(1)}, u32[]{:S(2)}, u32[]{:S(2)}) collective-permute-start(bf16[512,768]{1,0:T(8,128)(2,1)S(1)} %stack.18.token_ref.refs_2_.refs_1_), channel_id=1, source_target_pairs={{0,8},{1,9},{2,10},{3,11},{4,12},{5,13},{6,14},{7,15},{8,0},{9,1},... | collective-permute-start | bytes 2359304 | tf_op jit(solution)/shard_map/ppermute | solution.py:547
  21.0 4.3 %opening.1 = (f32[2,3072]{1,0:T(2,128)S(1)}, f32[2,1536]{1,0:T(2,128)S(1)}, f32[128,1536]{1,0:T(8,128)S(1)}, bf16[128,1152]{1,0:T(8,128)(2,1)S(1)}, bf16[128,115...) custom-call(s32[5]{0:T(128)S(1)} %pad_add_fusion.place_ref, ...), custom_call_target="tpu_custom_call" | custom-call | flops 10000000000 | bytes 10000000 | tf_op jit(solution)/shard_map/opening/pallas_call | solution.py:232
  25.3 2.7 %collective-permute-start.5 = (bf16[128,1152]{1,0:T(8,128)(2,1)S(1)}, bf16[128,1152]{1,0:T(8,128)(2,1)S(1)}, u32[]{:S(2)}, u32[]{:S(2)}) collective-permute-start(bf16[128,1152]{1,0:T(8,128)(2,1)S(1)} %get-tuple-element.45.refs_2_.refs_6_.refs_10_), channel_id=1, source_target_pairs={{0,4},{1,5},{2,6},{3,7},{4,0},{5,1},{6,2},{7,3},{8,12},{9,13},{10,... | collective-permute-start | bytes 884744 | tf_op jit(solution)/shard_map/ppermute | solution.py:535
  28.9 2.3 %collective-permute-start.7 = (bf16[128,1152]{1,0:T(8,128)(2,1)S(1)}, bf16[128,1152]{1,0:T(8,128)(2,1)S(1)}, u32[]{:S(2)}, u32[]{:S(2)}) collective-permute-start(bf16[128,1152]{1,0:T(8,128)(2,1)S(1)} %get-tuple-element.47.refs_3_.refs_7_.refs_11_), channel_id=1, source_target_pairs={{0,6},{1,7},{2,0},{3,1},{4,2},{5,3},{6,4},{7,5},{8,14},{9,15},{10,... | collective-permute-start | bytes 884744 | tf_op jit(solution)/shard_map/ppermute | solution.py:535
  31.3 2.3 %aside.1 = (f32[2,1536]{1,0:T(2,128)S(1)}, f32[16,512]{1,0:T(8,128)S(1)}) custom-call(s32[5]{0:T(128)S(1)} %pad_add_fusion.place_ref, s32[16]{0:T(128)S(1)} %copy-done.1, f32[256,4608]{1,0:T(8,128)} %w_mod_ref.3, f32[128,1536]{1,0:T(8,128)S(1)} %get-tuple-element.49.token_ref.refs_12_.mixed_ref), custom_call_target="tpu_custom_call" | custom-call | flops 100000000 | bytes 100000 | tf_op jit(solution)/shard_map/aside/pallas_call | solution.py:283
  34.4 2.5 %collective-permute-done.5.refs_0_ = bf16[128,1152]{1,0:T(8,128)(2,1)S(1)} collective-permute-done((bf16[128,1152]{1,0:T(8,128)(2,1)S(1)}, bf16[128,1152]{1,0:T(8,128)(2,1)S(1)}, u32[]{:S(2)}, u32[]{:S(2)}) %collective-permute-start.5) | collective-permute-done | bytes 294944 | tf_op jit(solution)/shard_map/ppermute | solution.py:535
  36.9 4.3 %collective-permute-done.6.refs_1_ = bf16[128,1152]{1,0:T(8,128)(2,1)S(1)} collective-permute-done((bf16[128,1152]{1,0:T(8,128)(2,1)S(1)}, bf16[128,1152]{1,0:T(8,128)(2,1)S(1)}, u32[]{:S(2)}, u32[]{:S(2)}) %collective-permute-start.6) | collective-permute-done | bytes 294944 | tf_op jit(solution)/shard_map/ppermute | solution.py:535
  41.7 3.3 %collective-permute-start.19 = (bf16[512,768]{1,0:T(8,128)(2,1)S(1)}, bf16[512,768]{1,0:T(8,128)(2,1)S(1)}, u32[]{:S(2)}, u32[]{:S(2)}) collective-permute-start(bf16[512,768]{1,0:T(8,128)(2,1)S(1)} %stack.19.refs_1_.token_ref.refs_2_), channel_id=1, source_target_pairs={{0,8},{1,9},{2,10},{3,11},{4,12},{5,13},{6,14},{7,15},{8,0},{9,1},... | collective-permute-start | bytes 2359304 | tf_op jit(solution)/shard_map/ppermute | solution.py:556
  45.0 2.5 %attend.6 = (bf16[144,384]{1,0:T(8,128)(2,1)S(1)}, bf16[144,384]{1,0:T(8,128)(2,1)S(1)}) custom-call(bf16[512,768]{1,0:T(8,128)(2,1)S(1)} %stack.19.refs_1_.token_ref.refs_2_, bf16[128,1152]{1,0:T(8,128)(2,1)S(1)} %collective-permute-done.5.refs_0_, bf16[128,1152]{1,0:T(8,128)(2,1)S(1)} %collective-permute-done.6.refs_1_, ...), custom_call_target="tpu_custom_call" | custom-call | flops 4000000000 | bytes 4000000 | tf_op jit(solution)/shard_map/attend/pallas_call | solution.py:463
  48.7 2.0 %collective-permute-start.13 = (bf16[144,384]{1,0:T(8,128)(2,1)S(1)}, bf16[144,384]{1,0:T(8,128)(2,1)S(1)}, u32[]{:S(2)}, u32[]{:S(2)}) collective-permute-start(bf16[144,384]{1,0:T(8,128)(2,1)S(1)} %get-tuple-element.54), channel_id=1, source_target_pairs={{0,6},{1,7},{2,0},{3,1},{4,2},{5,3},{6,4},{7,5},{8,14},{9,15},{10,... | collective-permute-start | bytes 331784 | tf_op jit(solution)/shard_map/ppermute | solution.py:535
  50.7 1.6 %attend.7.token_ref = bf16[144,384]{1,0:T(8,128)(2,1)S(1)} custom-call(bf16[144,384]{1,0:T(8,128)(2,1)S(1)} %get-tuple-element.52.token_ref, bf16[128,1152]{1,0:T(8,128)(2,1)S(1)} %collective-permute-done.7.refs_2_.refs_0_, bf16[512,768]{1,0:T(8,128)(2,1)S(1)} %stack.18.token_ref.refs_2_.refs_1_, ...), custom_call_target="tpu_custom_call" | custom-call | flops 4000000000 | bytes 4000000 | tf_op jit(solution)/shard_map/attend/pallas_call | solution.py:463
  52.4 1.6 %attend.8.a0 = bf16[144,384]{1,0:T(8,128)(2,1)S(1)} custom-call(bf16[144,384]{1,0:T(8,128)(2,1)S(1)} %attend.7.token_ref, bf16[128,1152]{1,0:T(8,128)(2,1)S(1)} %get-tuple-element.48.refs_0_.refs_4_.refs_8_.refs_3_, bf16[512,768]{1,0:T(8,128)(2,1)S(1)} %stack.18.token_ref.refs_2_.refs_1_, bf16[512,768]{1,0:T(8,128)(2,1)S(1)} %collective-permute-done.8.refs_3_.refs_2_, ...), custom_call_target="tpu_custom_call" | custom-call | flops 4000000000 | bytes 4000000 | tf_op jit(solution)/shard_map/attend/pallas_call | solution.py:463
  54.1 1.3 %collective-permute-done.13.a1 = bf16[144,384]{1,0:T(8,128)(2,1)S(1)} collective-permute-done((bf16[144,384]{1,0:T(8,128)(2,1)S(1)}, bf16[144,384]{1,0:T(8,128)(2,1)S(1)}, u32[]{:S(2)}, u32[]{:S(2)}) %collective-permute-start.13) | collective-permute-done | bytes 110624 | tf_op jit(solution)/shard_map/ppermute | solution.py:535
  55.5 1.8 %early_output.2.early_ref = f32[128,1536]{1,0:T(8,128)S(1)} custom-call(s32[5]{0:T(128)S(1)} %pad_add_fusion.place_ref, bf16[144,384]{1,0:T(8,128)(2,1)S(1)} %collective-permute-done.12.a2, bf16[144,384]{1,0:T(8,128)(2,1)S(1)} %collective-permute-done.13.a1, bf16[144,384]{1,0:T(8,128)(2,1)S(1)} %attend.8.a0, bf16[1536,1536]{1,0:T(8,128)(2,1)S(1)} %bitcast.6, ...), custom_call_target="tpu_custom_call" | custom-call | flops 3000000000 | bytes 3000000 | tf_op jit(solution)/shard_map/early_output/pallas_call | solution.py:501
  60.3 2.0 %collective-permute-start.18 = (bf16[512,768]{1,0:T(8,128)(2,1)S(1)}, bf16[512,768]{1,0:T(8,128)(2,1)S(1)}, u32[]{:S(2)}, u32[]{:S(2)}) collective-permute-start(bf16[512,768]{1,0:T(8,128)(2,1)S(1)} %stack.19.refs_1_.token_ref.refs_2_), channel_id=1, source_target_pairs={{0,1},{1,0},{2,3},{3,2},{4,5},{5,4},{6,7},{7,6},{8,9},{9,8},{10,11... | collective-permute-start | bytes 2359304 | tf_op jit(solution)/shard_map/ppermute | solution.py:557
  62.3 2.0 %next_queries.1 = (f32[128,1536]{1,0:T(8,128)S(1)}, bf16[128,1536]{1,0:T(8,128)(2,1)S(1)}, bf16[128,384]{1,0:T(8,128)(2,1)S(1)}, bf16[128,384]{1,0:T(8,128)(2,1)...) custom-call(s32[5]{0:T(128)S(1)} %pad_add_fusion.place_ref, ...), custom_call_target="tpu_custom_call" | custom-call | flops 100000000 | bytes 100000 | tf_op jit(solution)/shard_map/next_queries/pallas_call | solution.py:304
  64.4 5.4 %collective-permute-start.20 = (bf16[512,768]{1,0:T(8,128)(2,1)S(1)}, bf16[512,768]{1,0:T(8,128)(2,1)S(1)}, u32[]{:S(2)}, u32[]{:S(2)}) collective-permute-start(bf16[512,768]{1,0:T(8,128)(2,1)S(1)} %hold.3.refs_4_.refs_3_), channel_id=1, source_target_pairs={{0,1},{1,0},{2,3},{3,2},{4,5},{5,4},{6,7},{7,6},{8,9},{9,8},{10,11... | collective-permute-start | bytes 2359304 | tf_op jit(solution)/shard_map/ppermute | solution.py:574
  70.9 4.9 %collective-permute-start.17 = (bf16[128,384]{1,0:T(8,128)(2,1)S(1)}, bf16[128,384]{1,0:T(8,128)(2,1)S(1)}, u32[]{:S(2)}, u32[]{:S(2)}) collective-permute-start(bf16[128,384]{1,0:T(8,128)(2,1)S(1)} %get-tuple-element.64.refs_1_), channel_id=1, source_target_pairs={{0,2},{1,3},{2,4},{3,5},{4,6},{5,7},{6,0},{7,1},{8,10},{9,11},{10,... | collective-permute-start | bytes 294920 | tf_op jit(solution)/shard_map/ppermute | solution.py:535
  75.9 2.7 %last_keys.1 = (bf16[128,768]{1,0:T(8,128)(2,1)S(1)}, bf16[128,768]{1,0:T(8,128)(2,1)S(1)}, bf16[128,768]{1,0:T(8,128)(2,1)S(1)}, bf16[128,768]{1,0:T(8,128)(2,1)S(1)}, bf16[128,3072]{1,0:T(8,128)(2,1)}) custom-call(s32[5]{0:T(128)S(1)} %pad_add_fusion.place_ref, bf16[128,1536]{1,0:T(8,128)(2,1)S(1)} %get-tuple-element.61.normed_ref.token_ref.refs_12_, ...), custom_call_target="tpu_custom_call" | custom-call | flops 100000000 | bytes 100000 | tf_op jit(solution)/shard_map/last_keys/pallas_call | solution.py:382
  79.5 2.5 %attend.9 = (bf16[144,384]{1,0:T(8,128)(2,1)S(1)}, bf16[144,384]{1,0:T(8,128)(2,1)S(1)}) custom-call(bf16[128,768]{1,0:T(8,128)(2,1)S(1)} %get-tuple-element.62.token_ref.refs_5_.refs_9_, bf16[128,384]{1,0:T(8,128)(2,1)S(1)} %collective-permute-done.16.refs_0_, bf16[128,384]{1,0:T(8,128)(2,1)S(1)} %collective-permute-done.17.refs_1_, ...), custom_call_target="tpu_custom_call" | custom-call | flops 4000000000 | bytes 4000000 | tf_op jit(solution)/shard_map/attend/pallas_call | solution.py:463
  82.0 2.1 %collective-permute-start.23 = (bf16[144,384]{1,0:T(8,128)(2,1)S(1)}, bf16[144,384]{1,0:T(8,128)(2,1)S(1)}, u32[]{:S(2)}, u32[]{:S(2)}) collective-permute-start(bf16[144,384]{1,0:T(8,128)(2,1)S(1)} %get-tuple-element.66.token_ref), channel_id=1, source_target_pairs={{0,4},{1,5},{2,6},{3,7},{4,0},{5,1},{6,2},{7,3},{8,12},{9,13},{10,... | collective-permute-start | bytes 331784 | tf_op jit(solution)/shard_map/ppermute | solution.py:535
  84.1 2.6 %collective-permute-start.24 = (bf16[144,384]{1,0:T(8,128)(2,1)S(1)}, bf16[144,384]{1,0:T(8,128)(2,1)S(1)}, u32[]{:S(2)}, u32[]{:S(2)}) collective-permute-start(bf16[144,384]{1,0:T(8,128)(2,1)S(1)} %get-tuple-element.73), channel_id=1, source_target_pairs={{0,6},{1,7},{2,0},{3,1},{4,2},{5,3},{6,4},{7,5},{8,14},{9,15},{10,... | collective-permute-start | bytes 331784 | tf_op jit(solution)/shard_map/ppermute | solution.py:535
  86.8 1.6 %attend.10.token_ref = bf16[144,384]{1,0:T(8,128)(2,1)S(1)} custom-call(bf16[144,384]{1,0:T(8,128)(2,1)S(1)} %get-tuple-element.66.token_ref, bf16[128,384]{1,0:T(8,128)(2,1)S(1)} %collective-permute-done.21.refs_0_, bf16[512,768]{1,0:T(8,128)(2,1)S(1)} %stack.19.refs_1_.token_ref.refs_2_, bf16[512,768]{1,0:T(8,128)(2,1)S(1)} %collective-permute-done.18.refs_3_.refs_2_, ...), custom_call_target="tpu_custom_call" | custom-call | flops 4000000000 | bytes 4000000 | tf_op jit(solution)/shard_map/attend/pallas_call | solution.py:463
  88.4 1.6 %attend.11.a0 = bf16[144,384]{1,0:T(8,128)(2,1)S(1)} custom-call(bf16[144,384]{1,0:T(8,128)(2,1)S(1)} %attend.10.token_ref, bf16[128,384]{1,0:T(8,128)(2,1)S(1)} %get-tuple-element.65.refs_1_.refs_0_, bf16[512,768]{1,0:T(8,128)(2,1)S(1)} %stack.19.refs_1_.token_ref.refs_2_, bf16[512,768]{1,0:T(8,128)(2,1)S(1)} %collective-permute-done.18.refs_3_.refs_2_, ...), custom_call_target="tpu_custom_call" | custom-call | flops 4000000000 | bytes 4000000 | tf_op jit(solution)/shard_map/attend/pallas_call | solution.py:463
  90.0 1.8 %early_output.3.early_ref = f32[128,1536]{1,0:T(8,128)S(1)} custom-call(s32[5]{0:T(128)S(1)} %pad_add_fusion.place_ref, bf16[144,384]{1,0:T(8,128)(2,1)S(1)} %collective-permute-done.23.a2, bf16[144,384]{1,0:T(8,128)(2,1)S(1)} %collective-permute-done.24.a1, bf16[144,384]{1,0:T(8,128)(2,1)S(1)} %attend.11.a0, bf16[1536,1536]{1,0:T(8,128)(2,1)S(1)} %bitcast.6, ...), custom_call_target="tpu_custom_call" | custom-call | flops 3000000000 | bytes 3000000 | tf_op jit(solution)/shard_map/early_output/pallas_call | solution.py:501
  91.8 2.6 %collective-permute-done.22.away = bf16[144,384]{1,0:T(8,128)(2,1)S(1)} collective-permute-done((bf16[144,384]{1,0:T(8,128)(2,1)S(1)}, bf16[144,384]{1,0:T(8,128)(2,1)S(1)}, u32[]{:S(2)}, u32[]{:S(2)}) %collective-permute-start.22) | collective-permute-done | bytes 110624 | tf_op jit(solution)/shard_map/ppermute | solution.py:535
  94.3 1.9 %output.3 = bf16[128,1536]{1,0:T(8,128)(2,1)} custom-call(s32[5]{0:T(128)S(1)} %pad_add_fusion.place_ref, bf16[144,384]{1,0:T(8,128)(2,1)S(1)} %collective-permute-done.22.away, bf16[1536,1536]{1,0:T(8,128)(2,1)S(1)} %bitcast.6, f32[128,1536]{1,0:T(8,128)S(1)} %get-tuple-element.71.summed_ref, f32[128,512]{1,0:T(8,128)S(1)} %get-tuple-element.72.lse_ref, ...), custom_call_target="tpu_custom_call" | custom-call | flops 100000000 | bytes 100000 | tf_op jit(solution)/shard_map/output/pallas_call | solution.py:526
  (63 shorter events, 11.7 us)
Async XLA Ops:
  1.4 19.5 %slice-start = ((s8[14155776]{0:T(1024)(128)(4,1)}), s8[4194304]{0:T(1024)(128)(4,1)S(1)}, s32[]{:S(2)}) async-start(s8[14155776]{0:T(1024)(128)(4,1)} %bitcast.3), calls=%async_computation | async-start | bytes 8388608
  1.4 19.5 %slice-start.1 = ((s8[14155776]{0:T(1024)(128)(4,1)}), s8[4194304]{0:T(1024)(128)(4,1)S(1)}, s32[]{:S(2)}) async-start(s8[14155776]{0:T(1024)(128)(4,1)} %bitcast.3), calls=%async_computation.1 | async-start | bytes 8388608
  1.4 19.5 %slice-start.6 = ((s8[4718592]{0:T(1024)(128)(4,1)}), s8[4194304]{0:T(1024)(128)(4,1)S(1)}, s32[]{:S(2)}) async-start(s8[4718592]{0:T(1024)(128)(4,1)} %bitcast.7), calls=%async_computation.6 | async-start | bytes 8388608
  3.7 9.8 %collective-permute-start.2 = (bf16[128,768]{1,0:T(8,128)(2,1)S(1)}, bf16[128,768]{1,0:T(8,128)(2,1)S(1)}, u32[]{:S(2)}, u32[]{:S(2)}) collective-permute-start(bf16[128,768]{1,0:T(8,128)(2,1)S(1)} %get-tuple-element.41), channel_id=1, source_target_pairs={{0,4},{1,5},{2,6},{3,7},{4,0},{5,1},{6,2},{7,3},{8,12},{9,13},{10,... | collective-permute-start | bytes 589832 | tf_op jit(solution)/shard_map/ppermute | solution.py:535
  7.7 9.5 %collective-permute-start.3 = (bf16[128,768]{1,0:T(8,128)(2,1)S(1)}, bf16[128,768]{1,0:T(8,128)(2,1)S(1)}, u32[]{:S(2)}, u32[]{:S(2)}) collective-permute-start(bf16[128,768]{1,0:T(8,128)(2,1)S(1)} %get-tuple-element.42), channel_id=1, source_target_pairs={{0,2},{1,3},{2,4},{3,5},{4,6},{5,7},{6,0},{7,1},{8,10},{9,11},{10,... | collective-permute-start | bytes 589832 | tf_op jit(solution)/shard_map/ppermute | solution.py:535
  8.7 12.2 %slice-start.2 = ((s8[14155776]{0:T(1024)(128)(4,1)}), s8[4194304]{0:T(1024)(128)(4,1)S(1)}, s32[]{:S(2)}) async-start(s8[14155776]{0:T(1024)(128)(4,1)} %bitcast.3), calls=%async_computation.2 | async-start | bytes 8388608
  8.7 12.2 %slice-start.7 = ((s8[4718592]{0:T(1024)(128)(4,1)}), s8[524288]{0:T(1024)(128)(4,1)S(1)}, s32[]{:S(2)}) async-start(s8[4718592]{0:T(1024)(128)(4,1)} %bitcast.7), calls=%async_computation.7 | async-start | bytes 1048576
  8.8 8.8 %collective-permute-start.4 = (bf16[128,768]{1,0:T(8,128)(2,1)S(1)}, bf16[128,768]{1,0:T(8,128)(2,1)S(1)}, u32[]{:S(2)}, u32[]{:S(2)}) collective-permute-start(bf16[128,768]{1,0:T(8,128)(2,1)S(1)} %get-tuple-element.43), channel_id=1, source_target_pairs={{0,6},{1,7},{2,0},{3,1},{4,2},{5,3},{6,4},{7,5},{8,14},{9,15},{10,... | collective-permute-start | bytes 589832 | tf_op jit(solution)/shard_map/ppermute | solution.py:535
  11.0 10.0 %collective-permute-start = (bf16[80,1536]{1,0:T(8,128)(2,1)S(1)}, bf16[80,1536]{1,0:T(8,128)(2,1)S(1)}, u32[]{:S(2)}, u32[]{:S(2)}) collective-permute-start(bf16[80,1536]{1,0:T(8,128)(2,1)S(1)} %get-tuple-element.39), channel_id=1, source_target_pairs={{0,1},{1,0},{2,3},{3,2},{4,5},{5,4},{6,7},{7,6},{8,9},{9,8},{10,11... | collective-permute-start | bytes 737288 | tf_op jit(solution)/shard_map/ppermute | solution.py:544
  11.0 10.0 %collective-permute-start.1 = (bf16[80,1536]{1,0:T(8,128)(2,1)S(1)}, bf16[80,1536]{1,0:T(8,128)(2,1)S(1)}, u32[]{:S(2)}, u32[]{:S(2)}) collective-permute-start(bf16[80,1536]{1,0:T(8,128)(2,1)S(1)} %get-tuple-element.40), channel_id=1, source_target_pairs={{1,2},{3,4},{5,6},{7,8},{9,10},{11,12},{13,14},{2,1},{4,3},{6,5},{... | collective-permute-start | bytes 737288 | tf_op jit(solution)/shard_map/ppermute | solution.py:543
  17.6 13.6 %copy-start.1 = (s32[16]{0:T(128)S(1)}, s32[16]{0:T(128)}, u32[]{:S(2)}) copy-start(s32[16]{0:T(128)} %counts_ref.1) | copy-start | bytes 196
  17.6 23.9 %collective-permute-start.9 = (bf16[512,768]{1,0:T(8,128)(2,1)S(1)}, bf16[512,768]{1,0:T(8,128)(2,1)S(1)}, u32[]{:S(2)}, u32[]{:S(2)}) collective-permute-start(bf16[512,768]{1,0:T(8,128)(2,1)S(1)} %stack.18.token_ref.refs_2_.refs_1_), channel_id=1, source_target_pairs={{0,8},{1,9},{2,10},{3,11},{4,12},{5,13},{6,14},{7,15},{8,0},{9,1},... | collective-permute-start | bytes 2359304 | tf_op jit(solution)/shard_map/ppermute | solution.py:547
  25.3 11.6 %collective-permute-start.5 = (bf16[128,1152]{1,0:T(8,128)(2,1)S(1)}, bf16[128,1152]{1,0:T(8,128)(2,1)S(1)}, u32[]{:S(2)}, u32[]{:S(2)}) collective-permute-start(bf16[128,1152]{1,0:T(8,128)(2,1)S(1)} %get-tuple-element.45.refs_2_.refs_6_.refs_10_), channel_id=1, source_target_pairs={{0,4},{1,5},{2,6},{3,7},{4,0},{5,1},{6,2},{7,3},{8,12},{9,13},{10,... | collective-permute-start | bytes 884744 | tf_op jit(solution)/shard_map/ppermute | solution.py:535
  28.0 13.2 %collective-permute-start.6 = (bf16[128,1152]{1,0:T(8,128)(2,1)S(1)}, bf16[128,1152]{1,0:T(8,128)(2,1)S(1)}, u32[]{:S(2)}, u32[]{:S(2)}) collective-permute-start(bf16[128,1152]{1,0:T(8,128)(2,1)S(1)} %get-tuple-element.46.refs_1_.refs_5_.refs_9_), channel_id=1, source_target_pairs={{0,2},{1,3},{2,4},{3,5},{4,6},{5,7},{6,0},{7,1},{8,10},{9,11},{10,... | collective-permute-start | bytes 884744 | tf_op jit(solution)/shard_map/ppermute | solution.py:535
  28.9 12.6 %collective-permute-start.7 = (bf16[128,1152]{1,0:T(8,128)(2,1)S(1)}, bf16[128,1152]{1,0:T(8,128)(2,1)S(1)}, u32[]{:S(2)}, u32[]{:S(2)}) collective-permute-start(bf16[128,1152]{1,0:T(8,128)(2,1)S(1)} %get-tuple-element.47.refs_3_.refs_7_.refs_11_), channel_id=1, source_target_pairs={{0,6},{1,7},{2,0},{3,1},{4,2},{5,3},{6,4},{7,5},{8,14},{9,15},{10,... | collective-permute-start | bytes 884744 | tf_op jit(solution)/shard_map/ppermute | solution.py:535
  31.2 13.7 %collective-permute-start.8 = (bf16[512,768]{1,0:T(8,128)(2,1)S(1)}, bf16[512,768]{1,0:T(8,128)(2,1)S(1)}, u32[]{:S(2)}, u32[]{:S(2)}) collective-permute-start(bf16[512,768]{1,0:T(8,128)(2,1)S(1)} %stack.18.token_ref.refs_2_.refs_1_), channel_id=1, source_target_pairs={{0,1},{1,0},{2,3},{3,2},{4,5},{5,4},{6,7},{7,6},{8,9},{9,8},{10,11... | collective-permute-start | bytes 2359304 | tf_op jit(solution)/shard_map/ppermute | solution.py:548
  41.6 3.4 %collective-permute-start.10 = (bf16[512,768]{1,0:T(8,128)(2,1)S(1)}, bf16[512,768]{1,0:T(8,128)(2,1)S(1)}, u32[]{:S(2)}, u32[]{:S(2)}) collective-permute-start(bf16[512,768]{1,0:T(8,128)(2,1)S(1)} %hold.2.refs_4_.refs_3_), channel_id=1, source_target_pairs={{0,1},{1,0},{2,3},{3,2},{4,5},{5,4},{6,7},{7,6},{8,9},{9,8},{10,11... | collective-permute-start | bytes 2359304 | tf_op jit(solution)/shard_map/ppermute | solution.py:559
  41.7 22.7 %collective-permute-start.19 = (bf16[512,768]{1,0:T(8,128)(2,1)S(1)}, bf16[512,768]{1,0:T(8,128)(2,1)S(1)}, u32[]{:S(2)}, u32[]{:S(2)}) collective-permute-start(bf16[512,768]{1,0:T(8,128)(2,1)S(1)} %stack.19.refs_1_.token_ref.refs_2_), channel_id=1, source_target_pairs={{0,8},{1,9},{2,10},{3,11},{4,12},{5,13},{6,14},{7,15},{8,0},{9,1},... | collective-permute-start | bytes 2359304 | tf_op jit(solution)/shard_map/ppermute | solution.py:556
  47.5 6.7 %collective-permute-start.12 = (bf16[144,384]{1,0:T(8,128)(2,1)S(1)}, bf16[144,384]{1,0:T(8,128)(2,1)S(1)}, u32[]{:S(2)}, u32[]{:S(2)}) collective-permute-start(bf16[144,384]{1,0:T(8,128)(2,1)S(1)} %get-tuple-element.52.token_ref), channel_id=1, source_target_pairs={{0,4},{1,5},{2,6},{3,7},{4,0},{5,1},{6,2},{7,3},{8,12},{9,13},{10,... | collective-permute-start | bytes 331784 | tf_op jit(solution)/shard_map/ppermute | solution.py:535
  48.7 6.7 %collective-permute-start.13 = (bf16[144,384]{1,0:T(8,128)(2,1)S(1)}, bf16[144,384]{1,0:T(8,128)(2,1)S(1)}, u32[]{:S(2)}, u32[]{:S(2)}) collective-permute-start(bf16[144,384]{1,0:T(8,128)(2,1)S(1)} %get-tuple-element.54), channel_id=1, source_target_pairs={{0,6},{1,7},{2,0},{3,1},{4,2},{5,3},{6,4},{7,5},{8,14},{9,15},{10,... | collective-permute-start | bytes 331784 | tf_op jit(solution)/shard_map/ppermute | solution.py:535
  52.3 6.0 %collective-permute-start.11 = (bf16[144,384]{1,0:T(8,128)(2,1)S(1)}, bf16[144,384]{1,0:T(8,128)(2,1)S(1)}, u32[]{:S(2)}, u32[]{:S(2)}) collective-permute-start(bf16[144,384]{1,0:T(8,128)(2,1)S(1)} %attend.7.token_ref), channel_id=1, source_target_pairs={{0,2},{1,3},{2,4},{3,5},{4,6},{5,7},{6,0},{7,1},{8,10},{9,11},{10,... | collective-permute-start | bytes 331784 | tf_op jit(solution)/shard_map/ppermute | solution.py:535
  57.2 5.1 %copy-start = (f32[3,1536]{1,0:T(4,128)S(1)}, f32[3,1536]{1,0:T(4,128)}, u32[]{:S(2)}) copy-start(f32[3,1536]{1,0:T(4,128)} %conv_ref.1) | copy-start | bytes 55300
  59.5 2.8 %collective-permute-start.14 = (bf16[80,1536]{1,0:T(8,128)(2,1)S(1)}, bf16[80,1536]{1,0:T(8,128)(2,1)S(1)}, u32[]{:S(2)}, u32[]{:S(2)}) collective-permute-start(bf16[80,1536]{1,0:T(8,128)(2,1)S(1)} %get-tuple-element.57), channel_id=1, source_target_pairs={{0,1},{1,0},{2,3},{3,2},{4,5},{5,4},{6,7},{7,6},{8,9},{9,8},{10,11... | collective-permute-start | bytes 737288 | tf_op jit(solution)/shard_map/ppermute | solution.py:568
  59.6 2.7 %collective-permute-start.15 = (bf16[80,1536]{1,0:T(8,128)(2,1)S(1)}, bf16[80,1536]{1,0:T(8,128)(2,1)S(1)}, u32[]{:S(2)}, u32[]{:S(2)}) collective-permute-start(bf16[80,1536]{1,0:T(8,128)(2,1)S(1)} %get-tuple-element.58), channel_id=1, source_target_pairs={{1,2},{3,4},{5,6},{7,8},{9,10},{11,12},{13,14},{2,1},{4,3},{6,5},{... | collective-permute-start | bytes 737288 | tf_op jit(solution)/shard_map/ppermute | solution.py:567
  60.3 19.1 %collective-permute-start.18 = (bf16[512,768]{1,0:T(8,128)(2,1)S(1)}, bf16[512,768]{1,0:T(8,128)(2,1)S(1)}, u32[]{:S(2)}, u32[]{:S(2)}) collective-permute-start(bf16[512,768]{1,0:T(8,128)(2,1)S(1)} %stack.19.refs_1_.token_ref.refs_2_), channel_id=1, source_target_pairs={{0,1},{1,0},{2,3},{3,2},{4,5},{5,4},{6,7},{7,6},{8,9},{9,8},{10,11... | collective-permute-start | bytes 2359304 | tf_op jit(solution)/shard_map/ppermute | solution.py:557
  64.4 15.1 %collective-permute-start.20 = (bf16[512,768]{1,0:T(8,128)(2,1)S(1)}, bf16[512,768]{1,0:T(8,128)(2,1)S(1)}, u32[]{:S(2)}, u32[]{:S(2)}) collective-permute-start(bf16[512,768]{1,0:T(8,128)(2,1)S(1)} %hold.3.refs_4_.refs_3_), channel_id=1, source_target_pairs={{0,1},{1,0},{2,3},{3,2},{4,5},{5,4},{6,7},{7,6},{8,9},{9,8},{10,11... | collective-permute-start | bytes 2359304 | tf_op jit(solution)/shard_map/ppermute | solution.py:574
  69.7 9.7 %collective-permute-start.16 = (bf16[128,384]{1,0:T(8,128)(2,1)S(1)}, bf16[128,384]{1,0:T(8,128)(2,1)S(1)}, u32[]{:S(2)}, u32[]{:S(2)}) collective-permute-start(bf16[128,384]{1,0:T(8,128)(2,1)S(1)} %get-tuple-element.63.refs_2_), channel_id=1, source_target_pairs={{0,4},{1,5},{2,6},{3,7},{4,0},{5,1},{6,2},{7,3},{8,12},{9,13},{10,... | collective-permute-start | bytes 294920 | tf_op jit(solution)/shard_map/ppermute | solution.py:535
  70.9 8.5 %collective-permute-start.17 = (bf16[128,384]{1,0:T(8,128)(2,1)S(1)}, bf16[128,384]{1,0:T(8,128)(2,1)S(1)}, u32[]{:S(2)}, u32[]{:S(2)}) collective-permute-start(bf16[128,384]{1,0:T(8,128)(2,1)S(1)} %get-tuple-element.64.refs_1_), channel_id=1, source_target_pairs={{0,2},{1,3},{2,4},{3,5},{4,6},{5,7},{6,0},{7,1},{8,10},{9,11},{10,... | collective-permute-start | bytes 294920 | tf_op jit(solution)/shard_map/ppermute | solution.py:535
  75.9 10.9 %collective-permute-start.21 = (bf16[128,384]{1,0:T(8,128)(2,1)S(1)}, bf16[128,384]{1,0:T(8,128)(2,1)S(1)}, u32[]{:S(2)}, u32[]{:S(2)}) collective-permute-start(bf16[128,384]{1,0:T(8,128)(2,1)S(1)} %get-tuple-element.67.refs_3_), channel_id=1, source_target_pairs={{0,6},{1,7},{2,0},{3,1},{4,2},{5,3},{6,4},{7,5},{8,14},{9,15},{10,... | collective-permute-start | bytes 294920 | tf_op jit(solution)/shard_map/ppermute | solution.py:535
  82.0 8.0 %collective-permute-start.23 = (bf16[144,384]{1,0:T(8,128)(2,1)S(1)}, bf16[144,384]{1,0:T(8,128)(2,1)S(1)}, u32[]{:S(2)}, u32[]{:S(2)}) collective-permute-start(bf16[144,384]{1,0:T(8,128)(2,1)S(1)} %get-tuple-element.66.token_ref), channel_id=1, source_target_pairs={{0,4},{1,5},{2,6},{3,7},{4,0},{5,1},{6,2},{7,3},{8,12},{9,13},{10,... | collective-permute-start | bytes 331784 | tf_op jit(solution)/shard_map/ppermute | solution.py:535
  84.1 5.8 %collective-permute-start.24 = (bf16[144,384]{1,0:T(8,128)(2,1)S(1)}, bf16[144,384]{1,0:T(8,128)(2,1)S(1)}, u32[]{:S(2)}, u32[]{:S(2)}) collective-permute-start(bf16[144,384]{1,0:T(8,128)(2,1)S(1)} %get-tuple-element.73), channel_id=1, source_target_pairs={{0,6},{1,7},{2,0},{3,1},{4,2},{5,3},{6,4},{7,5},{8,14},{9,15},{10,... | collective-permute-start | bytes 331784 | tf_op jit(solution)/shard_map/ppermute | solution.py:535
  88.3 6.0 %collective-permute-start.22 = (bf16[144,384]{1,0:T(8,128)(2,1)S(1)}, bf16[144,384]{1,0:T(8,128)(2,1)S(1)}, u32[]{:S(2)}, u32[]{:S(2)}) collective-permute-start(bf16[144,384]{1,0:T(8,128)(2,1)S(1)} %attend.10.token_ref), channel_id=1, source_target_pairs={{0,2},{1,3},{2,4},{3,5},{4,6},{5,7},{6,0},{7,1},{8,10},{9,11},{10,... | collective-permute-start | bytes 331784 | tf_op jit(solution)/shard_map/ppermute | solution.py:535
  (3 other events, 11.2 us)
